TPU v7x, 32 devices: a whole 2x2x4 slice. The times are simulated.
32 devices in a mesh: groups: 2 (over x), space: 8 (over z, y), member: 2 (over core).
Axes of the slice: x: 2, y: 2, z: 4, core: 2. Of those that a mesh axis runs over, the one named last changes fastest.
Arguments:
- latent: bfloat16 [8, 512, 1024], P(('groups', 'member'), 'space'), parts along dimension 0, may hold values from -6 to 6
- edge_node_index: int32 [8192, 4], P(('groups', 'space')), parts along dimension 0, may hold values from 0 to 511, as said below
- edge_mask: int32 [8192, 4], P(('groups', 'space')), parts along dimension 0, may hold values 0 or 1
- edge_weight: float32 [8192, 4], P(('groups', 'space')), parts along dimension 0, may hold values from 0.2 to 1
- valid: int32 [8192], P(('groups', 'space')), parts along dimension 0, may hold values 0 or 1
- area: float32 [8192], P(('groups', 'space')), parts along dimension 0, may hold values from 0.3 to 3
- state: float32 [8192, 100], P(('groups', 'space')), parts along dimension 0, may hold values from -6 to 6
- target: float32 [8192, 100], P(('groups', 'space')), parts along dimension 0, may hold values from -8 to 8
- var_weight: float32 [100], replicated, may hold values from 0.1 to 1
- gain: float32 [1024], replicated, may hold values from 0.25 to 1.75
- hidden_weight: bfloat16 [1024, 1024], replicated, may hold values from -0.1875 to 0.1875
- output_weight: bfloat16 [1024, 100], replicated, may hold values from -0.1875 to 0.1875
Outputs:
- loss: float32 [2], P('groups'), parts along dimension 0
- grad_hidden: float32 [2048, 1024], P('groups'), parts along dimension 0
- grad_out: float32 [2048, 100], P('groups'), parts along dimension 0
- grad_gain: float32 [2048], P('groups'), parts along dimension 0
- grad_latent: float32 [8, 512, 1024], P(('groups', 'member'), 'space'), parts along dimension 0
There are 2 independent parts, one for each index of `groups`. A program takes and returns all parts, laid end to end along the dimension named above; an argument that names none is the same for every part. Nothing has to cross between parts.
Inputs may be any that keep to these rules, and one draw needn't show every extreme that they name: `edge_node_index`: grid points p * 512 to (p+1) * 512 - 1 name only mesh nodes from p * 64 - 16 to (p+1) * 64 + 15; within every such block both ends of that range are named where they lie inside the mesh.
All inputs are finite; a program needn't handle non-finite values. No bound on the sum of `edge_mask` or of `valid` on one device may be relied on, other than what follows from the above.
Results may differ from a plain program's by a relative error of at most 0.015.
Values may be sent and summed in bfloat16 or wider, within the bound.
No kernel may reach another device: no remote copies, remote signals or barrier semaphores. Data moves between devices by JAX's collectives and lax.ppermute only.
A program may use at most 64 MiB of HBM per device.

v0:
```python
import jax
import jax.numpy as jnp
from jax import lax
from jax.sharding import PartitionSpec as P

RIM = 16


SMOOTH_SQ = 0.01


def with_halo(block, sides, width):
    for axis, dim in sides:
        count = lax.axis_size(axis)
        forward = [(i, i + 1) for i in range(count - 1)]
        backward = [(target, source) for source, target in forward]
        low = lax.ppermute(
            lax.slice_in_dim(block, block.shape[dim] - width, None, axis=dim), axis, forward
        )
        high = lax.ppermute(lax.slice_in_dim(block, 0, width, axis=dim), axis, backward)
        block = jnp.concatenate([low, block, high], axis=dim)
    return block


def from_behind(value, axis, steps):
    count = lax.axis_size(axis)
    first, last = (max(0, -steps), min(count, count - steps))
    return lax.ppermute(value, axis, [(source, source + steps) for source in range(first, last)])


def smooth(diff):
    return jnp.sqrt(diff * diff + SMOOTH_SQ)


def split_parts(values):
    upper = values.astype(jnp.bfloat16)
    lower = (values - upper.astype(jnp.float32)).astype(jnp.bfloat16)
    return (upper, lower)


def local(
    latent,
    edge_node_index,
    edge_mask,
    edge_weight,
    valid,
    area,
    state,
    target,
    var_weight,
    gain,
    hidden_weight,
    output_weight,
):
    members, nodes, width = latent.shape
    points = state.shape[0]
    extended = with_halo(latent, (("space", 1),), RIM)
    span = nodes + 2 * RIM
    anchor = lax.axis_index("space") * nodes - RIM
    local_index = edge_node_index - anchor
    coefficient = edge_weight * edge_mask.astype(jnp.float32)
    slots = jnp.arange(span, dtype=jnp.int32)
    adjacency = jnp.zeros((points, span), jnp.float32)
    for slot in range(edge_node_index.shape[1]):
        adjacency = adjacency + coefficient[:, slot][:, None] * (
            local_index[:, slot][:, None] == slots[None, :]
        ).astype(jnp.float32)
    adj_upper, adj_lower = split_parts(adjacency)
    summed = jnp.einsum("ge,mec->mgc", adj_upper, extended, preferred_element_type=jnp.float32)
    summed = summed + jnp.einsum(
        "ge,mec->mgc", adj_lower, extended, preferred_element_type=jnp.float32
    )
    summed = summed.reshape(members * points, width)
    centered_values = summed - jnp.mean(summed, axis=1, keepdims=True)
    inverse_deviation = 1.0 / jnp.sqrt(
        jnp.mean(centered_values * centered_values, axis=1, keepdims=True) + 1e-05
    )
    standardized_input = centered_values * inverse_deviation
    normed_rows = (standardized_input * gain[None, :]).astype(jnp.bfloat16)
    preactivation = jnp.dot(normed_rows, hidden_weight, preferred_element_type=jnp.float32)
    hidden_rows = jax.nn.silu(preactivation).astype(jnp.bfloat16)
    outputs = jnp.dot(hidden_rows, output_weight, preferred_element_type=jnp.float32)
    preds = state[None] + outputs.reshape(members, points, -1)
    ensemble = lax.all_gather(preds, "member", axis=0, tiled=True)
    total = ensemble.shape[0]
    weight = (valid.astype(jnp.float32) * area / points)[:, None] * var_weight[None, :]
    own_err = preds - target[None]
    pair = preds[:, None] - ensemble[None]
    loss_local = jnp.sum(
        weight
        * (
            jnp.sum(smooth(own_err), axis=0) / total
            - jnp.sum(smooth(pair), axis=(0, 1)) / (2.0 * total * (total - 1))
        )
    )
    gpred = (
        weight[None]
        * (
            own_err / smooth(own_err) / total
            - jnp.sum(pair / smooth(pair), axis=1) / (total * (total - 1))
        )
    ).astype(jnp.bfloat16)
    gpred = gpred.reshape(members * points, -1)
    part_out = jnp.dot(hidden_rows.T, gpred, preferred_element_type=jnp.float32)
    ghid = jnp.dot(gpred, output_weight.T, preferred_element_type=jnp.float32)
    sig = jax.nn.sigmoid(preactivation)
    gpre = (ghid * sig * (1.0 + preactivation * (1.0 - sig))).astype(jnp.bfloat16)
    part_hidden = jnp.dot(normed_rows.T, gpre, preferred_element_type=jnp.float32)
    grad_preact_normed = jnp.dot(gpre, hidden_weight.T, preferred_element_type=jnp.float32)
    partial_gain = jnp.sum(grad_preact_normed * standardized_input, axis=0)
    scaled_rows = grad_preact_normed * gain[None, :]
    grad_preact = inverse_deviation * (
        scaled_rows
        - jnp.mean(scaled_rows, axis=1, keepdims=True)
        - standardized_input * jnp.mean(scaled_rows * standardized_input, axis=1, keepdims=True)
    )
    grad_preact = grad_preact.reshape(members, points, width)
    gz_upper, gz_lower = split_parts(grad_preact)
    grad_ext = jnp.einsum("ge,mgc->mec", adj_upper, gz_upper, preferred_element_type=jnp.float32)
    grad_ext = grad_ext + jnp.einsum(
        "ge,mgc->mec", adj_upper, gz_lower, preferred_element_type=jnp.float32
    )
    grad_ext = grad_ext + jnp.einsum(
        "ge,mgc->mec", adj_lower, gz_upper, preferred_element_type=jnp.float32
    )
    lower_rim = grad_ext[:, :RIM]
    upper_rim = grad_ext[:, RIM + nodes :]
    from_below = from_behind(upper_rim.astype(jnp.bfloat16), "space", 1).astype(upper_rim.dtype)
    from_above = from_behind(lower_rim.astype(jnp.bfloat16), "space", -1).astype(lower_rim.dtype)
    grad_latent = grad_ext[:, RIM : RIM + nodes]
    grad_latent = grad_latent.at[:, :RIM].add(from_below)
    grad_latent = grad_latent.at[:, nodes - RIM :].add(from_above)
    grad_hidden, grad_out, grad_gain, loss = lax.psum(
        (part_hidden, part_out, partial_gain, loss_local), ("space", "member")
    )
    return (loss.reshape(1), grad_hidden, grad_out, grad_gain, grad_latent)


def solution(mesh):
    in_specs = (
        P(("groups", "member"), "space", None),
        P(("groups", "space"), None),
        P(("groups", "space"), None),
        P(("groups", "space"), None),
        P(("groups", "space")),
        P(("groups", "space")),
        P(("groups", "space"), None),
        P(("groups", "space"), None),
        P(),
        P(),
        P(),
        P(),
    )
    out_specs = (
        P("groups"),
        P("groups", None),
        P("groups", None),
        P("groups"),
        P(("groups", "member"), "space", None),
    )
    return jax.shard_map(local, mesh=mesh, in_specs=in_specs, out_specs=out_specs, check_vma=False)
```

profile of v0, /device:TPU:0, one launch (start us, length us, event | category | flops | bytes accessed | tf_op | source)
XLA Modules:
  0.0 190.7 jit_solution(3367471380881891875)
XLA Ops:
  7.2 1.1 fusion.33
  8.3 1.3 collective-permute-start.1
  9.6 5.5 %collective-permute-start = (bf16[2,16,1024]{2,1,0:T(8,128)(2,1)S(1)}, bf16[2,16,1024]{2,1,0:T(8,128)(2,1)S(1)}, u32[]{:S(2)}, u32[]{:S(2)}) collective-permute-start(bf16[2,16,1024]{2,1,0:T(8,128)(2,1)S(1)} %get-tuple-element.43), channel_id=1, source_target_pairs={{0,2},{2,4},{4,6},{6,8},{8,10},{10,12},{12,14},{1,3},{3,5},{5,7},{... | collective-permute-start | bytes 196616 | tf_op jit(solution)/shard_map/ppermute | solution.py:17
  15.1 0.7 broadcast_subtract_fusion
  15.8 0.7 convert_multiply_fusion
  16.6 1.1 broadcast_bitcast_fusion.1
  17.6 1.1 broadcast_bitcast_fusion
  18.7 0.7 multiply_multiply_fusion
  20.0 0.8 fusion.25
  20.7 0.9 bitcast_reduce_fusion
  23.6 4.7 %multiply_convert_fusion.1 = (bf16[1024,1024]{1,0:T(8,128)(2,1)S(1)}, f32[1024,1024]{1,0:T(8,128)}) fusion(bf16[1024,1024]{1,0:T(8,128)(2,1)S(1)} %multiply_convert_fusion.2, bf16[1024,1024]{1,0:T(8,128)(2,1)S(1)} %copy-done), kind=kOutput, calls=%fused_computation.11 | convolution fusion | flops 2152726528 | bytes 10485760 | tf_op jit(solution)/shard_map/dot_general | solution.py:80
  28.3 1.3 copy-done.2
  29.6 0.8 fusion.37
  30.4 1.1 reshape.165
  31.5 1.4 sqrt_reduce_fusion
  32.9 2.6 %all_gather.3 = f32[4,512,100]{1,2,0:T(8,128)S(1)} all-gather(f32[2,512,100]{1,2,0:T(8,128)S(1)} %get-tuple-element.39), channel_id=1, replica_groups=mesh['groups'=2,'space'=8,'member'=2] {'member'}, dimensions={0}, use_global_device_ids=true | all-gather | bytes 1228800 | tf_op jit(solution)/shard_map/all_gather | solution.py:84
  36.1 3.2 %fusion.7 = (f32[2,512,100]{1,2,0:T(8,128)S(1)}, f32[512,100]{0,1:T(8,128)S(1)}) fusion(f32[4,512,100]{1,0,2:T(4,128)S(1)} %copy.25, f32[2,512,100]{1,2,0:T(8,128)S(1)} %get-tuple-element.39), kind=kLoop, calls=%fused_computation.22 | loop fusion | flops 2304000 | bytes 1843200 | tf_op jit(solution)/shard_map/reduce_sum | solution.py:100
  39.9 0.7 broadcast_multiply_fusion.1
  41.2 1.2 fusion.39
  42.5 0.8 copy-done.14
  43.2 1.7 multiply_convert_fusion
  45.0 1.4 copy-done.13
  46.4 4.4 %fusion.38 = f32[1024,1024]{1,0:T(8,128)} fusion(bf16[1024,1024]{1,0:T(8,128)(2,1)S(1)} %copy-done.5, bf16[1024,1024]{1,0:T(8,128)(2,1)S(1)} %multiply_convert_fusion), kind=kOutput, calls=%fused_computation.74 | convolution fusion | flops 2147483648 | bytes 8388608 | tf_op jit(solution)/shard_map/dot_general | solution.py:108
  50.8 7.5 %multiply_reduce_fusion = (f32[1024]{0:T(1024)S(1)}, f32[1024]{0:T(1024)S(1)}, f32[1024]{0:T(1024)S(1)}, f32[1024,1024]{1,0:T(8,128)}) fusion(f32[2,1024,512]{1,2,0:T(8,128)} %copy-done.1, f32[1024]{0:T(1024)S(1)} %copy-done.11, f32[1024]{0:T(1024)S(1)} %bitcast.150, f32[1024]{0:T(1024)S(1)} %bitcast.147, bf16[1024,1024]{1,0:T(8,128)(2,1)} %copy-done.13, ...), kind=kOutput, calls=%fused_computation.8 | convolution fusion | flops 2155869184 | bytes 12607488 | tf_op jit(solution)/shard_map/dot_general | solution.py:109
  58.3 4.1 %subtract_multiply_fusion = f32[1024,1024]{1,0:T(8,128)S(1)} fusion(f32[1024,1024]{1,0:T(8,128)} %get-tuple-element.60, f32[2,1024,512]{1,2,0:T(8,128)} %copy-done.1, f32[1024]{0:T(1024)S(1)} %get-tuple-element.63, f32[1024]{0:T(1024)S(1)} %get-tuple-element.64, f32[1024]{0:T(1024)S(1)} %copy-done.11, f32[1024]{0:T(1024)S(1)} %bitcast.151, f32[1024]{0:T(1024)S(1)} %bitcast.148), kind=kLoop, calls=%fused_computation.7 | loop fusion | flops 7340032 | bytes 12603392 | tf_op jit(solution)/shard_map/mul | solution.py:112
  64.0 0.7 fusion.32
  64.7 4.8 %collective-permute-start.2 = (bf16[2,16,1024]{2,1,0:T(8,128)(2,1)}, bf16[2,16,1024]{2,1,0:T(8,128)(2,1)S(1)}, u32[]{:S(2)}, u32[]{:S(2)}) collective-permute-start(bf16[2,16,1024]{2,1,0:T(8,128)(2,1)} %get-tuple-element.41), channel_id=1, source_target_pairs={{0,2},{2,4},{4,6},{6,8},{8,10},{10,12},{12,14},{1,3},{3,5},{5,7},{... | collective-permute-start | bytes 196616 | tf_op jit(solution)/shard_map/ppermute | solution.py:28
  69.5 1.3 collective-permute-start.3
  70.8 34.3 %all-reduce = (f32[1]{0:T(128)}, f32[1024]{0:T(1024)}) all-reduce(f32[1]{0:T(128)} %bitcast.12, f32[1024]{0:T(1024)S(1)} %get-tuple-element.30), channel_id=1, replica_groups=mesh['groups'=2,'space'=8,'member'=2] {'space','member'}, use_global_device_ids=true, to_apply=%region_5.6 | all-reduce | flops 1025 | bytes 8200 | tf_op jit(solution)/shard_map/psum | solution.py:133
  105.3 73.0 %all-reduce.4.cloned.1.call-done = (f32[1024,1024]{1,0:T(8,128)}, f32[1024,100]{0,1:T(8,128)}) async-done(((f32[1024,1024]{1,0:T(8,128)}, f32[1024,100]{0,1:T(8,128)}), (f32[1024,1024]{1,0:T(8,128)}, f32[1024,100]{0,1:T(8,128)})) %all-reduce.4.cloned.1.call-update) | async-done | bytes 4603920 | tf_op jit(solution)/shard_map/psum | solution.py:133
  178.2 4.8 %copy.47 = f32[1024,1024]{1,0:T(8,128)} copy(f32[1024,1024]{1,0:T(8,128)} %get-tuple-element.66) | data formatting | bytes 8388608
  183.1 0.8 copy.48
  (64 shorter events, 5.8 us)
Async XLA Ops:
  7.2 16.5 %copy-start = (bf16[1024,1024]{1,0:T(8,128)(2,1)S(1)}, bf16[1024,1024]{1,0:T(8,128)(2,1)}, u32[]{:S(2)}) copy-start(bf16[1024,1024]{1,0:T(8,128)(2,1)} %param.26) | copy-start | bytes 6291460
  7.2 12.7 %copy-start.7 = (bf16[2,64,1024]{2,1,0:T(8,128)(2,1)S(1)}, bf16[2,64,1024]{2,1,0:T(8,128)(2,1)}, u32[]{:S(2)}) copy-start(bf16[2,64,1024]{2,1,0:T(8,128)(2,1)} %param.16) | copy-start | bytes 786436
  7.2 171.0 %all-reduce.4.cloned.1.call-start = ((), (), s32[]{:S(2)}) async-start(), calls=%async_computation | async-start | bytes 9240576 | tf_op jit(solution)/shard_map/psum | solution.py:133
  8.3 11.7 %collective-permute-start.1 = (bf16[2,16,1024]{2,1,0:T(8,128)(2,1)S(1)}, bf16[2,16,1024]{2,1,0:T(8,128)(2,1)S(1)}, u32[]{:S(2)}, u32[]{:S(2)}) collective-permute-start(bf16[2,16,1024]{2,1,0:T(8,128)(2,1)S(1)} %get-tuple-element.42), channel_id=1, source_target_pairs={{2,0},{4,2},{6,4},{8,6},{10,8},{12,10},{14,12},{3,1},{5,3},{7,5},{... | collective-permute-start | bytes 196616 | tf_op jit(solution)/shard_map/ppermute | solution.py:20
  9.6 10.3 %collective-permute-start = (bf16[2,16,1024]{2,1,0:T(8,128)(2,1)S(1)}, bf16[2,16,1024]{2,1,0:T(8,128)(2,1)S(1)}, u32[]{:S(2)}, u32[]{:S(2)}) collective-permute-start(bf16[2,16,1024]{2,1,0:T(8,128)(2,1)S(1)} %get-tuple-element.43), channel_id=1, source_target_pairs={{0,2},{2,4},{4,6},{6,8},{8,10},{10,12},{12,14},{1,3},{3,5},{5,7},{... | collective-permute-start | bytes 196616 | tf_op jit(solution)/shard_map/ppermute | solution.py:17
  21.7 1.9 %copy-start.1 = (f32[2,1024,512]{1,2,0:T(8,128)}, f32[2,1024,512]{1,2,0:T(8,128)S(1)}, u32[]{:S(2)}) copy-start(f32[2,1024,512]{1,2,0:T(8,128)S(1)} %get-tuple-element.57) | copy-start | bytes 12582916
  21.7 0.7 copy-start.11
  23.6 4.7 %copy-start.4 = (bf16[1024,1024]{1,0:T(8,128)(2,1)}, bf16[1024,1024]{1,0:T(8,128)(2,1)S(1)}, u32[]{:S(2)}) copy-start(bf16[1024,1024]{1,0:T(8,128)(2,1)S(1)} %multiply_convert_fusion.2) | copy-start | bytes 6291460
  23.6 6.0 %copy-start.9 = (bf16[1024,100]{0,1:T(8,128)(2,1)S(1)}, bf16[1024,100]{0,1:T(8,128)(2,1)}, u32[]{:S(2)}) copy-start(bf16[1024,100]{0,1:T(8,128)(2,1)} %param.27) | copy-start | bytes 614404
  28.3 1.4 copy-start.2
  32.9 7.0 %copy-start.12 = (f32[100]{0:T(128)S(1)}, f32[100]{0:T(128)}, u32[]{:S(2)}) copy-start(f32[100]{0:T(128)} %param.24) | copy-start | bytes 1204
  39.3 1.9 %copy-start.3 = (bf16[1024,1024]{1,0:T(8,128)(2,1)S(1)}, bf16[1024,1024]{1,0:T(8,128)(2,1)}, u32[]{:S(2)}) copy-start(bf16[1024,1024]{1,0:T(8,128)(2,1)} %copy-done.2) | copy-start | bytes 6291460
  40.8 1.7 copy-start.10
  40.8 2.4 %copy-start.14 = (f32[1024,1024]{1,0:T(8,128)S(1)}, f32[1024,1024]{1,0:T(8,128)}, u32[]{:S(2)}) copy-start(f32[1024,1024]{1,0:T(8,128)} %get-tuple-element.59) | copy-start | bytes 12582916
  43.2 3.1 %copy-start.5 = (bf16[1024,1024]{1,0:T(8,128)(2,1)S(1)}, bf16[1024,1024]{1,0:T(8,128)(2,1)}, u32[]{:S(2)}) copy-start(bf16[1024,1024]{1,0:T(8,128)(2,1)} %copy-done.4) | copy-start | bytes 6291460
  45.0 1.4 copy-start.13
  64.7 40.5 %collective-permute-start.2 = (bf16[2,16,1024]{2,1,0:T(8,128)(2,1)}, bf16[2,16,1024]{2,1,0:T(8,128)(2,1)S(1)}, u32[]{:S(2)}, u32[]{:S(2)}) collective-permute-start(bf16[2,16,1024]{2,1,0:T(8,128)(2,1)} %get-tuple-element.41), channel_id=1, source_target_pairs={{0,2},{2,4},{4,6},{6,8},{8,10},{10,12},{12,14},{1,3},{3,5},{5,7},{... | collective-permute-start | bytes 196616 | tf_op jit(solution)/shard_map/ppermute | solution.py:28
  69.5 35.7 %collective-permute-start.3 = (bf16[2,16,1024]{2,1,0:T(8,128)(2,1)}, bf16[2,16,1024]{2,1,0:T(8,128)(2,1)S(1)}, u32[]{:S(2)}, u32[]{:S(2)}) collective-permute-start(bf16[2,16,1024]{2,1,0:T(8,128)(2,1)} %get-tuple-element.40), channel_id=1, source_target_pairs={{2,0},{4,2},{6,4},{8,6},{10,8},{12,10},{14,12},{3,1},{5,3},{7,5},{... | collective-permute-start | bytes 196616 | tf_op jit(solution)/shard_map/ppermute | solution.py:28
  105.3 77.8 %copy-start.6 = (f32[2,64,1024]{2,1,0:T(8,128)}, f32[2,64,1024]{2,1,0:T(8,128)S(1)}, u32[]{:S(2)}) copy-start(f32[2,64,1024]{2,1,0:T(8,128)S(1)} %fusion.12) | copy-start | bytes 1572868
  178.2 4.8 %copy-start.8 = (f32[1024,100]{0,1:T(8,128)S(1)}, f32[1024,100]{0,1:T(8,128)}, u32[]{:S(2)}) copy-start(f32[1024,100]{0,1:T(8,128)} %get-tuple-element.67) | copy-start | bytes 1228804
Sparse Core Ops, SparseCore 0:
  58.4 119.7 all-reduce.3
where the time goes:
time: 191 us
  waiting for transfers between devices  73 us (38%)
  blocking collectives  36.9 us (19%)
  matrix products  23.6 us (12%)
  local copies, waits for them, and re-layouts  16.8 us (9%)
  between operations  14.4 us (8%)
  other arithmetic  13 us (7%)
  starting transfers between devices  12.9 us (7%)
    psum x1, waiting for transfers between devices, local(): lax.psum((part_hidden, part_out, partial_gain, loss_local), ('space', 'me...  73 us
    psum x1, blocking collectives, local(): lax.psum((part_hidden, part_out, partial_gain, loss_local), ('space', 'me...  34.3 us
    unnamed x47, local copies, waits for them, and re-layouts  13.1 us
    dot_general x1, matrix products, local(): jnp.dot(gpre, hidden_weight.T, preferred_element_type=jnp.float32)  7.51 us
    ppermute x2, starting transfers between devices, from_behind(): lax.ppermute(value, axis, [(source, source + steps) for source in range(f...  6.09 us
    ppermute x1, starting transfers between devices, with_halo(): lax.ppermute(lax.slice_in_dim(block, block.shape[dim] - width, None, axis...  5.5 us
    dot_general x1, matrix products, local(): jnp.dot(normed_rows, hidden_weight, preferred_element_type=jnp.float32)  4.66 us
    dot_general x1, matrix products, local(): jnp.dot(normed_rows.T, gpre, preferred_element_type=jnp.float32)  4.41 us
  transfers between devices with their start and end apart: 5, of which 1 were waited for; matrix products, arithmetic and copies ran while one was open for 6% of the time, Pallas kernels for 0%

commit v1 on v0

--- a/solution.py
+++ b/solution.py
@@ -9,17 +9,15 @@
 SMOOTH_SQ = 0.01
 
 
-def with_halo(block, sides, width):
-    for axis, dim in sides:
-        count = lax.axis_size(axis)
-        forward = [(i, i + 1) for i in range(count - 1)]
-        backward = [(target, source) for source, target in forward]
-        low = lax.ppermute(
-            lax.slice_in_dim(block, block.shape[dim] - width, None, axis=dim), axis, forward
-        )
-        high = lax.ppermute(lax.slice_in_dim(block, 0, width, axis=dim), axis, backward)
-        block = jnp.concatenate([low, block, high], axis=dim)
-    return block
+def with_halo(block, axis, dim, width):
+    count = lax.axis_size(axis)
+    forward = [(i, i + 1) for i in range(count - 1)]
+    backward = [(target, source) for source, target in forward]
+    low = lax.ppermute(
+        lax.slice_in_dim(block, block.shape[dim] - width, None, axis=dim), axis, forward
+    )
+    high = lax.ppermute(lax.slice_in_dim(block, 0, width, axis=dim), axis, backward)
+    return jnp.concatenate([low, block, high], axis=dim)
 
 
 def from_behind(value, axis, steps):
@@ -36,6 +34,55 @@
     upper = values.astype(jnp.bfloat16)
     lower = (values - upper.astype(jnp.float32)).astype(jnp.bfloat16)
     return (upper, lower)
+
+
+def swap(value, axis, bit):
+    count = lax.axis_size(axis)
+    return lax.ppermute(value, axis, [(i, i ^ (1 << bit)) for i in range(count)])
+
+
+def halve(value, axis, bit):
+    rows = value.shape[0] // 2
+    upper = (lax.axis_index(axis) >> bit) & 1
+    low, high = value[:rows], value[rows:]
+    sent = jnp.where(upper == 0, high, low).astype(jnp.bfloat16)
+    kept = jnp.where(upper == 0, low, high)
+    return kept + swap(sent, axis, bit).astype(jnp.float32)
+
+
+def double(value, axis, bit):
+    upper = (lax.axis_index(axis) >> bit) & 1
+    other = swap(value, axis, bit)
+    return jnp.where(
+        upper == 0, jnp.concatenate([value, other]), jnp.concatenate([other, value])
+    )
+
+
+def sum_stream(value, axis, order):
+    for bit in order[:-1]:
+        value = halve(value, axis, bit)
+    mine = value.astype(jnp.bfloat16)
+    other = swap(mine, axis, order[-1])
+    value = (mine.astype(jnp.float32) + other.astype(jnp.float32)).astype(jnp.bfloat16)
+    for bit in reversed(order[:-1]):
+        value = double(value, axis, bit)
+    return value
+
+
+def sum_small(value, axis):
+    for bit in range(lax.axis_size(axis).bit_length() - 1):
+        value = value + swap(value, axis, bit)
+    return value
+
+
+def sum_weights(value):
+    bits = lax.axis_size("space").bit_length() - 1
+    value = halve(value, "member", 0)
+    half = value.shape[0] // 2
+    rest = list(range(2, bits))
+    first = sum_stream(value[:half], "space", [0, 1] + rest)
+    second = sum_stream(value[half:], "space", [1, 0] + rest)
+    return double(jnp.concatenate([first, second]), "member", 0)
 
 
 def local(
@@ -54,7 +101,7 @@
 ):
     members, nodes, width = latent.shape
     points = state.shape[0]
-    extended = with_halo(latent, (("space", 1),), RIM)
+    extended = with_halo(latent, "space", 1, RIM)
     span = nodes + 2 * RIM
     anchor = lax.axis_index("space") * nodes - RIM
     local_index = edge_node_index - anchor
@@ -81,8 +128,9 @@
     hidden_rows = jax.nn.silu(preactivation).astype(jnp.bfloat16)
     outputs = jnp.dot(hidden_rows, output_weight, preferred_element_type=jnp.float32)
     preds = state[None] + outputs.reshape(members, points, -1)
-    ensemble = lax.all_gather(preds, "member", axis=0, tiled=True)
-    total = ensemble.shape[0]
+    others = swap(preds, "member", 0)
+    total = 2 * members
+    ensemble = jnp.concatenate([preds, others], axis=0)
     weight = (valid.astype(jnp.float32) * area / points)[:, None] * var_weight[None, :]
     own_err = preds - target[None]
     pair = preds[:, None] - ensemble[None]
@@ -101,13 +149,21 @@
         )
     ).astype(jnp.bfloat16)
     gpred = gpred.reshape(members * points, -1)
+    variables = gpred.shape[1]
     part_out = jnp.dot(hidden_rows.T, gpred, preferred_element_type=jnp.float32)
     ghid = jnp.dot(gpred, output_weight.T, preferred_element_type=jnp.float32)
     sig = jax.nn.sigmoid(preactivation)
     gpre = (ghid * sig * (1.0 + preactivation * (1.0 - sig))).astype(jnp.bfloat16)
     part_hidden = jnp.dot(normed_rows.T, gpre, preferred_element_type=jnp.float32)
+    part_out = jnp.pad(part_out, ((0, 0), (0, -variables % 128)))
+    weights = sum_weights(jnp.concatenate([part_hidden, part_out], axis=1))
+    grad_hidden = weights[:, :width].astype(jnp.float32)
+    grad_out = weights[:, width : width + variables].astype(jnp.float32)
     grad_preact_normed = jnp.dot(gpre, hidden_weight.T, preferred_element_type=jnp.float32)
     partial_gain = jnp.sum(grad_preact_normed * standardized_input, axis=0)
+    small = jnp.concatenate([partial_gain, jnp.full((128,), loss_local)])
+    small = sum_small(sum_small(small, "member"), "space")
+    grad_gain, loss = small[:width], small[width : width + 1]
     scaled_rows = grad_preact_normed * gain[None, :]
     grad_preact = inverse_deviation * (
         scaled_rows
@@ -130,10 +186,7 @@
     grad_latent = grad_ext[:, RIM : RIM + nodes]
     grad_latent = grad_latent.at[:, :RIM].add(from_below)
     grad_latent = grad_latent.at[:, nodes - RIM :].add(from_above)
-    grad_hidden, grad_out, grad_gain, loss = lax.psum(
-        (part_hidden, part_out, partial_gain, loss_local), ("space", "member")
-    )
-    return (loss.reshape(1), grad_hidden, grad_out, grad_gain, grad_latent)
+    return (loss, grad_hidden, grad_out, grad_gain, grad_latent)
 
 
 def solution(mesh):

time: 191 us -> 147 us (0.77)
  blocking collectives: 36.9 us -> 0 us
  starting transfers between devices: 12.9 us -> 34.4 us
  waiting for transfers between devices: 73 us -> 54.9 us
  between operations: 14.4 us -> 1.44 us
  other arithmetic: 13 us -> 22.4 us
  matrix products: 23.6 us -> 16.3 us
    psum x1 -> x0, waiting for transfers between devices: 73 us -> none  [local(): lax.psum((part_hidden, part_out, partial_gain, loss_local), ('space', 'me...]
    ppermute x0 -> x17, waiting for transfers between devices: none -> 51.3 us  [swap(): return lax.ppermute(value, axis, [(i, i ^ 1 << bit) for i in range(count)])]
    psum x1 -> x0, blocking collectives: 34.3 us -> none  [local(): lax.psum((part_hidden, part_out, partial_gain, loss_local), ('space', 'me...]
    ppermute x0 -> x17, starting transfers between devices: none -> 22.9 us  [swap(): return lax.ppermute(value, axis, [(i, i ^ 1 << bit) for i in range(count)])]
    dot_general x1, matrix products: 7.51 us -> 2.97 us  [local(): jnp.dot(gpre, hidden_weight.T, preferred_element_type=jnp.float32)]
    convert_element_type x0 -> x10, other arithmetic: none -> 4.45 us  [the longest x1 2.44 us: local(): grad_hidden = weights[:, :width].astype(jnp.float32)]
    ppermute x2, waiting for transfers between devices: 0.01 us -> 3.1 us  [from_behind(): lax.ppermute(value, axis, [(source, source + steps) for source in range(f...]
    all_gather x1 -> x0, blocking collectives: 2.6 us -> none  [local(): ensemble = lax.all_gather(preds, 'member', axis=0, tiled=True)]
  transfers between devices with their start and end apart: 5 -> 21, of which waited for: 1 -> 14; matrix products, arithmetic and copies ran while one was open for 6% -> 11% of each run, Pallas kernels for 0% -> 0%
where the time goes in v1:
time: 147 us
  waiting for transfers between devices  54.9 us (37%)
  starting transfers between devices  34.4 us (23%)
  other arithmetic  22.4 us (15%)
  local copies, waits for them, and re-layouts  17.1 us (12%)
  matrix products  16.3 us (11%)
    ppermute x17, waiting for transfers between devices, swap(): return lax.ppermute(value, axis, [(i, i ^ 1 << bit) for i in range(count)])  51.3 us
    ppermute x17, starting transfers between devices, swap(): return lax.ppermute(value, axis, [(i, i ^ 1 << bit) for i in range(count)])  22.9 us
    unnamed x84, local copies, waits for them, and re-layouts  12.7 us
    ppermute x1, starting transfers between devices, with_halo(): lax.ppermute(lax.slice_in_dim(block, block.shape[dim] - width, None, axis...  5.5 us
    ppermute x2, starting transfers between devices, from_behind(): lax.ppermute(value, axis, [(source, source + steps) for source in range(f...  4.71 us
    dot_general x1, matrix products, local(): jnp.dot(normed_rows, hidden_weight, preferred_element_type=jnp.float32)  4.62 us
    reduce_sum x1, other arithmetic, local(): jnp.sum(smooth(pair), axis=(0, 1)) / (2.0 * total * (total - 1))  3.44 us
    ppermute x2, waiting for transfers between devices, from_behind(): lax.ppermute(value, axis, [(source, source + steps) for source in range(f...  3.1 us
  transfers between devices with their start and end apart: 21, of which 14 were waited for; matrix products, arithmetic and copies ran while one was open for 11% of the time, Pallas kernels for 0%

profile of v1, /device:TPU:0, one launch (start us, length us, event | category | flops | bytes accessed | tf_op | source)
XLA Modules:
  0.0 146.5 jit_solution(8211135797736771104)
XLA Ops:
  3.0 5.5 %collective-permute-start = (bf16[2,16,1024]{2,1,0:T(8,128)(2,1)S(1)}, bf16[2,16,1024]{2,1,0:T(8,128)(2,1)S(1)}, u32[]{:S(2)}, u32[]{:S(2)}) collective-permute-start(bf16[2,16,1024]{2,1,0:T(8,128)(2,1)S(1)} %get-tuple-element.53), channel_id=1, source_target_pairs={{0,2},{2,4},{4,6},{6,8},{8,10},{10,12},{12,14},{1,3},{3,5},{5,7},{... | collective-permute-start | bytes 196616 | tf_op jit(solution)/shard_map/ppermute | solution.py:16
  15.3 4.6 %multiply_convert_fusion.1 = (bf16[1024,1024]{1,0:T(8,128)(2,1)S(1)}, f32[1024,1024]{1,0:T(8,128)}) fusion(bf16[1024,1024]{1,0:T(8,128)(2,1)S(1)} %multiply_convert_fusion.2, bf16[1024,1024]{1,0:T(8,128)(2,1)S(1)} %copy-done), kind=kOutput, calls=%fused_computation.13 | convolution fusion | flops 2152726528 | bytes 10485760 | tf_op jit(solution)/shard_map/dot_general | solution.py:127
  20.0 1.4 copy-done.4
  23.3 2.9 %sqrt_reduce_fusion = (f32[512,100]{0,1:T(8,128)S(1)}, f32[2,512,100]{1,0,2:T(2,128)S(1)}, f32[100,2,512]{2,1,0:T(2,128)}, f32[100,2,512]{2,1,0:T(2,128)S(1)}) fusion(f32[512,100]{0,1:T(8,128)} %param.23, f32[2,512,100]{1,0,2:T(2,128)} %reshape.164, f32[512,100]{0,1:T(8,128)} %param.22), kind=kLoop, calls=%fused_computation.48 | loop fusion | flops 460800 | bytes 2252800 | tf_op jit(solution)/shard_map/reduce_sum | solution.py:140
  28.5 1.4 pad_maximum_fusion.1
  29.8 3.4 %fusion.6 = (f32[512,100]{0,1:T(8,128)S(1)}, f32[2,512,100]{1,2,0:T(8,128)S(1)}) fusion(f32[4,512,100]{1,0,2:T(4,128)S(1)} %pad_maximum_fusion.1, f32[2,512,100]{1,2,0:T(8,128)S(1)} %copy.20), kind=kLoop, calls=%fused_computation.27 | loop fusion | flops 2304000 | bytes 1843200 | tf_op jit(solution)/shard_map/reduce_sum | solution.py:141
  37.1 1.7 %multiply_convert_fusion = bf16[1024,1024]{1,0:T(8,128)(2,1)S(1)} fusion(f32[1024,1024]{1,0:T(8,128)S(1)} %copy-done.34, bf16[1024,100]{0,1:T(8,128)(2,1)S(1)} %multiply_convert_fusion.3, bf16[1024,100]{0,1:T(8,128)(2,1)S(1)} %copy-done.10), kind=kOutput, calls=%fused_computation.12 | convolution fusion | flops 219152384 | bytes 6701056 | tf_op jit(solution)/shard_map/dot_general | solution.py:154
  38.8 2.5 %fusion.38 = f32[1024,1024]{0,1:T(8,128)S(1)} fusion(bf16[1024,1024]{1,0:T(8,128)(2,1)S(1)} %copy-done.7, bf16[1024,1024]{1,0:T(8,128)(2,1)S(1)} %multiply_convert_fusion), kind=kOutput, calls=%fused_computation.98 | convolution fusion | flops 2147483648 | bytes 8388608 | tf_op jit(solution)/shard_map/dot_general | solution.py:157
  43.5 3.0 %multiply_reduce_fusion = (f32[1024]{0:T(1024)S(1)}, f32[1024]{0:T(1024)S(1)}, f32[1024]{0:T(1024)S(1)}, f32[1024,1024]{1,0:T(8,128)S(1)}) fusion(f32[2,1024,512]{1,2,0:T(8,128)S(1)} %copy-done.3, f32[1024]{0:T(1024)S(1)} %copy-done.32, f32[1024]{0:T(1024)S(1)} %bitcast.149, f32[1024]{0:T(1024)S(1)} %bitcast.146, ...), kind=kOutput, calls=%fused_computation.10 | convolution fusion | flops 2155869184 | bytes 12607488 | tf_op jit(solution)/shard_map/dot_general | solution.py:162
  46.5 1.8 %subtract_multiply_fusion = f32[1024,1024]{1,0:T(8,128)S(1)} fusion(f32[1024,1024]{1,0:T(8,128)S(1)} %get-tuple-element.72, f32[2,1024,512]{1,2,0:T(8,128)S(1)} %copy-done.3, f32[1024]{0:T(1024)S(1)} %get-tuple-element.75, f32[1024]{0:T(1024)S(1)} %get-tuple-element.76, f32[1024]{0:T(1024)S(1)} %copy-done.32, f32[1024]{0:T(1024)S(1)} %bitcast.150, ...), kind=kLoop, calls=%fused_computation.9 | loop fusion | flops 7340032 | bytes 12603392 | tf_op jit(solution)/shard_map/mul | solution.py:168
  49.3 2.8 %collective-permute-start.8 = (bf16[128,1152]{0,1:T(8,128)(2,1)S(1)}, bf16[128,1152]{0,1:T(8,128)(2,1)S(1)}, u32[]{:S(2)}, u32[]{:S(2)}) collective-permute-start(bf16[128,1152]{0,1:T(8,128)(2,1)S(1)} %get-tuple-element.48), channel_id=1, source_target_pairs={{0,2},{2,0},{4,6},{6,4},{8,10},{10,8},{12,14},{14,12},{1,3},{3,1},... | collective-permute-start | bytes 884744 | tf_op jit(solution)/shard_map/ppermute | solution.py:41
  52.1 1.9 %collective-permute-start.13 = (bf16[128,1152]{0,1:T(8,128)(2,1)S(1)}, bf16[128,1152]{0,1:T(8,128)(2,1)S(1)}, u32[]{:S(2)}, u32[]{:S(2)}) collective-permute-start(bf16[128,1152]{0,1:T(8,128)(2,1)S(1)} %get-tuple-element.49), channel_id=1, source_target_pairs={{0,4},{2,6},{4,0},{6,2},{8,12},{10,14},{12,8},{14,10},{1,5},{3,7},... | collective-permute-start | bytes 884744 | tf_op jit(solution)/shard_map/ppermute | solution.py:41
  54.6 5.3 %collective-permute-done.8 = bf16[128,1152]{0,1:T(8,128)(2,1)S(1)} collective-permute-done((bf16[128,1152]{0,1:T(8,128)(2,1)S(1)}, bf16[128,1152]{0,1:T(8,128)(2,1)S(1)}, u32[]{:S(2)}, u32[]{:S(2)}) %collective-permute-start.8) | collective-permute-done | bytes 294944 | tf_op jit(solution)/shard_map/ppermute | solution.py:41
  59.8 1.8 %collective-permute-done.13 = bf16[128,1152]{0,1:T(8,128)(2,1)S(1)} collective-permute-done((bf16[128,1152]{0,1:T(8,128)(2,1)S(1)}, bf16[128,1152]{0,1:T(8,128)(2,1)S(1)}, u32[]{:S(2)}, u32[]{:S(2)}) %collective-permute-start.13) | collective-permute-done | bytes 294944 | tf_op jit(solution)/shard_map/ppermute | solution.py:41
  62.0 1.7 %collective-permute-start.14 = (bf16[64,1152]{0,1:T(8,128)(2,1)S(1)}, bf16[64,1152]{0,1:T(8,128)(2,1)S(1)}, u32[]{:S(2)}, u32[]{:S(2)}) collective-permute-start(bf16[64,1152]{0,1:T(8,128)(2,1)S(1)} %select_convert_fusion.1), channel_id=1, source_target_pairs={{0,2},{2,0},{4,6},{6,4},{8,10},{10,8},{12,14},{14,12},{1,3},{3,1},... | collective-permute-start | bytes 442376 | tf_op jit(solution)/shard_map/ppermute | solution.py:41
  63.9 1.8 %collective-permute-start.9 = (bf16[64,1152]{0,1:T(8,128)(2,1)S(1)}, bf16[64,1152]{0,1:T(8,128)(2,1)S(1)}, u32[]{:S(2)}, u32[]{:S(2)}) collective-permute-start(bf16[64,1152]{0,1:T(8,128)(2,1)S(1)} %select_convert_fusion.3), channel_id=1, source_target_pairs={{0,4},{2,6},{4,0},{6,2},{8,12},{10,14},{12,8},{14,10},{1,5},{3,7},... | collective-permute-start | bytes 442376 | tf_op jit(solution)/shard_map/ppermute | solution.py:41
  65.7 5.1 %collective-permute-done.14 = bf16[64,1152]{0,1:T(8,128)(2,1)S(1)} collective-permute-done((bf16[64,1152]{0,1:T(8,128)(2,1)S(1)}, bf16[64,1152]{0,1:T(8,128)(2,1)S(1)}, u32[]{:S(2)}, u32[]{:S(2)}) %collective-permute-start.14) | collective-permute-done | bytes 147488 | tf_op jit(solution)/shard_map/ppermute | solution.py:41
  71.0 2.8 %collective-permute-start.15 = (bf16[64,1152]{0,1:T(8,128)(2,1)S(1)}, bf16[64,1152]{0,1:T(8,128)(2,1)S(1)}, u32[]{:S(2)}, u32[]{:S(2)}) collective-permute-start(bf16[64,1152]{0,1:T(8,128)(2,1)S(1)} %add_convert_fusion.1), channel_id=1, source_target_pairs={{0,8},{2,10},{4,12},{6,14},{8,0},{10,2},{12,4},{14,6},{1,9},{3,11}... | collective-permute-start | bytes 442376 | tf_op jit(solution)/shard_map/ppermute | solution.py:41
  75.1 18.6 %collective-permute-done.15 = bf16[64,1152]{0,1:T(8,128)(2,1)S(1)} collective-permute-done((bf16[64,1152]{0,1:T(8,128)(2,1)S(1)}, bf16[64,1152]{0,1:T(8,128)(2,1)S(1)}, u32[]{:S(2)}, u32[]{:S(2)}) %collective-permute-start.15) | collective-permute-done | bytes 147488 | tf_op jit(solution)/shard_map/ppermute | solution.py:41
  94.8 4.0 %collective-permute-done.10 = bf16[64,1152]{0,1:T(8,128)(2,1)S(1)} collective-permute-done((bf16[64,1152]{0,1:T(8,128)(2,1)S(1)}, bf16[64,1152]{0,1:T(8,128)(2,1)S(1)}, u32[]{:S(2)}, u32[]{:S(2)}) %collective-permute-start.10) | collective-permute-done | bytes 147488 | tf_op jit(solution)/shard_map/ppermute | solution.py:41
  101.1 1.6 %collective-permute-start.17 = (bf16[128,1152]{0,1:T(8,128)(2,1)S(1)}, bf16[128,1152]{0,1:T(8,128)(2,1)S(1)}, u32[]{:S(2)}, u32[]{:S(2)}) collective-permute-start(bf16[128,1152]{0,1:T(8,128)(2,1)S(1)} %maximum_select_fusion.4), channel_id=1, source_target_pairs={{0,4},{2,6},{4,0},{6,2},{8,12},{10,14},{12,8},{14,10},{1,5},{3,7},... | collective-permute-start | bytes 884744 | tf_op jit(solution)/shard_map/ppermute | solution.py:41
  102.6 6.2 %collective-permute-done.11 = bf16[64,1152]{0,1:T(8,128)(2,1)S(1)} collective-permute-done((bf16[64,1152]{0,1:T(8,128)(2,1)S(1)}, bf16[64,1152]{0,1:T(8,128)(2,1)S(1)}, u32[]{:S(2)}, u32[]{:S(2)}) %collective-permute-start.11) | collective-permute-done | bytes 147488 | tf_op jit(solution)/shard_map/ppermute | solution.py:41
  109.2 1.6 %collective-permute-start.12 = (bf16[128,1152]{0,1:T(8,128)(2,1)S(1)}, bf16[128,1152]{0,1:T(8,128)(2,1)S(1)}, u32[]{:S(2)}, u32[]{:S(2)}) collective-permute-start(bf16[128,1152]{0,1:T(8,128)(2,1)S(1)} %maximum_select_fusion.3), channel_id=1, source_target_pairs={{0,2},{2,0},{4,6},{6,4},{8,10},{10,8},{12,14},{14,12},{1,3},{3,1},... | collective-permute-start | bytes 884744 | tf_op jit(solution)/shard_map/ppermute | solution.py:41
  113.3 2.6 %collective-permute-done.12 = bf16[128,1152]{0,1:T(8,128)(2,1)S(1)} collective-permute-done((bf16[128,1152]{0,1:T(8,128)(2,1)S(1)}, bf16[128,1152]{0,1:T(8,128)(2,1)S(1)}, u32[]{:S(2)}, u32[]{:S(2)}) %collective-permute-start.12) | collective-permute-done | bytes 294944 | tf_op jit(solution)/shard_map/ppermute | solution.py:41
  117.0 3.4 %collective-permute-start.19 = (bf16[2,16,1024]{2,1,0:T(8,128)(2,1)S(1)}, bf16[2,16,1024]{2,1,0:T(8,128)(2,1)S(1)}, u32[]{:S(2)}, u32[]{:S(2)}) collective-permute-start(bf16[2,16,1024]{2,1,0:T(8,128)(2,1)S(1)} %get-tuple-element.51), channel_id=1, source_target_pairs={{0,2},{2,4},{4,6},{6,8},{8,10},{10,12},{12,14},{1,3},{3,5},{5,7},{... | collective-permute-start | bytes 196616 | tf_op jit(solution)/shard_map/ppermute | solution.py:26
  122.1 2.7 %collective-permute-done.4 = f32[1152]{0:T(1024)S(1)} collective-permute-done((f32[1152]{0:T(1024)S(1)}, f32[1152]{0:T(1024)S(1)}, u32[]{:S(2)}, u32[]{:S(2)}) %collective-permute-start.4) | collective-permute-done | bytes 4640 | tf_op jit(solution)/shard_map/ppermute | solution.py:41
  124.8 1.5 %collective-permute-start.5 = (f32[1152]{0:T(1024)S(1)}, f32[1152]{0:T(1024)S(1)}, u32[]{:S(2)}, u32[]{:S(2)}) collective-permute-start(f32[1152]{0:T(1024)S(1)} %add.142), channel_id=1, source_target_pairs={{0,4},{2,6},{4,0},{6,2},{8,12},{10,14},{12,8},{14,10},{1,5},{3,7},... | collective-permute-start | bytes 13832 | tf_op jit(solution)/shard_map/ppermute | solution.py:41
  126.3 2.2 %collective-permute-done.5 = f32[1152]{0:T(1024)S(1)} collective-permute-done((f32[1152]{0:T(1024)S(1)}, f32[1152]{0:T(1024)S(1)}, u32[]{:S(2)}, u32[]{:S(2)}) %collective-permute-start.5) | collective-permute-done | bytes 4640 | tf_op jit(solution)/shard_map/ppermute | solution.py:41
  128.4 2.6 %collective-permute-start.6 = (f32[1152]{0:T(1024)S(1)}, f32[1152]{0:T(1024)S(1)}, u32[]{:S(2)}, u32[]{:S(2)}) collective-permute-start(f32[1152]{0:T(1024)S(1)} %add.143), channel_id=1, source_target_pairs={{0,8},{2,10},{4,12},{6,14},{8,0},{10,2},{12,4},{14,6},{1,9},{3,11}... | collective-permute-start | bytes 13832 | tf_op jit(solution)/shard_map/ppermute | solution.py:41
  134.1 3.1 %collective-permute-done.20 = bf16[2,16,1024]{2,1,0:T(8,128)(2,1)S(1)} collective-permute-done((bf16[2,16,1024]{2,1,0:T(8,128)(2,1)S(1)}, bf16[2,16,1024]{2,1,0:T(8,128)(2,1)S(1)}, u32[]{:S(2)}, u32[]{:S(2)}) %collective-permute-start.20) | collective-permute-done | bytes 65568 | tf_op jit(solution)/shard_map/ppermute | solution.py:26
  138.7 2.4 %slice_convert_fusion = f32[1024,1024]{0,1:T(8,128)} fusion(bf16[1024,1152]{0,1:T(8,128)(2,1)S(1)} %maximum_select_fusion), kind=kLoop, calls=%fused_computation.24 | loop fusion | flops 1048576 | bytes 6291456 | tf_op jit(solution)/shard_map/convert_element_type | solution.py:160
  141.2 5.3 %copy.22 = f32[1024,1024]{1,0:T(8,128)} copy(f32[1024,1024]{0,1:T(8,128)} %slice_convert_fusion) | data formatting | bytes 8388608
  (157 shorter events, 35.8 us)
Async XLA Ops:
  0.6 14.7 %copy-start = (bf16[1024,1024]{1,0:T(8,128)(2,1)S(1)}, bf16[1024,1024]{1,0:T(8,128)(2,1)}, u32[]{:S(2)}) copy-start(bf16[1024,1024]{1,0:T(8,128)(2,1)} %param.26) | copy-start | bytes 6291460
  1.7 9.8 %collective-permute-start.1 = (bf16[2,16,1024]{2,1,0:T(8,128)(2,1)S(1)}, bf16[2,16,1024]{2,1,0:T(8,128)(2,1)S(1)}, u32[]{:S(2)}, u32[]{:S(2)}) collective-permute-start(bf16[2,16,1024]{2,1,0:T(8,128)(2,1)S(1)} %get-tuple-element.52), channel_id=1, source_target_pairs={{2,0},{4,2},{6,4},{8,6},{10,8},{12,10},{14,12},{3,1},{5,3},{7,5},{... | collective-permute-start | bytes 196616 | tf_op jit(solution)/shard_map/ppermute | solution.py:19
  3.0 7.5 %collective-permute-start = (bf16[2,16,1024]{2,1,0:T(8,128)(2,1)S(1)}, bf16[2,16,1024]{2,1,0:T(8,128)(2,1)S(1)}, u32[]{:S(2)}, u32[]{:S(2)}) collective-permute-start(bf16[2,16,1024]{2,1,0:T(8,128)(2,1)S(1)} %get-tuple-element.53), channel_id=1, source_target_pairs={{0,2},{2,4},{4,6},{6,8},{8,10},{10,12},{12,14},{1,3},{3,5},{5,7},{... | collective-permute-start | bytes 196616 | tf_op jit(solution)/shard_map/ppermute | solution.py:16
  13.9 6.0 %copy-start.29 = (f32[1,4,2,128]{3,1,2,0:T(4,128)}, f32[1,4,2,128]{3,1,2,0:T(4,128)S(1)}, u32[]{:S(2)}) copy-start(f32[1,4,2,128]{3,1,2,0:T(4,128)S(1)} %copy.24) | copy-start | bytes 12292
  15.3 6.0 %copy-start.9 = (bf16[1024,100]{0,1:T(8,128)(2,1)S(1)}, bf16[1024,100]{0,1:T(8,128)(2,1)}, u32[]{:S(2)}) copy-start(bf16[1024,100]{0,1:T(8,128)(2,1)} %param.27) | copy-start | bytes 614404
  26.2 2.3 %collective-permute-start.2 = (f32[2,512,100]{1,0,2:T(2,128)S(1)}, f32[2,512,100]{1,0,2:T(2,128)}, u32[]{:S(2)}, u32[]{:S(2)}) collective-permute-start(f32[2,512,100]{1,0,2:T(2,128)S(1)} %get-tuple-element.45), channel_id=1, source_target_pairs={{0,1},{1,0},{2,3},{3,2},{4,5},{5,4},{6,7},{7,6},{8,9},{9,8},{10,11... | collective-permute-start | bytes 1228808 | tf_op jit(solution)/shard_map/ppermute | solution.py:41
  26.2 7.1 %copy-start.33 = (f32[100]{0:T(128)S(1)}, f32[100]{0:T(128)}, u32[]{:S(2)}) copy-start(f32[100]{0:T(128)} %param.24) | copy-start | bytes 1204
  42.3 6.2 %collective-permute-start.7 = (bf16[512,1152]{0,1:T(8,128)(2,1)S(1)}, bf16[512,1152]{0,1:T(8,128)(2,1)S(1)}, u32[]{:S(2)}, u32[]{:S(2)}) collective-permute-start(bf16[512,1152]{0,1:T(8,128)(2,1)S(1)} %select_convert_fusion), channel_id=1, source_target_pairs={{0,1},{1,0},{2,3},{3,2},{4,5},{5,4},{6,7},{7,6},{8,9},{9,8},{10,11... | collective-permute-start | bytes 3538952 | tf_op jit(solution)/shard_map/ppermute | solution.py:41
  48.4 5.7 %copy-start.12 = (s32[512,1]{0,1:T(1,128)S(1)}, s32[512,1]{0,1:T(1,128)}, u32[]{:S(2)}) copy-start(s32[512,1]{0,1:T(1,128)} %copy-done.11) | copy-start | bytes 6148
  48.4 5.7 %copy-start.14 = (s32[512,1]{0,1:T(1,128)S(1)}, s32[512,1]{0,1:T(1,128)}, u32[]{:S(2)}) copy-start(s32[512,1]{0,1:T(1,128)} %copy-done.13) | copy-start | bytes 6148
  48.4 5.6 %copy-start.16 = (s32[512,1]{0,1:T(1,128)S(1)}, s32[512,1]{0,1:T(1,128)}, u32[]{:S(2)}) copy-start(s32[512,1]{0,1:T(1,128)} %copy-done.15) | copy-start | bytes 6148
  48.4 5.6 %copy-start.18 = (s32[512,1]{0,1:T(1,128)S(1)}, s32[512,1]{0,1:T(1,128)}, u32[]{:S(2)}) copy-start(s32[512,1]{0,1:T(1,128)} %copy-done.17) | copy-start | bytes 6148
  48.4 5.6 %copy-start.20 = (f32[512,1]{0,1:T(1,128)S(1)}, f32[512,1]{0,1:T(1,128)}, u32[]{:S(2)}) copy-start(f32[512,1]{0,1:T(1,128)} %copy-done.19) | copy-start | bytes 6148
  48.4 5.6 %copy-start.22 = (f32[512,1]{0,1:T(1,128)S(1)}, f32[512,1]{0,1:T(1,128)}, u32[]{:S(2)}) copy-start(f32[512,1]{0,1:T(1,128)} %copy-done.21) | copy-start | bytes 6148
  49.3 10.5 %collective-permute-start.8 = (bf16[128,1152]{0,1:T(8,128)(2,1)S(1)}, bf16[128,1152]{0,1:T(8,128)(2,1)S(1)}, u32[]{:S(2)}, u32[]{:S(2)}) collective-permute-start(bf16[128,1152]{0,1:T(8,128)(2,1)S(1)} %get-tuple-element.48), channel_id=1, source_target_pairs={{0,2},{2,0},{4,6},{6,4},{8,10},{10,8},{12,14},{14,12},{1,3},{3,1},... | collective-permute-start | bytes 884744 | tf_op jit(solution)/shard_map/ppermute | solution.py:41
  52.1 9.6 %collective-permute-start.13 = (bf16[128,1152]{0,1:T(8,128)(2,1)S(1)}, bf16[128,1152]{0,1:T(8,128)(2,1)S(1)}, u32[]{:S(2)}, u32[]{:S(2)}) collective-permute-start(bf16[128,1152]{0,1:T(8,128)(2,1)S(1)} %get-tuple-element.49), channel_id=1, source_target_pairs={{0,4},{2,6},{4,0},{6,2},{8,12},{10,14},{12,8},{14,10},{1,5},{3,7},... | collective-permute-start | bytes 884744 | tf_op jit(solution)/shard_map/ppermute | solution.py:41
  62.0 8.8 %collective-permute-start.14 = (bf16[64,1152]{0,1:T(8,128)(2,1)S(1)}, bf16[64,1152]{0,1:T(8,128)(2,1)S(1)}, u32[]{:S(2)}, u32[]{:S(2)}) collective-permute-start(bf16[64,1152]{0,1:T(8,128)(2,1)S(1)} %select_convert_fusion.1), channel_id=1, source_target_pairs={{0,2},{2,0},{4,6},{6,4},{8,10},{10,8},{12,14},{14,12},{1,3},{3,1},... | collective-permute-start | bytes 442376 | tf_op jit(solution)/shard_map/ppermute | solution.py:41
  63.9 9.9 %collective-permute-start.9 = (bf16[64,1152]{0,1:T(8,128)(2,1)S(1)}, bf16[64,1152]{0,1:T(8,128)(2,1)S(1)}, u32[]{:S(2)}, u32[]{:S(2)}) collective-permute-start(bf16[64,1152]{0,1:T(8,128)(2,1)S(1)} %select_convert_fusion.3), channel_id=1, source_target_pairs={{0,4},{2,6},{4,0},{6,2},{8,12},{10,14},{12,8},{14,10},{1,5},{3,7},... | collective-permute-start | bytes 442376 | tf_op jit(solution)/shard_map/ppermute | solution.py:41
  71.0 22.6 %collective-permute-start.15 = (bf16[64,1152]{0,1:T(8,128)(2,1)S(1)}, bf16[64,1152]{0,1:T(8,128)(2,1)S(1)}, u32[]{:S(2)}, u32[]{:S(2)}) collective-permute-start(bf16[64,1152]{0,1:T(8,128)(2,1)S(1)} %add_convert_fusion.1), channel_id=1, source_target_pairs={{0,8},{2,10},{4,12},{6,14},{8,0},{10,2},{12,4},{14,6},{1,9},{3,11}... | collective-permute-start | bytes 442376 | tf_op jit(solution)/shard_map/ppermute | solution.py:41
  74.0 24.8 %collective-permute-start.10 = (bf16[64,1152]{0,1:T(8,128)(2,1)S(1)}, bf16[64,1152]{0,1:T(8,128)(2,1)S(1)}, u32[]{:S(2)}, u32[]{:S(2)}) collective-permute-start(bf16[64,1152]{0,1:T(8,128)(2,1)S(1)} %add_convert_fusion.3), channel_id=1, source_target_pairs={{0,8},{2,10},{4,12},{6,14},{8,0},{10,2},{12,4},{14,6},{1,9},{3,11}... | collective-permute-start | bytes 442376 | tf_op jit(solution)/shard_map/ppermute | solution.py:41
  93.7 7.0 %collective-permute-start.16 = (bf16[64,1152]{0,1:T(8,128)(2,1)S(1)}, bf16[64,1152]{0,1:T(8,128)(2,1)S(1)}, u32[]{:S(2)}, u32[]{:S(2)}) collective-permute-start(bf16[64,1152]{0,1:T(8,128)(2,1)S(1)} %add_convert_fusion), channel_id=1, source_target_pairs={{0,2},{2,0},{4,6},{6,4},{8,10},{10,8},{12,14},{14,12},{1,3},{3,1},... | collective-permute-start | bytes 442376 | tf_op jit(solution)/shard_map/ppermute | solution.py:41
  98.8 10.0 %collective-permute-start.11 = (bf16[64,1152]{0,1:T(8,128)(2,1)S(1)}, bf16[64,1152]{0,1:T(8,128)(2,1)S(1)}, u32[]{:S(2)}, u32[]{:S(2)}) collective-permute-start(bf16[64,1152]{0,1:T(8,128)(2,1)S(1)} %add_convert_fusion.2), channel_id=1, source_target_pairs={{0,4},{2,6},{4,0},{6,2},{8,12},{10,14},{12,8},{14,10},{1,5},{3,7},... | collective-permute-start | bytes 442376 | tf_op jit(solution)/shard_map/ppermute | solution.py:41
  101.1 12.1 %collective-permute-start.17 = (bf16[128,1152]{0,1:T(8,128)(2,1)S(1)}, bf16[128,1152]{0,1:T(8,128)(2,1)S(1)}, u32[]{:S(2)}, u32[]{:S(2)}) collective-permute-start(bf16[128,1152]{0,1:T(8,128)(2,1)S(1)} %maximum_select_fusion.4), channel_id=1, source_target_pairs={{0,4},{2,6},{4,0},{6,2},{8,12},{10,14},{12,8},{14,10},{1,5},{3,7},... | collective-permute-start | bytes 884744 | tf_op jit(solution)/shard_map/ppermute | solution.py:41
  109.2 6.8 %collective-permute-start.12 = (bf16[128,1152]{0,1:T(8,128)(2,1)S(1)}, bf16[128,1152]{0,1:T(8,128)(2,1)S(1)}, u32[]{:S(2)}, u32[]{:S(2)}) collective-permute-start(bf16[128,1152]{0,1:T(8,128)(2,1)S(1)} %maximum_select_fusion.3), channel_id=1, source_target_pairs={{0,2},{2,0},{4,6},{6,4},{8,10},{10,8},{12,14},{14,12},{1,3},{3,1},... | collective-permute-start | bytes 884744 | tf_op jit(solution)/shard_map/ppermute | solution.py:41
  111.9 8.5 %collective-permute-start.3 = (f32[1152]{0:T(1024)S(1)}, f32[1152]{0:T(1024)S(1)}, u32[]{:S(2)}, u32[]{:S(2)}) collective-permute-start(f32[1152]{0:T(1024)S(1)} %concatenate.53), channel_id=1, source_target_pairs={{0,1},{1,0},{2,3},{3,2},{4,5},{5,4},{6,7},{7,6},{8,9},{9,8},{10,11... | collective-permute-start | bytes 13832 | tf_op jit(solution)/shard_map/ppermute | solution.py:41
  116.3 21.0 %collective-permute-start.18 = (bf16[512,1152]{0,1:T(8,128)(2,1)S(1)}, bf16[512,1152]{0,1:T(8,128)(2,1)S(1)}, u32[]{:S(2)}, u32[]{:S(2)}) collective-permute-start(bf16[512,1152]{0,1:T(8,128)(2,1)S(1)} %pad_maximum_fusion), channel_id=1, source_target_pairs={{0,1},{1,0},{2,3},{3,2},{4,5},{5,4},{6,7},{7,6},{8,9},{9,8},{10,11... | collective-permute-start | bytes 3538952 | tf_op jit(solution)/shard_map/ppermute | solution.py:41
  117.0 17.1 %collective-permute-start.19 = (bf16[2,16,1024]{2,1,0:T(8,128)(2,1)S(1)}, bf16[2,16,1024]{2,1,0:T(8,128)(2,1)S(1)}, u32[]{:S(2)}, u32[]{:S(2)}) collective-permute-start(bf16[2,16,1024]{2,1,0:T(8,128)(2,1)S(1)} %get-tuple-element.51), channel_id=1, source_target_pairs={{0,2},{2,4},{4,6},{6,8},{8,10},{10,12},{12,14},{1,3},{3,5},{5,7},{... | collective-permute-start | bytes 196616 | tf_op jit(solution)/shard_map/ppermute | solution.py:26
  121.1 3.7 %collective-permute-start.4 = (f32[1152]{0:T(1024)S(1)}, f32[1152]{0:T(1024)S(1)}, u32[]{:S(2)}, u32[]{:S(2)}) collective-permute-start(f32[1152]{0:T(1024)S(1)} %pad_add_fusion), channel_id=1, source_target_pairs={{0,2},{2,0},{4,6},{6,4},{8,10},{10,8},{12,14},{14,12},{1,3},{3,1},... | collective-permute-start | bytes 13832 | tf_op jit(solution)/shard_map/ppermute | solution.py:41
  124.8 3.7 %collective-permute-start.5 = (f32[1152]{0:T(1024)S(1)}, f32[1152]{0:T(1024)S(1)}, u32[]{:S(2)}, u32[]{:S(2)}) collective-permute-start(f32[1152]{0:T(1024)S(1)} %add.142), channel_id=1, source_target_pairs={{0,4},{2,6},{4,0},{6,2},{8,12},{10,14},{12,8},{14,10},{1,5},{3,7},... | collective-permute-start | bytes 13832 | tf_op jit(solution)/shard_map/ppermute | solution.py:41
  128.4 4.5 %collective-permute-start.6 = (f32[1152]{0:T(1024)S(1)}, f32[1152]{0:T(1024)S(1)}, u32[]{:S(2)}, u32[]{:S(2)}) collective-permute-start(f32[1152]{0:T(1024)S(1)} %add.143), channel_id=1, source_target_pairs={{0,8},{2,10},{4,12},{6,14},{8,0},{10,2},{12,4},{14,6},{1,9},{3,11}... | collective-permute-start | bytes 13832 | tf_op jit(solution)/shard_map/ppermute | solution.py:41
  131.1 6.1 %collective-permute-start.20 = (bf16[2,16,1024]{2,1,0:T(8,128)(2,1)S(1)}, bf16[2,16,1024]{2,1,0:T(8,128)(2,1)S(1)}, u32[]{:S(2)}, u32[]{:S(2)}) collective-permute-start(bf16[2,16,1024]{2,1,0:T(8,128)(2,1)S(1)} %get-tuple-element.50), channel_id=1, source_target_pairs={{2,0},{4,2},{6,4},{8,6},{10,8},{12,10},{14,12},{3,1},{5,3},{7,5},{... | collective-permute-start | bytes 196616 | tf_op jit(solution)/shard_map/ppermute | solution.py:26
  138.7 7.8 %copy-start.1 = (bf16[1024,1024]{1,0:T(8,128)(2,1)S(1)}, bf16[1024,1024]{1,0:T(8,128)(2,1)}, u32[]{:S(2)}) copy-start(bf16[1024,1024]{1,0:T(8,128)(2,1)} %param.26) | copy-start | bytes 6291460
  (24 other events, 70.8 us)

commit v2 on v0

v2 whole, which is shorter than its diff:
```python
import jax
import jax.numpy as jnp
from jax import lax
from jax.experimental import pallas as pl
from jax.experimental.pallas import tpu as pltpu
from jax.sharding import PartitionSpec as P

RIM = 16
SMOOTH_SQ = 0.01
LANES = 128
BF16 = jnp.bfloat16
F32 = jnp.float32
VMEM = pl.BlockSpec(memory_space=pltpu.VMEM)
SMEM = pl.BlockSpec(memory_space=pltpu.SMEM)
PARAMS = pltpu.CompilerParams(vmem_limit_bytes=32 * 1024 * 1024)


def shift(value, axis, steps):
    count = lax.axis_size(axis)
    first, last = (max(0, -steps), min(count, count - steps))
    return lax.ppermute(value, axis, [(source, source + steps) for source in range(first, last)])


def swap_cores(value):
    return lax.ppermute(value, "member", [(0, 1), (1, 0)])


def swap_bits(value, bits):
    pairs = [
        (s * 2 + c, (s ^ (1 << bits[c])) * 2 + c)
        for s in range(lax.axis_size("space"))
        for c in range(2)
    ]
    return lax.ppermute(value, ("space", "member"), pairs)


def orders(chunk, count):
    first = [[(0, 1), (1, 0), (2, 2)], [(0, 2), (2, 0), (1, 1)]][chunk]
    return first + [(bit, bit) for bit in range(3, count)]


def turn(chunk, count, space, half):
    value = 0
    stages = orders(chunk, count)[:-1]
    for level, bits in enumerate(stages):
        value = value + ((1 - ((space >> bits[half]) & 1)) << (len(stages) - 1 - level))
    return value


def dot(a, b, dims=((1,), (0,))):
    return lax.dot_general(a, b, (dims, ((), ())), preferred_element_type=F32)


def adjacency_kernel(place, index, mask, weight, valid, area, var_weight, adj, adj_t, score_weight):
    points = index.shape[1]
    nodes = jax.lax.broadcasted_iota(jnp.int32, (LANES, points), 0) + place[0]
    total = jnp.zeros((LANES, points), F32)
    for slot in range(index.shape[0]):
        coefficient = weight[slot : slot + 1, :] * mask[slot : slot + 1, :].astype(F32)
        total = total + jnp.where(index[slot : slot + 1, :] == nodes, coefficient, 0.0)
    upper = total.astype(BF16).astype(F32)
    lower = total - upper
    adj_t[:LANES, :] = upper.astype(BF16)
    adj_t[LANES:, :] = lower.astype(BF16)
    adj[:, :LANES] = upper.T.astype(BF16)
    adj[:, LANES:] = lower.T.astype(BF16)
    score_weight[...] = var_weight[...] * (valid[...].astype(F32) * area[...] / points)


def forward_kernel(
    adj, low, own, high, gain, hidden_weight, output_weight,
    normed, hidden, slope, outputs, deviation, extended, summed, projected,
):
    members, nodes, width = own.shape
    points = adj.shape[0]
    tile = 256
    for member in range(members):
        for part in range(2):
            start = part * LANES
            extended[start : start + RIM, :] = low[member]
            extended[start + RIM : start + RIM + nodes, :] = own[member]
            extended[start + RIM + nodes : start + 2 * RIM + nodes, :] = high[member]
            extended[start + 2 * RIM + nodes : start + LANES, :] = jnp.zeros(
                (LANES - 2 * RIM - nodes, width), BF16
            )
        summed[...] = dot(adj[...], extended[...])

        @pl.loop(0, points // 32, unroll=4)
        def _(step):
            rows = pl.ds(pl.multiple_of(step * 32, 32), 32)
            target = pl.ds(pl.multiple_of(member * points + step * 32, 32), 32)
            value = summed[rows, :]
            value = value - jnp.sum(value, axis=1, keepdims=True) * (1.0 / width)
            spread = jnp.sum(value * value, axis=1, keepdims=True) * (1.0 / width)
            inverse = lax.rsqrt(spread + 1e-05)
            deviation[target, :] = inverse
            normed[target, :] = (value * inverse * gain[...]).astype(BF16)

    for member in range(members):
        rows = slice(member * points, (member + 1) * points)
        for column in range(0, width, tile):
            columns = slice(column, column + tile)
            pre = dot(normed[rows, :], hidden_weight[:, columns])
            sig = 0.5 * jnp.tanh(0.5 * pre) + 0.5
            hid = pre * sig
            slope[rows, columns] = (sig + hid * (1.0 - sig)).astype(BF16)
            hid = hid.astype(BF16)
            hidden[rows, columns] = hid
            term = dot(hid, output_weight[:, columns], ((1,), (1,)))
            if column == 0:
                projected[...] = term
            else:
                projected[...] += term
        outputs[member] = projected[...].T[: outputs.shape[1], :]


def own_rows(place, count, width):
    half_rows, chunk_rows = width // 2, width // 4
    size = chunk_rows >> (count - 1)
    for half in range(2):
        for chunk in range(2):
            mask = turn(chunk, count, place[0], half)
            for block in range(chunk_rows // size):
                row = half * half_rows + chunk * chunk_rows
                start = (1 - (place[1] ^ half)) * half_rows + chunk * chunk_rows
                start = start + (block ^ mask) * size
                yield row + block * size, size, pl.multiple_of(start, size)


def transpose_kernel(count, place, normed, normed_t):
    width = normed.shape[1]
    value = None
    for row, size, target in own_rows(place, count, width):
        if row % LANES == 0:
            value = normed[:, row : row + LANES].T
        offset = row % LANES
        normed_t[pl.ds(target, size), :] = value[offset : offset + size]


def score_kernel(
    count, place, outputs, others, state, target, score_weight, output_weight, slope, hidden, normed_t,
    loss, grad_pre, grad_out, sent,
    grad_pred, grad_pred_t,
):
    members, variables, points = outputs.shape
    width = hidden.shape[1]
    total = 2 * members
    weight = score_weight[...]
    grad_pred_t[...] = jnp.zeros_like(grad_pred_t)
    grad_pred[...] = jnp.zeros_like(grad_pred)
    base = state[...] - target[...]
    values = [outputs[m] for m in range(members)]
    grads = [None] * members
    pair_grads = [jnp.zeros((variables, points), F32) for _ in range(members)]
    errors = jnp.zeros((variables, points), F32)
    pairs = jnp.full((variables, points), members * SMOOTH_SQ**0.5, F32)
    for m in range(members):
        diff = values[m] + base
        square = diff * diff + SMOOTH_SQ
        inverse = lax.rsqrt(square)
        errors = errors + square * inverse
        grads[m] = diff * inverse
        for n in range(m + 1, members):
            diff = values[m] - values[n]
            square = diff * diff + SMOOTH_SQ
            inverse = lax.rsqrt(square)
            pairs = pairs + 2.0 * (square * inverse)
            pair_grads[m] = pair_grads[m] + diff * inverse
            pair_grads[n] = pair_grads[n] - diff * inverse
        for n in range(members):
            diff = values[m] - others[n]
            square = diff * diff + SMOOTH_SQ
            inverse = lax.rsqrt(square)
            pairs = pairs + square * inverse
            pair_grads[m] = pair_grads[m] + diff * inverse
    score = weight * (errors * (1.0 / total) - pairs * (1.0 / (2.0 * total * (total - 1))))
    loss[...] = jnp.sum(jnp.sum(score, axis=0, keepdims=True), axis=1, keepdims=True)
    for m in range(members):
        grad = weight * (grads[m] * (1.0 / total) - pair_grads[m] * (1.0 / (total * (total - 1))))
        columns = slice(m * points, (m + 1) * points)
        grad_pred_t[:variables, columns] = grad
        grad_pred[columns, :] = grad_pred_t[:, columns].T.astype(BF16)
    for m in range(members):
        rows = slice(m * points, (m + 1) * points)
        for column in range(0, width, 256):
            columns = slice(column, column + 256)
            grad_hid = dot(grad_pred[rows, :], output_weight[:, columns])
            grad_pre[rows, columns] = (grad_hid * slope[rows, columns].astype(F32)).astype(BF16)
    value = dot(grad_pred_t[...].astype(BF16), hidden[...]).T
    for row, size, place_row in own_rows(place, count, width):
        grad_out[pl.ds(place_row, size), :] = value[row : row + size]
    half = width // 2
    for column in range(0, width, 256):
        columns = slice(column, column + 256)
        sent[:, columns] = dot(normed_t[:half, :], grad_pre[:, columns]).astype(BF16)
    sent[:, width:] = grad_out[:half, :].astype(BF16)


def product_kernel(normed_t, grad_pre, grad_out, kept):
    width = grad_pre.shape[1]
    half = width // 2
    for column in range(0, width, 256):
        columns = slice(column, column + 256)
        kept[:, columns] = dot(normed_t[half:, :], grad_pre[:, columns])
    kept[:, width:] = grad_out[half:, :]


def backward_kernel(
    grad_pre, hidden_weight, normed, gain, deviation, adj_t,
    grad_gain, inner, below, above,
    product, rows_grad,
):
    members, nodes, width = inner.shape
    points = adj_t.shape[1]
    inverse_gain = 1.0 / gain[...]
    total = jnp.zeros((8, width), F32)
    for member in range(members):
        rows = slice(member * points, (member + 1) * points)
        for column in range(0, width, 256):
            columns = slice(column, column + 256)
            product[:, columns] = dot(grad_pre[rows, :], hidden_weight[columns, :], ((1,), (1,)))

        def step(index, total):
            here = pl.ds(pl.multiple_of(index * 32, 32), 32)
            there = pl.ds(pl.multiple_of(member * points + index * 32, 32), 32)
            value = product[here, :]
            zn = normed[there, :].astype(F32)
            both = value * zn
            scaled = value * gain[...]
            mean = jnp.sum(scaled, axis=1, keepdims=True) * (1.0 / width)
            slant = jnp.sum(both, axis=1, keepdims=True) * (1.0 / width)
            grad = deviation[there, :] * (scaled - mean - (zn * inverse_gain) * slant)
            rows_grad[here, :] = grad.astype(BF16)
            return total + jnp.sum(both.reshape(4, 8, width), axis=0)

        total = lax.fori_loop(0, points // 32, step, total, unroll=4)
        value = dot(adj_t[...], rows_grad[...])
        value = value[:LANES] + value[LANES:]
        below[member] = value[:RIM].astype(BF16)
        inner[member] = value[RIM : RIM + nodes]
        above[member] = value[RIM + nodes : nodes + 2 * RIM].astype(BF16)
    grad_gain[...] = jnp.sum(total, axis=0, keepdims=True) * inverse_gain


def write_half(count, place, half, source, target, wide, sems):
    rows, width = wide.shape
    chunk_rows = rows // 2
    size = chunk_rows >> (count - 1)
    copies = []
    for chunk in range(2):
        mask = jnp.where(half == 0, turn(chunk, count, place[0], 0), turn(chunk, count, place[0], 1))
        for block in range(chunk_rows // size):
            start = chunk * chunk_rows + block * size
            here = slice(start, start + size)
            wide[here, :] = source[here, :width].astype(F32)
            row = half * rows + chunk * chunk_rows + (block ^ mask) * size
            copy = pltpu.make_async_copy(
                wide.at[here, :],
                target.at[pl.ds(pl.multiple_of(row, size), size), :],
                sems.at[start // size],
            )
            copy.start()
            copies.append(copy)
    return copies


def first_write_kernel(count, place, source, target, wide, sems):
    for copy in write_half(count, place, place[1], source, target, wide, sems):
        copy.wait()


def last_write_kernel(count, place, own, source, before, target, grad_out_t, wide, narrow, sems):
    del before
    copies = write_half(count, place, 1 - place[1], source, target, wide, sems)
    half, width = wide.shape
    for row, size, place_row in own_rows(place, count, width):
        here = pl.ds(pl.multiple_of(place_row % half, size), size)
        mine = own[here, width:].astype(F32)
        other = source[here, width:].astype(F32)
        narrow[row : row + size, :] = jnp.where(place_row >= half, mine, other)
    grad_out_t[...] = narrow[...].T[: grad_out_t.shape[0], :]
    for copy in copies:
        copy.wait()


def add_parts(mine, other):
    return (mine.astype(F32) + other.astype(F32)).astype(BF16)


def sum_chunk(value, chunk, count):
    stages = orders(chunk, count)
    for bits in stages[:-1]:
        rows = value.shape[0] // 2
        value = add_parts(value[rows:], swap_bits(value[:rows], bits))
    value = add_parts(value, swap_bits(value, stages[-1]))
    for bits in reversed(stages[:-1]):
        value = jnp.concatenate([swap_bits(value, bits), value])
    return value


def sum_small(value):
    value = value + swap_cores(value)
    for bit in range(lax.axis_size("space").bit_length() - 1):
        value = value + swap_bits(value, (bit, bit))
    return value


def cost(flops, moved):
    return pl.CostEstimate(flops=flops, bytes_accessed=moved, transcendentals=0)


def local(
    latent,
    edge_node_index,
    edge_mask,
    edge_weight,
    valid,
    area,
    state,
    target,
    var_weight,
    gain,
    hidden_weight,
    output_weight,
):
    members, nodes, width = latent.shape
    points, variables = state.shape
    rows = members * points
    count = lax.axis_size("space").bit_length() - 1
    space, core = lax.axis_index("space"), lax.axis_index("member")
    place = jnp.stack([space, core]).astype(jnp.int32)
    low = shift(latent[:, nodes - RIM :], "space", 1)
    high = shift(latent[:, :RIM], "space", -1)
    gain = gain.reshape(1, width)
    output_weight = jnp.pad(output_weight.T, ((0, LANES - variables), (0, 0)))

    adj, adj_t, score_weight = pl.pallas_call(
        adjacency_kernel,
        out_shape=(
            pltpu.VMEM((points, 2 * LANES), BF16),
            pltpu.VMEM((2 * LANES, points), BF16),
            pltpu.VMEM((variables, points), F32),
        ),
        in_specs=[SMEM] + [VMEM] * 6,
        out_specs=(VMEM,) * 3,
        compiler_params=PARAMS,
        name="adjacency",
    )(
        (space * nodes - RIM).astype(jnp.int32).reshape(1),
        edge_node_index.T,
        edge_mask.T,
        edge_weight.T,
        valid.reshape(1, points),
        area.reshape(1, points),
        var_weight.reshape(variables, 1),
    )
    normed, hidden, slope, outputs, deviation = pl.pallas_call(
        forward_kernel,
        out_shape=(
            pltpu.VMEM((rows, width), BF16),
            pltpu.VMEM((rows, width), BF16),
            pltpu.VMEM((rows, width), BF16),
            jax.ShapeDtypeStruct((members, variables, points), F32),
            pltpu.VMEM((rows, 1), F32),
        ),
        in_specs=[VMEM] * 7,
        out_specs=(VMEM,) * 5,
        scratch_shapes=[
            pltpu.VMEM((2 * LANES, width), BF16),
            pltpu.VMEM((points, width), F32),
            pltpu.VMEM((points, LANES), F32),
        ],
        compiler_params=PARAMS,
        name="forward",
    )(adj, low, latent, high, gain, hidden_weight, output_weight)
    others = swap_cores(outputs)
    normed_t = pl.pallas_call(
        lambda *refs: transpose_kernel(count, *refs),
        out_shape=pltpu.VMEM((width, rows), BF16),
        in_specs=[SMEM, VMEM],
        out_specs=VMEM,
        compiler_params=PARAMS,
        cost_estimate=cost(10**9, 4 * 10**6),
        name="transpose",
    )(place, normed)
    loss, grad_pre, grad_out, sent = pl.pallas_call(
        lambda *refs: score_kernel(count, *refs),
        out_shape=(
            jax.ShapeDtypeStruct((1, 1), F32),
            pltpu.VMEM((rows, width), BF16),
            pltpu.VMEM((width, LANES), F32),
            jax.ShapeDtypeStruct((width // 2, width + LANES), BF16),
        ),
        in_specs=[SMEM] + [VMEM] * 9,
        out_specs=(VMEM,) * 4,
        scratch_shapes=[pltpu.VMEM((rows, LANES), BF16), pltpu.VMEM((LANES, rows), F32)],
        compiler_params=PARAMS,
        name="score",
    )(place, outputs, others, state.T, target.T, score_weight, output_weight, slope, hidden, normed_t)
    received = swap_cores(sent)
    kept = pl.pallas_call(
        product_kernel,
        out_shape=jax.ShapeDtypeStruct((width // 2, width + LANES), F32),
        in_specs=[VMEM] * 3,
        out_specs=VMEM,
        compiler_params=PARAMS,
        cost_estimate=cost(2 * 10**9, 4 * 10**6),
        name="product",
    )(normed_t, grad_pre, grad_out)
    value = add_parts(kept, received)
    grad_gain, inner, below, above = pl.pallas_call(
        backward_kernel,
        out_shape=(
            jax.ShapeDtypeStruct((1, width), F32),
            jax.ShapeDtypeStruct((members, nodes, width), F32),
            jax.ShapeDtypeStruct((members, RIM, width), BF16),
            jax.ShapeDtypeStruct((members, RIM, width), BF16),
        ),
        in_specs=[VMEM] * 6,
        out_specs=(VMEM,) * 4,
        scratch_shapes=[pltpu.VMEM((points, width), F32), pltpu.VMEM((points, width), BF16)],
        compiler_params=PARAMS,
        cost_estimate=cost(5 * 10**9, 8 * 10**6),
        name="backward",
    )(grad_pre, hidden_weight, normed, gain, deviation, adj_t)
    small = jnp.concatenate([grad_gain.reshape(width), jnp.broadcast_to(loss.reshape(1), (LANES,))])
    small = sum_small(small)
    from_below, from_above = shift(above, "space", 1), shift(below, "space", -1)
    grad_latent = inner.at[:, :RIM].add(from_below.astype(F32))
    grad_latent = grad_latent.at[:, nodes - RIM :].add(from_above.astype(F32))

    chunk_rows = width // 4
    own = jnp.concatenate(
        [sum_chunk(value[k * chunk_rows : (k + 1) * chunk_rows], k, count) for k in range(2)]
    )
    other = swap_cores(own)
    blocks = 1 << count
    write_scratch = [pltpu.VMEM((width // 2, width), F32), pltpu.SemaphoreType.DMA((blocks,))]
    hidden_shape = jax.ShapeDtypeStruct((width, width), F32)
    grad_hidden = pl.pallas_call(
        lambda *refs: first_write_kernel(count, *refs),
        out_shape=hidden_shape,
        in_specs=[SMEM, VMEM],
        out_specs=pl.BlockSpec(memory_space=pl.ANY),
        scratch_shapes=write_scratch,
        compiler_params=PARAMS,
        cost_estimate=cost(10**6, 3 * 10**6),
        name="first_write",
    )(place, own)
    grad_hidden, grad_out = pl.pallas_call(
        lambda *refs: last_write_kernel(count, *refs),
        out_shape=(hidden_shape, jax.ShapeDtypeStruct((variables, width), F32)),
        in_specs=[SMEM, VMEM, VMEM, pl.BlockSpec(memory_space=pl.ANY)],
        out_specs=(pl.BlockSpec(memory_space=pl.ANY), VMEM),
        scratch_shapes=[write_scratch[0], pltpu.VMEM((width, LANES), F32), write_scratch[1]],
        input_output_aliases={3: 0},
        compiler_params=PARAMS,
        name="last_write",
    )(place, own, other, grad_hidden)
    return (small[width : width + 1], grad_hidden, grad_out.T, small[:width], grad_latent)


def solution(mesh):
    in_specs = (
        P(("groups", "member"), "space", None),
        P(("groups", "space"), None),
        P(("groups", "space"), None),
        P(("groups", "space"), None),
        P(("groups", "space")),
        P(("groups", "space")),
        P(("groups", "space"), None),
        P(("groups", "space"), None),
        P(),
        P(),
        P(),
        P(),
    )
    out_specs = (
        P("groups"),
        P("groups", None),
        P("groups", None),
        P("groups"),
        P(("groups", "member"), "space", None),
    )
    return jax.shard_map(local, mesh=mesh, in_specs=in_specs, out_specs=out_specs, check_vma=False)
```

time: 191 us -> 122 us (0.64)
  waiting for transfers between devices: 73 us -> 34.5 us
  blocking collectives: 36.9 us -> 0 us
  starting transfers between devices: 12.9 us -> 39.5 us
  Pallas kernels: 0 us -> 24.3 us
  matrix products: 23.6 us -> 0 us
  between operations: 14.4 us -> 0.96 us
  other arithmetic: 13 us -> 4.42 us
    psum x1 -> x0, waiting for transfers between devices: 73 us -> none  [local(): lax.psum((part_hidden, part_out, partial_gain, loss_local), ('space', 'me...]
    ppermute x4 -> x21, waiting for transfers between devices: 0.01 us -> 34.5 us  [the longest x13 31 us: swap_bits(): return lax.ppermute(value, ('space', 'member'), pairs)]
    psum x1 -> x0, blocking collectives: 34.3 us -> none  [local(): lax.psum((part_hidden, part_out, partial_gain, loss_local), ('space', 'me...]
    ppermute x4 -> x21, starting transfers between devices: 12.9 us -> 39.5 us  [the longest x13 26.9 us: swap_bits(): return lax.ppermute(value, ('space', 'member'), pairs)]
    pallas_call x0 -> x8, Pallas kernels: none -> 24.3 us  [the longest x1 6.99 us: local(): pl.pallas_call(forward_kernel, out_shape=(pltpu.VMEM((rows, width), BF16)...]
    dot_general x11 -> x0, matrix products: 23.6 us -> none  [the longest x1 7.51 us: local(): jnp.dot(gpre, hidden_weight.T, preferred_element_type=jnp.float32)]
    mul x3 -> x0, other arithmetic: 5.57 us -> none  [the longest x1 4.12 us: local(): inverse_deviation * (scaled_rows - jnp.mean(scaled_rows, axis=1, keepdims...]
    reduce_sum x3 -> x0, other arithmetic: 5.17 us -> none  [the longest x1 3.24 us: local(): jnp.sum(pair / smooth(pair), axis=1) / (total * (total - 1))]
  transfers between devices with their start and end apart: 5 -> 21, of which waited for: 1 -> 16; matrix products, arithmetic and copies ran while one was open for 6% -> 6% of each run, Pallas kernels for 0% -> 9%
where the time goes in v2:
time: 122 us
  starting transfers between devices  39.5 us (32%)
  waiting for transfers between devices  34.5 us (28%)
  Pallas kernels  24.3 us (20%)
  local copies, waits for them, and re-layouts  17.9 us (15%)
  other arithmetic  4.42 us (4%)
    ppermute x13, waiting for transfers between devices, swap_bits(): return lax.ppermute(value, ('space', 'member'), pairs)  31 us
    ppermute x13, starting transfers between devices, swap_bits(): return lax.ppermute(value, ('space', 'member'), pairs)  26.9 us
    unnamed x49, local copies, waits for them, and re-layouts  13.4 us
    ppermute x4, starting transfers between devices, shift(): lax.ppermute(value, axis, [(source, source + steps) for source in range(f...  11.5 us
    pallas_call x1, Pallas kernels, local(): pl.pallas_call(forward_kernel, out_shape=(pltpu.VMEM((rows, width), BF16)...  6.99 us
    pallas_call x1, Pallas kernels, local(): pl.pallas_call(backward_kernel, out_shape=(jax.ShapeDtypeStruct((1, width...  6.31 us
    pallas_call x1, Pallas kernels, local(): pl.pallas_call(lambda *refs: score_kernel(count, *refs), out_shape=(jax.S...  3.59 us
    pallas_call x1, Pallas kernels, local(): pl.pallas_call(lambda *refs: last_write_kernel(count, *refs), out_shape=(...  2.8 us
  transfers between devices with their start and end apart: 21, of which 16 were waited for; matrix products, arithmetic and copies ran while one was open for 6% of the time, Pallas kernels for 9%

profile of v2, /device:TPU:0, one launch (start us, length us, event | category | flops | bytes accessed | tf_op | source)
XLA Modules:
  0.0 121.6 jit_solution(2680616214517155148)
XLA Ops:
  2.8 5.5 %collective-permute-start = (bf16[2,16,1024]{2,1,0:T(8,128)(2,1)S(1)}, bf16[2,16,1024]{2,1,0:T(8,128)(2,1)S(1)}, u32[]{:S(2)}, u32[]{:S(2)}) collective-permute-start(bf16[2,16,1024]{2,1,0:T(8,128)(2,1)S(1)} %get-tuple-element.70), channel_id=1, source_target_pairs={{0,2},{2,4},{4,6},{6,8},{8,10},{10,12},{12,14},{1,3},{3,5},{5,7},{... | collective-permute-start | bytes 196616 | tf_op jit(solution)/shard_map/ppermute | solution.py:21
  14.5 1.7 %copy-done = bf16[1024,1024]{1,0:T(8,128)(2,1)S(1)} copy-done((bf16[1024,1024]{1,0:T(8,128)(2,1)S(1)}, bf16[1024,1024]{1,0:T(8,128)(2,1)}, u32[]{:S(2)}) %copy-start) | copy-done | bytes 2097176
  17.8 7.0 %forward.1 = (bf16[1024,1024]{1,0:T(8,128)(2,1)S(1)}, bf16[1024,1024]{1,0:T(8,128)(2,1)S(1)}, bf16[1024,1024]{1,0:T(8,128)(2,1)S(1)}, f32[2,100,512]{2,1,0:T(8,128)S(1)}, f32[1024,1]{1,0:T(8,128)S(1)}) custom-call(bf16[512,256]{1,0:T(8,128)(2,1)S(1)} %get-tuple-element.47.adj, bf16[2,16,1024]{2,1,0:T(8,128)(2,1)S(1)} %collective-permute-done.low, ...), custom_call_target="tpu_custom_call" | custom-call | tf_op jit(solution)/shard_map/forward/pallas_call | solution.py:357
  24.8 1.3 %copy-done.2 = bf16[1024,1024]{1,0:T(8,128)(2,1)} copy-done((bf16[1024,1024]{1,0:T(8,128)(2,1)}, bf16[1024,1024]{1,0:T(8,128)(2,1)S(1)}, u32[]{:S(2)}) %copy-start.2) | copy-done | bytes 2097176
  32.5 3.6 %score.1 = (f32[1,1]{1,0:T(1,128)}, bf16[1024,1024]{1,0:T(8,128)(2,1)S(1)}, f32[1024,128]{1,0:T(8,128)S(1)}, bf16[512,1152]{1,0:T(8,128)(2,1)S(1)}) custom-call(s32[2]{0:T(128)S(1)} %pad_add_fusion.1.refs_0_, f32[2,100,512]{2,1,0:T(8,128)S(1)} %get-tuple-element.48.refs_1_, f32[2,100,512]{2,1,0:T(8,128)S(1)} %collective-permute-done.2.refs_2_, ...), custom_call_target="tpu_custom_call" | custom-call | tf_op jit(solution)/shard_map/score/pallas_call | solution.py:386
  39.3 3.0 %collective-permute-start.13 = (bf16[128,1152]{1,0:T(8,128)(2,1)S(1)}, bf16[128,1152]{1,0:T(8,128)(2,1)S(1)}, u32[]{:S(2)}, u32[]{:S(2)}) collective-permute-start(bf16[128,1152]{1,0:T(8,128)(2,1)S(1)} %get-tuple-element.67), channel_id=1, source_target_pairs={{0,2},{1,9},{2,0},{3,11},{4,6},{5,13},{6,4},{7,15},{8,10},{9,1},{1... | collective-permute-start | bytes 884744 | tf_op jit(solution)/shard_map/ppermute | solution.py:34
  42.3 4.6 %collective-permute-done.13 = bf16[128,1152]{1,0:T(8,128)(2,1)S(1)} collective-permute-done((bf16[128,1152]{1,0:T(8,128)(2,1)S(1)}, bf16[128,1152]{1,0:T(8,128)(2,1)S(1)}, u32[]{:S(2)}, u32[]{:S(2)}) %collective-permute-start.13) | collective-permute-done | bytes 294944 | tf_op jit(solution)/shard_map/ppermute | solution.py:34
  47.0 3.2 %collective-permute-done.8 = bf16[128,1152]{1,0:T(8,128)(2,1)S(1)} collective-permute-done((bf16[128,1152]{1,0:T(8,128)(2,1)S(1)}, bf16[128,1152]{1,0:T(8,128)(2,1)S(1)}, u32[]{:S(2)}, u32[]{:S(2)}) %collective-permute-start.8) | collective-permute-done | bytes 294944 | tf_op jit(solution)/shard_map/ppermute | solution.py:34
  50.3 1.6 %collective-permute-start.9 = (bf16[64,1152]{1,0:T(8,128)(2,1)S(1)}, bf16[64,1152]{1,0:T(8,128)(2,1)S(1)}, u32[]{:S(2)}, u32[]{:S(2)}) collective-permute-start(bf16[64,1152]{1,0:T(8,128)(2,1)S(1)} %slice.108), channel_id=1, source_target_pairs={{0,4},{1,3},{2,6},{3,1},{4,0},{5,7},{6,2},{7,5},{8,12},{9,11},{10,... | collective-permute-start | bytes 442376 | tf_op jit(solution)/shard_map/ppermute | solution.py:34
  52.0 2.3 %collective-permute-start.14 = (bf16[64,1152]{1,0:T(8,128)(2,1)S(1)}, bf16[64,1152]{1,0:T(8,128)(2,1)S(1)}, u32[]{:S(2)}, u32[]{:S(2)}) collective-permute-start(bf16[64,1152]{1,0:T(8,128)(2,1)S(1)} %slice.112), channel_id=1, source_target_pairs={{0,8},{1,3},{2,10},{3,1},{4,12},{5,7},{6,14},{7,5},{8,0},{9,11},{1... | collective-permute-start | bytes 442376 | tf_op jit(solution)/shard_map/ppermute | solution.py:34
  55.5 2.6 %collective-permute-start.10 = (bf16[64,1152]{1,0:T(8,128)(2,1)S(1)}, bf16[64,1152]{1,0:T(8,128)(2,1)S(1)}, u32[]{:S(2)}, u32[]{:S(2)}) collective-permute-start(bf16[64,1152]{1,0:T(8,128)(2,1)S(1)} %add_convert_fusion.6), channel_id=1, source_target_pairs={{0,8},{1,9},{2,10},{3,11},{4,12},{5,13},{6,14},{7,15},{8,0},{9,1},... | collective-permute-start | bytes 442376 | tf_op jit(solution)/shard_map/ppermute | solution.py:34
  58.2 3.9 %collective-permute-done.14 = bf16[64,1152]{1,0:T(8,128)(2,1)S(1)} collective-permute-done((bf16[64,1152]{1,0:T(8,128)(2,1)S(1)}, bf16[64,1152]{1,0:T(8,128)(2,1)S(1)}, u32[]{:S(2)}, u32[]{:S(2)}) %collective-permute-start.14) | collective-permute-done | bytes 147488 | tf_op jit(solution)/shard_map/ppermute | solution.py:34
  62.2 3.8 %collective-permute-done.10 = bf16[64,1152]{1,0:T(8,128)(2,1)S(1)} collective-permute-done((bf16[64,1152]{1,0:T(8,128)(2,1)S(1)}, bf16[64,1152]{1,0:T(8,128)(2,1)S(1)}, u32[]{:S(2)}, u32[]{:S(2)}) %collective-permute-start.10) | collective-permute-done | bytes 147488 | tf_op jit(solution)/shard_map/ppermute | solution.py:34
  66.1 1.4 %collective-permute-done.15 = bf16[64,1152]{1,0:T(8,128)(2,1)S(1)} collective-permute-done((bf16[64,1152]{1,0:T(8,128)(2,1)S(1)}, bf16[64,1152]{1,0:T(8,128)(2,1)S(1)}, u32[]{:S(2)}, u32[]{:S(2)}) %collective-permute-start.15) | collective-permute-done | bytes 147488 | tf_op jit(solution)/shard_map/ppermute | solution.py:34
  67.6 1.6 %collective-permute-start.16 = (bf16[64,1152]{1,0:T(8,128)(2,1)S(1)}, bf16[64,1152]{1,0:T(8,128)(2,1)S(1)}, u32[]{:S(2)}, u32[]{:S(2)}) collective-permute-start(bf16[64,1152]{1,0:T(8,128)(2,1)S(1)} %add_convert_fusion.3), channel_id=1, source_target_pairs={{0,8},{1,3},{2,10},{3,1},{4,12},{5,7},{6,14},{7,5},{8,0},{9,11},{1... | collective-permute-start | bytes 442376 | tf_op jit(solution)/shard_map/ppermute | solution.py:34
  69.2 2.0 %collective-permute-done.11 = bf16[64,1152]{1,0:T(8,128)(2,1)S(1)} collective-permute-done((bf16[64,1152]{1,0:T(8,128)(2,1)S(1)}, bf16[64,1152]{1,0:T(8,128)(2,1)S(1)}, u32[]{:S(2)}, u32[]{:S(2)}) %collective-permute-start.11) | collective-permute-done | bytes 147488 | tf_op jit(solution)/shard_map/ppermute | solution.py:34
  71.3 2.1 %collective-permute-start.12 = (bf16[128,1152]{1,0:T(8,128)(2,1)S(1)}, bf16[128,1152]{1,0:T(8,128)(2,1)S(1)}, u32[]{:S(2)}, u32[]{:S(2)}) collective-permute-start(bf16[128,1152]{1,0:T(8,128)(2,1)S(1)} %pad_maximum_fusion), channel_id=1, source_target_pairs={{0,2},{1,5},{2,0},{3,7},{4,6},{5,1},{6,4},{7,3},{8,10},{9,13},{10,... | collective-permute-start | bytes 884744 | tf_op jit(solution)/shard_map/ppermute | solution.py:34
  73.3 2.0 %collective-permute-done.16 = bf16[64,1152]{1,0:T(8,128)(2,1)S(1)} collective-permute-done((bf16[64,1152]{1,0:T(8,128)(2,1)S(1)}, bf16[64,1152]{1,0:T(8,128)(2,1)S(1)}, u32[]{:S(2)}, u32[]{:S(2)}) %collective-permute-start.16) | collective-permute-done | bytes 147488 | tf_op jit(solution)/shard_map/ppermute | solution.py:34
  75.4 1.6 %collective-permute-start.17 = (bf16[128,1152]{1,0:T(8,128)(2,1)S(1)}, bf16[128,1152]{1,0:T(8,128)(2,1)S(1)}, u32[]{:S(2)}, u32[]{:S(2)}) collective-permute-start(bf16[128,1152]{1,0:T(8,128)(2,1)S(1)} %pad_maximum_fusion.1), channel_id=1, source_target_pairs={{0,2},{1,9},{2,0},{3,11},{4,6},{5,13},{6,4},{7,15},{8,10},{9,1},{1... | collective-permute-start | bytes 884744 | tf_op jit(solution)/shard_map/ppermute | solution.py:34
  78.1 4.1 %collective-permute-done.17 = bf16[128,1152]{1,0:T(8,128)(2,1)S(1)} collective-permute-done((bf16[128,1152]{1,0:T(8,128)(2,1)S(1)}, bf16[128,1152]{1,0:T(8,128)(2,1)S(1)}, u32[]{:S(2)}, u32[]{:S(2)}) %collective-permute-start.17) | collective-permute-done | bytes 294944 | tf_op jit(solution)/shard_map/ppermute | solution.py:34
  82.4 6.3 %backward.1 = (f32[1,1024]{1,0:T(1,128)S(1)}, f32[2,64,1024]{2,1,0:T(8,128)}, bf16[2,16,1024]{2,1,0:T(8,128)(2,1)S(1)}, bf16[2,16,1024]{2,1,0:T(8,128)(2,1)S(1)}) custom-call(bf16[1024,1024]{1,0:T(8,128)(2,1)S(1)} %get-tuple-element.53.grad_pre, bf16[1024,1024]{1,0:T(8,128)(2,1)S(1)} %copy-done.1, bf16[1024,1024]{1,0:T(8,128)(2,1)S(1)} %get-tuple-element.52.refs_1_.normed, ...), custom_call_target="tpu_custom_call" | custom-call | flops 5000000000 | bytes 8000000 | tf_op jit(solution)/shard_map/backward/pallas_call | solution.py:411
  89.9 3.4 %collective-permute-start.19 = (bf16[2,16,1024]{2,1,0:T(8,128)(2,1)S(1)}, bf16[2,16,1024]{2,1,0:T(8,128)(2,1)S(1)}, u32[]{:S(2)}, u32[]{:S(2)}) collective-permute-start(bf16[2,16,1024]{2,1,0:T(8,128)(2,1)S(1)} %get-tuple-element.63), channel_id=1, source_target_pairs={{0,2},{2,4},{4,6},{6,8},{8,10},{10,12},{12,14},{1,3},{3,5},{5,7},{... | collective-permute-start | bytes 196616 | tf_op jit(solution)/shard_map/ppermute | solution.py:21
  94.0 6.0 %collective-permute-start.4 = (f32[1152]{0:T(1024)S(1)}, f32[1152]{0:T(1024)S(1)}, u32[]{:S(2)}, u32[]{:S(2)}) collective-permute-start(f32[1152]{0:T(1024)S(1)} %pad_add_fusion), channel_id=1, source_target_pairs={{0,2},{1,3},{2,0},{3,1},{4,6},{5,7},{6,4},{7,5},{8,10},{9,11},{10,... | collective-permute-start | bytes 13832 | tf_op jit(solution)/shard_map/ppermute | solution.py:34
  100.0 1.6 %collective-permute-done.4 = f32[1152]{0:T(1024)S(1)} collective-permute-done((f32[1152]{0:T(1024)S(1)}, f32[1152]{0:T(1024)S(1)}, u32[]{:S(2)}, u32[]{:S(2)}) %collective-permute-start.4) | collective-permute-done | bytes 4640 | tf_op jit(solution)/shard_map/ppermute | solution.py:34
  101.6 2.6 %collective-permute-start.5 = (f32[1152]{0:T(1024)S(1)}, f32[1152]{0:T(1024)S(1)}, u32[]{:S(2)}, u32[]{:S(2)}) collective-permute-start(f32[1152]{0:T(1024)S(1)} %add.53), channel_id=1, source_target_pairs={{0,4},{1,5},{2,6},{3,7},{4,0},{5,1},{6,2},{7,3},{8,12},{9,13},{10,... | collective-permute-start | bytes 13832 | tf_op jit(solution)/shard_map/ppermute | solution.py:34
  104.2 1.6 %collective-permute-done.5 = f32[1152]{0:T(1024)S(1)} collective-permute-done((f32[1152]{0:T(1024)S(1)}, f32[1152]{0:T(1024)S(1)}, u32[]{:S(2)}, u32[]{:S(2)}) %collective-permute-start.5) | collective-permute-done | bytes 4640 | tf_op jit(solution)/shard_map/ppermute | solution.py:34
  105.8 3.4 %collective-permute-start.6 = (f32[1152]{0:T(1024)S(1)}, f32[1152]{0:T(1024)S(1)}, u32[]{:S(2)}, u32[]{:S(2)}) collective-permute-start(f32[1152]{0:T(1024)S(1)} %add.54), channel_id=1, source_target_pairs={{0,8},{1,9},{2,10},{3,11},{4,12},{5,13},{6,14},{7,15},{8,0},{9,1},... | collective-permute-start | bytes 13832 | tf_op jit(solution)/shard_map/ppermute | solution.py:34
  111.9 1.6 %add_dynamic-update-slice_fusion = f32[2,64,1024]{2,1,0:T(8,128)} fusion(f32[2,64,1024]{2,1,0:T(8,128)} %get-tuple-element.62, bf16[2,16,1024]{2,1,0:T(8,128)(2,1)S(1)} %collective-permute-done.19), kind=kLoop, calls=%fused_computation.11 | loop fusion | flops 65536 | bytes 327680 | tf_op jit(solution)/shard_map/scatter-add | solution.py:429
  113.5 1.8 %collective-permute-done.20 = bf16[2,16,1024]{2,1,0:T(8,128)(2,1)S(1)} collective-permute-done((bf16[2,16,1024]{2,1,0:T(8,128)(2,1)S(1)}, bf16[2,16,1024]{2,1,0:T(8,128)(2,1)S(1)}, u32[]{:S(2)}, u32[]{:S(2)}) %collective-permute-start.20) | collective-permute-done | bytes 65568 | tf_op jit(solution)/shard_map/ppermute | solution.py:21
  115.3 1.6 %fusion = f32[2,64,1024]{2,1,0:T(8,128)} fusion(f32[2,64,1024]{2,1,0:T(8,128)} %add_dynamic-update-slice_fusion, bf16[2,16,1024]{2,1,0:T(8,128)(2,1)S(1)} %collective-permute-done.20), kind=kLoop, calls=%fused_computation.10 | loop fusion | flops 65536 | bytes 327680 | tf_op jit(solution)/shard_map/scatter-add | solution.py:430
  116.9 1.9 %first_write.1.refs_3_ = f32[1024,1024]{1,0:T(8,128)} custom-call(s32[2]{0:T(128)S(1)} %pad_add_fusion.1.refs_0_, bf16[512,1152]{1,0:T(8,128)(2,1)S(1)} %constant_dynamic-update-slice_fusion.refs_1_), custom_call_target="tpu_custom_call" | custom-call | flops 1000000 | bytes 3000000 | tf_op jit(solution)/shard_map/first_write/pallas_call | solution.py:440
  118.8 2.8 %last_write.1 = (f32[1024,1024]{1,0:T(8,128)}, f32[100,1024]{1,0:T(8,128)}) custom-call(s32[2]{0:T(128)S(1)} %pad_add_fusion.1.refs_0_, bf16[512,1152]{1,0:T(8,128)(2,1)S(1)} %constant_dynamic-update-slice_fusion.refs_1_, bf16[512,1152]{1,0:T(8,128)(2,1)S(1)} %collective-permute-done.18.refs_2_, ...), custom_call_target="tpu_custom_call", output_to_operand_aliasing={{0}: (3, {})} | custom-call | tf_op jit(solution)/shard_map/last_write/pallas_call | solution.py:450
  (92 shorter events, 27.2 us)
Async XLA Ops:
  1.5 13.0 %collective-permute-start.1 = (bf16[2,16,1024]{2,1,0:T(8,128)(2,1)S(1)}, bf16[2,16,1024]{2,1,0:T(8,128)(2,1)S(1)}, u32[]{:S(2)}, u32[]{:S(2)}) collective-permute-start(bf16[2,16,1024]{2,1,0:T(8,128)(2,1)S(1)} %get-tuple-element.69), channel_id=1, source_target_pairs={{2,0},{4,2},{6,4},{8,6},{10,8},{12,10},{14,12},{3,1},{5,3},{7,5},{... | collective-permute-start | bytes 196616 | tf_op jit(solution)/shard_map/ppermute | solution.py:21
  2.8 11.7 %collective-permute-start = (bf16[2,16,1024]{2,1,0:T(8,128)(2,1)S(1)}, bf16[2,16,1024]{2,1,0:T(8,128)(2,1)S(1)}, u32[]{:S(2)}, u32[]{:S(2)}) collective-permute-start(bf16[2,16,1024]{2,1,0:T(8,128)(2,1)S(1)} %get-tuple-element.70), channel_id=1, source_target_pairs={{0,2},{2,4},{4,6},{6,8},{8,10},{10,12},{12,14},{1,3},{3,5},{5,7},{... | collective-permute-start | bytes 196616 | tf_op jit(solution)/shard_map/ppermute | solution.py:21
  14.5 10.3 %copy-start.9 = (f32[100,512]{1,0:T(8,128)}, f32[100,512]{1,0:T(8,128)S(1)}, u32[]{:S(2)}) copy-start(f32[100,512]{1,0:T(8,128)S(1)} %get-tuple-element.49.refs_5_) | copy-start | bytes 614404
  14.5 1.7 %copy-start = (bf16[1024,1024]{1,0:T(8,128)(2,1)S(1)}, bf16[1024,1024]{1,0:T(8,128)(2,1)}, u32[]{:S(2)}) copy-start(bf16[1024,1024]{1,0:T(8,128)(2,1)} %hidden_weight.3) | copy-start | bytes 6291460
  17.8 12.2 %copy-start.7 = (f32[512,100]{0,1:T(8,128)S(1)}, f32[512,100]{0,1:T(8,128)}, u32[]{:S(2)}) copy-start(f32[512,100]{0,1:T(8,128)} %param.22) | copy-start | bytes 614404
  24.8 1.3 %copy-start.2 = (bf16[1024,1024]{1,0:T(8,128)(2,1)}, bf16[1024,1024]{1,0:T(8,128)(2,1)S(1)}, u32[]{:S(2)}) copy-start(bf16[1024,1024]{1,0:T(8,128)(2,1)S(1)} %get-tuple-element.51.refs_8_) | copy-start | bytes 6291460
  26.2 1.3 %copy-start.4 = (bf16[1024,1024]{1,0:T(8,128)(2,1)}, bf16[1024,1024]{1,0:T(8,128)(2,1)S(1)}, u32[]{:S(2)}) copy-start(bf16[1024,1024]{1,0:T(8,128)(2,1)S(1)} %get-tuple-element.50.refs_7_) | copy-start | bytes 6291460
  28.3 1.8 %collective-permute-start.2 = (f32[2,100,512]{2,1,0:T(8,128)S(1)}, f32[2,100,512]{2,1,0:T(8,128)S(1)}, u32[]{:S(2)}, u32[]{:S(2)}) collective-permute-start(f32[2,100,512]{2,1,0:T(8,128)S(1)} %get-tuple-element.48.refs_1_), channel_id=1, source_target_pairs={{0,1},{1,0},{2,3},{3,2},{4,5},{5,4},{6,7},{7,6},{8,9},{9,8},{10,11... | collective-permute-start | bytes 1228808 | tf_op jit(solution)/shard_map/ppermute | solution.py:25
  28.4 1.7 %copy-start.3 = (bf16[1024,1024]{1,0:T(8,128)(2,1)S(1)}, bf16[1024,1024]{1,0:T(8,128)(2,1)}, u32[]{:S(2)}) copy-start(bf16[1024,1024]{1,0:T(8,128)(2,1)} %copy-done.2) | copy-start | bytes 6291460
  28.4 2.2 %copy-start.5 = (bf16[1024,1024]{1,0:T(8,128)(2,1)S(1)}, bf16[1024,1024]{1,0:T(8,128)(2,1)}, u32[]{:S(2)}) copy-start(bf16[1024,1024]{1,0:T(8,128)(2,1)} %copy-done.4) | copy-start | bytes 6291460
  36.0 3.0 %collective-permute-start.7 = (bf16[512,1152]{1,0:T(8,128)(2,1)S(1)}, bf16[512,1152]{1,0:T(8,128)(2,1)S(1)}, u32[]{:S(2)}, u32[]{:S(2)}) collective-permute-start(bf16[512,1152]{1,0:T(8,128)(2,1)S(1)} %get-tuple-element.59), channel_id=1, source_target_pairs={{0,1},{1,0},{2,3},{3,2},{4,5},{5,4},{6,7},{7,6},{8,9},{9,8},{10,11... | collective-permute-start | bytes 3538952 | tf_op jit(solution)/shard_map/ppermute | solution.py:25
  39.3 7.7 %collective-permute-start.13 = (bf16[128,1152]{1,0:T(8,128)(2,1)S(1)}, bf16[128,1152]{1,0:T(8,128)(2,1)S(1)}, u32[]{:S(2)}, u32[]{:S(2)}) collective-permute-start(bf16[128,1152]{1,0:T(8,128)(2,1)S(1)} %get-tuple-element.67), channel_id=1, source_target_pairs={{0,2},{1,9},{2,0},{3,11},{4,6},{5,13},{6,4},{7,15},{8,10},{9,1},{1... | collective-permute-start | bytes 884744 | tf_op jit(solution)/shard_map/ppermute | solution.py:34
  42.3 7.9 %collective-permute-start.8 = (bf16[128,1152]{1,0:T(8,128)(2,1)S(1)}, bf16[128,1152]{1,0:T(8,128)(2,1)S(1)}, u32[]{:S(2)}, u32[]{:S(2)}) collective-permute-start(bf16[128,1152]{1,0:T(8,128)(2,1)S(1)} %get-tuple-element.68), channel_id=1, source_target_pairs={{0,2},{1,5},{2,0},{3,7},{4,6},{5,1},{6,4},{7,3},{8,10},{9,13},{10,... | collective-permute-start | bytes 884744 | tf_op jit(solution)/shard_map/ppermute | solution.py:34
  50.3 5.2 %collective-permute-start.9 = (bf16[64,1152]{1,0:T(8,128)(2,1)S(1)}, bf16[64,1152]{1,0:T(8,128)(2,1)S(1)}, u32[]{:S(2)}, u32[]{:S(2)}) collective-permute-start(bf16[64,1152]{1,0:T(8,128)(2,1)S(1)} %slice.108), channel_id=1, source_target_pairs={{0,4},{1,3},{2,6},{3,1},{4,0},{5,7},{6,2},{7,5},{8,12},{9,11},{10,... | collective-permute-start | bytes 442376 | tf_op jit(solution)/shard_map/ppermute | solution.py:34
  52.0 10.1 %collective-permute-start.14 = (bf16[64,1152]{1,0:T(8,128)(2,1)S(1)}, bf16[64,1152]{1,0:T(8,128)(2,1)S(1)}, u32[]{:S(2)}, u32[]{:S(2)}) collective-permute-start(bf16[64,1152]{1,0:T(8,128)(2,1)S(1)} %slice.112), channel_id=1, source_target_pairs={{0,8},{1,3},{2,10},{3,1},{4,12},{5,7},{6,14},{7,5},{8,0},{9,11},{1... | collective-permute-start | bytes 442376 | tf_op jit(solution)/shard_map/ppermute | solution.py:34
  55.5 10.4 %collective-permute-start.10 = (bf16[64,1152]{1,0:T(8,128)(2,1)S(1)}, bf16[64,1152]{1,0:T(8,128)(2,1)S(1)}, u32[]{:S(2)}, u32[]{:S(2)}) collective-permute-start(bf16[64,1152]{1,0:T(8,128)(2,1)S(1)} %add_convert_fusion.6), channel_id=1, source_target_pairs={{0,8},{1,9},{2,10},{3,11},{4,12},{5,13},{6,14},{7,15},{8,0},{9,1},... | collective-permute-start | bytes 442376 | tf_op jit(solution)/shard_map/ppermute | solution.py:34
  62.1 5.4 %collective-permute-start.15 = (bf16[64,1152]{1,0:T(8,128)(2,1)S(1)}, bf16[64,1152]{1,0:T(8,128)(2,1)S(1)}, u32[]{:S(2)}, u32[]{:S(2)}) collective-permute-start(bf16[64,1152]{1,0:T(8,128)(2,1)S(1)} %add_convert_fusion.4), channel_id=1, source_target_pairs={{0,4},{1,5},{2,6},{3,7},{4,0},{5,1},{6,2},{7,3},{8,12},{9,13},{10,... | collective-permute-start | bytes 442376 | tf_op jit(solution)/shard_map/ppermute | solution.py:34
  66.0 5.2 %collective-permute-start.11 = (bf16[64,1152]{1,0:T(8,128)(2,1)S(1)}, bf16[64,1152]{1,0:T(8,128)(2,1)S(1)}, u32[]{:S(2)}, u32[]{:S(2)}) collective-permute-start(bf16[64,1152]{1,0:T(8,128)(2,1)S(1)} %add_convert_fusion.5), channel_id=1, source_target_pairs={{0,4},{1,3},{2,6},{3,1},{4,0},{5,7},{6,2},{7,5},{8,12},{9,11},{10,... | collective-permute-start | bytes 442376 | tf_op jit(solution)/shard_map/ppermute | solution.py:34
  67.6 7.8 %collective-permute-start.16 = (bf16[64,1152]{1,0:T(8,128)(2,1)S(1)}, bf16[64,1152]{1,0:T(8,128)(2,1)S(1)}, u32[]{:S(2)}, u32[]{:S(2)}) collective-permute-start(bf16[64,1152]{1,0:T(8,128)(2,1)S(1)} %add_convert_fusion.3), channel_id=1, source_target_pairs={{0,8},{1,3},{2,10},{3,1},{4,12},{5,7},{6,14},{7,5},{8,0},{9,11},{1... | collective-permute-start | bytes 442376 | tf_op jit(solution)/shard_map/ppermute | solution.py:34
  71.3 6.8 %collective-permute-start.12 = (bf16[128,1152]{1,0:T(8,128)(2,1)S(1)}, bf16[128,1152]{1,0:T(8,128)(2,1)S(1)}, u32[]{:S(2)}, u32[]{:S(2)}) collective-permute-start(bf16[128,1152]{1,0:T(8,128)(2,1)S(1)} %pad_maximum_fusion), channel_id=1, source_target_pairs={{0,2},{1,5},{2,0},{3,7},{4,6},{5,1},{6,4},{7,3},{8,10},{9,13},{10,... | collective-permute-start | bytes 884744 | tf_op jit(solution)/shard_map/ppermute | solution.py:34
  75.4 7.0 %copy-start.19 = (f32[1024,1]{1,0:T(8,128)S(1)}, f32[1024,1]{1,0:T(8,128)}, u32[]{:S(2)}) copy-start(f32[1024,1]{1,0:T(8,128)} %copy-done.18) | copy-start | bytes 12292
  75.4 7.0 %copy-start.21 = (bf16[256,512]{1,0:T(8,128)(2,1)S(1)}, bf16[256,512]{1,0:T(8,128)(2,1)}, u32[]{:S(2)}) copy-start(bf16[256,512]{1,0:T(8,128)(2,1)} %copy-done.20) | copy-start | bytes 786436
  75.4 7.0 %copy-start.1 = (bf16[1024,1024]{1,0:T(8,128)(2,1)S(1)}, bf16[1024,1024]{1,0:T(8,128)(2,1)}, u32[]{:S(2)}) copy-start(bf16[1024,1024]{1,0:T(8,128)(2,1)} %hidden_weight.3) | copy-start | bytes 6291460
  75.4 7.0 %copy-start.15 = (f32[1024]{0:T(1024)S(1)}, f32[1024]{0:T(1024)}, u32[]{:S(2)}) copy-start(f32[1024]{0:T(1024)} %param.25) | copy-start | bytes 12292
  75.4 6.8 %collective-permute-start.17 = (bf16[128,1152]{1,0:T(8,128)(2,1)S(1)}, bf16[128,1152]{1,0:T(8,128)(2,1)S(1)}, u32[]{:S(2)}, u32[]{:S(2)}) collective-permute-start(bf16[128,1152]{1,0:T(8,128)(2,1)S(1)} %pad_maximum_fusion.1), channel_id=1, source_target_pairs={{0,2},{1,9},{2,0},{3,11},{4,6},{5,13},{6,4},{7,15},{8,10},{9,1},{1... | collective-permute-start | bytes 884744 | tf_op jit(solution)/shard_map/ppermute | solution.py:34
  82.3 36.5 %collective-permute-start.18 = (bf16[512,1152]{1,0:T(8,128)(2,1)S(1)}, bf16[512,1152]{1,0:T(8,128)(2,1)S(1)}, u32[]{:S(2)}, u32[]{:S(2)}) collective-permute-start(bf16[512,1152]{1,0:T(8,128)(2,1)S(1)} %constant_dynamic-update-slice_fusion.refs_1_), channel_id=1, source_target_pairs={{0,1},{1,0},{2,3},{3,2},{4,5},{5,4},{6,7},{7,6},{8,9},{9,8},{10,11... | collective-permute-start | bytes 3538952 | tf_op jit(solution)/shard_map/ppermute | solution.py:25
  89.4 3.9 %collective-permute-start.3 = (f32[1152]{0:T(1024)S(1)}, f32[1152]{0:T(1024)S(1)}, u32[]{:S(2)}, u32[]{:S(2)}) collective-permute-start(f32[1152]{0:T(1024)S(1)} %concatenate.17), channel_id=1, source_target_pairs={{0,1},{1,0},{2,3},{3,2},{4,5},{5,4},{6,7},{7,6},{8,9},{9,8},{10,11... | collective-permute-start | bytes 13832 | tf_op jit(solution)/shard_map/ppermute | solution.py:25
  89.9 22.0 %collective-permute-start.19 = (bf16[2,16,1024]{2,1,0:T(8,128)(2,1)S(1)}, bf16[2,16,1024]{2,1,0:T(8,128)(2,1)S(1)}, u32[]{:S(2)}, u32[]{:S(2)}) collective-permute-start(bf16[2,16,1024]{2,1,0:T(8,128)(2,1)S(1)} %get-tuple-element.63), channel_id=1, source_target_pairs={{0,2},{2,4},{4,6},{6,8},{8,10},{10,12},{12,14},{1,3},{3,5},{5,7},{... | collective-permute-start | bytes 196616 | tf_op jit(solution)/shard_map/ppermute | solution.py:21
  94.0 7.6 %collective-permute-start.4 = (f32[1152]{0:T(1024)S(1)}, f32[1152]{0:T(1024)S(1)}, u32[]{:S(2)}, u32[]{:S(2)}) collective-permute-start(f32[1152]{0:T(1024)S(1)} %pad_add_fusion), channel_id=1, source_target_pairs={{0,2},{1,3},{2,0},{3,1},{4,6},{5,7},{6,4},{7,5},{8,10},{9,11},{10,... | collective-permute-start | bytes 13832 | tf_op jit(solution)/shard_map/ppermute | solution.py:34
  101.6 4.2 %collective-permute-start.5 = (f32[1152]{0:T(1024)S(1)}, f32[1152]{0:T(1024)S(1)}, u32[]{:S(2)}, u32[]{:S(2)}) collective-permute-start(f32[1152]{0:T(1024)S(1)} %add.53), channel_id=1, source_target_pairs={{0,4},{1,5},{2,6},{3,7},{4,0},{5,1},{6,2},{7,3},{8,12},{9,13},{10,... | collective-permute-start | bytes 13832 | tf_op jit(solution)/shard_map/ppermute | solution.py:34
  105.8 5.0 %collective-permute-start.6 = (f32[1152]{0:T(1024)S(1)}, f32[1152]{0:T(1024)S(1)}, u32[]{:S(2)}, u32[]{:S(2)}) collective-permute-start(f32[1152]{0:T(1024)S(1)} %add.54), channel_id=1, source_target_pairs={{0,8},{1,9},{2,10},{3,11},{4,12},{5,13},{6,14},{7,15},{8,0},{9,1},... | collective-permute-start | bytes 13832 | tf_op jit(solution)/shard_map/ppermute | solution.py:34
  109.2 6.1 %collective-permute-start.20 = (bf16[2,16,1024]{2,1,0:T(8,128)(2,1)S(1)}, bf16[2,16,1024]{2,1,0:T(8,128)(2,1)S(1)}, u32[]{:S(2)}, u32[]{:S(2)}) collective-permute-start(bf16[2,16,1024]{2,1,0:T(8,128)(2,1)S(1)} %get-tuple-element.64), channel_id=1, source_target_pairs={{2,0},{4,2},{6,4},{8,6},{10,8},{12,10},{14,12},{3,1},{5,3},{7,5},{... | collective-permute-start | bytes 196616 | tf_op jit(solution)/shard_map/ppermute | solution.py:21
  (11 other events, 8.5 us)

commit v3 on v2

--- a/solution.py
+++ b/solution.py
@@ -12,7 +12,8 @@
 F32 = jnp.float32
 VMEM = pl.BlockSpec(memory_space=pltpu.VMEM)
 SMEM = pl.BlockSpec(memory_space=pltpu.SMEM)
-PARAMS = pltpu.CompilerParams(vmem_limit_bytes=32 * 1024 * 1024)
+HBM = pl.BlockSpec(memory_space=pltpu.HBM)
+PARAMS = pltpu.CompilerParams(vmem_limit_bytes=16 * 1024 * 1024)
 
 
 def shift(value, axis, steps):
@@ -51,9 +52,31 @@
     return lax.dot_general(a, b, (dims, ((), ())), preferred_element_type=F32)
 
 
-def adjacency_kernel(place, index, mask, weight, valid, area, var_weight, adj, adj_t, score_weight):
+def fetch(sources, targets, sems):
+    copies = [
+        pltpu.make_async_copy(source, target, sems.at[i])
+        for i, (source, target) in enumerate(zip(sources, targets))
+    ]
+    for copy in copies:
+        copy.start()
+    return copies
+
+
+def prepare_kernel(
+    place, index_in, mask_in, weight_in, valid_in, area_in, var_weight_in, state_in, target_in, projection_in, gain_in,
+    adj, adj_t, score_weight, base, projection, gain,
+    index, mask, weight, valid, area, var_weight, state, target, narrow, sems,
+):
+    sources = (
+        index_in, mask_in, weight_in, valid_in, area_in, var_weight_in, projection_in, state_in, target_in, gain_in
+    )
+    targets = (index, mask, weight, valid, area, var_weight, narrow, state, target, gain)
+    copies = fetch(sources, targets, sems)
+    for copy in copies[:6]:
+        copy.wait()
     points = index.shape[1]
-    nodes = jax.lax.broadcasted_iota(jnp.int32, (LANES, points), 0) + place[0]
+    variables = state.shape[0]
+    nodes = jax.lax.broadcasted_iota(jnp.int32, (LANES, points), 0) + place[2]
     total = jnp.zeros((LANES, points), F32)
     for slot in range(index.shape[0]):
         coefficient = weight[slot : slot + 1, :] * mask[slot : slot + 1, :].astype(F32)
@@ -64,16 +87,29 @@
     adj_t[LANES:, :] = lower.astype(BF16)
     adj[:, :LANES] = upper.T.astype(BF16)
     adj[:, LANES:] = lower.T.astype(BF16)
-    score_weight[...] = var_weight[...] * (valid[...].astype(F32) * area[...] / points)
+    diagonal = jax.lax.broadcasted_iota(jnp.int32, (variables, variables), 0) == (
+        jax.lax.broadcasted_iota(jnp.int32, (variables, variables), 1)
+    )
+    column = jnp.sum(jnp.where(diagonal, var_weight[...], 0.0), axis=1, keepdims=True)
+    score_weight[...] = column * (valid[...].astype(F32) * area[...] / points)
+    copies[6].wait()
+    projection[...] = jnp.zeros_like(projection)
+    projection[:variables, :] = narrow[...]
+    copies[7].wait()
+    copies[8].wait()
+    copies[9].wait()
+    base[...] = state[...] - target[...]
 
 
 def forward_kernel(
-    adj, low, own, high, gain, hidden_weight, output_weight,
-    normed, hidden, slope, outputs, deviation, extended, summed, projected,
+    adj, low, own_in, high, gain, hidden_weight_in, output_weight,
+    normed, hidden, slope, outputs, deviation, extended, summed, projected, own, hidden_weight, sems,
 ):
     members, nodes, width = own.shape
     points = adj.shape[0]
     tile = 256
+    copies = fetch((own_in, hidden_weight_in), (own, hidden_weight), sems)
+    copies[0].wait()
     for member in range(members):
         for part in range(2):
             start = part * LANES
@@ -96,6 +132,7 @@
             deviation[target, :] = inverse
             normed[target, :] = (value * inverse * gain[...]).astype(BF16)
 
+    copies[1].wait()
     for member in range(members):
         rows = slice(member * points, (member + 1) * points)
         for column in range(0, width, tile):
@@ -138,7 +175,7 @@
 
 
 def score_kernel(
-    count, place, outputs, others, state, target, score_weight, output_weight, slope, hidden, normed_t,
+    count, place, outputs, others, base, score_weight, output_weight, slope, hidden, normed_t,
     loss, grad_pre, grad_out, sent,
     grad_pred, grad_pred_t,
 ):
@@ -148,14 +185,13 @@
     weight = score_weight[...]
     grad_pred_t[...] = jnp.zeros_like(grad_pred_t)
     grad_pred[...] = jnp.zeros_like(grad_pred)
-    base = state[...] - target[...]
     values = [outputs[m] for m in range(members)]
     grads = [None] * members
     pair_grads = [jnp.zeros((variables, points), F32) for _ in range(members)]
     errors = jnp.zeros((variables, points), F32)
     pairs = jnp.full((variables, points), members * SMOOTH_SQ**0.5, F32)
     for m in range(members):
-        diff = values[m] + base
+        diff = values[m] + base[...]
         square = diff * diff + SMOOTH_SQ
         inverse = lax.rsqrt(square)
         errors = errors + square * inverse
@@ -206,18 +242,24 @@
 
 
 def backward_kernel(
-    grad_pre, hidden_weight, normed, gain, deviation, adj_t,
+    grad_pre, hidden_weight_in, normed, gain, deviation, adj_t,
     grad_gain, inner, below, above,
-    product, rows_grad,
+    product, rows_grad, hidden_weight, sems,
 ):
     members, nodes, width = inner.shape
     points = adj_t.shape[1]
+    parts = [pl.ds(column, 256) for column in range(0, width, 256)]
+    copies = fetch(
+        [hidden_weight_in.at[part, :] for part in parts], [hidden_weight.at[part, :] for part in parts], sems
+    )
     inverse_gain = 1.0 / gain[...]
     total = jnp.zeros((8, width), F32)
     for member in range(members):
         rows = slice(member * points, (member + 1) * points)
         for column in range(0, width, 256):
             columns = slice(column, column + 256)
+            if member == 0:
+                copies[column // 256].wait()
             product[:, columns] = dot(grad_pre[rows, :], hidden_weight[columns, :], ((1,), (1,)))
 
         def step(index, total):
@@ -240,6 +282,13 @@
         inner[member] = value[RIM : RIM + nodes]
         above[member] = value[RIM + nodes : nodes + 2 * RIM].astype(BF16)
     grad_gain[...] = jnp.sum(total, axis=0, keepdims=True) * inverse_gain
+
+
+def latent_kernel(inner, from_below, from_above, grad_latent):
+    nodes = inner.shape[1]
+    grad_latent[...] = inner[...]
+    grad_latent[:, :RIM, :] += from_below[...].astype(F32)
+    grad_latent[:, nodes - RIM :, :] += from_above[...].astype(F32)
 
 
 def write_half(count, place, half, source, target, wide, sems):
@@ -287,22 +336,40 @@
     return (mine.astype(F32) + other.astype(F32)).astype(BF16)
 
 
-def sum_chunk(value, chunk, count):
+def swap_with(value, small, bits):
+    upper = small.astype(BF16)
+    lower = (small - upper.astype(F32)).astype(BF16)
+    rest = jnp.zeros((6, small.shape[1]), BF16)
+    other = swap_bits(jnp.concatenate([value, upper, lower, rest]), bits)
+    rows = value.shape[0]
+    mine = upper.astype(F32) + lower.astype(F32)
+    small = mine + (other[rows : rows + 1].astype(F32) + other[rows + 1 : rows + 2].astype(F32))
+    return other[:rows], small
+
+
+def sum_chunk(value, chunk, count, small=None, beside=()):
     stages = orders(chunk, count)
-    for bits in stages[:-1]:
-        rows = value.shape[0] // 2
-        value = add_parts(value[rows:], swap_bits(value[:rows], bits))
-    value = add_parts(value, swap_bits(value, stages[-1]))
-    for bits in reversed(stages[:-1]):
-        value = jnp.concatenate([swap_bits(value, bits), value])
-    return value
-
-
-def sum_small(value):
-    value = value + swap_cores(value)
-    for bit in range(lax.axis_size("space").bit_length() - 1):
-        value = value + swap_bits(value, (bit, bit))
-    return value
+    for level, bits in enumerate(stages):
+        rows = value.shape[0] // 2 if level < count - 1 else 0
+        sent = value[:rows] if rows else value
+        if small is None or level == 0:
+            other = swap_bits(sent, bits)
+        else:
+            other, small = swap_with(sent, small, bits)
+        value = add_parts(value[rows:], other)
+    for level, bits in reversed(list(enumerate(stages[:-1]))):
+        if level == 0:
+            value, beside = lax.optimization_barrier((value, beside))
+        if small is None or level > 0:
+            other = swap_bits(value, bits)
+        else:
+            other, small = swap_with(value, small, bits)
+        value = jnp.concatenate([other, value])
+    return value, small, beside
+
+
+def in_hbm(*values):
+    return [pltpu.with_memory_space_constraint(value, pltpu.HBM) for value in values]
 
 
 def cost(flops, moved):
@@ -328,31 +395,49 @@
     rows = members * points
     count = lax.axis_size("space").bit_length() - 1
     space, core = lax.axis_index("space"), lax.axis_index("member")
-    place = jnp.stack([space, core]).astype(jnp.int32)
+    place = jnp.stack([space, core, space * nodes - RIM]).astype(jnp.int32)
     low = shift(latent[:, nodes - RIM :], "space", 1)
     high = shift(latent[:, :RIM], "space", -1)
-    gain = gain.reshape(1, width)
-    output_weight = jnp.pad(output_weight.T, ((0, LANES - variables), (0, 0)))
-
-    adj, adj_t, score_weight = pl.pallas_call(
-        adjacency_kernel,
+    adj, adj_t, score_weight, base, projection, gain = pl.pallas_call(
+        prepare_kernel,
         out_shape=(
             pltpu.VMEM((points, 2 * LANES), BF16),
             pltpu.VMEM((2 * LANES, points), BF16),
             pltpu.VMEM((variables, points), F32),
+            pltpu.VMEM((variables, points), F32),
+            pltpu.VMEM((LANES, width), BF16),
+            pltpu.VMEM((1, width), F32),
         ),
-        in_specs=[SMEM] + [VMEM] * 6,
-        out_specs=(VMEM,) * 3,
-        compiler_params=PARAMS,
-        name="adjacency",
+        in_specs=[SMEM] + [HBM] * 10,
+        out_specs=(VMEM,) * 6,
+        scratch_shapes=[
+            pltpu.VMEM(edge_mask.T.shape, jnp.int32),
+            pltpu.VMEM(edge_mask.T.shape, jnp.int32),
+            pltpu.VMEM(edge_mask.T.shape, F32),
+            pltpu.VMEM((1, points), jnp.int32),
+            pltpu.VMEM((1, points), F32),
+            pltpu.VMEM((1, variables), F32),
+            pltpu.VMEM((variables, points), F32),
+            pltpu.VMEM((variables, points), F32),
+            pltpu.VMEM((variables, width), BF16),
+            pltpu.SemaphoreType.DMA((10,)),
+        ],
+        compiler_params=PARAMS,
+        name="prepare",
     )(
-        (space * nodes - RIM).astype(jnp.int32).reshape(1),
-        edge_node_index.T,
-        edge_mask.T,
-        edge_weight.T,
-        valid.reshape(1, points),
-        area.reshape(1, points),
-        var_weight.reshape(variables, 1),
+        place,
+        *in_hbm(
+            edge_node_index.T,
+            edge_mask.T,
+            edge_weight.T,
+            valid.reshape(1, points),
+            area.reshape(1, points),
+            var_weight.reshape(1, variables),
+            state.T,
+            target.T,
+            output_weight.T,
+            gain.reshape(1, width),
+        ),
     )
     normed, hidden, slope, outputs, deviation = pl.pallas_call(
         forward_kernel,
@@ -363,16 +448,19 @@
             jax.ShapeDtypeStruct((members, variables, points), F32),
             pltpu.VMEM((rows, 1), F32),
         ),
-        in_specs=[VMEM] * 7,
+        in_specs=[VMEM, VMEM, HBM, VMEM, VMEM, HBM, VMEM],
         out_specs=(VMEM,) * 5,
         scratch_shapes=[
             pltpu.VMEM((2 * LANES, width), BF16),
             pltpu.VMEM((points, width), F32),
             pltpu.VMEM((points, LANES), F32),
+            pltpu.VMEM(latent.shape, BF16),
+            pltpu.VMEM((width, width), BF16),
+            pltpu.SemaphoreType.DMA((2,)),
         ],
         compiler_params=PARAMS,
         name="forward",
-    )(adj, low, latent, high, gain, hidden_weight, output_weight)
+    )(adj, low, *in_hbm(latent), high, gain, *in_hbm(hidden_weight), projection)
     others = swap_cores(outputs)
     normed_t = pl.pallas_call(
         lambda *refs: transpose_kernel(count, *refs),
@@ -391,12 +479,12 @@
             pltpu.VMEM((width, LANES), F32),
             jax.ShapeDtypeStruct((width // 2, width + LANES), BF16),
         ),
-        in_specs=[SMEM] + [VMEM] * 9,
+        in_specs=[SMEM] + [VMEM] * 8,
         out_specs=(VMEM,) * 4,
         scratch_shapes=[pltpu.VMEM((rows, LANES), BF16), pltpu.VMEM((LANES, rows), F32)],
         compiler_params=PARAMS,
         name="score",
-    )(place, outputs, others, state.T, target.T, score_weight, output_weight, slope, hidden, normed_t)
+    )(place, outputs, others, base, score_weight, projection, slope, hidden, normed_t)
     received = swap_cores(sent)
     kept = pl.pallas_call(
         product_kernel,
@@ -412,27 +500,38 @@
         backward_kernel,
         out_shape=(
             jax.ShapeDtypeStruct((1, width), F32),
-            jax.ShapeDtypeStruct((members, nodes, width), F32),
+            pltpu.VMEM((members, nodes, width), F32),
             jax.ShapeDtypeStruct((members, RIM, width), BF16),
             jax.ShapeDtypeStruct((members, RIM, width), BF16),
         ),
-        in_specs=[VMEM] * 6,
+        in_specs=[VMEM, HBM] + [VMEM] * 4,
         out_specs=(VMEM,) * 4,
-        scratch_shapes=[pltpu.VMEM((points, width), F32), pltpu.VMEM((points, width), BF16)],
+        scratch_shapes=[
+            pltpu.VMEM((points, width), F32),
+            pltpu.VMEM((points, width), BF16),
+            pltpu.VMEM((width, width), BF16),
+            pltpu.SemaphoreType.DMA((width // 256,)),
+        ],
         compiler_params=PARAMS,
         cost_estimate=cost(5 * 10**9, 8 * 10**6),
         name="backward",
-    )(grad_pre, hidden_weight, normed, gain, deviation, adj_t)
-    small = jnp.concatenate([grad_gain.reshape(width), jnp.broadcast_to(loss.reshape(1), (LANES,))])
-    small = sum_small(small)
-    from_below, from_above = shift(above, "space", 1), shift(below, "space", -1)
-    grad_latent = inner.at[:, :RIM].add(from_below.astype(F32))
-    grad_latent = grad_latent.at[:, nodes - RIM :].add(from_above.astype(F32))
-
+    )(grad_pre, *in_hbm(hidden_weight), normed, gain, deviation, adj_t)
+    small = jnp.concatenate([grad_gain, jnp.broadcast_to(loss, (1, LANES))], axis=1)
+    rims = (shift(above, "space", 1), shift(below, "space", -1))
     chunk_rows = width // 4
-    own = jnp.concatenate(
-        [sum_chunk(value[k * chunk_rows : (k + 1) * chunk_rows], k, count) for k in range(2)]
-    )
+    first, small, _ = sum_chunk(value[:chunk_rows], 0, count, small)
+    second, _, rims = sum_chunk(value[chunk_rows:], 1, count, beside=rims)
+    grad_latent = pl.pallas_call(
+        latent_kernel,
+        out_shape=jax.ShapeDtypeStruct((members, nodes, width), F32),
+        in_specs=[VMEM] * 3,
+        out_specs=VMEM,
+        compiler_params=PARAMS,
+        cost_estimate=cost(10**6, 10**6),
+        name="latent",
+    )(inner, *rims)
+    own = jnp.concatenate([first, second])
+    small = (small + swap_cores(small)).reshape(width + LANES)
     other = swap_cores(own)
     blocks = 1 << count
     write_scratch = [pltpu.VMEM((width // 2, width), F32), pltpu.SemaphoreType.DMA((blocks,))]

time: 122 us -> 94.8 us (0.78)
  local copies, waits for them, and re-layouts: 17.9 us -> 2.75 us
  starting transfers between devices: 39.5 us -> 29.1 us
  Pallas kernels: 24.3 us -> 29.7 us
  waiting for transfers between devices: 34.5 us -> 29.8 us
  other arithmetic: 4.42 us -> 2.26 us
    unnamed x49 -> x0, local copies, waits for them, and re-layouts: 13.4 us -> none
    ppermute x13 -> x10, starting transfers between devices: 26.9 us -> 16.9 us  [swap_bits(): return lax.ppermute(value, ('space', 'member'), pairs)]
    ppermute x13 -> x10, waiting for transfers between devices: 31 us -> 24.8 us  [swap_bits(): return lax.ppermute(value, ('space', 'member'), pairs)]
    scatter-add x2 -> x0, other arithmetic: 3.15 us -> none  [the longest x1 1.57 us: local(): grad_latent = inner.at[:, :RIM].add(from_below.astype(F32))]
    pallas_call x1 -> x2, Pallas kernels: 0.27 us -> 2.72 us  [the longest x1 1.89 us: local(): pl.pallas_call(prepare_kernel, out_shape=(pltpu.VMEM((points, 2 * LANES),...]
    pallas_call x1, Pallas kernels: 6.31 us -> 8.27 us  [local(): pl.pallas_call(backward_kernel, out_shape=(jax.ShapeDtypeStruct((1, width...]
    convert_element_type x0 -> x5, other arithmetic: none -> 1.34 us  [the longest x2 0.68 us: swap_with(): upper = small.astype(BF16)]
  transfers between devices with their start and end apart: 21 -> 18, of which waited for: 16 -> 10; matrix products, arithmetic and copies ran while one was open for 6% -> 4% of each run, Pallas kernels for 9% -> 16%
where the time goes in v3:
time: 94.8 us; the launch traced here: 94.5 us
  waiting for transfers between devices  29.8 us (31%)
  Pallas kernels  29.7 us (31%)
  starting transfers between devices  29.1 us (31%)
  local copies, waits for them, and re-layouts  2.75 us (3%)
  other arithmetic  2.26 us (2%)
    ppermute x10, waiting for transfers between devices, swap_bits(): return lax.ppermute(value, ('space', 'member'), pairs)  24.8 us
    ppermute x10, starting transfers between devices, swap_bits(): return lax.ppermute(value, ('space', 'member'), pairs)  16.9 us
    ppermute x4, starting transfers between devices, shift(): lax.ppermute(value, axis, [(source, source + steps) for source in range(f...  11.3 us
    pallas_call x1, Pallas kernels, local(): pl.pallas_call(backward_kernel, out_shape=(jax.ShapeDtypeStruct((1, width...  8.27 us
    pallas_call x1, Pallas kernels, local(): pl.pallas_call(forward_kernel, out_shape=(pltpu.VMEM((rows, width), BF16)...  7.97 us
    pallas_call x1, Pallas kernels, local(): pl.pallas_call(lambda *refs: score_kernel(count, *refs), out_shape=(jax.S...  3.59 us
    ppermute x4, waiting for transfers between devices, shift(): lax.ppermute(value, axis, [(source, source + steps) for source in range(f...  2.88 us
    pallas_call x1, Pallas kernels, local(): pl.pallas_call(lambda *refs: last_write_kernel(count, *refs), out_shape=(...  2.8 us
  transfers between devices with their start and end apart: 18, of which 10 were waited for; matrix products, arithmetic and copies ran while one was open for 4% of the time, Pallas kernels for 16%

profile of v3, /device:TPU:0, one launch (start us, length us, event | category | flops | bytes accessed | tf_op | source)
XLA Modules:
  0.0 94.5 jit_solution(10139138831066890474)
XLA Ops:
  0.6 0.9 fusion.11
  1.5 4.9 %collective-permute-start = (bf16[2,16,1024]{2,1,0:T(8,128)(2,1)S(1)}, bf16[2,16,1024]{2,1,0:T(8,128)(2,1)S(1)}, u32[]{:S(2)}, u32[]{:S(2)}) collective-permute-start(bf16[2,16,1024]{2,1,0:T(8,128)(2,1)S(1)} %get-tuple-element.62), channel_id=1, source_target_pairs={{0,2},{2,4},{4,6},{6,8},{8,10},{10,12},{12,14},{1,3},{3,5},{5,7},{... | collective-permute-start | bytes 196616 | tf_op jit(solution)/shard_map/ppermute | solution.py:22
  6.4 1.3 %collective-permute-start.1 = (bf16[2,16,1024]{2,1,0:T(8,128)(2,1)S(1)}, bf16[2,16,1024]{2,1,0:T(8,128)(2,1)S(1)}, u32[]{:S(2)}, u32[]{:S(2)}) collective-permute-start(bf16[2,16,1024]{2,1,0:T(8,128)(2,1)S(1)} %get-tuple-element.61), channel_id=1, source_target_pairs={{2,0},{4,2},{6,4},{8,6},{10,8},{12,10},{14,12},{3,1},{5,3},{7,5},{... | collective-permute-start | bytes 196616 | tf_op jit(solution)/shard_map/ppermute | solution.py:22
  7.8 1.9 %prepare.1 = (bf16[512,256]{1,0:T(8,128)(2,1)S(1)}, bf16[256,512]{1,0:T(8,128)(2,1)S(1)}, f32[100,512]{1,0:T(8,128)S(1)}, f32[100,512]{1,0:T(8,128)S(1)}, bf16[1...) custom-call(s32[3]{0:T(128)S(1)} %pad_add_fusion.place.refs_0_, s32[4,512]{1,0:T(4,128)} %bitcast.20, s32[4,512]{1,0:T(4,128)} %bitcast.21, ...), custom_call_target="tpu_custom_call" | custom-call | tf_op jit(solution)/shard_map/prepare/pallas_call | solution.py:401
  9.7 2.9 %collective-permute-done.1.high = bf16[2,16,1024]{2,1,0:T(8,128)(2,1)S(1)} collective-permute-done((bf16[2,16,1024]{2,1,0:T(8,128)(2,1)S(1)}, bf16[2,16,1024]{2,1,0:T(8,128)(2,1)S(1)}, u32[]{:S(2)}, u32[]{:S(2)}) %collective-permute-start.1) | collective-permute-done | bytes 65568 | tf_op jit(solution)/shard_map/ppermute | solution.py:22
  12.6 8.0 %forward.1 = (bf16[1024,1024]{1,0:T(8,128)(2,1)S(1)}, bf16[1024,1024]{1,0:T(8,128)(2,1)S(1)}, bf16[1024,1024]{1,0:T(8,128)(2,1)S(1)}, f32[2,100,512]{2,1,0:T(8,128)S(1)}, f32[1024,1]{1,0:T(8,128)S(1)}) custom-call(bf16[512,256]{1,0:T(8,128)(2,1)S(1)} %get-tuple-element.29.adj, bf16[2,16,1024]{2,1,0:T(8,128)(2,1)S(1)} %collective-permute-done.low, ...), custom_call_target="tpu_custom_call" | custom-call | tf_op jit(solution)/shard_map/forward/pallas_call | solution.py:442
  20.6 1.2 %transpose.30.refs_8_.normed_t = bf16[1024,1024]{1,0:T(8,128)(2,1)S(1)} custom-call(s32[3]{0:T(128)S(1)} %pad_add_fusion.place.refs_0_, bf16[1024,1024]{1,0:T(8,128)(2,1)S(1)} %get-tuple-element.37.refs_1_.normed), custom_call_target="tpu_custom_call" | custom-call | flops 1000000000 | bytes 4000000 | tf_op jit(solution)/shard_map/transpose/pallas_call | solution.py:465
  22.4 3.6 %score.1 = (f32[1,1]{1,0:T(1,128)}, bf16[1024,1024]{1,0:T(8,128)(2,1)S(1)}, f32[1024,128]{1,0:T(8,128)S(1)}, bf16[512,1152]{1,0:T(8,128)(2,1)S(1)}) custom-call(s32[3]{0:T(128)S(1)} %pad_add_fusion.place.refs_0_, f32[2,100,512]{2,1,0:T(8,128)S(1)} %get-tuple-element.32.refs_1_, f32[2,100,512]{2,1,0:T(8,128)S(1)} %collective-permute-done.2.refs_2_, ...), custom_call_target="tpu_custom_call" | custom-call | tf_op jit(solution)/shard_map/score/pallas_call | solution.py:474
  26.1 1.2 %product.1 = f32[512,1152]{1,0:T(8,128)S(1)} custom-call(bf16[1024,1024]{1,0:T(8,128)(2,1)S(1)} %transpose.30.refs_8_.normed_t, bf16[1024,1024]{1,0:T(8,128)(2,1)S(1)} %get-tuple-element.38.grad_pre, f32[1024,128]{1,0:T(8,128)S(1)} %get-tuple-element.43.grad_out), custom_call_target="tpu_custom_call" | custom-call | flops 2000000000 | bytes 4000000 | tf_op jit(solution)/shard_map/product/pallas_call | solution.py:489
  27.4 1.5 %collective-permute-done.3 = bf16[512,1152]{1,0:T(8,128)(2,1)S(1)} collective-permute-done((bf16[512,1152]{1,0:T(8,128)(2,1)S(1)}, bf16[512,1152]{1,0:T(8,128)(2,1)S(1)}, u32[]{:S(2)}, u32[]{:S(2)}) %collective-permute-start.3) | collective-permute-done | bytes 1179680 | tf_op jit(solution)/shard_map/ppermute | solution.py:26
  29.2 2.5 %collective-permute-start.10 = (bf16[128,1152]{1,0:T(8,128)(2,1)S(1)}, bf16[128,1152]{1,0:T(8,128)(2,1)S(1)}, u32[]{:S(2)}, u32[]{:S(2)}) collective-permute-start(bf16[128,1152]{1,0:T(8,128)(2,1)S(1)} %get-tuple-element.59), channel_id=1, source_target_pairs={{0,2},{1,9},{2,0},{3,11},{4,6},{5,13},{6,4},{7,15},{8,10},{9,1},{1... | collective-permute-start | bytes 884744 | tf_op jit(solution)/shard_map/ppermute | solution.py:35
  31.7 8.3 %backward.1 = (f32[1,1024]{1,0:T(1,128)S(1)}, f32[2,64,1024]{2,1,0:T(8,128)S(1)}, bf16[2,16,1024]{2,1,0:T(8,128)(2,1)S(1)}, bf16[2,16,1024]{2,1,0:T(8,128)(2,1)S(1)}) custom-call(bf16[1024,1024]{1,0:T(8,128)(2,1)S(1)} %get-tuple-element.38.grad_pre, bf16[1024,1024]{1,0:T(8,128)(2,1)} %hidden_weight_in.3, ...), custom_call_target="tpu_custom_call" | custom-call | flops 5000000000 | bytes 8000000 | tf_op jit(solution)/shard_map/backward/pallas_call | solution.py:499
  40.0 3.9 %collective-permute-start.14 = (bf16[2,16,1024]{2,1,0:T(8,128)(2,1)S(1)}, bf16[2,16,1024]{2,1,0:T(8,128)(2,1)S(1)}, u32[]{:S(2)}, u32[]{:S(2)}) collective-permute-start(bf16[2,16,1024]{2,1,0:T(8,128)(2,1)S(1)} %get-tuple-element.45), channel_id=1, source_target_pairs={{0,2},{2,4},{4,6},{6,8},{8,10},{10,12},{12,14},{1,3},{3,5},{5,7},{... | collective-permute-start | bytes 196616 | tf_op jit(solution)/shard_map/ppermute | solution.py:22
  43.9 1.3 %collective-permute-start.15 = (bf16[2,16,1024]{2,1,0:T(8,128)(2,1)S(1)}, bf16[2,16,1024]{2,1,0:T(8,128)(2,1)S(1)}, u32[]{:S(2)}, u32[]{:S(2)}) collective-permute-start(bf16[2,16,1024]{2,1,0:T(8,128)(2,1)S(1)} %get-tuple-element.46), channel_id=1, source_target_pairs={{2,0},{4,2},{6,4},{8,6},{10,8},{12,10},{14,12},{3,1},{5,3},{7,5},{... | collective-permute-start | bytes 196616 | tf_op jit(solution)/shard_map/ppermute | solution.py:22
  45.2 0.7 concatenate.36
  45.8 0.7 subtract_convert_fusion.2
  46.7 4.3 %collective-permute-start.11 = (bf16[64,1152]{1,0:T(8,128)(2,1)S(1)}, bf16[64,1152]{1,0:T(8,128)(2,1)S(1)}, u32[]{:S(2)}, u32[]{:S(2)}) collective-permute-start(bf16[64,1152]{1,0:T(8,128)(2,1)S(1)} %slice.115), channel_id=1, source_target_pairs={{0,8},{1,3},{2,10},{3,1},{4,12},{5,7},{6,14},{7,5},{8,0},{9,11},{1... | collective-permute-start | bytes 442376 | tf_op jit(solution)/shard_map/ppermute | solution.py:35
  51.0 1.2 %collective-permute-start.5 = (bf16[72,1152]{1,0:T(8,128)(2,1)S(1)}, bf16[72,1152]{1,0:T(8,128)(2,1)S(1)}, u32[]{:S(2)}, u32[]{:S(2)}) collective-permute-start(bf16[72,1152]{1,0:T(8,128)(2,1)S(1)} %pad_maximum_fusion.5), channel_id=1, source_target_pairs={{0,4},{1,3},{2,6},{3,1},{4,0},{5,7},{6,2},{7,5},{8,12},{9,11},{10,... | collective-permute-start | bytes 497672 | tf_op jit(solution)/shard_map/ppermute | solution.py:35
  52.2 3.6 %collective-permute-done.11 = bf16[64,1152]{1,0:T(8,128)(2,1)S(1)} collective-permute-done((bf16[64,1152]{1,0:T(8,128)(2,1)S(1)}, bf16[64,1152]{1,0:T(8,128)(2,1)S(1)}, u32[]{:S(2)}, u32[]{:S(2)}) %collective-permute-start.11) | collective-permute-done | bytes 147488 | tf_op jit(solution)/shard_map/ppermute | solution.py:35
  56.4 1.5 %collective-permute-done.5 = bf16[72,1152]{1,0:T(8,128)(2,1)S(1)} collective-permute-done((bf16[72,1152]{1,0:T(8,128)(2,1)S(1)}, bf16[72,1152]{1,0:T(8,128)(2,1)S(1)}, u32[]{:S(2)}, u32[]{:S(2)}) %collective-permute-start.5) | collective-permute-done | bytes 165920 | tf_op jit(solution)/shard_map/ppermute | solution.py:35
  57.9 0.7 fusion.8
  58.7 2.0 %collective-permute-start.6 = (bf16[72,1152]{1,0:T(8,128)(2,1)S(1)}, bf16[72,1152]{1,0:T(8,128)(2,1)S(1)}, u32[]{:S(2)}, u32[]{:S(2)}) collective-permute-start(bf16[72,1152]{1,0:T(8,128)(2,1)S(1)} %pad_maximum_fusion.4), channel_id=1, source_target_pairs={{0,8},{1,9},{2,10},{3,11},{4,12},{5,13},{6,14},{7,15},{8,0},{9,1},... | collective-permute-start | bytes 497672 | tf_op jit(solution)/shard_map/ppermute | solution.py:35
  61.0 2.3 %collective-permute-start.13 = (bf16[64,1152]{1,0:T(8,128)(2,1)S(1)}, bf16[64,1152]{1,0:T(8,128)(2,1)S(1)}, u32[]{:S(2)}, u32[]{:S(2)}) collective-permute-start(bf16[64,1152]{1,0:T(8,128)(2,1)S(1)} %add_convert_fusion.3), channel_id=1, source_target_pairs={{0,8},{1,3},{2,10},{3,1},{4,12},{5,7},{6,14},{7,5},{8,0},{9,11},{1... | collective-permute-start | bytes 442376 | tf_op jit(solution)/shard_map/ppermute | solution.py:35
  63.4 3.4 %collective-permute-done.6 = bf16[72,1152]{1,0:T(8,128)(2,1)S(1)} collective-permute-done((bf16[72,1152]{1,0:T(8,128)(2,1)S(1)}, bf16[72,1152]{1,0:T(8,128)(2,1)S(1)}, u32[]{:S(2)}, u32[]{:S(2)}) %collective-permute-start.6) | collective-permute-done | bytes 165920 | tf_op jit(solution)/shard_map/ppermute | solution.py:35
  66.8 1.7 %collective-permute-start.7 = (bf16[64,1152]{1,0:T(8,128)(2,1)S(1)}, bf16[64,1152]{1,0:T(8,128)(2,1)S(1)}, u32[]{:S(2)}, u32[]{:S(2)}) collective-permute-start(bf16[64,1152]{1,0:T(8,128)(2,1)S(1)} %add_convert_fusion.5), channel_id=1, source_target_pairs={{0,4},{1,3},{2,6},{3,1},{4,0},{5,7},{6,2},{7,5},{8,12},{9,11},{10,... | collective-permute-start | bytes 442376 | tf_op jit(solution)/shard_map/ppermute | solution.py:35
  68.5 8.2 %collective-permute-done.7 = bf16[64,1152]{1,0:T(8,128)(2,1)S(1)} collective-permute-done((bf16[64,1152]{1,0:T(8,128)(2,1)S(1)}, bf16[64,1152]{1,0:T(8,128)(2,1)S(1)}, u32[]{:S(2)}, u32[]{:S(2)}) %collective-permute-start.7) | collective-permute-done | bytes 147488 | tf_op jit(solution)/shard_map/ppermute | solution.py:35
  76.7 2.2 %collective-permute-start.8 = (bf16[136,1152]{1,0:T(8,128)(2,1)S(1)}, bf16[136,1152]{1,0:T(8,128)(2,1)S(1)}, u32[]{:S(2)}, u32[]{:S(2)}) collective-permute-start(bf16[136,1152]{1,0:T(8,128)(2,1)S(1)} %pad_maximum_fusion.1), channel_id=1, source_target_pairs={{0,2},{1,5},{2,0},{3,7},{4,6},{5,1},{6,4},{7,3},{8,10},{9,13},{10,... | collective-permute-start | bytes 940040 | tf_op jit(solution)/shard_map/ppermute | solution.py:35
  79.1 4.8 %collective-permute-done.8 = bf16[136,1152]{1,0:T(8,128)(2,1)S(1)} collective-permute-done((bf16[136,1152]{1,0:T(8,128)(2,1)S(1)}, bf16[136,1152]{1,0:T(8,128)(2,1)S(1)}, u32[]{:S(2)}, u32[]{:S(2)}) %collective-permute-start.8) | collective-permute-done | bytes 313376 | tf_op jit(solution)/shard_map/ppermute | solution.py:35
  83.9 3.1 %collective-permute-done.16 = bf16[128,1152]{1,0:T(8,128)(2,1)S(1)} collective-permute-done((bf16[128,1152]{1,0:T(8,128)(2,1)S(1)}, bf16[128,1152]{1,0:T(8,128)(2,1)S(1)}, u32[]{:S(2)}, u32[]{:S(2)}) %collective-permute-start.16) | collective-permute-done | bytes 294944 | tf_op jit(solution)/shard_map/ppermute | solution.py:35
  87.7 0.8 latent.1
  88.6 1.9 %first_write.1.refs_3_ = f32[1024,1024]{1,0:T(8,128)} custom-call(s32[3]{0:T(128)S(1)} %pad_add_fusion.place.refs_0_, bf16[512,1152]{1,0:T(8,128)(2,1)S(1)} %pad_maximum_fusion.refs_1_), custom_call_target="tpu_custom_call" | custom-call | flops 1000000 | bytes 3000000 | tf_op jit(solution)/shard_map/first_write/pallas_call | solution.py:539
  91.7 2.8 %last_write.1 = (f32[1024,1024]{1,0:T(8,128)}, f32[100,1024]{1,0:T(8,128)}) custom-call(s32[3]{0:T(128)S(1)} %pad_add_fusion.place.refs_0_, bf16[512,1152]{1,0:T(8,128)(2,1)S(1)} %pad_maximum_fusion.refs_1_, bf16[512,1152]{1,0:T(8,128)(2,1)S(1)} %collective-permute-done.17.refs_2_, f32[1024,1024]{1,0:T(8,128)} %first_write.1.refs_3_), custom_call_target="tpu_custom_call", output_to_operand_aliasing={{0}: (3, {})} | custom-call | tf_op jit(solution)/shard_map/last_write/pallas_call | solution.py:549
  (42 shorter events, 4.7 us)
Async XLA Ops:
  1.5 8.2 %collective-permute-start = (bf16[2,16,1024]{2,1,0:T(8,128)(2,1)S(1)}, bf16[2,16,1024]{2,1,0:T(8,128)(2,1)S(1)}, u32[]{:S(2)}, u32[]{:S(2)}) collective-permute-start(bf16[2,16,1024]{2,1,0:T(8,128)(2,1)S(1)} %get-tuple-element.62), channel_id=1, source_target_pairs={{0,2},{2,4},{4,6},{6,8},{8,10},{10,12},{12,14},{1,3},{3,5},{5,7},{... | collective-permute-start | bytes 196616 | tf_op jit(solution)/shard_map/ppermute | solution.py:22
  6.4 6.2 %collective-permute-start.1 = (bf16[2,16,1024]{2,1,0:T(8,128)(2,1)S(1)}, bf16[2,16,1024]{2,1,0:T(8,128)(2,1)S(1)}, u32[]{:S(2)}, u32[]{:S(2)}) collective-permute-start(bf16[2,16,1024]{2,1,0:T(8,128)(2,1)S(1)} %get-tuple-element.61), channel_id=1, source_target_pairs={{2,0},{4,2},{6,4},{8,6},{10,8},{12,10},{14,12},{3,1},{5,3},{7,5},{... | collective-permute-start | bytes 196616 | tf_op jit(solution)/shard_map/ppermute | solution.py:22
  20.5 1.8 %collective-permute-start.2 = (f32[2,100,512]{2,1,0:T(8,128)S(1)}, f32[2,100,512]{2,1,0:T(8,128)S(1)}, u32[]{:S(2)}, u32[]{:S(2)}) collective-permute-start(f32[2,100,512]{2,1,0:T(8,128)S(1)} %get-tuple-element.32.refs_1_), channel_id=1, source_target_pairs={{0,1},{1,0},{2,3},{3,2},{4,5},{5,4},{6,7},{7,6},{8,9},{9,8},{10,11... | collective-permute-start | bytes 1228808 | tf_op jit(solution)/shard_map/ppermute | solution.py:26
  26.0 2.8 %collective-permute-start.3 = (bf16[512,1152]{1,0:T(8,128)(2,1)S(1)}, bf16[512,1152]{1,0:T(8,128)(2,1)S(1)}, u32[]{:S(2)}, u32[]{:S(2)}) collective-permute-start(bf16[512,1152]{1,0:T(8,128)(2,1)S(1)} %get-tuple-element.44), channel_id=1, source_target_pairs={{0,1},{1,0},{2,3},{3,2},{4,5},{5,4},{6,7},{7,6},{8,9},{9,8},{10,11... | collective-permute-start | bytes 3538952 | tf_op jit(solution)/shard_map/ppermute | solution.py:26
  29.2 17.3 %collective-permute-start.10 = (bf16[128,1152]{1,0:T(8,128)(2,1)S(1)}, bf16[128,1152]{1,0:T(8,128)(2,1)S(1)}, u32[]{:S(2)}, u32[]{:S(2)}) collective-permute-start(bf16[128,1152]{1,0:T(8,128)(2,1)S(1)} %get-tuple-element.59), channel_id=1, source_target_pairs={{0,2},{1,9},{2,0},{3,11},{4,6},{5,13},{6,4},{7,15},{8,10},{9,1},{1... | collective-permute-start | bytes 884744 | tf_op jit(solution)/shard_map/ppermute | solution.py:35
  31.6 14.9 %collective-permute-start.4 = (bf16[128,1152]{1,0:T(8,128)(2,1)S(1)}, bf16[128,1152]{1,0:T(8,128)(2,1)S(1)}, u32[]{:S(2)}, u32[]{:S(2)}) collective-permute-start(bf16[128,1152]{1,0:T(8,128)(2,1)S(1)} %get-tuple-element.60), channel_id=1, source_target_pairs={{0,2},{1,5},{2,0},{3,7},{4,6},{5,1},{6,4},{7,3},{8,10},{9,13},{10,... | collective-permute-start | bytes 884744 | tf_op jit(solution)/shard_map/ppermute | solution.py:35
  40.0 39.0 %collective-permute-start.14 = (bf16[2,16,1024]{2,1,0:T(8,128)(2,1)S(1)}, bf16[2,16,1024]{2,1,0:T(8,128)(2,1)S(1)}, u32[]{:S(2)}, u32[]{:S(2)}) collective-permute-start(bf16[2,16,1024]{2,1,0:T(8,128)(2,1)S(1)} %get-tuple-element.45), channel_id=1, source_target_pairs={{0,2},{2,4},{4,6},{6,8},{8,10},{10,12},{12,14},{1,3},{3,5},{5,7},{... | collective-permute-start | bytes 196616 | tf_op jit(solution)/shard_map/ppermute | solution.py:22
  43.9 35.1 %collective-permute-start.15 = (bf16[2,16,1024]{2,1,0:T(8,128)(2,1)S(1)}, bf16[2,16,1024]{2,1,0:T(8,128)(2,1)S(1)}, u32[]{:S(2)}, u32[]{:S(2)}) collective-permute-start(bf16[2,16,1024]{2,1,0:T(8,128)(2,1)S(1)} %get-tuple-element.46), channel_id=1, source_target_pairs={{2,0},{4,2},{6,4},{8,6},{10,8},{12,10},{14,12},{3,1},{5,3},{7,5},{... | collective-permute-start | bytes 196616 | tf_op jit(solution)/shard_map/ppermute | solution.py:22
  46.7 9.1 %collective-permute-start.11 = (bf16[64,1152]{1,0:T(8,128)(2,1)S(1)}, bf16[64,1152]{1,0:T(8,128)(2,1)S(1)}, u32[]{:S(2)}, u32[]{:S(2)}) collective-permute-start(bf16[64,1152]{1,0:T(8,128)(2,1)S(1)} %slice.115), channel_id=1, source_target_pairs={{0,8},{1,3},{2,10},{3,1},{4,12},{5,7},{6,14},{7,5},{8,0},{9,11},{1... | collective-permute-start | bytes 442376 | tf_op jit(solution)/shard_map/ppermute | solution.py:35
  51.0 6.9 %collective-permute-start.5 = (bf16[72,1152]{1,0:T(8,128)(2,1)S(1)}, bf16[72,1152]{1,0:T(8,128)(2,1)S(1)}, u32[]{:S(2)}, u32[]{:S(2)}) collective-permute-start(bf16[72,1152]{1,0:T(8,128)(2,1)S(1)} %pad_maximum_fusion.5), channel_id=1, source_target_pairs={{0,4},{1,3},{2,6},{3,1},{4,0},{5,7},{6,2},{7,5},{8,12},{9,11},{10,... | collective-permute-start | bytes 497672 | tf_op jit(solution)/shard_map/ppermute | solution.py:35
  55.8 5.2 %collective-permute-start.12 = (bf16[64,1152]{1,0:T(8,128)(2,1)S(1)}, bf16[64,1152]{1,0:T(8,128)(2,1)S(1)}, u32[]{:S(2)}, u32[]{:S(2)}) collective-permute-start(bf16[64,1152]{1,0:T(8,128)(2,1)S(1)} %add_convert_fusion.4), channel_id=1, source_target_pairs={{0,4},{1,5},{2,6},{3,7},{4,0},{5,1},{6,2},{7,3},{8,12},{9,13},{10,... | collective-permute-start | bytes 442376 | tf_op jit(solution)/shard_map/ppermute | solution.py:35
  58.7 8.1 %collective-permute-start.6 = (bf16[72,1152]{1,0:T(8,128)(2,1)S(1)}, bf16[72,1152]{1,0:T(8,128)(2,1)S(1)}, u32[]{:S(2)}, u32[]{:S(2)}) collective-permute-start(bf16[72,1152]{1,0:T(8,128)(2,1)S(1)} %pad_maximum_fusion.4), channel_id=1, source_target_pairs={{0,8},{1,9},{2,10},{3,11},{4,12},{5,13},{6,14},{7,15},{8,0},{9,1},... | collective-permute-start | bytes 497672 | tf_op jit(solution)/shard_map/ppermute | solution.py:35
  61.0 17.9 %collective-permute-start.13 = (bf16[64,1152]{1,0:T(8,128)(2,1)S(1)}, bf16[64,1152]{1,0:T(8,128)(2,1)S(1)}, u32[]{:S(2)}, u32[]{:S(2)}) collective-permute-start(bf16[64,1152]{1,0:T(8,128)(2,1)S(1)} %add_convert_fusion.3), channel_id=1, source_target_pairs={{0,8},{1,3},{2,10},{3,1},{4,12},{5,7},{6,14},{7,5},{8,0},{9,11},{1... | collective-permute-start | bytes 442376 | tf_op jit(solution)/shard_map/ppermute | solution.py:35
  66.8 9.9 %collective-permute-start.7 = (bf16[64,1152]{1,0:T(8,128)(2,1)S(1)}, bf16[64,1152]{1,0:T(8,128)(2,1)S(1)}, u32[]{:S(2)}, u32[]{:S(2)}) collective-permute-start(bf16[64,1152]{1,0:T(8,128)(2,1)S(1)} %add_convert_fusion.5), channel_id=1, source_target_pairs={{0,4},{1,3},{2,6},{3,1},{4,0},{5,7},{6,2},{7,5},{8,12},{9,11},{10,... | collective-permute-start | bytes 442376 | tf_op jit(solution)/shard_map/ppermute | solution.py:35
  76.7 7.1 %collective-permute-start.8 = (bf16[136,1152]{1,0:T(8,128)(2,1)S(1)}, bf16[136,1152]{1,0:T(8,128)(2,1)S(1)}, u32[]{:S(2)}, u32[]{:S(2)}) collective-permute-start(bf16[136,1152]{1,0:T(8,128)(2,1)S(1)} %pad_maximum_fusion.1), channel_id=1, source_target_pairs={{0,2},{1,5},{2,0},{3,7},{4,6},{5,1},{6,4},{7,3},{8,10},{9,13},{10,... | collective-permute-start | bytes 940040 | tf_op jit(solution)/shard_map/ppermute | solution.py:35
  79.0 8.0 %collective-permute-start.16 = (bf16[128,1152]{1,0:T(8,128)(2,1)S(1)}, bf16[128,1152]{1,0:T(8,128)(2,1)S(1)}, u32[]{:S(2)}, u32[]{:S(2)}) collective-permute-start(bf16[128,1152]{1,0:T(8,128)(2,1)S(1)} %pad_maximum_fusion.3), channel_id=1, source_target_pairs={{0,2},{1,9},{2,0},{3,11},{4,6},{5,13},{6,4},{7,15},{8,10},{9,1},{1... | collective-permute-start | bytes 884744 | tf_op jit(solution)/shard_map/ppermute | solution.py:35
  87.1 4.6 %collective-permute-start.17 = (bf16[512,1152]{1,0:T(8,128)(2,1)S(1)}, bf16[512,1152]{1,0:T(8,128)(2,1)S(1)}, u32[]{:S(2)}, u32[]{:S(2)}) collective-permute-start(bf16[512,1152]{1,0:T(8,128)(2,1)S(1)} %pad_maximum_fusion.refs_1_), channel_id=1, source_target_pairs={{0,1},{1,0},{2,3},{3,2},{4,5},{5,4},{6,7},{7,6},{8,9},{9,8},{10,11... | collective-permute-start | bytes 3538952 | tf_op jit(solution)/shard_map/ppermute | solution.py:26
  87.2 3.3 %collective-permute-start.9 = (f32[1,1152]{1,0:T(1,128)S(1)}, f32[1,1152]{1,0:T(1,128)S(1)}, u32[]{:S(2)}, u32[]{:S(2)}) collective-permute-start(f32[1,1152]{1,0:T(1,128)S(1)} %fusion.1), channel_id=1, source_target_pairs={{0,1},{1,0},{2,3},{3,2},{4,5},{5,4},{6,7},{7,6},{8,9},{9,8},{10,11... | collective-permute-start | bytes 13832 | tf_op jit(solution)/shard_map/ppermute | solution.py:26

commit v4 on v3

v4 whole, which is shorter than its diff:
```python
import jax
import jax.numpy as jnp
from jax import lax
from jax.experimental import pallas as pl
from jax.experimental.pallas import tpu as pltpu
from jax.sharding import PartitionSpec as P

RIM = 16
SMOOTH_SQ = 0.01
LANES = 128
BF16 = jnp.bfloat16
F32 = jnp.float32
VMEM = pl.BlockSpec(memory_space=pltpu.VMEM)
SMEM = pl.BlockSpec(memory_space=pltpu.SMEM)
HBM = pl.BlockSpec(memory_space=pltpu.HBM)
PARAMS = pltpu.CompilerParams(vmem_limit_bytes=16 * 1024 * 1024)


def shift(value, axis, steps):
    count = lax.axis_size(axis)
    first, last = (max(0, -steps), min(count, count - steps))
    return lax.ppermute(value, axis, [(source, source + steps) for source in range(first, last)])


def swap_cores(value):
    return lax.ppermute(value, "member", [(0, 1), (1, 0)])


def swap_bits(value, bits):
    pairs = [
        (s * 2 + c, (s ^ (1 << bits[c])) * 2 + c)
        for s in range(lax.axis_size("space"))
        for c in range(2)
    ]
    return lax.ppermute(value, ("space", "member"), pairs)


def orders(count):
    return [(0, 1), (1, 0)] + [(bit, bit) for bit in range(2, count)]


def turn(count, space, half):
    value = 0
    stages = orders(count)[:-1]
    for level, bits in enumerate(stages):
        value = value + ((1 - ((space >> bits[half]) & 1)) << (len(stages) - 1 - level))
    return value


def dot(a, b, dims=((1,), (0,))):
    return lax.dot_general(a, b, (dims, ((), ())), preferred_element_type=F32)


def fetch(sources, targets, sems):
    copies = [
        pltpu.make_async_copy(source, target, sems.at[i])
        for i, (source, target) in enumerate(zip(sources, targets))
    ]
    for copy in copies:
        copy.start()
    return copies


def prepare_kernel(
    place, index_in, mask_in, weight_in, valid_in, area_in, var_weight_in, state_in, target_in, projection_in, gain_in, hidden_weight_in,
    own_in, adj, adj_t, score_weight, base, projection, gain, hidden_weight, own,
    index, mask, weight, valid, area, var_weight, state, target, narrow, sems,
):
    sources = (
        index_in, mask_in, weight_in, valid_in, area_in, var_weight_in, projection_in, state_in, target_in, gain_in,
        hidden_weight_in, own_in,
    )
    targets = (index, mask, weight, valid, area, var_weight, narrow, state, target, gain, hidden_weight, own)
    copies = fetch(sources, targets, sems)
    for copy in copies[:6]:
        copy.wait()
    points = index.shape[1]
    variables = state.shape[0]
    nodes = jax.lax.broadcasted_iota(jnp.int32, (LANES, points), 0) + place[2]
    total = jnp.zeros((LANES, points), F32)
    for slot in range(index.shape[0]):
        coefficient = weight[slot : slot + 1, :] * mask[slot : slot + 1, :].astype(F32)
        total = total + jnp.where(index[slot : slot + 1, :] == nodes, coefficient, 0.0)
    upper = total.astype(BF16).astype(F32)
    lower = total - upper
    adj_t[:LANES, :] = upper.astype(BF16)
    adj_t[LANES:, :] = lower.astype(BF16)
    adj[:, :LANES] = upper.T.astype(BF16)
    adj[:, LANES:] = lower.T.astype(BF16)
    diagonal = jax.lax.broadcasted_iota(jnp.int32, (variables, variables), 0) == (
        jax.lax.broadcasted_iota(jnp.int32, (variables, variables), 1)
    )
    column = jnp.sum(jnp.where(diagonal, var_weight[...], 0.0), axis=1, keepdims=True)
    score_weight[...] = column * (valid[...].astype(F32) * area[...] / points)
    copies[6].wait()
    projection[...] = jnp.zeros_like(projection)
    projection[:variables, :] = narrow[...]
    copies[7].wait()
    copies[8].wait()
    base[...] = state[...] - target[...]
    for copy in copies[9:]:
        copy.wait()


def forward_kernel(
    adj, low, own, high, gain, hidden_weight, output_weight,
    normed, hidden, slope, outputs, deviation, extended, summed, projected,
):
    members, nodes, width = own.shape
    points = adj.shape[0]
    tile = 256
    for member in range(members):
        for part in range(2):
            start = part * LANES
            extended[member, start : start + RIM, :] = low[member]
            extended[member, start + RIM : start + RIM + nodes, :] = own[member]
            extended[member, start + RIM + nodes : start + 2 * RIM + nodes, :] = high[member]
            extended[member, start + 2 * RIM + nodes : start + LANES, :] = jnp.zeros(
                (LANES - 2 * RIM - nodes, width), BF16
            )

    def gather(member):
        summed[member] = dot(adj[...], extended[member])

    def norm(member, first, size):
        for row in range(first, first + size, 32):
            value = summed[member, row : row + 32, :]
            value = value - jnp.sum(value, axis=1, keepdims=True) * (1.0 / width)
            spread = jnp.sum(value * value, axis=1, keepdims=True) * (1.0 / width)
            inverse = lax.rsqrt(spread + 1e-05)
            target = slice(member * points + row, member * points + row + 32)
            deviation[target, :] = inverse
            normed[target, :] = (value * inverse * gain[...]).astype(BF16)

    def layer(member, column):
        rows = slice(member * points, (member + 1) * points)
        columns = slice(column, column + tile)
        pre = dot(normed[rows, :], hidden_weight[:, columns])
        sig = 0.5 * jnp.tanh(0.5 * pre) + 0.5
        hid = pre * sig
        slope[rows, columns] = (sig + hid * (1.0 - sig)).astype(BF16)
        hid = hid.astype(BF16)
        hidden[rows, columns] = hid
        term = dot(hid, output_weight[:, columns], ((1,), (1,)))
        if column == 0:
            projected[...] = term
        else:
            projected[...] += term

    gather(0)
    norm(0, 0, points)
    for member in range(members):
        if member + 1 < members:
            gather(member + 1)
        for column in range(0, width, tile):
            if member + 1 < members:
                size = points * tile // width
                norm(member + 1, points * column // width, size)
            layer(member, column)
        outputs[member] = projected[...].T[: outputs.shape[1], :]


def own_rows(place, count, width):
    half_rows, chunk_rows = width // 2, width // 4
    size = chunk_rows >> (count - 1)
    for half in range(2):
        for chunk in range(2):
            mask = turn(count, place[0], half)
            for block in range(chunk_rows // size):
                row = half * half_rows + chunk * chunk_rows
                start = (1 - (place[1] ^ half)) * half_rows + chunk * chunk_rows
                start = start + (block ^ mask) * size
                yield row + block * size, size, pl.multiple_of(start, size)


def narrow_rows(place, count, width):
    chunk_rows = width // 4
    size = chunk_rows >> (count - 1)
    for half in range(2):
        mask = turn(count, place[0], half)
        for block in range(chunk_rows // size):
            row = half * 2 * chunk_rows + block * 2 * size
            yield (row, row + size), size, 1 - (place[1] ^ half), pl.multiple_of((block ^ mask) * size, size)


def transpose_kernel(count, place, normed, normed_t):
    width = normed.shape[1]
    value = None
    for row, size, target in own_rows(place, count, width):
        if row % LANES == 0:
            value = normed[:, row : row + LANES].T
        offset = row % LANES
        normed_t[pl.ds(target, size), :] = value[offset : offset + size]


def score_kernel(
    place, outputs, others, base, score_weight, output_weight, slope, normed_t,
    loss, grad_pre, grad_pred_t, sent,
    grad_pred, grad_wide,
):
    members, variables, points = outputs.shape
    width = slope.shape[1]
    total = 2 * members
    weight = score_weight[...]
    grad_wide[...] = jnp.zeros_like(grad_wide)
    grad_pred[...] = jnp.zeros_like(grad_pred)
    values = [outputs[m] for m in range(members)]
    grads = [None] * members
    pair_grads = [jnp.zeros((variables, points), F32) for _ in range(members)]
    errors = jnp.zeros((variables, points), F32)
    pairs = jnp.full((variables, points), members * SMOOTH_SQ**0.5, F32)
    for m in range(members):
        diff = values[m] + base[...]
        square = diff * diff + SMOOTH_SQ
        inverse = lax.rsqrt(square)
        errors = errors + square * inverse
        grads[m] = diff * inverse
        for n in range(m + 1, members):
            diff = values[m] - values[n]
            square = diff * diff + SMOOTH_SQ
            inverse = lax.rsqrt(square)
            pairs = pairs + 2.0 * (square * inverse)
            pair_grads[m] = pair_grads[m] + diff * inverse
            pair_grads[n] = pair_grads[n] - diff * inverse
        for n in range(members):
            diff = values[m] - others[n]
            square = diff * diff + SMOOTH_SQ
            inverse = lax.rsqrt(square)
            pairs = pairs + square * inverse
            pair_grads[m] = pair_grads[m] + diff * inverse
    score = weight * (errors * (1.0 / total) - pairs * (1.0 / (2.0 * total * (total - 1))))
    loss[...] = jnp.sum(jnp.sum(score, axis=0, keepdims=True), axis=1, keepdims=True)
    for m in range(members):
        grad = weight * (grads[m] * (1.0 / total) - pair_grads[m] * (1.0 / (total * (total - 1))))
        columns = slice(m * points, (m + 1) * points)
        grad_wide[:variables, columns] = grad
        grad_pred[columns, :] = grad_wide[:, columns].T.astype(BF16)
    grad_pred_t[...] = grad_wide[...].astype(BF16)
    for m in range(members):
        rows = slice(m * points, (m + 1) * points)
        for column in range(0, width, 256):
            columns = slice(column, column + 256)
            grad_hid = dot(grad_pred[rows, :], output_weight[:, columns])
            grad_pre[rows, columns] = (grad_hid * slope[rows, columns].astype(F32)).astype(BF16)
    products(normed_t, grad_pre, slice(width // 4, width // 2), sent)


def products(normed_t, grad_pre, rows, target):
    width = grad_pre.shape[1]
    for column in range(0, width, 256):
        columns = slice(column, column + 256)
        target[:, columns] = dot(normed_t[rows, :], grad_pre[:, columns]).astype(target.dtype)


def sent_kernel(count, place, normed_t, grad_pre, grad_pred_t, hidden, sent, kept_narrow):
    width = grad_pre.shape[1]
    products(normed_t, grad_pre, slice(0, width // 4), sent)
    value = dot(grad_pred_t[...], hidden[...]).T
    for rows, size, own, place_row in narrow_rows(place, count, width):
        here = pl.ds(place_row, size)
        for side, row in enumerate(rows):
            part = value[row : row + size]
            start = width + side * LANES

            @pl.when(own == 1)
            def _():
                kept_narrow[here, side * LANES : (side + 1) * LANES] = part

            @pl.when(own == 0)
            def _():
                sent[here, start : start + LANES] = part.astype(BF16)


def kept_kernel(normed_t, grad_pre, *refs):
    width = grad_pre.shape[1]
    kept = refs[-1]
    if len(refs) == 1:
        products(normed_t, grad_pre, slice(3 * width // 4, width), kept)
    else:
        products(normed_t, grad_pre, slice(width // 2, 3 * width // 4), kept)
        kept[:, width:] = refs[0][...]


def backward_kernel(member, grad_pre, hidden_weight, normed, gain, deviation, adj_t, *refs):
    before, (small, inner, below, above, product, rows_grad) = refs[:-6], refs[-6:]
    nodes, width = inner.shape
    points = adj_t.shape[1]
    inverse_gain = 1.0 / gain[...]
    for column in range(0, width, 256):
        columns = slice(column, column + 256)
        product[:, columns] = dot(
            grad_pre[member * points : (member + 1) * points, :], hidden_weight[columns, :], ((1,), (1,))
        )

    def step(index, total):
        here = pl.ds(pl.multiple_of(index * 32, 32), 32)
        there = pl.ds(pl.multiple_of(member * points + index * 32, 32), 32)
        value = product[here, :]
        zn = normed[there, :].astype(F32)
        both = value * zn
        scaled = value * gain[...]
        mean = jnp.sum(scaled, axis=1, keepdims=True) * (1.0 / width)
        slant = jnp.sum(both, axis=1, keepdims=True) * (1.0 / width)
        grad = deviation[there, :] * (scaled - mean - (zn * inverse_gain) * slant)
        rows_grad[here, :] = grad.astype(BF16)
        return total + jnp.sum(both.reshape(4, 8, width), axis=0)

    total = before[0][...] if before else jnp.zeros((8, width), F32)
    total = lax.fori_loop(0, points // 32, step, total, unroll=4)
    value = dot(adj_t[...], rows_grad[...])
    value = value[:LANES] + value[LANES:]
    below[...] = value[:RIM].astype(BF16)
    inner[...] = value[RIM : RIM + nodes]
    above[...] = value[RIM + nodes : nodes + 2 * RIM].astype(BF16)
    if not before:
        small[...] = total
        return
    row = jnp.concatenate(
        [
            jnp.sum(total, axis=0, keepdims=True) * inverse_gain,
            jnp.broadcast_to(before[1][...], (1, 2 * LANES)),
        ],
        axis=1,
    )
    upper = row.astype(BF16).astype(F32)
    index = jax.lax.broadcasted_iota(jnp.int32, (8, row.shape[1]), 0)
    small[...] = jnp.where(index == 0, upper, jnp.where(index == 1, row - upper, 0.0)).astype(BF16)


def latent_kernel(*refs):
    grad_latent = refs[-1]
    members, nodes = grad_latent.shape[:2]
    inner, (from_below, from_above) = refs[:members], refs[members:-1]
    for member in range(members):
        grad_latent[member] = inner[member][...]
    grad_latent[:, :RIM, :] += from_below[...].astype(F32)
    grad_latent[:, nodes - RIM :, :] += from_above[...].astype(F32)


def write_rows(count, chunk, side, place, source, target, wide, start, sems):
    chunk_rows, width = source.shape[0], target.shape[1]
    size = chunk_rows >> (count - 1)
    half = place[1] ^ side
    mask = jnp.where(half == 0, turn(count, place[0], 0), turn(count, place[0], 1))
    copies = []
    for block in range(chunk_rows // size):
        here = slice(block * size, (block + 1) * size)
        there = slice(start + block * size, start + (block + 1) * size)
        wide[there, :] = source[here, :width].astype(F32)
        row = (half * 2 + chunk) * chunk_rows + (block ^ mask) * size
        copy = pltpu.make_async_copy(
            wide.at[there, :],
            target.at[pl.ds(pl.multiple_of(row, size), size), :],
            sems.at[start // size + block],
        )
        copy.start()
        copies.append(copy)
    return copies


def write_kernel(count, place, second, other_second, first, target, wide, sems):
    rows = first.shape[0]
    copies = write_rows(count, 1, 0, place, second, target, wide, 0, sems)
    copies += write_rows(count, 1, 1, place, other_second, target, wide, rows, sems)
    copies += write_rows(count, 0, 0, place, first, target, wide, 2 * rows, sems)
    for copy in copies:
        copy.wait()


def last_write_kernel(
    count, place, own, other, small, other_small, before,
    target, grad_out_t, grad_gain, loss,
    wide, narrow, narrow_t, gain_row, loss_cell, sems, last_sems,
):
    del before
    copies = write_rows(count, 0, 1, place, other, target, wide, 0, sems)
    width = target.shape[1]
    for rows, size, mine, place_row in narrow_rows(place, count, width):
        here = pl.ds(place_row, size)
        for side, row in enumerate(rows):
            lanes = slice(width + side * LANES, width + (side + 1) * LANES)
            value = jnp.where(mine == 1, own[here, lanes].astype(F32), other[here, lanes].astype(F32))
            narrow[row : row + size, :] = value
    narrow_t[...] = narrow[...].T[: grad_out_t.shape[0], :]
    total = small[...].astype(F32) + other_small[...].astype(F32)
    total = total[:1] + total[1:2]
    gain_row[...] = total[:, :width]
    loss_cell[...] = total[:, width : width + 1]
    copies += fetch((narrow_t, gain_row, loss_cell), (grad_out_t, grad_gain, loss), last_sems)
    for copy in copies:
        copy.wait()


def add_parts(mine, other):
    return (mine.astype(F32) + other.astype(F32)).astype(BF16)


def unpack(small):
    return small[:1].astype(F32) + small[1:2].astype(F32)


def swap_with(value, small, bits):
    rows = value.shape[0]
    other = swap_bits(jnp.concatenate([value, small]), bits)
    total = unpack(small) + unpack(other[rows:])
    upper = total.astype(BF16)
    lower = (total - upper.astype(F32)).astype(BF16)
    rest = jnp.zeros((small.shape[0] - 2, small.shape[1]), BF16)
    return other[:rows], jnp.concatenate([upper, lower, rest])


def first_stage(value, count):
    rows = value.shape[0] // 2
    return value[:rows], swap_bits(value[:rows], orders(count)[0]), value[rows:]


def next_stages(value, count, small=None):
    stages = orders(count)
    for level, bits in list(enumerate(stages))[1:]:
        rows = value.shape[0] // 2 if level < count - 1 else 0
        sent = value[:rows] if rows else value
        if small is None:
            other = swap_bits(sent, bits)
        else:
            other, small = swap_with(sent, small, bits)
        value = add_parts(value[rows:], other)
    for bits in reversed(stages[1:-1]):
        value = jnp.concatenate([swap_bits(value, bits), value])
    return value, small


def after(value, *others):
    return lax.optimization_barrier((value, *others))[0]


def in_hbm(*values):
    return [pltpu.with_memory_space_constraint(value, pltpu.HBM) for value in values]


def cost(flops, moved):
    return pl.CostEstimate(flops=flops, bytes_accessed=moved, transcendentals=0)


def local(
    latent,
    edge_node_index,
    edge_mask,
    edge_weight,
    valid,
    area,
    state,
    target,
    var_weight,
    gain,
    hidden_weight,
    output_weight,
):
    members, nodes, width = latent.shape
    points, variables = state.shape
    rows = members * points
    count = lax.axis_size("space").bit_length() - 1
    space, core = lax.axis_index("space"), lax.axis_index("member")
    place = jnp.stack([space, core, space * nodes - RIM]).astype(jnp.int32)
    low = shift(latent[:, nodes - RIM :], "space", 1)
    high = shift(latent[:, :RIM], "space", -1)
    adj, adj_t, score_weight, base, projection, gain, hidden_weight, own = pl.pallas_call(
        prepare_kernel,
        out_shape=(
            pltpu.VMEM((points, 2 * LANES), BF16),
            pltpu.VMEM((2 * LANES, points), BF16),
            pltpu.VMEM((variables, points), F32),
            pltpu.VMEM((variables, points), F32),
            pltpu.VMEM((LANES, width), BF16),
            pltpu.VMEM((1, width), F32),
            pltpu.VMEM((width, width), BF16),
            pltpu.VMEM(latent.shape, BF16),
        ),
        in_specs=[SMEM] + [HBM] * 12,
        out_specs=(VMEM,) * 8,
        scratch_shapes=[
            pltpu.VMEM(edge_mask.T.shape, jnp.int32),
            pltpu.VMEM(edge_mask.T.shape, jnp.int32),
            pltpu.VMEM(edge_mask.T.shape, F32),
            pltpu.VMEM((1, points), jnp.int32),
            pltpu.VMEM((1, points), F32),
            pltpu.VMEM((1, variables), F32),
            pltpu.VMEM((variables, points), F32),
            pltpu.VMEM((variables, points), F32),
            pltpu.VMEM((variables, width), BF16),
            pltpu.SemaphoreType.DMA((12,)),
        ],
        compiler_params=PARAMS,
        name="prepare",
    )(
        place,
        *in_hbm(
            edge_node_index.T,
            edge_mask.T,
            edge_weight.T,
            valid.reshape(1, points),
            area.reshape(1, points),
            var_weight.reshape(1, variables),
            state.T,
            target.T,
            output_weight.T,
            gain.reshape(1, width),
            hidden_weight,
            latent,
        ),
    )
    normed, hidden, slope, outputs, deviation = pl.pallas_call(
        forward_kernel,
        out_shape=(
            pltpu.VMEM((rows, width), BF16),
            pltpu.VMEM((rows, width), BF16),
            pltpu.VMEM((rows, width), BF16),
            jax.ShapeDtypeStruct((members, variables, points), F32),
            pltpu.VMEM((rows, 1), F32),
        ),
        in_specs=[VMEM] * 7,
        out_specs=(VMEM,) * 5,
        scratch_shapes=[
            pltpu.VMEM((members, 2 * LANES, width), BF16),
            pltpu.VMEM((members, points, width), F32),
            pltpu.VMEM((points, LANES), F32),
        ],
        compiler_params=PARAMS,
        name="forward",
    )(adj, low, own, high, gain, hidden_weight, projection)
    others = swap_cores(outputs)
    normed_t = pl.pallas_call(
        lambda *refs: transpose_kernel(count, *refs),
        out_shape=pltpu.VMEM((width, rows), BF16),
        in_specs=[SMEM, VMEM],
        out_specs=VMEM,
        compiler_params=PARAMS,
        cost_estimate=cost(10**9, 4 * 10**6),
        name="transpose",
    )(place, normed)
    chunk_rows = width // 4
    loss, grad_pre, grad_pred_t, sent_second = pl.pallas_call(
        score_kernel,
        out_shape=(
            jax.ShapeDtypeStruct((1, 1), F32),
            pltpu.VMEM((rows, width), BF16),
            pltpu.VMEM((LANES, rows), BF16),
            jax.ShapeDtypeStruct((chunk_rows, width), BF16),
        ),
        in_specs=[SMEM] + [VMEM] * 7,
        out_specs=(VMEM,) * 4,
        scratch_shapes=[pltpu.VMEM((rows, LANES), BF16), pltpu.VMEM((LANES, rows), F32)],
        compiler_params=PARAMS,
        name="score",
    )(place, outputs, others, base, score_weight, projection, slope, normed_t)
    received_second = swap_cores(sent_second)
    kept = lambda normed_t, grad_pre, *narrow: pl.pallas_call(
        kept_kernel,
        out_shape=jax.ShapeDtypeStruct((chunk_rows, width + 2 * LANES * len(narrow)), F32),
        in_specs=[VMEM] * (2 + len(narrow)),
        out_specs=VMEM,
        compiler_params=PARAMS,
        cost_estimate=cost(10**9, 2 * 10**6),
        name="kept",
    )(normed_t, grad_pre, *narrow)
    second = add_parts(kept(normed_t, grad_pre), received_second)
    second_sent, second_other, second = first_stage(second, count)
    sent_first, kept_narrow = pl.pallas_call(
        lambda *refs: sent_kernel(count, *refs),
        out_shape=(
            jax.ShapeDtypeStruct((chunk_rows, width + 2 * LANES), BF16),
            pltpu.VMEM((chunk_rows, 2 * LANES), F32),
        ),
        in_specs=[SMEM] + [VMEM] * 4,
        out_specs=(VMEM,) * 2,
        compiler_params=PARAMS,
        cost_estimate=cost(10**9, 4 * 10**6),
        name="sent",
    )(place, normed_t, grad_pre, after(grad_pred_t, second_sent), hidden)
    first = add_parts(kept(normed_t, grad_pre, kept_narrow), swap_cores(sent_first))
    first_sent, first_other, first = first_stage(first, count)

    def backward(member, adj_t, *before):
        last = len(before) > 0
        return pl.pallas_call(
            lambda *refs: backward_kernel(member, *refs),
            out_shape=(
                jax.ShapeDtypeStruct((8, width + 2 * LANES), BF16) if last else pltpu.VMEM((8, width), F32),
                pltpu.VMEM((nodes, width), F32),
                jax.ShapeDtypeStruct((RIM, width), BF16),
                jax.ShapeDtypeStruct((RIM, width), BF16),
            ),
            in_specs=[VMEM] * (6 + len(before)),
            out_specs=(VMEM,) * 4,
            scratch_shapes=[pltpu.VMEM((points, width), F32), pltpu.VMEM((points, width), BF16)],
            compiler_params=PARAMS,
            cost_estimate=cost(3 * 10**9, 4 * 10**6),
            name="backward",
        )(grad_pre, hidden_weight, normed, gain, deviation, adj_t, *before)

    parts = []
    for member in range(members):
        if member == 0:
            parts.append(backward(0, after(adj_t, first_sent)))
            second_other = after(second_other, parts[0][1])
            second = add_parts(second, second_other)
        else:
            total = (parts[-1][0], loss) if member == members - 1 else (parts[-1][0],)
            parts.append(backward(member, after(adj_t, second), *total))
    small = parts[-1][0]
    inner, below, above = zip(*(part[1:] for part in parts))
    below, above = jnp.stack(below), jnp.stack(above)
    first = add_parts(first, first_other)
    first, small = next_stages(first, count, small)
    second, _ = next_stages(second, count)
    first, below, above = lax.optimization_barrier((first, below, above))
    first_other, small = swap_with(first, small, orders(count)[0])
    second = jnp.concatenate([swap_bits(second, orders(count)[0]), second])
    other_second = swap_cores(second)
    rims = (shift(above, "space", 1), shift(below, "space", -1))
    grad_latent = pl.pallas_call(
        latent_kernel,
        out_shape=jax.ShapeDtypeStruct((members, nodes, width), F32),
        in_specs=[VMEM] * (members + 2),
        out_specs=VMEM,
        compiler_params=PARAMS,
        cost_estimate=cost(10**6, 10**6),
        name="latent",
    )(*inner, *rims)

    first = jnp.concatenate([first_other, first])
    other_first = swap_cores(first)
    other_small = swap_cores(small)
    hidden_shape = jax.ShapeDtypeStruct((width, width), F32)
    blocks = 1 << (count - 1)
    grad_hidden = pl.pallas_call(
        lambda *refs: write_kernel(count, *refs),
        out_shape=hidden_shape,
        in_specs=[SMEM] + [VMEM] * 3,
        out_specs=HBM,
        scratch_shapes=[pltpu.VMEM((3 * chunk_rows, width), F32), pltpu.SemaphoreType.DMA((3 * blocks,))],
        compiler_params=PARAMS,
        cost_estimate=cost(10**6, 6 * 10**6),
        name="write",
    )(place, second, other_second, first)
    grad_hidden, grad_out, grad_gain, loss = pl.pallas_call(
        lambda *refs: last_write_kernel(count, *refs),
        out_shape=(
            hidden_shape,
            jax.ShapeDtypeStruct((variables, width), F32),
            jax.ShapeDtypeStruct((1, width), F32),
            jax.ShapeDtypeStruct((1, 1), F32),
        ),
        in_specs=[SMEM] + [VMEM] * 4 + [HBM],
        out_specs=(HBM,) * 4,
        scratch_shapes=[
            pltpu.VMEM((chunk_rows, width), F32),
            pltpu.VMEM((width, LANES), F32),
            pltpu.VMEM((variables, width), F32),
            pltpu.VMEM((1, width), F32),
            pltpu.VMEM((1, 1), F32),
            pltpu.SemaphoreType.DMA((blocks,)),
            pltpu.SemaphoreType.DMA((3,)),
        ],
        input_output_aliases={5: 0},
        compiler_params=PARAMS,
        name="last_write",
    )(place, first, other_first, small, other_small, grad_hidden)
    return (loss.reshape(1), grad_hidden, grad_out.T, grad_gain.reshape(width), grad_latent)


def solution(mesh):
    in_specs = (
        P(("groups", "member"), "space", None),
        P(("groups", "space"), None),
        P(("groups", "space"), None),
        P(("groups", "space"), None),
        P(("groups", "space")),
        P(("groups", "space")),
        P(("groups", "space"), None),
        P(("groups", "space"), None),
        P(),
        P(),
        P(),
        P(),
    )
    out_specs = (
        P("groups"),
        P("groups", None),
        P("groups", None),
        P("groups"),
        P(("groups", "member"), "space", None),
    )
    return jax.shard_map(local, mesh=mesh, in_specs=in_specs, out_specs=out_specs, check_vma=False)
```

time: 94.8 us -> 80.9 us (0.85)
  waiting for transfers between devices: 29.8 us -> 25.3 us
  starting transfers between devices: 29.1 us -> 25.5 us
  Pallas kernels: 29.7 us -> 26.7 us
  local copies, waits for them, and re-layouts: 2.75 us -> 0.98 us
  other arithmetic: 2.26 us -> 0.98 us
    ppermute x10, waiting for transfers between devices: 24.8 us -> 19.4 us  [swap_bits(): return lax.ppermute(value, ('space', 'member'), pairs)]
    pallas_call x1, Pallas kernels: 7.97 us -> 5.2 us  [local(): pl.pallas_call(forward_kernel, out_shape=(pltpu.VMEM((rows, width), BF16)...]
    ppermute x10, starting transfers between devices: 16.9 us -> 14.7 us  [swap_bits(): return lax.ppermute(value, ('space', 'member'), pairs)]
    ppermute x4, starting transfers between devices: 11.3 us -> 9.71 us  [shift(): lax.ppermute(value, axis, [(source, source + steps) for source in range(f...]
    ppermute x4, waiting for transfers between devices: 2.88 us -> 4.24 us  [shift(): lax.ppermute(value, axis, [(source, source + steps) for source in range(f...]
    convert_element_type x5 -> x6, other arithmetic: 1.34 us -> 0.07 us  [the longest x3 0.05 us: swap_with(): upper = total.astype(BF16)]
    slice x6 -> x5, local copies, waits for them, and re-layouts: 1.2 us -> 0.09 us  [the longest x2 0.04 us: first_stage(): value[:rows]]
    pallas_call x1, Pallas kernels: 2.8 us -> 1.81 us  [local(): pl.pallas_call(lambda *refs: last_write_kernel(count, *refs), out_shape=(...]
  transfers between devices with their start and end apart: 18 -> 20, of which waited for: 10 -> 10; matrix products, arithmetic and copies ran while one was open for 4% -> 1% of each run, Pallas kernels for 16% -> 18%
where the time goes in v4:
time: 80.9 us; the launch traced here: 80.7 us
  Pallas kernels  26.7 us (33%)
  starting transfers between devices  25.5 us (32%)
  waiting for transfers between devices  25.3 us (31%)
  between operations  1.17 us (1%)
  local copies, waits for them, and re-layouts  0.98 us (1%)
  other arithmetic  0.98 us (1%)
    ppermute x10, waiting for transfers between devices, swap_bits(): return lax.ppermute(value, ('space', 'member'), pairs)  19.4 us
    ppermute x10, starting transfers between devices, swap_bits(): return lax.ppermute(value, ('space', 'member'), pairs)  14.7 us
    ppermute x4, starting transfers between devices, shift(): lax.ppermute(value, axis, [(source, source + steps) for source in range(f...  9.71 us
    pallas_call x2, Pallas kernels, backward(): pl.pallas_call(lambda *refs: backward_kernel(member, *refs), out_shape=(j...  6.46 us
    pallas_call x1, Pallas kernels, local(): pl.pallas_call(forward_kernel, out_shape=(pltpu.VMEM((rows, width), BF16)...  5.2 us
    ppermute x4, waiting for transfers between devices, shift(): lax.ppermute(value, axis, [(source, source + steps) for source in range(f...  4.24 us
    pallas_call x1, Pallas kernels, local(): pl.pallas_call(score_kernel, out_shape=(jax.ShapeDtypeStruct((1, 1), F32)...  2.89 us
    pallas_call x1, Pallas kernels, local(): pl.pallas_call(prepare_kernel, out_shape=(pltpu.VMEM((points, 2 * LANES),...  2.66 us
  transfers between devices with their start and end apart: 20, of which 10 were waited for; matrix products, arithmetic and copies ran while one was open for 1% of the time, Pallas kernels for 18%

profile of v4, /device:TPU:0, one launch (start us, length us, event | category | flops | bytes accessed | tf_op | source)
XLA Modules:
  0.0 80.7 jit_solution(5081320886028404816)
XLA Ops:
  0.6 0.9 %fusion.12 = (bf16[2,16,1024]{2,1,0:T(8,128)(2,1)S(1)}, bf16[2,16,1024]{2,1,0:T(8,128)(2,1)S(1)}) fusion(bf16[2,64,1024]{2,1,0:T(8,128)(2,1)} %own_in.1), kind=kLoop, calls=%fused_computation.37 | loop fusion | bytes 262144 | tf_op jit(solution)/shard_map/slice | solution.py:465
  1.5 4.9 %collective-permute-start = (bf16[2,16,1024]{2,1,0:T(8,128)(2,1)S(1)}, bf16[2,16,1024]{2,1,0:T(8,128)(2,1)S(1)}, u32[]{:S(2)}, u32[]{:S(2)}) collective-permute-start(bf16[2,16,1024]{2,1,0:T(8,128)(2,1)S(1)} %get-tuple-element.88), channel_id=1, source_target_pairs={{0,2},{2,4},{4,6},{6,8},{8,10},{10,12},{12,14},{1,3},{3,5},{5,7},{... | collective-permute-start | bytes 196616 | tf_op jit(solution)/shard_map/ppermute | solution.py:22
  6.4 1.3 %collective-permute-start.1 = (bf16[2,16,1024]{2,1,0:T(8,128)(2,1)S(1)}, bf16[2,16,1024]{2,1,0:T(8,128)(2,1)S(1)}, u32[]{:S(2)}, u32[]{:S(2)}) collective-permute-start(bf16[2,16,1024]{2,1,0:T(8,128)(2,1)S(1)} %get-tuple-element.87), channel_id=1, source_target_pairs={{2,0},{4,2},{6,4},{8,6},{10,8},{12,10},{14,12},{3,1},{5,3},{7,5},{... | collective-permute-start | bytes 196616 | tf_op jit(solution)/shard_map/ppermute | solution.py:22
  7.8 2.7 %prepare.1 = (bf16[512,256]{1,0:T(8,128)(2,1)S(1)}, bf16[256,512]{1,0:T(8,128)(2,1)S(1)}, f32[100,512]{1,0:T(8,128)S(1)}, f32[100,512]{1,0:T(8,128)S(1)}, bf16[1...) custom-call(s32[3]{0:T(128)S(1)} %pad_add_fusion.place.refs_0_, ...), custom_call_target="tpu_custom_call" | custom-call | tf_op jit(solution)/shard_map/prepare/pallas_call | solution.py:466
  10.5 2.1 %collective-permute-done.1.high = bf16[2,16,1024]{2,1,0:T(8,128)(2,1)S(1)} collective-permute-done((bf16[2,16,1024]{2,1,0:T(8,128)(2,1)S(1)}, bf16[2,16,1024]{2,1,0:T(8,128)(2,1)S(1)}, u32[]{:S(2)}, u32[]{:S(2)}) %collective-permute-start.1) | collective-permute-done | bytes 65568 | tf_op jit(solution)/shard_map/ppermute | solution.py:22
  12.6 5.2 %forward.1 = (bf16[1024,1024]{1,0:T(8,128)(2,1)S(1)}, bf16[1024,1024]{1,0:T(8,128)(2,1)S(1)}, bf16[1024,1024]{1,0:T(8,128)(2,1)S(1)}, f32[2,100,512]{2,1,0:T(8,128)S(1)}, f32[1024,1]{1,0:T(8,128)S(1)}) custom-call(bf16[512,256]{1,0:T(8,128)(2,1)S(1)} %get-tuple-element.43.adj, bf16[2,16,1024]{2,1,0:T(8,128)(2,1)S(1)} %collective-permute-done.low, ...), custom_call_target="tpu_custom_call" | custom-call | tf_op jit(solution)/shard_map/forward/pallas_call | solution.py:511
  17.8 1.2 %transpose.29.normed_t.refs_1_ = bf16[1024,1024]{1,0:T(8,128)(2,1)S(1)} custom-call(s32[3]{0:T(128)S(1)} %pad_add_fusion.place.refs_0_, bf16[1024,1024]{1,0:T(8,128)(2,1)S(1)} %get-tuple-element.48.refs_1_.refs_2_), custom_call_target="tpu_custom_call" | custom-call | flops 1000000000 | bytes 4000000 | tf_op jit(solution)/shard_map/transpose/pallas_call | solution.py:531
  19.6 2.9 %score.1 = (f32[1,1]{1,0:T(1,128)}, bf16[1024,1024]{1,0:T(8,128)(2,1)S(1)}, bf16[128,1024]{1,0:T(8,128)(2,1)S(1)}, bf16[256,1024]{1,0:T(8,128)(2,1)S(1)}) custom-call(s32[3]{0:T(128)S(1)} %pad_add_fusion.place.refs_0_, f32[2,100,512]{2,1,0:T(8,128)S(1)} %get-tuple-element.49.outputs, f32[2,100,512]{2,1,0:T(8,128)S(1)} %collective-permute-done.2.others, ...), custom_call_target="tpu_custom_call" | custom-call | tf_op jit(solution)/shard_map/score/pallas_call | solution.py:541
  23.3 1.1 %collective-permute-done.3 = bf16[256,1024]{1,0:T(8,128)(2,1)S(1)} collective-permute-done((bf16[256,1024]{1,0:T(8,128)(2,1)S(1)}, bf16[256,1024]{1,0:T(8,128)(2,1)S(1)}, u32[]{:S(2)}, u32[]{:S(2)}) %collective-permute-start.3) | collective-permute-done | bytes 524320 | tf_op jit(solution)/shard_map/ppermute | solution.py:26
  24.6 2.0 %sent.1 = (bf16[256,1280]{1,0:T(8,128)(2,1)S(1)}, f32[256,256]{1,0:T(8,128)S(1)}) custom-call(s32[3]{0:T(128)S(1)} %pad_add_fusion.place.refs_0_, bf16[1024,1024]{1,0:T(8,128)(2,1)S(1)} %transpose.29.normed_t.refs_1_, bf16[1024,1024]{1,0:T(8,128)(2,1)S(1)} %get-tuple-element.53.grad_pre.refs_2_.refs_0_, bf16[128,1024]{1,0:T(8,128)(2,1)S(1)} %get-tuple-element.56.refs_3_, ...), custom_call_target="tpu_custom_call" | custom-call | flops 1000000000 | bytes 4000000 | tf_op jit(solution)/shard_map/sent/pallas_call | solution.py:567
  26.8 2.4 %collective-permute-start.6 = (bf16[128,1024]{1,0:T(8,128)(2,1)S(1)}, bf16[128,1024]{1,0:T(8,128)(2,1)S(1)}, u32[]{:S(2)}, u32[]{:S(2)}) collective-permute-start(bf16[128,1024]{1,0:T(8,128)(2,1)S(1)} %slice.95), channel_id=1, source_target_pairs={{0,2},{1,5},{2,0},{3,7},{4,6},{5,1},{6,4},{7,3},{8,10},{9,13},{10,... | collective-permute-start | bytes 786440 | tf_op jit(solution)/shard_map/ppermute | solution.py:35
  29.2 0.7 kept.3
  30.1 1.3 %collective-permute-start.5 = (bf16[128,1280]{1,0:T(8,128)(2,1)S(1)}, bf16[128,1280]{1,0:T(8,128)(2,1)S(1)}, u32[]{:S(2)}, u32[]{:S(2)}) collective-permute-start(bf16[128,1280]{1,0:T(8,128)(2,1)S(1)} %slice.97), channel_id=1, source_target_pairs={{0,2},{1,5},{2,0},{3,7},{4,6},{5,1},{6,4},{7,3},{8,10},{9,13},{10,... | collective-permute-start | bytes 983048 | tf_op jit(solution)/shard_map/ppermute | solution.py:35
  31.4 2.9 %backward.2 = (f32[8,1024]{1,0:T(8,128)S(1)}, f32[64,1024]{1,0:T(8,128)S(1)}, bf16[16,1024]{1,0:T(8,128)(2,1)S(1)}, bf16[16,1024]{1,0:T(8,128)(2,1)S(1)}) custom-call(bf16[1024,1024]{1,0:T(8,128)(2,1)S(1)} %get-tuple-element.53.grad_pre.refs_2_.refs_0_, bf16[1024,1024]{1,0:T(8,128)(2,1)S(1)} %get-tuple-element.46.hidden_weight.refs_1_, ...), custom_call_target="tpu_custom_call" | custom-call | flops 3000000000 | bytes 4000000 | tf_op jit(solution)/shard_map/backward/pallas_call | solution.py:584
  34.4 1.6 %collective-permute-start.13 = (bf16[64,1024]{1,0:T(8,128)(2,1)S(1)}, bf16[64,1024]{1,0:T(8,128)(2,1)S(1)}, u32[]{:S(2)}, u32[]{:S(2)}) collective-permute-start(bf16[64,1024]{1,0:T(8,128)(2,1)S(1)} %slice.111), channel_id=1, source_target_pairs={{0,4},{1,3},{2,6},{3,1},{4,0},{5,7},{6,2},{7,5},{8,12},{9,11},{10,... | collective-permute-start | bytes 393224 | tf_op jit(solution)/shard_map/ppermute | solution.py:35
  36.0 3.6 %backward.3 = (bf16[8,1280]{1,0:T(8,128)(2,1)S(1)}, f32[64,1024]{1,0:T(8,128)S(1)}, bf16[16,1024]{1,0:T(8,128)(2,1)S(1)}, bf16[16,1024]{1,0:T(8,128)(2,1)S(1)}) custom-call(bf16[1024,1024]{1,0:T(8,128)(2,1)S(1)} %get-tuple-element.53.grad_pre.refs_2_.refs_0_, bf16[1024,1024]{1,0:T(8,128)(2,1)S(1)} %get-tuple-element.46.hidden_weight.refs_1_, ...), custom_call_target="tpu_custom_call" | custom-call | flops 3000000000 | bytes 4000000 | tf_op jit(solution)/shard_map/backward/pallas_call | solution.py:584
  39.7 2.5 %collective-permute-start.14 = (bf16[64,1024]{1,0:T(8,128)(2,1)S(1)}, bf16[64,1024]{1,0:T(8,128)(2,1)S(1)}, u32[]{:S(2)}, u32[]{:S(2)}) collective-permute-start(bf16[64,1024]{1,0:T(8,128)(2,1)S(1)} %add_convert_fusion.7), channel_id=1, source_target_pairs={{0,8},{1,9},{2,10},{3,11},{4,12},{5,13},{6,14},{7,15},{8,0},{9,1},... | collective-permute-start | bytes 393224 | tf_op jit(solution)/shard_map/ppermute | solution.py:35
  43.0 5.5 %collective-permute-done.14 = bf16[64,1024]{1,0:T(8,128)(2,1)S(1)} collective-permute-done((bf16[64,1024]{1,0:T(8,128)(2,1)S(1)}, bf16[64,1024]{1,0:T(8,128)(2,1)S(1)}, u32[]{:S(2)}, u32[]{:S(2)}) %collective-permute-start.14) | collective-permute-done | bytes 131104 | tf_op jit(solution)/shard_map/ppermute | solution.py:35
  48.6 1.2 %collective-permute-done.7 = bf16[72,1280]{1,0:T(8,128)(2,1)S(1)} collective-permute-done((bf16[72,1280]{1,0:T(8,128)(2,1)S(1)}, bf16[72,1280]{1,0:T(8,128)(2,1)S(1)}, u32[]{:S(2)}, u32[]{:S(2)}) %collective-permute-start.7) | collective-permute-done | bytes 184352 | tf_op jit(solution)/shard_map/ppermute | solution.py:35
  50.0 2.0 %collective-permute-start.8 = (bf16[72,1280]{1,0:T(8,128)(2,1)S(1)}, bf16[72,1280]{1,0:T(8,128)(2,1)S(1)}, u32[]{:S(2)}, u32[]{:S(2)}) collective-permute-start(bf16[72,1280]{1,0:T(8,128)(2,1)S(1)} %pad_maximum_fusion.6), channel_id=1, source_target_pairs={{0,8},{1,9},{2,10},{3,11},{4,12},{5,13},{6,14},{7,15},{8,0},{9,1},... | collective-permute-start | bytes 552968 | tf_op jit(solution)/shard_map/ppermute | solution.py:35
  52.0 2.4 %collective-permute-done.15 = bf16[64,1024]{1,0:T(8,128)(2,1)S(1)} collective-permute-done((bf16[64,1024]{1,0:T(8,128)(2,1)S(1)}, bf16[64,1024]{1,0:T(8,128)(2,1)S(1)}, u32[]{:S(2)}, u32[]{:S(2)}) %collective-permute-start.15) | collective-permute-done | bytes 131104 | tf_op jit(solution)/shard_map/ppermute | solution.py:35
  54.4 2.3 %collective-permute-start.16 = (bf16[128,1024]{1,0:T(8,128)(2,1)S(1)}, bf16[128,1024]{1,0:T(8,128)(2,1)S(1)}, u32[]{:S(2)}, u32[]{:S(2)}) collective-permute-start(bf16[128,1024]{1,0:T(8,128)(2,1)S(1)} %pad_maximum_fusion.4), channel_id=1, source_target_pairs={{0,2},{1,5},{2,0},{3,7},{4,6},{5,1},{6,4},{7,3},{8,10},{9,13},{10,... | collective-permute-start | bytes 786440 | tf_op jit(solution)/shard_map/ppermute | solution.py:35
  56.8 3.0 %collective-permute-done.8 = bf16[72,1280]{1,0:T(8,128)(2,1)S(1)} collective-permute-done((bf16[72,1280]{1,0:T(8,128)(2,1)S(1)}, bf16[72,1280]{1,0:T(8,128)(2,1)S(1)}, u32[]{:S(2)}, u32[]{:S(2)}) %collective-permute-start.8) | collective-permute-done | bytes 184352 | tf_op jit(solution)/shard_map/ppermute | solution.py:35
  59.9 5.3 %collective-permute-done.9 = bf16[64,1280]{1,0:T(8,128)(2,1)S(1)} collective-permute-done((bf16[64,1280]{1,0:T(8,128)(2,1)S(1)}, bf16[64,1280]{1,0:T(8,128)(2,1)S(1)}, u32[]{:S(2)}, u32[]{:S(2)}) %collective-permute-start.9) | collective-permute-done | bytes 163872 | tf_op jit(solution)/shard_map/ppermute | solution.py:35
  65.2 1.7 %collective-permute-start.10 = (bf16[136,1280]{1,0:T(8,128)(2,1)S(1)}, bf16[136,1280]{1,0:T(8,128)(2,1)S(1)}, u32[]{:S(2)}, u32[]{:S(2)}) collective-permute-start(bf16[136,1280]{1,0:T(8,128)(2,1)S(1)} %pad_maximum_fusion.2), channel_id=1, source_target_pairs={{0,2},{1,5},{2,0},{3,7},{4,6},{5,1},{6,4},{7,3},{8,10},{9,13},{10,... | collective-permute-start | bytes 1044488 | tf_op jit(solution)/shard_map/ppermute | solution.py:35
  67.1 2.3 %collective-permute-start.18 = (bf16[2,16,1024]{2,1,0:T(8,128)(2,1)S(1)}, bf16[2,16,1024]{2,1,0:T(8,128)(2,1)S(1)}, u32[]{:S(2)}, u32[]{:S(2)}) collective-permute-start(bf16[2,16,1024]{2,1,0:T(8,128)(2,1)S(1)} %get-tuple-element.79), channel_id=1, source_target_pairs={{0,2},{2,4},{4,6},{6,8},{8,10},{10,12},{12,14},{1,3},{3,5},{5,7},{... | collective-permute-start | bytes 196616 | tf_op jit(solution)/shard_map/ppermute | solution.py:22
  69.4 1.3 %collective-permute-start.19 = (bf16[2,16,1024]{2,1,0:T(8,128)(2,1)S(1)}, bf16[2,16,1024]{2,1,0:T(8,128)(2,1)S(1)}, u32[]{:S(2)}, u32[]{:S(2)}) collective-permute-start(bf16[2,16,1024]{2,1,0:T(8,128)(2,1)S(1)} %get-tuple-element.80), channel_id=1, source_target_pairs={{2,0},{4,2},{6,4},{8,6},{10,8},{12,10},{14,12},{3,1},{5,3},{7,5},{... | collective-permute-start | bytes 196616 | tf_op jit(solution)/shard_map/ppermute | solution.py:22
  70.7 1.9 %collective-permute-done.10 = bf16[136,1280]{1,0:T(8,128)(2,1)S(1)} collective-permute-done((bf16[136,1280]{1,0:T(8,128)(2,1)S(1)}, bf16[136,1280]{1,0:T(8,128)(2,1)S(1)}, u32[]{:S(2)}, u32[]{:S(2)}) %collective-permute-start.10) | collective-permute-done | bytes 348192 | tf_op jit(solution)/shard_map/ppermute | solution.py:35
  73.4 2.1 %collective-permute-done.19.refs_3_ = bf16[2,16,1024]{2,1,0:T(8,128)(2,1)S(1)} collective-permute-done((bf16[2,16,1024]{2,1,0:T(8,128)(2,1)S(1)}, bf16[2,16,1024]{2,1,0:T(8,128)(2,1)S(1)}, u32[]{:S(2)}, u32[]{:S(2)}) %collective-permute-start.19) | collective-permute-done | bytes 65568 | tf_op jit(solution)/shard_map/ppermute | solution.py:22
  75.5 0.8 %latent.1 = f32[2,64,1024]{2,1,0:T(8,128)} custom-call(f32[64,1024]{1,0:T(8,128)S(1)} %get-tuple-element.63.refs_0_, f32[64,1024]{1,0:T(8,128)S(1)} %get-tuple-element.78.refs_1_, bf16[2,16,1024]{2,1,0:T(8,128)(2,1)S(1)} %collective-permute-done.18.refs_2_, bf16[2,16,1024]{2,1,0:T(8,128)(2,1)S(1)} %collective-permute-done.19.refs_3_), custom_call_target="tpu_custom_call" | custom-call | flops 1000000 | bytes 1000000 | tf_op jit(solution)/shard_map/latent/pallas_call | solution.py:620
  76.4 2.3 %write.1.refs_5_ = f32[1024,1024]{1,0:T(8,128)} custom-call(s32[3]{0:T(128)S(1)} %pad_add_fusion.place.refs_0_, bf16[256,1024]{1,0:T(8,128)(2,1)S(1)} %pad_maximum_fusion.1.refs_1_, bf16[256,1024]{1,0:T(8,128)(2,1)S(1)} %collective-permute-done.17.refs_2_, bf16[256,1280]{1,0:T(8,128)(2,1)S(1)} %pad_maximum_fusion.refs_3_.refs_1_), custom_call_target="tpu_custom_call" | custom-call | flops 1000000 | bytes 6000000 | tf_op jit(solution)/shard_map/write/pallas_call | solution.py:635
  78.7 1.8 %last_write.1 = (f32[1024,1024]{1,0:T(8,128)}, f32[100,1024]{1,0:T(8,128)}, f32[1,1024]{1,0:T(1,128)}, f32[1,1]{1,0:T(1,128)}) custom-call(s32[3]{0:T(128)S(1)} %pad_add_fusion.place.refs_0_, bf16[256,1280]{1,0:T(8,128)(2,1)S(1)} %pad_maximum_fusion.refs_3_.refs_1_, ...), custom_call_target="tpu_custom_call", output_to_operand_aliasing={{0}: (5, {})} | custom-call | tf_op jit(solution)/shard_map/last_write/pallas_call | solution.py:645
  (51 shorter events, 4.4 us)
Async XLA Ops:
  1.5 8.9 %collective-permute-start = (bf16[2,16,1024]{2,1,0:T(8,128)(2,1)S(1)}, bf16[2,16,1024]{2,1,0:T(8,128)(2,1)S(1)}, u32[]{:S(2)}, u32[]{:S(2)}) collective-permute-start(bf16[2,16,1024]{2,1,0:T(8,128)(2,1)S(1)} %get-tuple-element.88), channel_id=1, source_target_pairs={{0,2},{2,4},{4,6},{6,8},{8,10},{10,12},{12,14},{1,3},{3,5},{5,7},{... | collective-permute-start | bytes 196616 | tf_op jit(solution)/shard_map/ppermute | solution.py:22
  6.4 6.2 %collective-permute-start.1 = (bf16[2,16,1024]{2,1,0:T(8,128)(2,1)S(1)}, bf16[2,16,1024]{2,1,0:T(8,128)(2,1)S(1)}, u32[]{:S(2)}, u32[]{:S(2)}) collective-permute-start(bf16[2,16,1024]{2,1,0:T(8,128)(2,1)S(1)} %get-tuple-element.87), channel_id=1, source_target_pairs={{2,0},{4,2},{6,4},{8,6},{10,8},{12,10},{14,12},{3,1},{5,3},{7,5},{... | collective-permute-start | bytes 196616 | tf_op jit(solution)/shard_map/ppermute | solution.py:22
  17.8 1.8 %collective-permute-start.2 = (f32[2,100,512]{2,1,0:T(8,128)S(1)}, f32[2,100,512]{2,1,0:T(8,128)S(1)}, u32[]{:S(2)}, u32[]{:S(2)}) collective-permute-start(f32[2,100,512]{2,1,0:T(8,128)S(1)} %get-tuple-element.49.outputs), channel_id=1, source_target_pairs={{0,1},{1,0},{2,3},{3,2},{4,5},{5,4},{6,7},{7,6},{8,9},{9,8},{10,11... | collective-permute-start | bytes 1228808 | tf_op jit(solution)/shard_map/ppermute | solution.py:26
  22.5 1.9 %collective-permute-start.3 = (bf16[256,1024]{1,0:T(8,128)(2,1)S(1)}, bf16[256,1024]{1,0:T(8,128)(2,1)S(1)}, u32[]{:S(2)}, u32[]{:S(2)}) collective-permute-start(bf16[256,1024]{1,0:T(8,128)(2,1)S(1)} %get-tuple-element.55), channel_id=1, source_target_pairs={{0,1},{1,0},{2,3},{3,2},{4,5},{5,4},{6,7},{7,6},{8,9},{9,8},{10,11... | collective-permute-start | bytes 1572872 | tf_op jit(solution)/shard_map/ppermute | solution.py:26
  26.6 3.3 %collective-permute-start.4 = (bf16[256,1280]{1,0:T(8,128)(2,1)S(1)}, bf16[256,1280]{1,0:T(8,128)(2,1)S(1)}, u32[]{:S(2)}, u32[]{:S(2)}) collective-permute-start(bf16[256,1280]{1,0:T(8,128)(2,1)S(1)} %get-tuple-element.59), channel_id=1, source_target_pairs={{0,1},{1,0},{2,3},{3,2},{4,5},{5,4},{6,7},{7,6},{8,9},{9,8},{10,11... | collective-permute-start | bytes 1966088 | tf_op jit(solution)/shard_map/ppermute | solution.py:26
  26.8 7.5 %collective-permute-start.6 = (bf16[128,1024]{1,0:T(8,128)(2,1)S(1)}, bf16[128,1024]{1,0:T(8,128)(2,1)S(1)}, u32[]{:S(2)}, u32[]{:S(2)}) collective-permute-start(bf16[128,1024]{1,0:T(8,128)(2,1)S(1)} %slice.95), channel_id=1, source_target_pairs={{0,2},{1,5},{2,0},{3,7},{4,6},{5,1},{6,4},{7,3},{8,10},{9,13},{10,... | collective-permute-start | bytes 786440 | tf_op jit(solution)/shard_map/ppermute | solution.py:35
  30.1 12.1 %collective-permute-start.5 = (bf16[128,1280]{1,0:T(8,128)(2,1)S(1)}, bf16[128,1280]{1,0:T(8,128)(2,1)S(1)}, u32[]{:S(2)}, u32[]{:S(2)}) collective-permute-start(bf16[128,1280]{1,0:T(8,128)(2,1)S(1)} %slice.97), channel_id=1, source_target_pairs={{0,2},{1,5},{2,0},{3,7},{4,6},{5,1},{6,4},{7,3},{8,10},{9,13},{10,... | collective-permute-start | bytes 983048 | tf_op jit(solution)/shard_map/ppermute | solution.py:35
  34.4 5.2 %collective-permute-start.13 = (bf16[64,1024]{1,0:T(8,128)(2,1)S(1)}, bf16[64,1024]{1,0:T(8,128)(2,1)S(1)}, u32[]{:S(2)}, u32[]{:S(2)}) collective-permute-start(bf16[64,1024]{1,0:T(8,128)(2,1)S(1)} %slice.111), channel_id=1, source_target_pairs={{0,4},{1,3},{2,6},{3,1},{4,0},{5,7},{6,2},{7,5},{8,12},{9,11},{10,... | collective-permute-start | bytes 393224 | tf_op jit(solution)/shard_map/ppermute | solution.py:35
  39.7 8.9 %collective-permute-start.14 = (bf16[64,1024]{1,0:T(8,128)(2,1)S(1)}, bf16[64,1024]{1,0:T(8,128)(2,1)S(1)}, u32[]{:S(2)}, u32[]{:S(2)}) collective-permute-start(bf16[64,1024]{1,0:T(8,128)(2,1)S(1)} %add_convert_fusion.7), channel_id=1, source_target_pairs={{0,8},{1,9},{2,10},{3,11},{4,12},{5,13},{6,14},{7,15},{8,0},{9,1},... | collective-permute-start | bytes 393224 | tf_op jit(solution)/shard_map/ppermute | solution.py:35
  42.3 7.6 %collective-permute-start.7 = (bf16[72,1280]{1,0:T(8,128)(2,1)S(1)}, bf16[72,1280]{1,0:T(8,128)(2,1)S(1)}, u32[]{:S(2)}, u32[]{:S(2)}) collective-permute-start(bf16[72,1280]{1,0:T(8,128)(2,1)S(1)} %pad_maximum_fusion.5), channel_id=1, source_target_pairs={{0,4},{1,3},{2,6},{3,1},{4,0},{5,7},{6,2},{7,5},{8,12},{9,11},{10,... | collective-permute-start | bytes 552968 | tf_op jit(solution)/shard_map/ppermute | solution.py:35
  48.6 5.9 %collective-permute-start.15 = (bf16[64,1024]{1,0:T(8,128)(2,1)S(1)}, bf16[64,1024]{1,0:T(8,128)(2,1)S(1)}, u32[]{:S(2)}, u32[]{:S(2)}) collective-permute-start(bf16[64,1024]{1,0:T(8,128)(2,1)S(1)} %add_convert_fusion.6), channel_id=1, source_target_pairs={{0,4},{1,3},{2,6},{3,1},{4,0},{5,7},{6,2},{7,5},{8,12},{9,11},{10,... | collective-permute-start | bytes 393224 | tf_op jit(solution)/shard_map/ppermute | solution.py:35
  50.0 9.7 %collective-permute-start.8 = (bf16[72,1280]{1,0:T(8,128)(2,1)S(1)}, bf16[72,1280]{1,0:T(8,128)(2,1)S(1)}, u32[]{:S(2)}, u32[]{:S(2)}) collective-permute-start(bf16[72,1280]{1,0:T(8,128)(2,1)S(1)} %pad_maximum_fusion.6), channel_id=1, source_target_pairs={{0,8},{1,9},{2,10},{3,11},{4,12},{5,13},{6,14},{7,15},{8,0},{9,1},... | collective-permute-start | bytes 552968 | tf_op jit(solution)/shard_map/ppermute | solution.py:35
  54.4 12.5 %collective-permute-start.16 = (bf16[128,1024]{1,0:T(8,128)(2,1)S(1)}, bf16[128,1024]{1,0:T(8,128)(2,1)S(1)}, u32[]{:S(2)}, u32[]{:S(2)}) collective-permute-start(bf16[128,1024]{1,0:T(8,128)(2,1)S(1)} %pad_maximum_fusion.4), channel_id=1, source_target_pairs={{0,2},{1,5},{2,0},{3,7},{4,6},{5,1},{6,4},{7,3},{8,10},{9,13},{10,... | collective-permute-start | bytes 786440 | tf_op jit(solution)/shard_map/ppermute | solution.py:35
  59.8 5.4 %collective-permute-start.9 = (bf16[64,1280]{1,0:T(8,128)(2,1)S(1)}, bf16[64,1280]{1,0:T(8,128)(2,1)S(1)}, u32[]{:S(2)}, u32[]{:S(2)}) collective-permute-start(bf16[64,1280]{1,0:T(8,128)(2,1)S(1)} %add_convert_fusion.4), channel_id=1, source_target_pairs={{0,4},{1,3},{2,6},{3,1},{4,0},{5,7},{6,2},{7,5},{8,12},{9,11},{10,... | collective-permute-start | bytes 491528 | tf_op jit(solution)/shard_map/ppermute | solution.py:35
  65.2 7.4 %collective-permute-start.10 = (bf16[136,1280]{1,0:T(8,128)(2,1)S(1)}, bf16[136,1280]{1,0:T(8,128)(2,1)S(1)}, u32[]{:S(2)}, u32[]{:S(2)}) collective-permute-start(bf16[136,1280]{1,0:T(8,128)(2,1)S(1)} %pad_maximum_fusion.2), channel_id=1, source_target_pairs={{0,2},{1,5},{2,0},{3,7},{4,6},{5,1},{6,4},{7,3},{8,10},{9,13},{10,... | collective-permute-start | bytes 1044488 | tf_op jit(solution)/shard_map/ppermute | solution.py:35
  67.0 9.3 %collective-permute-start.17 = (bf16[256,1024]{1,0:T(8,128)(2,1)S(1)}, bf16[256,1024]{1,0:T(8,128)(2,1)S(1)}, u32[]{:S(2)}, u32[]{:S(2)}) collective-permute-start(bf16[256,1024]{1,0:T(8,128)(2,1)S(1)} %pad_maximum_fusion.1.refs_1_), channel_id=1, source_target_pairs={{0,1},{1,0},{2,3},{3,2},{4,5},{5,4},{6,7},{7,6},{8,9},{9,8},{10,11... | collective-permute-start | bytes 1572872 | tf_op jit(solution)/shard_map/ppermute | solution.py:26
  67.1 6.3 %collective-permute-start.18 = (bf16[2,16,1024]{2,1,0:T(8,128)(2,1)S(1)}, bf16[2,16,1024]{2,1,0:T(8,128)(2,1)S(1)}, u32[]{:S(2)}, u32[]{:S(2)}) collective-permute-start(bf16[2,16,1024]{2,1,0:T(8,128)(2,1)S(1)} %get-tuple-element.79), channel_id=1, source_target_pairs={{0,2},{2,4},{4,6},{6,8},{8,10},{10,12},{12,14},{1,3},{3,5},{5,7},{... | collective-permute-start | bytes 196616 | tf_op jit(solution)/shard_map/ppermute | solution.py:22
  69.4 6.2 %collective-permute-start.19 = (bf16[2,16,1024]{2,1,0:T(8,128)(2,1)S(1)}, bf16[2,16,1024]{2,1,0:T(8,128)(2,1)S(1)}, u32[]{:S(2)}, u32[]{:S(2)}) collective-permute-start(bf16[2,16,1024]{2,1,0:T(8,128)(2,1)S(1)} %get-tuple-element.80), channel_id=1, source_target_pairs={{2,0},{4,2},{6,4},{8,6},{10,8},{12,10},{14,12},{3,1},{5,3},{7,5},{... | collective-permute-start | bytes 196616 | tf_op jit(solution)/shard_map/ppermute | solution.py:22
  72.7 6.0 %collective-permute-start.11 = (bf16[256,1280]{1,0:T(8,128)(2,1)S(1)}, bf16[256,1280]{1,0:T(8,128)(2,1)S(1)}, u32[]{:S(2)}, u32[]{:S(2)}) collective-permute-start(bf16[256,1280]{1,0:T(8,128)(2,1)S(1)} %pad_maximum_fusion.refs_3_.refs_1_), channel_id=1, source_target_pairs={{0,1},{1,0},{2,3},{3,2},{4,5},{5,4},{6,7},{7,6},{8,9},{9,8},{10,11... | collective-permute-start | bytes 1966088 | tf_op jit(solution)/shard_map/ppermute | solution.py:26
  72.8 5.9 %collective-permute-start.12 = (bf16[8,1280]{1,0:T(8,128)(2,1)S(1)}, bf16[8,1280]{1,0:T(8,128)(2,1)S(1)}, u32[]{:S(2)}, u32[]{:S(2)}) collective-permute-start(bf16[8,1280]{1,0:T(8,128)(2,1)S(1)} %pad_maximum_fusion.9.refs_3_), channel_id=1, source_target_pairs={{0,1},{1,0},{2,3},{3,2},{4,5},{5,4},{6,7},{7,6},{8,9},{9,8},{10,11... | collective-permute-start | bytes 61448 | tf_op jit(solution)/shard_map/ppermute | solution.py:26

commit v5 on v4

v5 whole, which is shorter than its diff:
```python
import jax
import jax.numpy as jnp
from jax import lax
from jax.experimental import pallas as pl
from jax.experimental.pallas import tpu as pltpu
from jax.sharding import PartitionSpec as P

RIM = 16
SMOOTH_SQ = 0.01
LANES = 128
BF16 = jnp.bfloat16
F32 = jnp.float32
VMEM = pl.BlockSpec(memory_space=pltpu.VMEM)
HBM = pl.BlockSpec(memory_space=pltpu.HBM)
PARAMS = pltpu.CompilerParams(vmem_limit_bytes=16 * 1024 * 1024)


def swap_pairs(value, axis, first):
    count = lax.axis_size(axis)
    pairs = [(i, i + 1) for i in range(first, count - 1, 2)]
    return lax.ppermute(value, axis, pairs + [(b, a) for a, b in pairs])


def swap_cores(value):
    return lax.ppermute(value, "member", [(0, 1), (1, 0)])


def swap_bits(value, bits):
    pairs = [
        (s * 2 + c, (s ^ (1 << bits[c])) * 2 + c)
        for s in range(lax.axis_size("space"))
        for c in range(2)
    ]
    return lax.ppermute(value, ("space", "member"), pairs)


def orders(count):
    return [(0, 1), (1, 0)] + [(bit, bit) for bit in range(2, count)]


def here_index():
    return lax.axis_index("space")


def core_index():
    return lax.axis_index("member")


def chunks(width, count):
    half, unit = width // 2, 16 << (count - 1)
    last = max(unit, half // 2)
    return [(0, half - last), (half - last, last)]


def turn(count, space, half):
    value = 0
    stages = orders(count)[:-1]
    for level, bits in enumerate(stages):
        value = value + ((1 - ((space >> bits[half]) & 1)) << (len(stages) - 1 - level))
    return value


def dot(a, b, dims=((1,), (0,))):
    return lax.dot_general(a, b, (dims, ((), ())), preferred_element_type=F32)


def fetch(sources, targets, sems):
    copies = [
        pltpu.make_async_copy(source, target, sems.at[i])
        for i, (source, target) in enumerate(zip(sources, targets))
    ]
    for copy in copies:
        copy.start()
    return copies


def prepare_kernel(
    index_in, mask_in, weight_in, valid_in, area_in, var_weight_in, projection_in, gain_in, own_in, state_in, target_in,
    hidden_weight_in, adj, adj_t, score_weight, projection, gain, own, base, hidden_weight,
    index, mask, weight, valid, area, var_weight, narrow, state, target, sems,
):
    sources = (
        index_in, mask_in, weight_in, valid_in, area_in, var_weight_in, projection_in, gain_in, own_in,
        state_in, target_in, hidden_weight_in,
    )
    targets = (index, mask, weight, valid, area, var_weight, narrow, gain, own, state, target, hidden_weight)
    copies = fetch(sources, targets, sems)
    for copy in copies[:6]:
        copy.wait()
    points = index.shape[1]
    variables = narrow.shape[0]
    nodes = jax.lax.broadcasted_iota(jnp.int32, (LANES, points), 0) + (here_index() * (own.shape[1]) - RIM)
    total = jnp.zeros((LANES, points), F32)
    for slot in range(index.shape[0]):
        coefficient = weight[slot : slot + 1, :] * mask[slot : slot + 1, :].astype(F32)
        total = total + jnp.where(index[slot : slot + 1, :] == nodes, coefficient, 0.0)
    upper = total.astype(BF16).astype(F32)
    lower = total - upper
    adj_t[:LANES, :] = upper.astype(BF16)
    adj_t[LANES:, :] = lower.astype(BF16)
    adj[:, :LANES] = upper.T.astype(BF16)
    adj[:, LANES:] = lower.T.astype(BF16)
    diagonal = jax.lax.broadcasted_iota(jnp.int32, (variables, variables), 0) == (
        jax.lax.broadcasted_iota(jnp.int32, (variables, variables), 1)
    )
    column = jnp.sum(jnp.where(diagonal, var_weight[...], 0.0), axis=1, keepdims=True)
    score_weight[...] = column * (valid[...].astype(F32) * area[...] / points)
    copies[6].wait()
    projection[...] = jnp.zeros_like(projection)
    projection[:variables, :] = narrow[...]
    for copy in copies[7:]:
        copy.wait()
    base[...] = state[...] - target[...]


def forward_kernel(
    adj, near, own, far, gain, hidden_weight, output_weight,
    normed, hidden, slope, outputs, deviation, extended, summed, projected,
):
    members, nodes, width = own.shape
    points = adj.shape[0]
    tile = 256
    odd = (here_index() & 1) == 1
    for member in range(members):
        for part in range(2):
            start = part * LANES
            extended[member, start : start + RIM, :] = jnp.where(odd, near[member], far[member])
            extended[member, start + RIM : start + RIM + nodes, :] = own[member]
            extended[member, start + RIM + nodes : start + 2 * RIM + nodes, :] = jnp.where(
                odd, far[member], near[member]
            )
            extended[member, start + 2 * RIM + nodes : start + LANES, :] = jnp.zeros(
                (LANES - 2 * RIM - nodes, width), BF16
            )

    def gather(member):
        summed[member] = dot(adj[...], extended[member])

    def norm(member, first, size):
        for row in range(first, first + size, 32):
            value = summed[member, row : row + 32, :]
            value = value - jnp.sum(value, axis=1, keepdims=True) * (1.0 / width)
            spread = jnp.sum(value * value, axis=1, keepdims=True) * (1.0 / width)
            inverse = lax.rsqrt(spread + 1e-05)
            target = slice(member * points + row, member * points + row + 32)
            deviation[target, :] = inverse
            normed[target, :] = (value * inverse * gain[...]).astype(BF16)

    def layer(member, column):
        rows = slice(member * points, (member + 1) * points)
        columns = slice(column, column + tile)
        pre = dot(normed[rows, :], hidden_weight[:, columns])
        sig = 0.5 * jnp.tanh(0.5 * pre) + 0.5
        hid = pre * sig
        slope[rows, columns] = (sig + hid * (1.0 - sig)).astype(BF16)
        hid = hid.astype(BF16)
        hidden[rows, columns] = hid
        term = dot(hid, output_weight[:, columns], ((1,), (1,)))
        if column == 0:
            projected[...] = term
        else:
            projected[...] += term

    gather(0)
    norm(0, 0, points)
    for member in range(members):
        if member + 1 < members:
            gather(member + 1)
        for column in range(0, width, tile):
            if member + 1 < members:
                size = points * tile // width
                norm(member + 1, points * column // width, size)
            layer(member, column)
        outputs[member] = projected[...].T[: outputs.shape[1], :]


def own_rows(count, width):
    half_rows = width // 2
    for half in range(2):
        mask = turn(count, here_index(), half)
        for first, rows in chunks(width, count):
            size = rows >> (count - 1)
            for block in range(rows // size):
                start = (1 - (core_index() ^ half)) * half_rows + first + (block ^ mask) * size
                yield half * half_rows + first + block * size, size, pl.multiple_of(start, size)


def narrow_rows(count, width):
    rows = chunks(width, count)[-1][1]
    size = rows >> (count - 1)
    sides = width // 2 // rows
    for half in range(2):
        mask = turn(count, here_index(), half)
        for block in range(rows // size):
            row = half * (width // 2) + block * sides * size
            starts = tuple(row + side * size for side in range(sides))
            yield starts, size, 1 - (core_index() ^ half), pl.multiple_of((block ^ mask) * size, size)


def transpose_kernel(count, normed, normed_t):
    width = normed.shape[1]
    blocks = {}
    for row, size, there in own_rows(count, width):
        stop = row + size
        while row < stop:
            group, offset = row // LANES, row % LANES
            if group not in blocks:
                blocks = {group: normed[:, group * LANES : (group + 1) * LANES].T}
            part = min(stop - row, LANES - offset)
            normed_t[pl.ds(pl.multiple_of(there, 16), part), :] = blocks[group][offset : offset + part]
            row, there = row + part, there + part


def score_kernel(
    outputs, others, base, score_weight, output_weight, slope, normed_t,
    loss, grad_pre, grad_pred_t, sent,
    grad_pred, grad_wide,
):
    members, variables, points = outputs.shape
    width = slope.shape[1]
    total = 2 * members
    weight = score_weight[...]
    grad_wide[...] = jnp.zeros_like(grad_wide)
    grad_pred[...] = jnp.zeros_like(grad_pred)
    values = [outputs[m] for m in range(members)]
    grads = [None] * members
    pair_grads = [jnp.zeros((variables, points), F32) for _ in range(members)]
    errors = jnp.zeros((variables, points), F32)
    pairs = jnp.full((variables, points), members * SMOOTH_SQ**0.5, F32)
    for m in range(members):
        diff = values[m] + base[...]
        square = diff * diff + SMOOTH_SQ
        inverse = lax.rsqrt(square)
        errors = errors + square * inverse
        grads[m] = diff * inverse
        for n in range(m + 1, members):
            diff = values[m] - values[n]
            square = diff * diff + SMOOTH_SQ
            inverse = lax.rsqrt(square)
            pairs = pairs + 2.0 * (square * inverse)
            pair_grads[m] = pair_grads[m] + diff * inverse
            pair_grads[n] = pair_grads[n] - diff * inverse
        for n in range(members):
            diff = values[m] - others[n]
            square = diff * diff + SMOOTH_SQ
            inverse = lax.rsqrt(square)
            pairs = pairs + square * inverse
            pair_grads[m] = pair_grads[m] + diff * inverse
    score = weight * (errors * (1.0 / total) - pairs * (1.0 / (2.0 * total * (total - 1))))
    loss[...] = jnp.sum(jnp.sum(score, axis=0, keepdims=True), axis=1, keepdims=True)
    for m in range(members):
        grad = weight * (grads[m] * (1.0 / total) - pair_grads[m] * (1.0 / (total * (total - 1))))
        columns = slice(m * points, (m + 1) * points)
        grad_wide[:variables, columns] = grad
        grad_pred[columns, :] = grad_wide[:, columns].T.astype(BF16)
    grad_pred_t[...] = grad_wide[...].astype(BF16)
    for m in range(members):
        rows = slice(m * points, (m + 1) * points)
        for column in range(0, width, 256):
            columns = slice(column, column + 256)
            grad_hid = dot(grad_pred[rows, :], output_weight[:, columns])
            grad_pre[rows, columns] = (grad_hid * slope[rows, columns].astype(F32)).astype(BF16)
    products(normed_t, grad_pre, slice(0, sent.shape[0]), sent)


def products(normed_t, grad_pre, rows, target):
    width = grad_pre.shape[1]
    for column in range(0, width, 256):
        columns = slice(column, column + 256)
        target[:, columns] = dot(normed_t[rows, :], grad_pre[:, columns]).astype(target.dtype)


def product_kernel(first, normed_t, grad_pre, *refs):
    target = refs[-1]
    products(normed_t, grad_pre, slice(first, first + target.shape[0]), target)
    if len(refs) > 1:
        target[:, grad_pre.shape[1] :] = refs[0][...]


def sent_kernel(count, normed_t, grad_pre, grad_pred_t, hidden, sent, kept_narrow):
    width = grad_pre.shape[1]
    first, rows = chunks(width, count)[-1]
    products(normed_t, grad_pre, slice(first, first + rows), sent)
    value = dot(grad_pred_t[...], hidden[...]).T
    for starts, size, own, place_row in narrow_rows(count, width):
        here = pl.ds(place_row, size)
        for side, row in enumerate(starts):
            part = value[row : row + size]
            lanes = slice(side * LANES, (side + 1) * LANES)

            @pl.when(own == 1)
            def _():
                kept_narrow[here, lanes] = part

            @pl.when(own == 0)
            def _():
                sent[here, width + lanes.start : width + lanes.stop] = part.astype(BF16)


def backward_kernel(member, grad_pre, hidden_weight, normed, gain, deviation, adj_t, *refs):
    before, (small, inner, near, far, product, rows_grad) = refs[:-6], refs[-6:]
    nodes, width = inner.shape
    points = adj_t.shape[1]
    inverse_gain = 1.0 / gain[...]
    for column in range(0, width, 256):
        columns = slice(column, column + 256)
        product[:, columns] = dot(
            grad_pre[member * points : (member + 1) * points, :], hidden_weight[columns, :], ((1,), (1,))
        )

    def step(index, total):
        here = pl.ds(pl.multiple_of(index * 32, 32), 32)
        there = pl.ds(pl.multiple_of(member * points + index * 32, 32), 32)
        value = product[here, :]
        zn = normed[there, :].astype(F32)
        both = value * zn
        scaled = value * gain[...]
        mean = jnp.sum(scaled, axis=1, keepdims=True) * (1.0 / width)
        slant = jnp.sum(both, axis=1, keepdims=True) * (1.0 / width)
        grad = deviation[there, :] * (scaled - mean - (zn * inverse_gain) * slant)
        rows_grad[here, :] = grad.astype(BF16)
        return total + jnp.sum(both.reshape(4, 8, width), axis=0)

    total = before[0][...] if before else jnp.zeros((8, width), F32)
    total = lax.fori_loop(0, points // 32, step, total, unroll=4)
    value = dot(adj_t[...], rows_grad[...])
    value = value[:LANES] + value[LANES:]
    below, above = value[:RIM], value[RIM + nodes : nodes + 2 * RIM]
    odd = (here_index() & 1) == 1
    near[...] = jnp.where(odd, below, above).astype(BF16)
    far[...] = jnp.where(odd, above, below).astype(BF16)
    inner[...] = value[RIM : RIM + nodes]
    if not before:
        small[...] = total
        return
    row = jnp.concatenate(
        [
            jnp.sum(total, axis=0, keepdims=True) * inverse_gain,
            jnp.broadcast_to(before[1][...], (1, small.shape[1] - width)),
        ],
        axis=1,
    )
    upper = row.astype(BF16).astype(F32)
    index = jax.lax.broadcasted_iota(jnp.int32, (8, row.shape[1]), 0)
    small[...] = jnp.where(index == 0, upper, jnp.where(index == 1, row - upper, 0.0)).astype(BF16)


def latent_kernel(*refs):
    grad_latent = refs[-1]
    members, nodes = grad_latent.shape[:2]
    inner, (near, far) = refs[:members], refs[members:-1]
    odd = (here_index() & 1) == 1
    for member in range(members):
        low = jnp.where(odd, near[member].astype(F32), far[member].astype(F32))
        high = jnp.where(odd, far[member].astype(F32), near[member].astype(F32))
        value = inner[member]
        grad_latent[member, :RIM, :] = value[:RIM, :] + low
        grad_latent[member, RIM : nodes - RIM, :] = value[RIM : nodes - RIM, :]
        grad_latent[member, nodes - RIM :, :] = value[nodes - RIM :, :] + high


def write_rows(count, chunk, side, source, target, wide, start, sems):
    width = target.shape[1]
    first, rows = chunks(width, count)[chunk]
    size = rows >> (count - 1)
    half = core_index() ^ side
    mask = jnp.where(half == 0, turn(count, here_index(), 0), turn(count, here_index(), 1))
    copies = []
    for block in range(rows // size):
        here = slice(block * size, (block + 1) * size)
        there = slice(start + block * size, start + (block + 1) * size)
        wide[there, :] = source[here, :width].astype(F32)
        row = half * (width // 2) + first + (block ^ mask) * size
        copy = pltpu.make_async_copy(
            wide.at[there, :],
            target.at[pl.ds(pl.multiple_of(row, size), size), :],
            sems.at[block],
        )
        copy.start()
        copies.append(copy)
    return copies


def write_kernel(count, parts, *refs):
    sources, (target, wide, sems) = refs[: len(parts)], refs[-3:]
    copies = []
    start = 0
    for i, ((chunk, side), source) in enumerate(zip(parts, sources)):
        copies += write_rows(count, chunk, side, source, target, wide, start, sems.at[i])
        start += source.shape[0]
    for copy in copies:
        copy.wait()


def last_write_kernel(
    count, own, other, small, other_small, before,
    target, grad_out_t, grad_gain, loss,
    wide, narrow, narrow_t, gain_row, loss_cell, sems, last_sems,
):
    del before
    width = target.shape[1]
    last = len(chunks(width, count)) - 1
    copies = write_rows(count, last, 1, other, target, wide, 0, sems)
    for starts, size, mine, place_row in narrow_rows(count, width):
        here = pl.ds(place_row, size)
        for side, row in enumerate(starts):
            lanes = slice(width + side * LANES, width + (side + 1) * LANES)
            value = jnp.where(mine == 1, own[here, lanes].astype(F32), other[here, lanes].astype(F32))
            narrow[row : row + size, :] = value
    narrow_t[...] = narrow[...].T[: grad_out_t.shape[0], :]
    total = small[...].astype(F32) + other_small[...].astype(F32)
    total = total[:1] + total[1:2]
    gain_row[...] = total[:, :width]
    loss_cell[...] = total[:, width : width + 1]
    copies += fetch((narrow_t, gain_row, loss_cell), (grad_out_t, grad_gain, loss), last_sems)
    for copy in copies:
        copy.wait()


def add_parts(mine, other):
    return (mine.astype(F32) + other.astype(F32)).astype(BF16)


def unpack(small):
    return small[:1].astype(F32) + small[1:2].astype(F32)


def swap_with(value, small, bits):
    rows = value.shape[0]
    other = swap_bits(jnp.concatenate([value, small]), bits)
    total = unpack(small) + unpack(other[rows:])
    upper = total.astype(BF16)
    lower = (total - upper.astype(F32)).astype(BF16)
    rest = jnp.zeros((small.shape[0] - 2, small.shape[1]), BF16)
    return other[:rows], jnp.concatenate([upper, lower, rest])


class Sum:
    def __init__(self, value, count):
        self.value, self.small = value, None
        forth = orders(count)
        self.stages = forth + forth[-2::-1]
        self.halvings, self.stage = count - 1, 0

    def start(self, *others):
        rows = self.value.shape[0] // 2 if self.stage < self.halvings else 0
        sent = self.value[:rows] if rows else self.value
        if others:
            sent = after(sent, *others)
        bits = self.stages[self.stage]
        last = self.stage == len(self.stages) - 1
        if self.small is not None and (0 < self.stage <= self.halvings or last):
            self.other, self.small = swap_with(sent, self.small, bits)
        else:
            self.other = swap_bits(sent, bits)
        return sent

    def finish(self, *others):
        other = after(self.other, *others) if others else self.other
        if self.stage < self.halvings:
            self.value = add_parts(self.value[other.shape[0] :], other)
        elif self.stage == self.halvings:
            self.value = add_parts(self.value, other)
        else:
            self.value = jnp.concatenate([other, self.value])
        self.stage += 1


def after(value, *others):
    return lax.optimization_barrier((value, *others))[0]


def in_hbm(*values):
    return [pltpu.with_memory_space_constraint(value, pltpu.HBM) for value in values]


def cost(flops, moved):
    return pl.CostEstimate(flops=flops, bytes_accessed=moved, transcendentals=0)


def local(
    latent,
    edge_node_index,
    edge_mask,
    edge_weight,
    valid,
    area,
    state,
    target,
    var_weight,
    gain,
    hidden_weight,
    output_weight,
):
    members, nodes, width = latent.shape
    points, variables = state.shape
    rows = members * points
    count = lax.axis_size("space").bit_length() - 1
    space = lax.axis_index("space")
    parts = chunks(width, count)
    odd = (space & 1) == 1
    low, high = latent[:, :RIM], latent[:, nodes - RIM :]
    near, far = jnp.where(odd, low, high), jnp.where(odd, high, low)
    far = swap_pairs(far, "space", 1)
    near = swap_pairs(after(near, far) if False else near, "space", 0)

    adj, adj_t, score_weight, projection, gain, own, base, hidden_weight = pl.pallas_call(
        prepare_kernel,
        out_shape=(
            pltpu.VMEM((points, 2 * LANES), BF16),
            pltpu.VMEM((2 * LANES, points), BF16),
            pltpu.VMEM((variables, points), F32),
            pltpu.VMEM((LANES, width), BF16),
            pltpu.VMEM((1, width), F32),
            pltpu.VMEM(latent.shape, BF16),
            pltpu.VMEM((variables, points), F32),
            pltpu.VMEM((width, width), BF16),
        ),
        in_specs=[HBM] * 12,
        out_specs=(VMEM,) * 8,
        scratch_shapes=[
            pltpu.VMEM(edge_mask.T.shape, jnp.int32),
            pltpu.VMEM(edge_mask.T.shape, jnp.int32),
            pltpu.VMEM(edge_mask.T.shape, F32),
            pltpu.VMEM((1, points), jnp.int32),
            pltpu.VMEM((1, points), F32),
            pltpu.VMEM((1, variables), F32),
            pltpu.VMEM((variables, width), BF16),
            pltpu.VMEM((variables, points), F32),
            pltpu.VMEM((variables, points), F32),
            pltpu.SemaphoreType.DMA((12,)),
        ],
        compiler_params=PARAMS,
        name="prepare",
    )(
            *in_hbm(
            edge_node_index.T,
            edge_mask.T,
            edge_weight.T,
            valid.reshape(1, points),
            area.reshape(1, points),
            var_weight.reshape(1, variables),
            output_weight.T,
            gain.reshape(1, width),
            latent,
            state.T,
            target.T,
            hidden_weight,
        ),
    )
    normed, hidden, slope, outputs, deviation = pl.pallas_call(
        forward_kernel,
        out_shape=(
            pltpu.VMEM((rows, width), BF16),
            pltpu.VMEM((rows, width), BF16),
            pltpu.VMEM((rows, width), BF16),
            jax.ShapeDtypeStruct((members, variables, points), F32),
            pltpu.VMEM((rows, 1), F32),
        ),
        in_specs=[VMEM] * 7,
        out_specs=(VMEM,) * 5,
        scratch_shapes=[
            pltpu.VMEM((members, 2 * LANES, width), BF16),
            pltpu.VMEM((members, points, width), F32),
            pltpu.VMEM((points, LANES), F32),
        ],
        compiler_params=PARAMS,
        name="forward",
    )(adj, near, own, far, gain, hidden_weight, projection)
    others = swap_cores(outputs)
    normed_t = pl.pallas_call(
        lambda *refs: transpose_kernel(count, *refs),
        out_shape=pltpu.VMEM((width, rows), BF16),
        in_specs=[VMEM],
        out_specs=VMEM,
        compiler_params=PARAMS,
        cost_estimate=cost(10**9, 4 * 10**6),
        name="transpose",
    )(normed)
    loss, grad_pre, grad_pred_t, sent = pl.pallas_call(
        score_kernel,
        out_shape=(
            jax.ShapeDtypeStruct((1, 1), F32),
            pltpu.VMEM((rows, width), BF16),
            pltpu.VMEM((LANES, rows), BF16),
            jax.ShapeDtypeStruct((parts[0][1], width), BF16),
        ),
        in_specs=[VMEM] * 7,
        out_specs=(VMEM,) * 4,
        scratch_shapes=[pltpu.VMEM((rows, LANES), BF16), pltpu.VMEM((LANES, rows), F32)],
        compiler_params=PARAMS,
        name="score",
    )(outputs, others, base, score_weight, projection, slope, normed_t)

    def product(first, size, dtype, *narrow):
        columns = width + sum(value.shape[1] for value in narrow)
        return pl.pallas_call(
            lambda *refs: product_kernel(first, *refs),
            out_shape=jax.ShapeDtypeStruct((size, columns), dtype),
            in_specs=[VMEM] * (2 + len(narrow)),
            out_specs=VMEM,
            compiler_params=PARAMS,
            cost_estimate=cost(10**9, 2 * 10**6),
            name="product",
        )(normed_t, grad_pre, *narrow)

    last = len(parts) - 1
    last_rows = parts[last][1]
    extra = LANES * (width // 2 // last_rows)
    received, sums, token = [swap_cores(sent)], [], ()
    for chunk, (first, size) in enumerate(parts):
        if chunk + 1 < last:
            sent = product(*parts[chunk + 1], BF16)
            received.append(swap_cores(sent))
        elif chunk + 1 == last:
            sent, kept_narrow = pl.pallas_call(
                lambda *refs: sent_kernel(count, *refs),
                out_shape=(
                    jax.ShapeDtypeStruct((last_rows, width + extra), BF16),
                    pltpu.VMEM((last_rows, extra), F32),
                ),
                in_specs=[VMEM] * 4,
                out_specs=(VMEM,) * 2,
                compiler_params=PARAMS,
                cost_estimate=cost(10**9, 4 * 10**6),
                name="sent",
            )(normed_t, grad_pre, after(grad_pred_t, *token), hidden)
            received.append(swap_cores(sent))
        kept = product(width // 2 + first, size, F32, *([kept_narrow] if chunk == last else []))
        sums.append(Sum(add_parts(kept, received[chunk]), count))
        token = (sums[-1].start(*token),)

    def backward(member, adj_t, *before):
        last = len(before) > 1
        return pl.pallas_call(
            lambda *refs: backward_kernel(member, *refs),
            out_shape=(
                jax.ShapeDtypeStruct((8, width + extra), BF16) if last else pltpu.VMEM((8, width), F32),
                pltpu.VMEM((nodes, width), F32),
                jax.ShapeDtypeStruct((RIM, width), BF16),
                jax.ShapeDtypeStruct((RIM, width), BF16),
            ),
            in_specs=[VMEM] * (6 + len(before)),
            out_specs=(VMEM,) * 4,
            scratch_shapes=[pltpu.VMEM((points, width), F32), pltpu.VMEM((points, width), BF16)],
            compiler_params=PARAMS,
            cost_estimate=cost(3 * 10**9, 4 * 10**6),
            name="backward",
        )(grad_pre, hidden_weight, normed, gain, deviation, adj_t, *before)

    done = []
    for stage in range(2 * count - 1):
        for chunk in range(last + 1):
            if stage == 0 and len(done) < members:
                before = (done[-1][0],) if done else ()
                if len(done) == members - 1:
                    before = before + (loss,)
                done.append(backward(len(done), after(adj_t, *token), *before))
                token = token + (done[-1][1],)
                if len(done) == members:
                    sums[last].small = done[-1][0]
            sums[chunk].finish(*token)
            token = ()
            if stage < 2 * count - 2:
                token = (sums[chunk].start(),)
            if stage == 3 and chunk == last:
                inner, near, far = zip(*(part[1:] for part in done))
                near, far = after(jnp.stack(near), *token), after(jnp.stack(far), *token)
                near, far = swap_pairs(near, "space", 0), swap_pairs(far, "space", 1)
    grad_latent = pl.pallas_call(
        latent_kernel,
        out_shape=jax.ShapeDtypeStruct((members, nodes, width), F32),
        in_specs=[VMEM] * (members + 2),
        out_specs=VMEM,
        compiler_params=PARAMS,
        cost_estimate=cost(10**6, 10**6),
        name="latent",
    )(*inner, near, far)

    own = [chunk.value for chunk in sums]
    other = [swap_cores(value) for value in own]
    small = sums[last].small
    other_small = swap_cores(small)
    hidden_shape = jax.ShapeDtypeStruct((width, width), F32)
    blocks = 1 << (count - 1)

    def write(pieces, sources, *before):
        height = sum(source.shape[0] for source in sources)
        return pl.pallas_call(
            lambda *refs: write_kernel(count, pieces, *refs),
            out_shape=hidden_shape,
            in_specs=[VMEM] * len(sources) + [HBM] * len(before),
            out_specs=HBM,
            scratch_shapes=[
                pltpu.VMEM((height, width), F32),
                pltpu.SemaphoreType.DMA((len(pieces), blocks)),
            ],
            input_output_aliases={len(sources): 0} if before else {},
            compiler_params=PARAMS,
            cost_estimate=cost(10**6, 6 * 10**6),
            name="write",
        )(*sources, *before)

    grad_hidden = ()
    for chunk in range(last - 1):
        grad_hidden = (write([(chunk, 0), (chunk, 1)], [own[chunk], other[chunk]], *grad_hidden),)
    grad_hidden = write(
        [(last - 1, 0), (last - 1, 1), (last, 0)], [own[last - 1], other[last - 1], own[last]], *grad_hidden
    )
    grad_hidden, grad_out, grad_gain, loss = pl.pallas_call(
        lambda *refs: last_write_kernel(count, *refs),
        out_shape=(
            hidden_shape,
            jax.ShapeDtypeStruct((variables, width), F32),
            jax.ShapeDtypeStruct((1, width), F32),
            jax.ShapeDtypeStruct((1, 1), F32),
        ),
        in_specs=[VMEM] * 4 + [HBM],
        out_specs=(HBM,) * 4,
        scratch_shapes=[
            pltpu.VMEM((last_rows, width), F32),
            pltpu.VMEM((width, LANES), F32),
            pltpu.VMEM((variables, width), F32),
            pltpu.VMEM((1, width), F32),
            pltpu.VMEM((1, 1), F32),
            pltpu.SemaphoreType.DMA((blocks,)),
            pltpu.SemaphoreType.DMA((3,)),
        ],
        input_output_aliases={4: 0},
        compiler_params=PARAMS,
        name="last_write",
    )(own[last], other[last], small, other_small, grad_hidden)
    return (loss.reshape(1), grad_hidden, grad_out.T, grad_gain.reshape(width), grad_latent)


def solution(mesh):
    in_specs = (
        P(("groups", "member"), "space", None),
        P(("groups", "space"), None),
        P(("groups", "space"), None),
        P(("groups", "space"), None),
        P(("groups", "space")),
        P(("groups", "space")),
        P(("groups", "space"), None),
        P(("groups", "space"), None),
        P(),
        P(),
        P(),
        P(),
    )
    out_specs = (
        P("groups"),
        P("groups", None),
        P("groups", None),
        P("groups"),
        P(("groups", "member"), "space", None),
    )
    return jax.shard_map(local, mesh=mesh, in_specs=in_specs, out_specs=out_specs, check_vma=False)
```

time: 80.9 us -> 74.7 us (0.923)
  waiting for transfers between devices: 25.3 us -> 17.4 us
  starting transfers between devices: 25.5 us -> 30 us
  Pallas kernels: 26.7 us -> 23.5 us
    ppermute x10, starting transfers between devices: 14.7 us -> 20.1 us  [swap_bits(): return lax.ppermute(value, ('space', 'member'), pairs)]
    ppermute x4, waiting for transfers between devices: 4.24 us -> 0.01 us  [swap_pairs(): return lax.ppermute(value, axis, pairs + [(b, a) for a, b in pairs])]
    ppermute x10, waiting for transfers between devices: 19.4 us -> 16.3 us  [swap_bits(): return lax.ppermute(value, ('space', 'member'), pairs)]
    ppermute x4, starting transfers between devices: 9.71 us -> 8.49 us  [swap_pairs(): return lax.ppermute(value, axis, pairs + [(b, a) for a, b in pairs])]
    select_n x0 -> x1, other arithmetic: none -> 0.89 us  [local(): near, far = (jnp.where(odd, low, high), jnp.where(odd, high, low))]
    slice x5 -> x4, local copies, waits for them, and re-layouts: 0.95 us -> 0.07 us  [start(): sent = self.value[:rows] if rows else self.value]
  transfers between devices with their start and end apart: 20 -> 20, of which waited for: 10 -> 6; matrix products, arithmetic and copies ran while one was open for 1% -> 1% of each run, Pallas kernels for 18% -> 20%
where the time goes in v5:
time: 74.7 us; the launch traced here: 74.1 us
  starting transfers between devices  30 us (40%)
  Pallas kernels  23.5 us (31%)
  waiting for transfers between devices  17.4 us (23%)
  other arithmetic  1.77 us (2%)
  between operations  1.17 us (2%)
    ppermute x10, starting transfers between devices, swap_bits(): return lax.ppermute(value, ('space', 'member'), pairs)  20.1 us
    ppermute x10, waiting for transfers between devices, swap_bits(): return lax.ppermute(value, ('space', 'member'), pairs)  16.3 us
    ppermute x4, starting transfers between devices, swap_pairs(): return lax.ppermute(value, axis, pairs + [(b, a) for a, b in pairs])  8.49 us
    pallas_call x2, Pallas kernels, backward(): pl.pallas_call(lambda *refs: backward_kernel(member, *refs), out_shape=(j...  6.44 us
    pallas_call x1, Pallas kernels, local(): pl.pallas_call(forward_kernel, out_shape=(pltpu.VMEM((rows, width), BF16)...  5.2 us
    pallas_call x1, Pallas kernels, local(): pl.pallas_call(score_kernel, out_shape=(jax.ShapeDtypeStruct((1, 1), F32)...  2.35 us
    pallas_call x1, Pallas kernels, local(): pl.pallas_call(prepare_kernel, out_shape=(pltpu.VMEM((points, 2 * LANES),...  2.2 us
    pallas_call x1, Pallas kernels, write(): pl.pallas_call(lambda *refs: write_kernel(count, pieces, *refs), out_shap...  1.77 us
  transfers between devices with their start and end apart: 20, of which 6 were waited for; matrix products, arithmetic and copies ran while one was open for 1% of the time, Pallas kernels for 20%

profile of v5, /device:TPU:0, one launch (start us, length us, event | category | flops | bytes accessed | tf_op | source)
XLA Modules:
  0.0 74.1 jit_solution(6188003518098689544)
XLA Ops:
  0.6 0.9 %broadcast_select_fusion = (bf16[2,16,1024]{2,1,0:T(8,128)(2,1)S(1)}, bf16[2,16,1024]{2,1,0:T(8,128)(2,1)S(1)}) fusion(pred[]{:T(512)S(6)} %eq.3, bf16[2,64,1024]{2,1,0:T(8,128)(2,1)} %own_in.1), kind=kLoop, calls=%fused_computation.16 | loop fusion | flops 65536 | bytes 262145 | tf_op jit(solution)/shard_map/jit(_where)/select_n | solution.py:503
  1.5 3.0 %collective-permute-start = (bf16[2,16,1024]{2,1,0:T(8,128)(2,1)S(1)}, bf16[2,16,1024]{2,1,0:T(8,128)(2,1)S(1)}, u32[]{:S(2)}, u32[]{:S(2)}) collective-permute-start(bf16[2,16,1024]{2,1,0:T(8,128)(2,1)S(1)} %get-tuple-element.102), channel_id=1, source_target_pairs={{0,2},{4,6},{8,10},{12,14},{2,0},{6,4},{10,8},{14,12},{1,3},{5,7},... | collective-permute-start | bytes 196616 | tf_op jit(solution)/shard_map/ppermute | solution.py:21
  4.6 0.7 collective-permute-start.1
  5.2 2.2 %prepare.1 = (bf16[512,256]{1,0:T(8,128)(2,1)S(1)}, bf16[256,512]{1,0:T(8,128)(2,1)S(1)}, f32[100,512]{1,0:T(8,128)S(1)}, bf16[128,1024]{1,0:T(8,128)(2,1)S(1)},...) custom-call(s32[4,512]{1,0:T(4,128)} %bitcast.24, ...), custom_call_target="tpu_custom_call" | custom-call | tf_op jit(solution)/shard_map/prepare/pallas_call | solution.py:507
  7.5 5.2 %forward.1 = (bf16[1024,1024]{1,0:T(8,128)(2,1)S(1)}, bf16[1024,1024]{1,0:T(8,128)(2,1)S(1)}, bf16[1024,1024]{1,0:T(8,128)(2,1)S(1)}, f32[2,100,512]{2,1,0:T(8,128)S(1)}, f32[1024,1]{1,0:T(8,128)S(1)}) custom-call(bf16[512,256]{1,0:T(8,128)(2,1)S(1)} %get-tuple-element.50.adj, bf16[2,16,1024]{2,1,0:T(8,128)(2,1)S(1)} %collective-permute-done.near, ...), custom_call_target="tpu_custom_call" | custom-call | tf_op jit(solution)/shard_map/forward/pallas_call | solution.py:551
  12.7 0.6 transpose.29.normed_t.refs_0_
  13.4 1.1 %collective-permute-done.2.others = f32[2,100,512]{2,1,0:T(8,128)S(1)} collective-permute-done((f32[2,100,512]{2,1,0:T(8,128)S(1)}, f32[2,100,512]{2,1,0:T(8,128)S(1)}, u32[]{:S(2)}, u32[]{:S(2)}) %collective-permute-start.2) | collective-permute-done | bytes 409632 | tf_op jit(solution)/shard_map/ppermute | solution.py:25
  14.5 2.4 %score.1 = (f32[1,1]{1,0:T(1,128)}, bf16[1024,1024]{1,0:T(8,128)(2,1)S(1)}, bf16[128,1024]{1,0:T(8,128)(2,1)S(1)}, bf16[256,1024]{1,0:T(8,128)(2,1)S(1)}) custom-call(f32[2,100,512]{2,1,0:T(8,128)S(1)} %get-tuple-element.56.outputs, f32[2,100,512]{2,1,0:T(8,128)S(1)} %collective-permute-done.2.others, f32[100,512]{1,0:T(8,128)S(1)} %get-tuple-element.57.base, ...), custom_call_target="tpu_custom_call" | custom-call | tf_op jit(solution)/shard_map/score/pallas_call | solution.py:580
  17.0 1.4 %sent.1 = (bf16[256,1280]{1,0:T(8,128)(2,1)S(1)}, f32[256,256]{1,0:T(8,128)S(1)}) custom-call(bf16[1024,1024]{1,0:T(8,128)(2,1)S(1)} %transpose.29.normed_t.refs_0_, bf16[1024,1024]{1,0:T(8,128)(2,1)S(1)} %get-tuple-element.60.refs_1_.refs_0_, bf16[128,1024]{1,0:T(8,128)(2,1)S(1)} %get-tuple-element.61.refs_2_, bf16[1024,1024]{1,0:T(8,128)(2,1)S(1)} %get-tuple-element.62.refs_3_), custom_call_target="tpu_custom_call" | custom-call | flops 1000000000 | bytes 4000000 | tf_op jit(solution)/shard_map/sent/pallas_call | solution.py:616
  18.8 0.7 product.3
  19.5 0.7 product.2
  20.5 4.3 %collective-permute-start.6 = (bf16[128,1024]{1,0:T(8,128)(2,1)S(1)}, bf16[128,1024]{1,0:T(8,128)(2,1)S(1)}, u32[]{:S(2)}, u32[]{:S(2)}) collective-permute-start(bf16[128,1024]{1,0:T(8,128)(2,1)S(1)} %slice.95), channel_id=1, source_target_pairs={{0,2},{1,5},{2,0},{3,7},{4,6},{5,1},{6,4},{7,3},{8,10},{9,13},{10,... | collective-permute-start | bytes 786440 | tf_op jit(solution)/shard_map/ppermute | solution.py:34
  25.1 2.9 %backward.2 = (f32[8,1024]{1,0:T(8,128)S(1)}, f32[64,1024]{1,0:T(8,128)S(1)}, bf16[16,1024]{1,0:T(8,128)(2,1)S(1)}, bf16[16,1024]{1,0:T(8,128)(2,1)S(1)}) custom-call(bf16[1024,1024]{1,0:T(8,128)(2,1)S(1)} %get-tuple-element.60.refs_1_.refs_0_, bf16[1024,1024]{1,0:T(8,128)(2,1)S(1)} %get-tuple-element.53.hidden_weight.refs_1_, ...), custom_call_target="tpu_custom_call" | custom-call | flops 3000000000 | bytes 4000000 | tf_op jit(solution)/shard_map/backward/pallas_call | solution.py:635
  28.0 1.2 %collective-permute-done.6 = bf16[128,1024]{1,0:T(8,128)(2,1)S(1)} collective-permute-done((bf16[128,1024]{1,0:T(8,128)(2,1)S(1)}, bf16[128,1024]{1,0:T(8,128)(2,1)S(1)}, u32[]{:S(2)}, u32[]{:S(2)}) %collective-permute-start.6) | collective-permute-done | bytes 262176 | tf_op jit(solution)/shard_map/ppermute | solution.py:34
  29.3 3.5 %collective-permute-start.8 = (bf16[64,1024]{1,0:T(8,128)(2,1)S(1)}, bf16[64,1024]{1,0:T(8,128)(2,1)S(1)}, u32[]{:S(2)}, u32[]{:S(2)}) collective-permute-start(bf16[64,1024]{1,0:T(8,128)(2,1)S(1)} %slice.97), channel_id=1, source_target_pairs={{0,4},{1,3},{2,6},{3,1},{4,0},{5,7},{6,2},{7,5},{8,12},{9,11},{10,... | collective-permute-start | bytes 393224 | tf_op jit(solution)/shard_map/ppermute | solution.py:34
  32.8 3.5 %backward.3 = (bf16[8,1280]{1,0:T(8,128)(2,1)S(1)}, f32[64,1024]{1,0:T(8,128)S(1)}, bf16[16,1024]{1,0:T(8,128)(2,1)S(1)}, bf16[16,1024]{1,0:T(8,128)(2,1)S(1)}) custom-call(bf16[1024,1024]{1,0:T(8,128)(2,1)S(1)} %get-tuple-element.60.refs_1_.refs_0_, bf16[1024,1024]{1,0:T(8,128)(2,1)S(1)} %get-tuple-element.53.hidden_weight.refs_1_, ...), custom_call_target="tpu_custom_call" | custom-call | flops 3000000000 | bytes 4000000 | tf_op jit(solution)/shard_map/backward/pallas_call | solution.py:635
  36.5 1.3 %collective-permute-start.7 = (bf16[72,1280]{1,0:T(8,128)(2,1)S(1)}, bf16[72,1280]{1,0:T(8,128)(2,1)S(1)}, u32[]{:S(2)}, u32[]{:S(2)}) collective-permute-start(bf16[72,1280]{1,0:T(8,128)(2,1)S(1)} %pad_maximum_fusion.4), channel_id=1, source_target_pairs={{0,4},{1,3},{2,6},{3,1},{4,0},{5,7},{6,2},{7,5},{8,12},{9,11},{10,... | collective-permute-start | bytes 552968 | tf_op jit(solution)/shard_map/ppermute | solution.py:34
  37.9 2.7 %collective-permute-start.10 = (bf16[64,1024]{1,0:T(8,128)(2,1)S(1)}, bf16[64,1024]{1,0:T(8,128)(2,1)S(1)}, u32[]{:S(2)}, u32[]{:S(2)}) collective-permute-start(bf16[64,1024]{1,0:T(8,128)(2,1)S(1)} %add_convert_fusion.7), channel_id=1, source_target_pairs={{0,8},{1,9},{2,10},{3,11},{4,12},{5,13},{6,14},{7,15},{8,0},{9,1},... | collective-permute-start | bytes 393224 | tf_op jit(solution)/shard_map/ppermute | solution.py:34
  40.5 4.2 %collective-permute-done.7 = bf16[72,1280]{1,0:T(8,128)(2,1)S(1)} collective-permute-done((bf16[72,1280]{1,0:T(8,128)(2,1)S(1)}, bf16[72,1280]{1,0:T(8,128)(2,1)S(1)}, u32[]{:S(2)}, u32[]{:S(2)}) %collective-permute-start.7) | collective-permute-done | bytes 184352 | tf_op jit(solution)/shard_map/ppermute | solution.py:34
  44.9 2.5 %collective-permute-start.9 = (bf16[72,1280]{1,0:T(8,128)(2,1)S(1)}, bf16[72,1280]{1,0:T(8,128)(2,1)S(1)}, u32[]{:S(2)}, u32[]{:S(2)}) collective-permute-start(bf16[72,1280]{1,0:T(8,128)(2,1)S(1)} %pad_maximum_fusion.5), channel_id=1, source_target_pairs={{0,8},{1,9},{2,10},{3,11},{4,12},{5,13},{6,14},{7,15},{8,0},{9,1},... | collective-permute-start | bytes 552968 | tf_op jit(solution)/shard_map/ppermute | solution.py:34
  47.4 2.4 %collective-permute-start.12 = (bf16[64,1024]{1,0:T(8,128)(2,1)S(1)}, bf16[64,1024]{1,0:T(8,128)(2,1)S(1)}, u32[]{:S(2)}, u32[]{:S(2)}) collective-permute-start(bf16[64,1024]{1,0:T(8,128)(2,1)S(1)} %add_convert_fusion.6), channel_id=1, source_target_pairs={{0,4},{1,3},{2,6},{3,1},{4,0},{5,7},{6,2},{7,5},{8,12},{9,11},{10,... | collective-permute-start | bytes 393224 | tf_op jit(solution)/shard_map/ppermute | solution.py:34
  49.8 4.7 %collective-permute-done.9 = bf16[72,1280]{1,0:T(8,128)(2,1)S(1)} collective-permute-done((bf16[72,1280]{1,0:T(8,128)(2,1)S(1)}, bf16[72,1280]{1,0:T(8,128)(2,1)S(1)}, u32[]{:S(2)}, u32[]{:S(2)}) %collective-permute-start.9) | collective-permute-done | bytes 184352 | tf_op jit(solution)/shard_map/ppermute | solution.py:34
  55.0 2.0 %collective-permute-start.16 = (bf16[128,1024]{1,0:T(8,128)(2,1)S(1)}, bf16[128,1024]{1,0:T(8,128)(2,1)S(1)}, u32[]{:S(2)}, u32[]{:S(2)}) collective-permute-start(bf16[128,1024]{1,0:T(8,128)(2,1)S(1)} %pad_maximum_fusion.3), channel_id=1, source_target_pairs={{0,2},{1,5},{2,0},{3,7},{4,6},{5,1},{6,4},{7,3},{8,10},{9,13},{10,... | collective-permute-start | bytes 786440 | tf_op jit(solution)/shard_map/ppermute | solution.py:34
  57.0 4.7 %collective-permute-done.11 = bf16[64,1280]{1,0:T(8,128)(2,1)S(1)} collective-permute-done((bf16[64,1280]{1,0:T(8,128)(2,1)S(1)}, bf16[64,1280]{1,0:T(8,128)(2,1)S(1)}, u32[]{:S(2)}, u32[]{:S(2)}) %collective-permute-start.11) | collective-permute-done | bytes 163872 | tf_op jit(solution)/shard_map/ppermute | solution.py:34
  61.9 0.9 %collective-permute-start.13 = (bf16[136,1280]{1,0:T(8,128)(2,1)S(1)}, bf16[136,1280]{1,0:T(8,128)(2,1)S(1)}, u32[]{:S(2)}, u32[]{:S(2)}) collective-permute-start(bf16[136,1280]{1,0:T(8,128)(2,1)S(1)} %concatenate.30), channel_id=1, source_target_pairs={{0,2},{1,5},{2,0},{3,7},{4,6},{5,1},{6,4},{7,3},{8,10},{9,13},{10,... | collective-permute-start | bytes 1044488 | tf_op jit(solution)/shard_map/ppermute | solution.py:34
  62.8 0.7 collective-permute-start.19
  63.5 4.2 %collective-permute-start.18 = (bf16[2,16,1024]{2,1,0:T(8,128)(2,1)S(1)}, bf16[2,16,1024]{2,1,0:T(8,128)(2,1)S(1)}, u32[]{:S(2)}, u32[]{:S(2)}) collective-permute-start(bf16[2,16,1024]{2,1,0:T(8,128)(2,1)S(1)} %pad_maximum_fusion.6), channel_id=1, source_target_pairs={{0,2},{4,6},{8,10},{12,14},{2,0},{6,4},{10,8},{14,12},{1,3},{5,7},... | collective-permute-start | bytes 196616 | tf_op jit(solution)/shard_map/ppermute | solution.py:21
  67.7 1.5 %collective-permute-done.13 = bf16[136,1280]{1,0:T(8,128)(2,1)S(1)} collective-permute-done((bf16[136,1280]{1,0:T(8,128)(2,1)S(1)}, bf16[136,1280]{1,0:T(8,128)(2,1)S(1)}, u32[]{:S(2)}, u32[]{:S(2)}) %collective-permute-start.13) | collective-permute-done | bytes 348192 | tf_op jit(solution)/shard_map/ppermute | solution.py:34
  69.5 0.6 collective-permute-start.15
  70.1 0.8 %latent.1 = f32[2,64,1024]{2,1,0:T(8,128)} custom-call(f32[64,1024]{1,0:T(8,128)S(1)} %get-tuple-element.70.refs_0_, f32[64,1024]{1,0:T(8,128)S(1)} %get-tuple-element.75.refs_1_, bf16[2,16,1024]{2,1,0:T(8,128)(2,1)S(1)} %collective-permute-done.18.refs_2_, bf16[2,16,1024]{2,1,0:T(8,128)(2,1)S(1)} %collective-permute-done.19.refs_3_), custom_call_target="tpu_custom_call" | custom-call | flops 1000000 | bytes 1000000 | tf_op jit(solution)/shard_map/latent/pallas_call | solution.py:670
  70.9 1.8 %write.1.refs_4_ = f32[1024,1024]{1,0:T(8,128)} custom-call(bf16[256,1024]{1,0:T(8,128)(2,1)S(1)} %pad_maximum_fusion.1.refs_0_, bf16[256,1024]{1,0:T(8,128)(2,1)S(1)} %collective-permute-done.17.refs_1_, bf16[256,1280]{1,0:T(8,128)(2,1)S(1)} %pad_maximum_fusion.refs_2_.refs_0_), custom_call_target="tpu_custom_call" | custom-call | flops 1000000 | bytes 6000000 | tf_op jit(solution)/shard_map/write/pallas_call | solution.py:689
  72.7 1.3 %last_write.1 = (f32[1024,1024]{1,0:T(8,128)}, f32[100,1024]{1,0:T(8,128)}, f32[1,1024]{1,0:T(1,128)}, f32[1,1]{1,0:T(1,128)}) custom-call(bf16[256,1280]{1,0:T(8,128)(2,1)S(1)} %pad_maximum_fusion.refs_2_.refs_0_, bf16[256,1280]{1,0:T(8,128)(2,1)S(1)} %collective-permute-done.14.refs_1_, ...), custom_call_target="tpu_custom_call", output_to_operand_aliasing={{0}: (4, {})} | custom-call | tf_op jit(solution)/shard_map/last_write/pallas_call | solution.py:710
  (52 shorter events, 2.4 us)
Async XLA Ops:
  1.5 5.9 %collective-permute-start = (bf16[2,16,1024]{2,1,0:T(8,128)(2,1)S(1)}, bf16[2,16,1024]{2,1,0:T(8,128)(2,1)S(1)}, u32[]{:S(2)}, u32[]{:S(2)}) collective-permute-start(bf16[2,16,1024]{2,1,0:T(8,128)(2,1)S(1)} %get-tuple-element.102), channel_id=1, source_target_pairs={{0,2},{4,6},{8,10},{12,14},{2,0},{6,4},{10,8},{14,12},{1,3},{5,7},... | collective-permute-start | bytes 196616 | tf_op jit(solution)/shard_map/ppermute | solution.py:21
  4.6 2.9 %collective-permute-start.1 = (bf16[2,16,1024]{2,1,0:T(8,128)(2,1)S(1)}, bf16[2,16,1024]{2,1,0:T(8,128)(2,1)S(1)}, u32[]{:S(2)}, u32[]{:S(2)}) collective-permute-start(bf16[2,16,1024]{2,1,0:T(8,128)(2,1)S(1)} %get-tuple-element.101), channel_id=1, source_target_pairs={{2,4},{6,8},{10,12},{4,2},{8,6},{12,10},{3,5},{7,9},{11,13},{5,3},... | collective-permute-start | bytes 196616 | tf_op jit(solution)/shard_map/ppermute | solution.py:21
  12.7 1.8 %collective-permute-start.2 = (f32[2,100,512]{2,1,0:T(8,128)S(1)}, f32[2,100,512]{2,1,0:T(8,128)S(1)}, u32[]{:S(2)}, u32[]{:S(2)}) collective-permute-start(f32[2,100,512]{2,1,0:T(8,128)S(1)} %get-tuple-element.56.outputs), channel_id=1, source_target_pairs={{0,1},{1,0},{2,3},{3,2},{4,5},{5,4},{6,7},{7,6},{8,9},{9,8},{10,11... | collective-permute-start | bytes 1228808 | tf_op jit(solution)/shard_map/ppermute | solution.py:25
  16.9 3.4 %collective-permute-start.4 = (bf16[256,1024]{1,0:T(8,128)(2,1)S(1)}, bf16[256,1024]{1,0:T(8,128)(2,1)S(1)}, u32[]{:S(2)}, u32[]{:S(2)}) collective-permute-start(bf16[256,1024]{1,0:T(8,128)(2,1)S(1)} %get-tuple-element.65), channel_id=1, source_target_pairs={{0,1},{1,0},{2,3},{3,2},{4,5},{5,4},{6,7},{7,6},{8,9},{9,8},{10,11... | collective-permute-start | bytes 1572872 | tf_op jit(solution)/shard_map/ppermute | solution.py:25
  18.4 6.4 %collective-permute-start.3 = (bf16[256,1280]{1,0:T(8,128)(2,1)S(1)}, bf16[256,1280]{1,0:T(8,128)(2,1)S(1)}, u32[]{:S(2)}, u32[]{:S(2)}) collective-permute-start(bf16[256,1280]{1,0:T(8,128)(2,1)S(1)} %get-tuple-element.64), channel_id=1, source_target_pairs={{0,1},{1,0},{2,3},{3,2},{4,5},{5,4},{6,7},{7,6},{8,9},{9,8},{10,11... | collective-permute-start | bytes 1966088 | tf_op jit(solution)/shard_map/ppermute | solution.py:25
  20.5 8.7 %collective-permute-start.6 = (bf16[128,1024]{1,0:T(8,128)(2,1)S(1)}, bf16[128,1024]{1,0:T(8,128)(2,1)S(1)}, u32[]{:S(2)}, u32[]{:S(2)}) collective-permute-start(bf16[128,1024]{1,0:T(8,128)(2,1)S(1)} %slice.95), channel_id=1, source_target_pairs={{0,2},{1,5},{2,0},{3,7},{4,6},{5,1},{6,4},{7,3},{8,10},{9,13},{10,... | collective-permute-start | bytes 786440 | tf_op jit(solution)/shard_map/ppermute | solution.py:34
  25.0 11.4 %collective-permute-start.5 = (bf16[128,1280]{1,0:T(8,128)(2,1)S(1)}, bf16[128,1280]{1,0:T(8,128)(2,1)S(1)}, u32[]{:S(2)}, u32[]{:S(2)}) collective-permute-start(bf16[128,1280]{1,0:T(8,128)(2,1)S(1)} %slice.94), channel_id=1, source_target_pairs={{0,2},{1,5},{2,0},{3,7},{4,6},{5,1},{6,4},{7,3},{8,10},{9,13},{10,... | collective-permute-start | bytes 983048 | tf_op jit(solution)/shard_map/ppermute | solution.py:34
  29.3 7.2 %collective-permute-start.8 = (bf16[64,1024]{1,0:T(8,128)(2,1)S(1)}, bf16[64,1024]{1,0:T(8,128)(2,1)S(1)}, u32[]{:S(2)}, u32[]{:S(2)}) collective-permute-start(bf16[64,1024]{1,0:T(8,128)(2,1)S(1)} %slice.97), channel_id=1, source_target_pairs={{0,4},{1,3},{2,6},{3,1},{4,0},{5,7},{6,2},{7,5},{8,12},{9,11},{10,... | collective-permute-start | bytes 393224 | tf_op jit(solution)/shard_map/ppermute | solution.py:34
  36.5 8.2 %collective-permute-start.7 = (bf16[72,1280]{1,0:T(8,128)(2,1)S(1)}, bf16[72,1280]{1,0:T(8,128)(2,1)S(1)}, u32[]{:S(2)}, u32[]{:S(2)}) collective-permute-start(bf16[72,1280]{1,0:T(8,128)(2,1)S(1)} %pad_maximum_fusion.4), channel_id=1, source_target_pairs={{0,4},{1,3},{2,6},{3,1},{4,0},{5,7},{6,2},{7,5},{8,12},{9,11},{10,... | collective-permute-start | bytes 552968 | tf_op jit(solution)/shard_map/ppermute | solution.py:34
  37.9 6.9 %collective-permute-start.10 = (bf16[64,1024]{1,0:T(8,128)(2,1)S(1)}, bf16[64,1024]{1,0:T(8,128)(2,1)S(1)}, u32[]{:S(2)}, u32[]{:S(2)}) collective-permute-start(bf16[64,1024]{1,0:T(8,128)(2,1)S(1)} %add_convert_fusion.7), channel_id=1, source_target_pairs={{0,8},{1,9},{2,10},{3,11},{4,12},{5,13},{6,14},{7,15},{8,0},{9,1},... | collective-permute-start | bytes 393224 | tf_op jit(solution)/shard_map/ppermute | solution.py:34
  44.9 9.6 %collective-permute-start.9 = (bf16[72,1280]{1,0:T(8,128)(2,1)S(1)}, bf16[72,1280]{1,0:T(8,128)(2,1)S(1)}, u32[]{:S(2)}, u32[]{:S(2)}) collective-permute-start(bf16[72,1280]{1,0:T(8,128)(2,1)S(1)} %pad_maximum_fusion.5), channel_id=1, source_target_pairs={{0,8},{1,9},{2,10},{3,11},{4,12},{5,13},{6,14},{7,15},{8,0},{9,1},... | collective-permute-start | bytes 552968 | tf_op jit(solution)/shard_map/ppermute | solution.py:34
  47.4 7.6 %collective-permute-start.12 = (bf16[64,1024]{1,0:T(8,128)(2,1)S(1)}, bf16[64,1024]{1,0:T(8,128)(2,1)S(1)}, u32[]{:S(2)}, u32[]{:S(2)}) collective-permute-start(bf16[64,1024]{1,0:T(8,128)(2,1)S(1)} %add_convert_fusion.6), channel_id=1, source_target_pairs={{0,4},{1,3},{2,6},{3,1},{4,0},{5,7},{6,2},{7,5},{8,12},{9,11},{10,... | collective-permute-start | bytes 393224 | tf_op jit(solution)/shard_map/ppermute | solution.py:34
  54.6 7.1 %collective-permute-start.11 = (bf16[64,1280]{1,0:T(8,128)(2,1)S(1)}, bf16[64,1280]{1,0:T(8,128)(2,1)S(1)}, u32[]{:S(2)}, u32[]{:S(2)}) collective-permute-start(bf16[64,1280]{1,0:T(8,128)(2,1)S(1)} %add_convert_fusion.4), channel_id=1, source_target_pairs={{0,4},{1,3},{2,6},{3,1},{4,0},{5,7},{6,2},{7,5},{8,12},{9,11},{10,... | collective-permute-start | bytes 491528 | tf_op jit(solution)/shard_map/ppermute | solution.py:34
  55.0 12.6 %collective-permute-start.16 = (bf16[128,1024]{1,0:T(8,128)(2,1)S(1)}, bf16[128,1024]{1,0:T(8,128)(2,1)S(1)}, u32[]{:S(2)}, u32[]{:S(2)}) collective-permute-start(bf16[128,1024]{1,0:T(8,128)(2,1)S(1)} %pad_maximum_fusion.3), channel_id=1, source_target_pairs={{0,2},{1,5},{2,0},{3,7},{4,6},{5,1},{6,4},{7,3},{8,10},{9,13},{10,... | collective-permute-start | bytes 786440 | tf_op jit(solution)/shard_map/ppermute | solution.py:34
  61.9 7.4 %collective-permute-start.13 = (bf16[136,1280]{1,0:T(8,128)(2,1)S(1)}, bf16[136,1280]{1,0:T(8,128)(2,1)S(1)}, u32[]{:S(2)}, u32[]{:S(2)}) collective-permute-start(bf16[136,1280]{1,0:T(8,128)(2,1)S(1)} %concatenate.30), channel_id=1, source_target_pairs={{0,2},{1,5},{2,0},{3,7},{4,6},{5,1},{6,4},{7,3},{8,10},{9,13},{10,... | collective-permute-start | bytes 1044488 | tf_op jit(solution)/shard_map/ppermute | solution.py:34
  62.8 7.3 %collective-permute-start.19 = (bf16[2,16,1024]{2,1,0:T(8,128)(2,1)S(1)}, bf16[2,16,1024]{2,1,0:T(8,128)(2,1)S(1)}, u32[]{:S(2)}, u32[]{:S(2)}) collective-permute-start(bf16[2,16,1024]{2,1,0:T(8,128)(2,1)S(1)} %pad_maximum_fusion.7), channel_id=1, source_target_pairs={{2,4},{6,8},{10,12},{4,2},{8,6},{12,10},{3,5},{7,9},{11,13},{5,3},... | collective-permute-start | bytes 196616 | tf_op jit(solution)/shard_map/ppermute | solution.py:21
  63.5 6.6 %collective-permute-start.18 = (bf16[2,16,1024]{2,1,0:T(8,128)(2,1)S(1)}, bf16[2,16,1024]{2,1,0:T(8,128)(2,1)S(1)}, u32[]{:S(2)}, u32[]{:S(2)}) collective-permute-start(bf16[2,16,1024]{2,1,0:T(8,128)(2,1)S(1)} %pad_maximum_fusion.6), channel_id=1, source_target_pairs={{0,2},{4,6},{8,10},{12,14},{2,0},{6,4},{10,8},{14,12},{1,3},{5,7},... | collective-permute-start | bytes 196616 | tf_op jit(solution)/shard_map/ppermute | solution.py:21
  67.7 3.2 %collective-permute-start.17 = (bf16[256,1024]{1,0:T(8,128)(2,1)S(1)}, bf16[256,1024]{1,0:T(8,128)(2,1)S(1)}, u32[]{:S(2)}, u32[]{:S(2)}) collective-permute-start(bf16[256,1024]{1,0:T(8,128)(2,1)S(1)} %pad_maximum_fusion.1.refs_0_), channel_id=1, source_target_pairs={{0,1},{1,0},{2,3},{3,2},{4,5},{5,4},{6,7},{7,6},{8,9},{9,8},{10,11... | collective-permute-start | bytes 1572872 | tf_op jit(solution)/shard_map/ppermute | solution.py:25
  69.3 3.3 %collective-permute-start.14 = (bf16[256,1280]{1,0:T(8,128)(2,1)S(1)}, bf16[256,1280]{1,0:T(8,128)(2,1)S(1)}, u32[]{:S(2)}, u32[]{:S(2)}) collective-permute-start(bf16[256,1280]{1,0:T(8,128)(2,1)S(1)} %pad_maximum_fusion.refs_2_.refs_0_), channel_id=1, source_target_pairs={{0,1},{1,0},{2,3},{3,2},{4,5},{5,4},{6,7},{7,6},{8,9},{9,8},{10,11... | collective-permute-start | bytes 1966088 | tf_op jit(solution)/shard_map/ppermute | solution.py:25
  69.5 3.2 %collective-permute-start.15 = (bf16[8,1280]{1,0:T(8,128)(2,1)S(1)}, bf16[8,1280]{1,0:T(8,128)(2,1)S(1)}, u32[]{:S(2)}, u32[]{:S(2)}) collective-permute-start(bf16[8,1280]{1,0:T(8,128)(2,1)S(1)} %pad_maximum_fusion.8.refs_2_), channel_id=1, source_target_pairs={{0,1},{1,0},{2,3},{3,2},{4,5},{5,4},{6,7},{7,6},{8,9},{9,8},{10,11... | collective-permute-start | bytes 61448 | tf_op jit(solution)/shard_map/ppermute | solution.py:25

commit v6 on v5

--- a/solution.py
+++ b/solution.py
@@ -36,6 +36,9 @@
 
 def orders(count):
     return [(0, 1), (1, 0)] + [(bit, bit) for bit in range(2, count)]
+
+
+LIGHT = pl.CostEstimate(flops=1, bytes_accessed=1, transcendentals=0)
 
 
 def here_index():
@@ -197,8 +200,31 @@
             yield starts, size, 1 - (core_index() ^ half), pl.multiple_of((block ^ mask) * size, size)
 
 
-def transpose_kernel(count, normed, normed_t):
+def smooth(diff):
+    square = diff * diff + SMOOTH_SQ
+    inverse = lax.rsqrt(square)
+    return square * inverse, diff * inverse
+
+
+def transpose_kernel(count, normed, outputs, base, normed_t, own_score, own_grad):
     width = normed.shape[1]
+    members, variables, points = outputs.shape
+    total = 2 * members
+    values = [outputs[m] for m in range(members)]
+    zero = jnp.zeros((variables, points), F32)
+    grads, pair_grads = [zero] * members, [zero] * members
+    errors, pairs = zero, jnp.full((variables, points), members * SMOOTH_SQ**0.5, F32)
+    for m in range(members):
+        size, grads[m] = smooth(values[m] + base[...])
+        errors = errors + size
+        for n in range(m + 1, members):
+            size, grad = smooth(values[m] - values[n])
+            pairs = pairs + 2.0 * size
+            pair_grads[m] = pair_grads[m] + grad
+            pair_grads[n] = pair_grads[n] - grad
+    own_score[...] = errors * (1.0 / total) - pairs * (1.0 / (2.0 * total * (total - 1)))
+    for m in range(members):
+        own_grad[m] = grads[m] * (1.0 / total) - pair_grads[m] * (1.0 / (total * (total - 1)))
     blocks = {}
     for row, size, there in own_rows(count, width):
         stop = row + size
@@ -212,7 +238,7 @@
 
 
 def score_kernel(
-    outputs, others, base, score_weight, output_weight, slope, normed_t,
+    outputs, others, own_score, own_grad, score_weight, output_weight, slope, normed_t,
     loss, grad_pre, grad_pred_t, sent,
     grad_pred, grad_wide,
 ):
@@ -223,33 +249,17 @@
     grad_wide[...] = jnp.zeros_like(grad_wide)
     grad_pred[...] = jnp.zeros_like(grad_pred)
     values = [outputs[m] for m in range(members)]
-    grads = [None] * members
     pair_grads = [jnp.zeros((variables, points), F32) for _ in range(members)]
-    errors = jnp.zeros((variables, points), F32)
-    pairs = jnp.full((variables, points), members * SMOOTH_SQ**0.5, F32)
+    pairs = jnp.zeros((variables, points), F32)
     for m in range(members):
-        diff = values[m] + base[...]
-        square = diff * diff + SMOOTH_SQ
-        inverse = lax.rsqrt(square)
-        errors = errors + square * inverse
-        grads[m] = diff * inverse
-        for n in range(m + 1, members):
-            diff = values[m] - values[n]
-            square = diff * diff + SMOOTH_SQ
-            inverse = lax.rsqrt(square)
-            pairs = pairs + 2.0 * (square * inverse)
-            pair_grads[m] = pair_grads[m] + diff * inverse
-            pair_grads[n] = pair_grads[n] - diff * inverse
         for n in range(members):
-            diff = values[m] - others[n]
-            square = diff * diff + SMOOTH_SQ
-            inverse = lax.rsqrt(square)
-            pairs = pairs + square * inverse
-            pair_grads[m] = pair_grads[m] + diff * inverse
-    score = weight * (errors * (1.0 / total) - pairs * (1.0 / (2.0 * total * (total - 1))))
+            size, grad = smooth(values[m] - others[n])
+            pairs = pairs + size
+            pair_grads[m] = pair_grads[m] + grad
+    score = weight * (own_score[...] - pairs * (1.0 / (2.0 * total * (total - 1))))
     loss[...] = jnp.sum(jnp.sum(score, axis=0, keepdims=True), axis=1, keepdims=True)
     for m in range(members):
-        grad = weight * (grads[m] * (1.0 / total) - pair_grads[m] * (1.0 / (total * (total - 1))))
+        grad = weight * (own_grad[m] - pair_grads[m] * (1.0 / (total * (total - 1))))
         columns = slice(m * points, (m + 1) * points)
         grad_wide[:variables, columns] = grad
         grad_pred[columns, :] = grad_wide[:, columns].T.astype(BF16)
@@ -270,11 +280,19 @@
         target[:, columns] = dot(normed_t[rows, :], grad_pre[:, columns]).astype(target.dtype)
 
 
-def product_kernel(first, normed_t, grad_pre, *refs):
-    target = refs[-1]
-    products(normed_t, grad_pre, slice(first, first + target.shape[0]), target)
-    if len(refs) > 1:
-        target[:, grad_pre.shape[1] :] = refs[0][...]
+def product_kernel(first, normed_t, grad_pre, received, *refs):
+    narrow, (sent, kept) = refs[:-2], refs[-2:]
+    width, rows = grad_pre.shape[1], sent.shape[0]
+    for column in range(0, width, 256):
+        columns = slice(column, column + 256)
+        value = dot(normed_t[first : first + 2 * rows, :], grad_pre[:, columns])
+        value = (value + received[:, columns].astype(F32)).astype(BF16)
+        sent[:, columns] = value[:rows]
+        kept[:, columns] = value[rows:]
+    if narrow:
+        value = (narrow[0][...] + received[:, width:].astype(F32)).astype(BF16)
+        sent[:, width:] = value[:rows]
+        kept[:, width:] = value[rows:]
 
 
 def sent_kernel(count, normed_t, grad_pre, grad_pred_t, hidden, sent, kept_narrow):
@@ -345,10 +363,8 @@
     small[...] = jnp.where(index == 0, upper, jnp.where(index == 1, row - upper, 0.0)).astype(BF16)
 
 
-def latent_kernel(*refs):
-    grad_latent = refs[-1]
+def add_rims(inner, near, far, grad_latent):
     members, nodes = grad_latent.shape[:2]
-    inner, (near, far) = refs[:members], refs[members:-1]
     odd = (here_index() & 1) == 1
     for member in range(members):
         low = jnp.where(odd, near[member].astype(F32), far[member].astype(F32))
@@ -381,11 +397,13 @@
     return copies
 
 
-def write_kernel(count, parts, *refs):
-    sources, (target, wide, sems) = refs[: len(parts)], refs[-3:]
-    copies = []
+def write_kernel(count, pieces, members, *refs):
+    sources, inner, (near, far) = refs[: len(pieces)], refs[len(pieces) :][:members], refs[len(pieces) + members :][:2]
+    target, target_latent, wide, grad_latent, sems, last_sems = refs[len(pieces) + members + 2 :]
+    add_rims(inner, near, far, grad_latent)
+    copies = fetch((grad_latent,), (target_latent,), last_sems)
     start = 0
-    for i, ((chunk, side), source) in enumerate(zip(parts, sources)):
+    for i, ((chunk, side), source) in enumerate(zip(pieces, sources)):
         copies += write_rows(count, chunk, side, source, target, wide, start, sems.at[i])
         start += source.shape[0]
     for copy in copies:
@@ -436,15 +454,17 @@
 
 
 class Sum:
-    def __init__(self, value, count):
-        self.value, self.small = value, None
+    def __init__(self, sent, kept, count):
+        self.sent, self.value, self.small = sent, kept, None
         forth = orders(count)
         self.stages = forth + forth[-2::-1]
         self.halvings, self.stage = count - 1, 0
 
     def start(self, *others):
-        rows = self.value.shape[0] // 2 if self.stage < self.halvings else 0
+        rows = self.value.shape[0] // 2 if 0 < self.stage < self.halvings else 0
         sent = self.value[:rows] if rows else self.value
+        if self.stage == 0:
+            sent = self.sent
         if others:
             sent = after(sent, *others)
         bits = self.stages[self.stage]
@@ -457,10 +477,8 @@
 
     def finish(self, *others):
         other = after(self.other, *others) if others else self.other
-        if self.stage < self.halvings:
-            self.value = add_parts(self.value[other.shape[0] :], other)
-        elif self.stage == self.halvings:
-            self.value = add_parts(self.value, other)
+        if self.stage <= self.halvings:
+            self.value = add_parts(self.value[-other.shape[0] :], other)
         else:
             self.value = jnp.concatenate([other, self.value])
         self.stage += 1
@@ -472,10 +490,6 @@
 
 def in_hbm(*values):
     return [pltpu.with_memory_space_constraint(value, pltpu.HBM) for value in values]
-
-
-def cost(flops, moved):
-    return pl.CostEstimate(flops=flops, bytes_accessed=moved, transcendentals=0)
 
 
 def local(
@@ -500,9 +514,8 @@
     parts = chunks(width, count)
     odd = (space & 1) == 1
     low, high = latent[:, :RIM], latent[:, nodes - RIM :]
-    near, far = jnp.where(odd, low, high), jnp.where(odd, high, low)
-    far = swap_pairs(far, "space", 1)
-    near = swap_pairs(after(near, far) if False else near, "space", 0)
+    near = swap_pairs(jnp.where(odd, low, high), "space", 0)
+    far = swap_pairs(jnp.where(odd, high, low), "space", 1)
 
     adj, adj_t, score_weight, projection, gain, own, base, hidden_weight = pl.pallas_call(
         prepare_kernel,
@@ -568,15 +581,19 @@
         name="forward",
     )(adj, near, own, far, gain, hidden_weight, projection)
     others = swap_cores(outputs)
-    normed_t = pl.pallas_call(
+    normed_t, own_score, own_grad = pl.pallas_call(
         lambda *refs: transpose_kernel(count, *refs),
-        out_shape=pltpu.VMEM((width, rows), BF16),
-        in_specs=[VMEM],
-        out_specs=VMEM,
+        out_shape=(
+            pltpu.VMEM((width, rows), BF16),
+            pltpu.VMEM((variables, points), F32),
+            pltpu.VMEM((members, variables, points), F32),
+        ),
+        in_specs=[VMEM] * 3,
+        out_specs=(VMEM,) * 3,
         compiler_params=PARAMS,
-        cost_estimate=cost(10**9, 4 * 10**6),
+        cost_estimate=LIGHT,
         name="transpose",
-    )(normed)
+    )(normed, outputs, base)
     loss, grad_pre, grad_pred_t, sent = pl.pallas_call(
         score_kernel,
         out_shape=(
@@ -585,50 +602,47 @@
             pltpu.VMEM((LANES, rows), BF16),
             jax.ShapeDtypeStruct((parts[0][1], width), BF16),
         ),
-        in_specs=[VMEM] * 7,
+        in_specs=[VMEM] * 8,
         out_specs=(VMEM,) * 4,
         scratch_shapes=[pltpu.VMEM((rows, LANES), BF16), pltpu.VMEM((LANES, rows), F32)],
         compiler_params=PARAMS,
         name="score",
-    )(outputs, others, base, score_weight, projection, slope, normed_t)
-
-    def product(first, size, dtype, *narrow):
-        columns = width + sum(value.shape[1] for value in narrow)
+    )(outputs, others, own_score, own_grad, score_weight, projection, slope, normed_t)
+
+    def product(first, size, received, *narrow):
+        shape = jax.ShapeDtypeStruct((size // 2, received.shape[1]), BF16)
         return pl.pallas_call(
             lambda *refs: product_kernel(first, *refs),
-            out_shape=jax.ShapeDtypeStruct((size, columns), dtype),
-            in_specs=[VMEM] * (2 + len(narrow)),
-            out_specs=VMEM,
+            out_shape=(shape, shape),
+            in_specs=[VMEM] * (3 + len(narrow)),
+            out_specs=(VMEM, VMEM),
             compiler_params=PARAMS,
-            cost_estimate=cost(10**9, 2 * 10**6),
+            cost_estimate=LIGHT,
             name="product",
-        )(normed_t, grad_pre, *narrow)
+        )(normed_t, grad_pre, received, *narrow)
 
     last = len(parts) - 1
     last_rows = parts[last][1]
     extra = LANES * (width // 2 // last_rows)
-    received, sums, token = [swap_cores(sent)], [], ()
+    received = swap_cores(sent)
+    sent, kept_narrow = pl.pallas_call(
+        lambda *refs: sent_kernel(count, *refs),
+        out_shape=(
+            jax.ShapeDtypeStruct((last_rows, width + extra), BF16),
+            pltpu.VMEM((last_rows, extra), F32),
+        ),
+        in_specs=[VMEM] * 4,
+        out_specs=(VMEM,) * 2,
+        compiler_params=PARAMS,
+        cost_estimate=LIGHT,
+        name="sent",
+    )(normed_t, grad_pre, grad_pred_t, hidden)
+    sums, token = [], ()
+    received = (received, swap_cores(sent))
     for chunk, (first, size) in enumerate(parts):
-        if chunk + 1 < last:
-            sent = product(*parts[chunk + 1], BF16)
-            received.append(swap_cores(sent))
-        elif chunk + 1 == last:
-            sent, kept_narrow = pl.pallas_call(
-                lambda *refs: sent_kernel(count, *refs),
-                out_shape=(
-                    jax.ShapeDtypeStruct((last_rows, width + extra), BF16),
-                    pltpu.VMEM((last_rows, extra), F32),
-                ),
-                in_specs=[VMEM] * 4,
-                out_specs=(VMEM,) * 2,
-                compiler_params=PARAMS,
-                cost_estimate=cost(10**9, 4 * 10**6),
-                name="sent",
-            )(normed_t, grad_pre, after(grad_pred_t, *token), hidden)
-            received.append(swap_cores(sent))
-        kept = product(width // 2 + first, size, F32, *([kept_narrow] if chunk == last else []))
-        sums.append(Sum(add_parts(kept, received[chunk]), count))
-        token = (sums[-1].start(*token),)
+        narrow = [kept_narrow] if chunk == last else []
+        sums.append(Sum(*product(width // 2 + first, size, after(received[chunk], *token), *narrow), count))
+        token = (sums[-1].start(),)
 
     def backward(member, adj_t, *before):
         last = len(before) > 1
@@ -644,7 +658,7 @@
             out_specs=(VMEM,) * 4,
             scratch_shapes=[pltpu.VMEM((points, width), F32), pltpu.VMEM((points, width), BF16)],
             compiler_params=PARAMS,
-            cost_estimate=cost(3 * 10**9, 4 * 10**6),
+            cost_estimate=LIGHT,
             name="backward",
         )(grad_pre, hidden_weight, normed, gain, deviation, adj_t, *before)
 
@@ -659,7 +673,7 @@
                 token = token + (done[-1][1],)
                 if len(done) == members:
                     sums[last].small = done[-1][0]
-            sums[chunk].finish(*token)
+            sums[chunk].finish(*(token if stage == 0 else ()))
             token = ()
             if stage < 2 * count - 2:
                 token = (sums[chunk].start(),)
@@ -667,16 +681,6 @@
                 inner, near, far = zip(*(part[1:] for part in done))
                 near, far = after(jnp.stack(near), *token), after(jnp.stack(far), *token)
                 near, far = swap_pairs(near, "space", 0), swap_pairs(far, "space", 1)
-    grad_latent = pl.pallas_call(
-        latent_kernel,
-        out_shape=jax.ShapeDtypeStruct((members, nodes, width), F32),
-        in_specs=[VMEM] * (members + 2),
-        out_specs=VMEM,
-        compiler_params=PARAMS,
-        cost_estimate=cost(10**6, 10**6),
-        name="latent",
-    )(*inner, near, far)
-
     own = [chunk.value for chunk in sums]
     other = [swap_cores(value) for value in own]
     small = sums[last].small
@@ -684,29 +688,24 @@
     hidden_shape = jax.ShapeDtypeStruct((width, width), F32)
     blocks = 1 << (count - 1)
 
-    def write(pieces, sources, *before):
-        height = sum(source.shape[0] for source in sources)
-        return pl.pallas_call(
-            lambda *refs: write_kernel(count, pieces, *refs),
-            out_shape=hidden_shape,
-            in_specs=[VMEM] * len(sources) + [HBM] * len(before),
-            out_specs=HBM,
-            scratch_shapes=[
-                pltpu.VMEM((height, width), F32),
-                pltpu.SemaphoreType.DMA((len(pieces), blocks)),
-            ],
-            input_output_aliases={len(sources): 0} if before else {},
-            compiler_params=PARAMS,
-            cost_estimate=cost(10**6, 6 * 10**6),
-            name="write",
-        )(*sources, *before)
-
-    grad_hidden = ()
-    for chunk in range(last - 1):
-        grad_hidden = (write([(chunk, 0), (chunk, 1)], [own[chunk], other[chunk]], *grad_hidden),)
-    grad_hidden = write(
-        [(last - 1, 0), (last - 1, 1), (last, 0)], [own[last - 1], other[last - 1], own[last]], *grad_hidden
-    )
+    pieces = [(0, 0), (0, 1), (last, 0)]
+    sources = [own[0], other[0], own[last]]
+    latent_shape = (members, nodes, width)
+    grad_hidden, grad_latent = pl.pallas_call(
+        lambda *refs: write_kernel(count, pieces, members, *refs),
+        out_shape=(hidden_shape, jax.ShapeDtypeStruct(latent_shape, F32)),
+        in_specs=[VMEM] * (len(pieces) + members + 2),
+        out_specs=(HBM, HBM),
+        scratch_shapes=[
+            pltpu.VMEM((sum(source.shape[0] for source in sources), width), F32),
+            pltpu.VMEM(latent_shape, F32),
+            pltpu.SemaphoreType.DMA((len(pieces), blocks)),
+            pltpu.SemaphoreType.DMA((1,)),
+        ],
+        compiler_params=PARAMS,
+        cost_estimate=LIGHT,
+        name="write",
+    )(*sources, *inner, near, far)
     grad_hidden, grad_out, grad_gain, loss = pl.pallas_call(
         lambda *refs: last_write_kernel(count, *refs),
         out_shape=(

time: 74.7 us -> 73 us (0.977)
  waiting for transfers between devices: 17.4 us -> 14.8 us
  starting transfers between devices: 30 us -> 32.3 us
    ppermute x10, starting transfers between devices: 20.1 us -> 23.1 us  [swap_bits(): return lax.ppermute(value, ('space', 'member'), pairs)]
    ppermute x10, waiting for transfers between devices: 16.3 us -> 13.9 us  [swap_bits(): return lax.ppermute(value, ('space', 'member'), pairs)]
    pallas_call x5 -> x4, Pallas kernels: 4.63 us -> 4.25 us  [the longest x1 1.95 us: local(): pl.pallas_call(lambda *refs: write_kernel(count, pieces, members, *refs),...]
  transfers between devices with their start and end apart: 20 -> 20, of which waited for: 6 -> 9; matrix products, arithmetic and copies ran while one was open for 1% -> 1% of each run, Pallas kernels for 20% -> 20%
where the time goes in v6:
time: 73 us; the launch traced here: 72.8 us
  starting transfers between devices  32.3 us (44%)
  Pallas kernels  22.9 us (31%)
  waiting for transfers between devices  14.8 us (20%)
  other arithmetic  1.47 us (2%)
  between operations  1.08 us (1%)
    ppermute x10, starting transfers between devices, swap_bits(): return lax.ppermute(value, ('space', 'member'), pairs)  23.1 us
    ppermute x10, waiting for transfers between devices, swap_bits(): return lax.ppermute(value, ('space', 'member'), pairs)  13.9 us
    ppermute x4, starting transfers between devices, swap_pairs(): return lax.ppermute(value, axis, pairs + [(b, a) for a, b in pairs])  7.81 us
    pallas_call x2, Pallas kernels, backward(): pl.pallas_call(lambda *refs: backward_kernel(member, *refs), out_shape=(j...  6.45 us
    pallas_call x1, Pallas kernels, local(): pl.pallas_call(forward_kernel, out_shape=(pltpu.VMEM((rows, width), BF16)...  5.2 us
    pallas_call x1, Pallas kernels, local(): pl.pallas_call(prepare_kernel, out_shape=(pltpu.VMEM((points, 2 * LANES),...  2.2 us
    pallas_call x1, Pallas kernels, local(): pl.pallas_call(score_kernel, out_shape=(jax.ShapeDtypeStruct((1, 1), F32)...  2.13 us
    pallas_call x1, Pallas kernels, local(): pl.pallas_call(lambda *refs: write_kernel(count, pieces, members, *refs),...  1.95 us
  transfers between devices with their start and end apart: 20, of which 9 were waited for; matrix products, arithmetic and copies ran while one was open for 1% of the time, Pallas kernels for 20%

profile of v6, /device:TPU:0, one launch (start us, length us, event | category | flops | bytes accessed | tf_op | source)
XLA Modules:
  0.0 72.8 jit_solution(17830989778573228085)
XLA Ops:
  0.6 0.9 %broadcast_select_fusion = (bf16[2,16,1024]{2,1,0:T(8,128)(2,1)S(1)}, bf16[2,16,1024]{2,1,0:T(8,128)(2,1)S(1)}) fusion(pred[]{:T(512)S(6)} %eq.3, bf16[2,64,1024]{2,1,0:T(8,128)(2,1)} %own_in.1), kind=kLoop, calls=%fused_computation.14 | loop fusion | flops 65536 | bytes 262145 | tf_op jit(solution)/shard_map/jit(_where)/select_n | solution.py:518
  1.5 3.0 %collective-permute-start = (bf16[2,16,1024]{2,1,0:T(8,128)(2,1)S(1)}, bf16[2,16,1024]{2,1,0:T(8,128)(2,1)S(1)}, u32[]{:S(2)}, u32[]{:S(2)}) collective-permute-start(bf16[2,16,1024]{2,1,0:T(8,128)(2,1)S(1)} %get-tuple-element.106), channel_id=1, source_target_pairs={{0,2},{4,6},{8,10},{12,14},{2,0},{6,4},{10,8},{14,12},{1,3},{5,7},... | collective-permute-start | bytes 196616 | tf_op jit(solution)/shard_map/ppermute | solution.py:21
  4.6 0.7 collective-permute-start.1
  5.2 2.2 %prepare.1 = (bf16[512,256]{1,0:T(8,128)(2,1)S(1)}, bf16[256,512]{1,0:T(8,128)(2,1)S(1)}, f32[100,512]{1,0:T(8,128)S(1)}, bf16[128,1024]{1,0:T(8,128)(2,1)S(1)},...) custom-call(s32[4,512]{1,0:T(4,128)} %bitcast.24, ...), custom_call_target="tpu_custom_call" | custom-call | tf_op jit(solution)/shard_map/prepare/pallas_call | solution.py:520
  7.5 5.2 %forward.1 = (bf16[1024,1024]{1,0:T(8,128)(2,1)S(1)}, bf16[1024,1024]{1,0:T(8,128)(2,1)S(1)}, bf16[1024,1024]{1,0:T(8,128)(2,1)S(1)}, f32[2,100,512]{2,1,0:T(8,128)S(1)}, f32[1024,1]{1,0:T(8,128)S(1)}) custom-call(bf16[512,256]{1,0:T(8,128)(2,1)S(1)} %get-tuple-element.52.adj, bf16[2,16,1024]{2,1,0:T(8,128)(2,1)S(1)} %collective-permute-done.near, ...), custom_call_target="tpu_custom_call" | custom-call | tf_op jit(solution)/shard_map/forward/pallas_call | solution.py:564
  12.7 0.9 %transpose.29 = (bf16[1024,1024]{1,0:T(8,128)(2,1)S(1)}, f32[100,512]{1,0:T(8,128)S(1)}, f32[2,100,512]{2,1,0:T(8,128)S(1)}) custom-call(bf16[1024,1024]{1,0:T(8,128)(2,1)S(1)} %get-tuple-element.57.refs_0_.refs_2_, f32[2,100,512]{2,1,0:T(8,128)S(1)} %get-tuple-element.58.refs_1_.outputs, f32[100,512]{1,0:T(8,128)S(1)} %get-tuple-element.59.refs_2_), custom_call_target="tpu_custom_call" | custom-call | flops 1 | bytes 1 | tf_op jit(solution)/shard_map/transpose/pallas_call | solution.py:584
  13.6 0.9 %collective-permute-done.2.others = f32[2,100,512]{2,1,0:T(8,128)S(1)} collective-permute-done((f32[2,100,512]{2,1,0:T(8,128)S(1)}, f32[2,100,512]{2,1,0:T(8,128)S(1)}, u32[]{:S(2)}, u32[]{:S(2)}) %collective-permute-start.2) | collective-permute-done | bytes 409632 | tf_op jit(solution)/shard_map/ppermute | solution.py:25
  14.5 2.1 %score.1 = (f32[1,1]{1,0:T(1,128)}, bf16[1024,1024]{1,0:T(8,128)(2,1)S(1)}, bf16[128,1024]{1,0:T(8,128)(2,1)S(1)}, bf16[256,1024]{1,0:T(8,128)(2,1)S(1)}) custom-call(f32[2,100,512]{2,1,0:T(8,128)S(1)} %get-tuple-element.58.refs_1_.outputs, f32[2,100,512]{2,1,0:T(8,128)S(1)} %collective-permute-done.2.others, f32[100,512]{1,0:T(8,128)S(1)} %get-tuple-element.61.own_score, ...), custom_call_target="tpu_custom_call" | custom-call | tf_op jit(solution)/shard_map/score/pallas_call | solution.py:597
  16.8 1.4 %sent.1 = (bf16[256,1280]{1,0:T(8,128)(2,1)S(1)}, f32[256,256]{1,0:T(8,128)S(1)}) custom-call(bf16[1024,1024]{1,0:T(8,128)(2,1)S(1)} %get-tuple-element.60.normed_t.refs_0_, bf16[1024,1024]{1,0:T(8,128)(2,1)S(1)} %get-tuple-element.65.refs_1_.refs_0_, bf16[128,1024]{1,0:T(8,128)(2,1)S(1)} %get-tuple-element.66.refs_2_, ...), custom_call_target="tpu_custom_call" | custom-call | flops 1 | bytes 1 | tf_op jit(solution)/shard_map/sent/pallas_call | solution.py:628
  18.6 0.7 product.2
  19.3 4.3 %collective-permute-start.6 = (bf16[128,1024]{1,0:T(8,128)(2,1)S(1)}, bf16[128,1024]{1,0:T(8,128)(2,1)S(1)}, u32[]{:S(2)}, u32[]{:S(2)}) collective-permute-start(bf16[128,1024]{1,0:T(8,128)(2,1)S(1)} %get-tuple-element.70), channel_id=1, source_target_pairs={{0,2},{1,5},{2,0},{3,7},{4,6},{5,1},{6,4},{7,3},{8,10},{9,13},{10,... | collective-permute-start | bytes 786440 | tf_op jit(solution)/shard_map/ppermute | solution.py:34
  23.7 0.7 product.3
  24.4 2.9 %backward.2 = (f32[8,1024]{1,0:T(8,128)S(1)}, f32[64,1024]{1,0:T(8,128)S(1)}, bf16[16,1024]{1,0:T(8,128)(2,1)S(1)}, bf16[16,1024]{1,0:T(8,128)(2,1)S(1)}) custom-call(bf16[1024,1024]{1,0:T(8,128)(2,1)S(1)} %get-tuple-element.65.refs_1_.refs_0_, bf16[1024,1024]{1,0:T(8,128)(2,1)S(1)} %get-tuple-element.55.hidden_weight.refs_1_, ...), custom_call_target="tpu_custom_call" | custom-call | flops 1 | bytes 1 | tf_op jit(solution)/shard_map/backward/pallas_call | solution.py:649
  27.3 0.7 %collective-permute-done.6 = bf16[128,1024]{1,0:T(8,128)(2,1)S(1)} collective-permute-done((bf16[128,1024]{1,0:T(8,128)(2,1)S(1)}, bf16[128,1024]{1,0:T(8,128)(2,1)S(1)}, u32[]{:S(2)}, u32[]{:S(2)}) %collective-permute-start.6) | collective-permute-done | bytes 262176 | tf_op jit(solution)/shard_map/ppermute | solution.py:34
  28.1 3.5 %collective-permute-start.13 = (bf16[64,1024]{1,0:T(8,128)(2,1)S(1)}, bf16[64,1024]{1,0:T(8,128)(2,1)S(1)}, u32[]{:S(2)}, u32[]{:S(2)}) collective-permute-start(bf16[64,1024]{1,0:T(8,128)(2,1)S(1)} %slice.77), channel_id=1, source_target_pairs={{0,4},{1,3},{2,6},{3,1},{4,0},{5,7},{6,2},{7,5},{8,12},{9,11},{10,... | collective-permute-start | bytes 393224 | tf_op jit(solution)/shard_map/ppermute | solution.py:34
  32.1 3.6 %backward.3 = (bf16[8,1280]{1,0:T(8,128)(2,1)S(1)}, f32[64,1024]{1,0:T(8,128)S(1)}, bf16[16,1024]{1,0:T(8,128)(2,1)S(1)}, bf16[16,1024]{1,0:T(8,128)(2,1)S(1)}) custom-call(bf16[1024,1024]{1,0:T(8,128)(2,1)S(1)} %get-tuple-element.65.refs_1_.refs_0_, bf16[1024,1024]{1,0:T(8,128)(2,1)S(1)} %get-tuple-element.55.hidden_weight.refs_1_, ...), custom_call_target="tpu_custom_call" | custom-call | flops 1 | bytes 1 | tf_op jit(solution)/shard_map/backward/pallas_call | solution.py:649
  36.0 3.1 %collective-permute-start.14 = (bf16[64,1024]{1,0:T(8,128)(2,1)S(1)}, bf16[64,1024]{1,0:T(8,128)(2,1)S(1)}, u32[]{:S(2)}, u32[]{:S(2)}) collective-permute-start(bf16[64,1024]{1,0:T(8,128)(2,1)S(1)} %add_convert_fusion.5), channel_id=1, source_target_pairs={{0,8},{1,9},{2,10},{3,11},{4,12},{5,13},{6,14},{7,15},{8,0},{9,1},... | collective-permute-start | bytes 393224 | tf_op jit(solution)/shard_map/ppermute | solution.py:34
  39.3 1.6 %collective-permute-start.7 = (bf16[72,1280]{1,0:T(8,128)(2,1)S(1)}, bf16[72,1280]{1,0:T(8,128)(2,1)S(1)}, u32[]{:S(2)}, u32[]{:S(2)}) collective-permute-start(bf16[72,1280]{1,0:T(8,128)(2,1)S(1)} %pad_maximum_fusion.4), channel_id=1, source_target_pairs={{0,4},{1,3},{2,6},{3,1},{4,0},{5,7},{6,2},{7,5},{8,12},{9,11},{10,... | collective-permute-start | bytes 552968 | tf_op jit(solution)/shard_map/ppermute | solution.py:34
  41.0 2.8 %collective-permute-done.14 = bf16[64,1024]{1,0:T(8,128)(2,1)S(1)} collective-permute-done((bf16[64,1024]{1,0:T(8,128)(2,1)S(1)}, bf16[64,1024]{1,0:T(8,128)(2,1)S(1)}, u32[]{:S(2)}, u32[]{:S(2)}) %collective-permute-start.14) | collective-permute-done | bytes 131104 | tf_op jit(solution)/shard_map/ppermute | solution.py:34
  43.8 0.9 %collective-permute-start.15 = (bf16[64,1024]{1,0:T(8,128)(2,1)S(1)}, bf16[64,1024]{1,0:T(8,128)(2,1)S(1)}, u32[]{:S(2)}, u32[]{:S(2)}) collective-permute-start(bf16[64,1024]{1,0:T(8,128)(2,1)S(1)} %add_convert_fusion.4), channel_id=1, source_target_pairs={{0,4},{1,3},{2,6},{3,1},{4,0},{5,7},{6,2},{7,5},{8,12},{9,11},{10,... | collective-permute-start | bytes 393224 | tf_op jit(solution)/shard_map/ppermute | solution.py:34
  45.1 3.2 %collective-permute-start.8 = (bf16[72,1280]{1,0:T(8,128)(2,1)S(1)}, bf16[72,1280]{1,0:T(8,128)(2,1)S(1)}, u32[]{:S(2)}, u32[]{:S(2)}) collective-permute-start(bf16[72,1280]{1,0:T(8,128)(2,1)S(1)} %pad_maximum_fusion.5), channel_id=1, source_target_pairs={{0,8},{1,9},{2,10},{3,11},{4,12},{5,13},{6,14},{7,15},{8,0},{9,1},... | collective-permute-start | bytes 552968 | tf_op jit(solution)/shard_map/ppermute | solution.py:34
  48.3 0.6 collective-permute-done.15
  48.9 2.7 %collective-permute-start.16 = (bf16[128,1024]{1,0:T(8,128)(2,1)S(1)}, bf16[128,1024]{1,0:T(8,128)(2,1)S(1)}, u32[]{:S(2)}, u32[]{:S(2)}) collective-permute-start(bf16[128,1024]{1,0:T(8,128)(2,1)S(1)} %pad_maximum_fusion.3), channel_id=1, source_target_pairs={{0,2},{1,5},{2,0},{3,7},{4,6},{5,1},{6,4},{7,3},{8,10},{9,13},{10,... | collective-permute-start | bytes 786440 | tf_op jit(solution)/shard_map/ppermute | solution.py:34
  51.6 2.8 %collective-permute-done.8 = bf16[72,1280]{1,0:T(8,128)(2,1)S(1)} collective-permute-done((bf16[72,1280]{1,0:T(8,128)(2,1)S(1)}, bf16[72,1280]{1,0:T(8,128)(2,1)S(1)}, u32[]{:S(2)}, u32[]{:S(2)}) %collective-permute-start.8) | collective-permute-done | bytes 184352 | tf_op jit(solution)/shard_map/ppermute | solution.py:34
  54.5 1.6 %collective-permute-start.9 = (bf16[64,1280]{1,0:T(8,128)(2,1)S(1)}, bf16[64,1280]{1,0:T(8,128)(2,1)S(1)}, u32[]{:S(2)}, u32[]{:S(2)}) collective-permute-start(bf16[64,1280]{1,0:T(8,128)(2,1)S(1)} %add_convert_fusion.2), channel_id=1, source_target_pairs={{0,4},{1,3},{2,6},{3,1},{4,0},{5,7},{6,2},{7,5},{8,12},{9,11},{10,... | collective-permute-start | bytes 491528 | tf_op jit(solution)/shard_map/ppermute | solution.py:34
  56.1 3.8 %collective-permute-done.9 = bf16[64,1280]{1,0:T(8,128)(2,1)S(1)} collective-permute-done((bf16[64,1280]{1,0:T(8,128)(2,1)S(1)}, bf16[64,1280]{1,0:T(8,128)(2,1)S(1)}, u32[]{:S(2)}, u32[]{:S(2)}) %collective-permute-start.9) | collective-permute-done | bytes 163872 | tf_op jit(solution)/shard_map/ppermute | solution.py:34
  60.0 1.6 %collective-permute-start.10 = (bf16[136,1280]{1,0:T(8,128)(2,1)S(1)}, bf16[136,1280]{1,0:T(8,128)(2,1)S(1)}, u32[]{:S(2)}, u32[]{:S(2)}) collective-permute-start(bf16[136,1280]{1,0:T(8,128)(2,1)S(1)} %concatenate.29), channel_id=1, source_target_pairs={{0,2},{1,5},{2,0},{3,7},{4,6},{5,1},{6,4},{7,3},{8,10},{9,13},{10,... | collective-permute-start | bytes 1044488 | tf_op jit(solution)/shard_map/ppermute | solution.py:34
  61.8 0.7 collective-permute-start.19
  62.5 3.5 %collective-permute-start.18 = (bf16[2,16,1024]{2,1,0:T(8,128)(2,1)S(1)}, bf16[2,16,1024]{2,1,0:T(8,128)(2,1)S(1)}, u32[]{:S(2)}, u32[]{:S(2)}) collective-permute-start(bf16[2,16,1024]{2,1,0:T(8,128)(2,1)S(1)} %pad_maximum_fusion.6), channel_id=1, source_target_pairs={{0,2},{4,6},{8,10},{12,14},{2,0},{6,4},{10,8},{14,12},{1,3},{5,7},... | collective-permute-start | bytes 196616 | tf_op jit(solution)/shard_map/ppermute | solution.py:21
  65.9 2.6 %collective-permute-done.10 = bf16[136,1280]{1,0:T(8,128)(2,1)S(1)} collective-permute-done((bf16[136,1280]{1,0:T(8,128)(2,1)S(1)}, bf16[136,1280]{1,0:T(8,128)(2,1)S(1)}, u32[]{:S(2)}, u32[]{:S(2)}) %collective-permute-start.10) | collective-permute-done | bytes 348192 | tf_op jit(solution)/shard_map/ppermute | solution.py:34
  69.3 2.0 %write.1 = (f32[1024,1024]{1,0:T(8,128)}, f32[2,64,1024]{2,1,0:T(8,128)}) custom-call(bf16[256,1024]{1,0:T(8,128)(2,1)S(1)} %pad_maximum_fusion.1.refs_0_, bf16[256,1024]{1,0:T(8,128)(2,1)S(1)} %collective-permute-done.17.refs_1_, bf16[256,1280]{1,0:T(8,128)(2,1)S(1)} %pad_maximum_fusion.refs_2_.refs_0_, f32[64,1024]{1,0:T(8,128)S(1)} %get-tuple-element.79.refs_3_, ...), custom_call_target="tpu_custom_call" | custom-call | flops 1 | bytes 1 | tf_op jit(solution)/shard_map/write/pallas_call | solution.py:694
  71.3 1.3 %last_write.1 = (f32[1024,1024]{1,0:T(8,128)}, f32[100,1024]{1,0:T(8,128)}, f32[1,1024]{1,0:T(1,128)}, f32[1,1]{1,0:T(1,128)}) custom-call(bf16[256,1280]{1,0:T(8,128)(2,1)S(1)} %pad_maximum_fusion.refs_2_.refs_0_, bf16[256,1280]{1,0:T(8,128)(2,1)S(1)} %collective-permute-done.11.refs_1_, ...), custom_call_target="tpu_custom_call", output_to_operand_aliasing={{0}: (4, {})} | custom-call | tf_op jit(solution)/shard_map/last_write/pallas_call | solution.py:709
  (45 shorter events, 3.3 us)
Async XLA Ops:
  1.5 5.9 %collective-permute-start = (bf16[2,16,1024]{2,1,0:T(8,128)(2,1)S(1)}, bf16[2,16,1024]{2,1,0:T(8,128)(2,1)S(1)}, u32[]{:S(2)}, u32[]{:S(2)}) collective-permute-start(bf16[2,16,1024]{2,1,0:T(8,128)(2,1)S(1)} %get-tuple-element.106), channel_id=1, source_target_pairs={{0,2},{4,6},{8,10},{12,14},{2,0},{6,4},{10,8},{14,12},{1,3},{5,7},... | collective-permute-start | bytes 196616 | tf_op jit(solution)/shard_map/ppermute | solution.py:21
  4.6 2.9 %collective-permute-start.1 = (bf16[2,16,1024]{2,1,0:T(8,128)(2,1)S(1)}, bf16[2,16,1024]{2,1,0:T(8,128)(2,1)S(1)}, u32[]{:S(2)}, u32[]{:S(2)}) collective-permute-start(bf16[2,16,1024]{2,1,0:T(8,128)(2,1)S(1)} %get-tuple-element.105), channel_id=1, source_target_pairs={{2,4},{6,8},{10,12},{4,2},{8,6},{12,10},{3,5},{7,9},{11,13},{5,3},... | collective-permute-start | bytes 196616 | tf_op jit(solution)/shard_map/ppermute | solution.py:21
  12.7 1.8 %collective-permute-start.2 = (f32[2,100,512]{2,1,0:T(8,128)S(1)}, f32[2,100,512]{2,1,0:T(8,128)S(1)}, u32[]{:S(2)}, u32[]{:S(2)}) collective-permute-start(f32[2,100,512]{2,1,0:T(8,128)S(1)} %get-tuple-element.58.refs_1_.outputs), channel_id=1, source_target_pairs={{0,1},{1,0},{2,3},{3,2},{4,5},{5,4},{6,7},{7,6},{8,9},{9,8},{10,11... | collective-permute-start | bytes 1228808 | tf_op jit(solution)/shard_map/ppermute | solution.py:25
  16.6 2.0 %collective-permute-start.4 = (bf16[256,1024]{1,0:T(8,128)(2,1)S(1)}, bf16[256,1024]{1,0:T(8,128)(2,1)S(1)}, u32[]{:S(2)}, u32[]{:S(2)}) collective-permute-start(bf16[256,1024]{1,0:T(8,128)(2,1)S(1)} %get-tuple-element.69), channel_id=1, source_target_pairs={{0,1},{1,0},{2,3},{3,2},{4,5},{5,4},{6,7},{7,6},{8,9},{9,8},{10,11... | collective-permute-start | bytes 1572872 | tf_op jit(solution)/shard_map/ppermute | solution.py:25
  18.1 5.5 %collective-permute-start.3 = (bf16[256,1280]{1,0:T(8,128)(2,1)S(1)}, bf16[256,1280]{1,0:T(8,128)(2,1)S(1)}, u32[]{:S(2)}, u32[]{:S(2)}) collective-permute-start(bf16[256,1280]{1,0:T(8,128)(2,1)S(1)} %get-tuple-element.68), channel_id=1, source_target_pairs={{0,1},{1,0},{2,3},{3,2},{4,5},{5,4},{6,7},{7,6},{8,9},{9,8},{10,11... | collective-permute-start | bytes 1966088 | tf_op jit(solution)/shard_map/ppermute | solution.py:25
  19.3 8.7 %collective-permute-start.6 = (bf16[128,1024]{1,0:T(8,128)(2,1)S(1)}, bf16[128,1024]{1,0:T(8,128)(2,1)S(1)}, u32[]{:S(2)}, u32[]{:S(2)}) collective-permute-start(bf16[128,1024]{1,0:T(8,128)(2,1)S(1)} %get-tuple-element.70), channel_id=1, source_target_pairs={{0,2},{1,5},{2,0},{3,7},{4,6},{5,1},{6,4},{7,3},{8,10},{9,13},{10,... | collective-permute-start | bytes 786440 | tf_op jit(solution)/shard_map/ppermute | solution.py:34
  28.1 7.9 %collective-permute-start.13 = (bf16[64,1024]{1,0:T(8,128)(2,1)S(1)}, bf16[64,1024]{1,0:T(8,128)(2,1)S(1)}, u32[]{:S(2)}, u32[]{:S(2)}) collective-permute-start(bf16[64,1024]{1,0:T(8,128)(2,1)S(1)} %slice.77), channel_id=1, source_target_pairs={{0,4},{1,3},{2,6},{3,1},{4,0},{5,7},{6,2},{7,5},{8,12},{9,11},{10,... | collective-permute-start | bytes 393224 | tf_op jit(solution)/shard_map/ppermute | solution.py:34
  31.6 7.5 %collective-permute-start.5 = (bf16[128,1280]{1,0:T(8,128)(2,1)S(1)}, bf16[128,1280]{1,0:T(8,128)(2,1)S(1)}, u32[]{:S(2)}, u32[]{:S(2)}) collective-permute-start(bf16[128,1280]{1,0:T(8,128)(2,1)S(1)} %get-tuple-element.74), channel_id=1, source_target_pairs={{0,2},{1,5},{2,0},{3,7},{4,6},{5,1},{6,4},{7,3},{8,10},{9,13},{10,... | collective-permute-start | bytes 983048 | tf_op jit(solution)/shard_map/ppermute | solution.py:34
  36.0 7.7 %collective-permute-start.14 = (bf16[64,1024]{1,0:T(8,128)(2,1)S(1)}, bf16[64,1024]{1,0:T(8,128)(2,1)S(1)}, u32[]{:S(2)}, u32[]{:S(2)}) collective-permute-start(bf16[64,1024]{1,0:T(8,128)(2,1)S(1)} %add_convert_fusion.5), channel_id=1, source_target_pairs={{0,8},{1,9},{2,10},{3,11},{4,12},{5,13},{6,14},{7,15},{8,0},{9,1},... | collective-permute-start | bytes 393224 | tf_op jit(solution)/shard_map/ppermute | solution.py:34
  39.3 5.7 %collective-permute-start.7 = (bf16[72,1280]{1,0:T(8,128)(2,1)S(1)}, bf16[72,1280]{1,0:T(8,128)(2,1)S(1)}, u32[]{:S(2)}, u32[]{:S(2)}) collective-permute-start(bf16[72,1280]{1,0:T(8,128)(2,1)S(1)} %pad_maximum_fusion.4), channel_id=1, source_target_pairs={{0,4},{1,3},{2,6},{3,1},{4,0},{5,7},{6,2},{7,5},{8,12},{9,11},{10,... | collective-permute-start | bytes 552968 | tf_op jit(solution)/shard_map/ppermute | solution.py:34
  43.8 5.1 %collective-permute-start.15 = (bf16[64,1024]{1,0:T(8,128)(2,1)S(1)}, bf16[64,1024]{1,0:T(8,128)(2,1)S(1)}, u32[]{:S(2)}, u32[]{:S(2)}) collective-permute-start(bf16[64,1024]{1,0:T(8,128)(2,1)S(1)} %add_convert_fusion.4), channel_id=1, source_target_pairs={{0,4},{1,3},{2,6},{3,1},{4,0},{5,7},{6,2},{7,5},{8,12},{9,11},{10,... | collective-permute-start | bytes 393224 | tf_op jit(solution)/shard_map/ppermute | solution.py:34
  45.1 9.3 %collective-permute-start.8 = (bf16[72,1280]{1,0:T(8,128)(2,1)S(1)}, bf16[72,1280]{1,0:T(8,128)(2,1)S(1)}, u32[]{:S(2)}, u32[]{:S(2)}) collective-permute-start(bf16[72,1280]{1,0:T(8,128)(2,1)S(1)} %pad_maximum_fusion.5), channel_id=1, source_target_pairs={{0,8},{1,9},{2,10},{3,11},{4,12},{5,13},{6,14},{7,15},{8,0},{9,1},... | collective-permute-start | bytes 552968 | tf_op jit(solution)/shard_map/ppermute | solution.py:34
  48.9 12.7 %collective-permute-start.16 = (bf16[128,1024]{1,0:T(8,128)(2,1)S(1)}, bf16[128,1024]{1,0:T(8,128)(2,1)S(1)}, u32[]{:S(2)}, u32[]{:S(2)}) collective-permute-start(bf16[128,1024]{1,0:T(8,128)(2,1)S(1)} %pad_maximum_fusion.3), channel_id=1, source_target_pairs={{0,2},{1,5},{2,0},{3,7},{4,6},{5,1},{6,4},{7,3},{8,10},{9,13},{10,... | collective-permute-start | bytes 786440 | tf_op jit(solution)/shard_map/ppermute | solution.py:34
  54.5 5.4 %collective-permute-start.9 = (bf16[64,1280]{1,0:T(8,128)(2,1)S(1)}, bf16[64,1280]{1,0:T(8,128)(2,1)S(1)}, u32[]{:S(2)}, u32[]{:S(2)}) collective-permute-start(bf16[64,1280]{1,0:T(8,128)(2,1)S(1)} %add_convert_fusion.2), channel_id=1, source_target_pairs={{0,4},{1,3},{2,6},{3,1},{4,0},{5,7},{6,2},{7,5},{8,12},{9,11},{10,... | collective-permute-start | bytes 491528 | tf_op jit(solution)/shard_map/ppermute | solution.py:34
  60.0 8.5 %collective-permute-start.10 = (bf16[136,1280]{1,0:T(8,128)(2,1)S(1)}, bf16[136,1280]{1,0:T(8,128)(2,1)S(1)}, u32[]{:S(2)}, u32[]{:S(2)}) collective-permute-start(bf16[136,1280]{1,0:T(8,128)(2,1)S(1)} %concatenate.29), channel_id=1, source_target_pairs={{0,2},{1,5},{2,0},{3,7},{4,6},{5,1},{6,4},{7,3},{8,10},{9,13},{10,... | collective-permute-start | bytes 1044488 | tf_op jit(solution)/shard_map/ppermute | solution.py:34
  61.7 7.6 %collective-permute-start.17 = (bf16[256,1024]{1,0:T(8,128)(2,1)S(1)}, bf16[256,1024]{1,0:T(8,128)(2,1)S(1)}, u32[]{:S(2)}, u32[]{:S(2)}) collective-permute-start(bf16[256,1024]{1,0:T(8,128)(2,1)S(1)} %pad_maximum_fusion.1.refs_0_), channel_id=1, source_target_pairs={{0,1},{1,0},{2,3},{3,2},{4,5},{5,4},{6,7},{7,6},{8,9},{9,8},{10,11... | collective-permute-start | bytes 1572872 | tf_op jit(solution)/shard_map/ppermute | solution.py:25
  61.8 7.5 %collective-permute-start.19 = (bf16[2,16,1024]{2,1,0:T(8,128)(2,1)S(1)}, bf16[2,16,1024]{2,1,0:T(8,128)(2,1)S(1)}, u32[]{:S(2)}, u32[]{:S(2)}) collective-permute-start(bf16[2,16,1024]{2,1,0:T(8,128)(2,1)S(1)} %pad_maximum_fusion.7), channel_id=1, source_target_pairs={{2,4},{6,8},{10,12},{4,2},{8,6},{12,10},{3,5},{7,9},{11,13},{5,3},... | collective-permute-start | bytes 196616 | tf_op jit(solution)/shard_map/ppermute | solution.py:21
  62.5 6.9 %collective-permute-start.18 = (bf16[2,16,1024]{2,1,0:T(8,128)(2,1)S(1)}, bf16[2,16,1024]{2,1,0:T(8,128)(2,1)S(1)}, u32[]{:S(2)}, u32[]{:S(2)}) collective-permute-start(bf16[2,16,1024]{2,1,0:T(8,128)(2,1)S(1)} %pad_maximum_fusion.6), channel_id=1, source_target_pairs={{0,2},{4,6},{8,10},{12,14},{2,0},{6,4},{10,8},{14,12},{1,3},{5,7},... | collective-permute-start | bytes 196616 | tf_op jit(solution)/shard_map/ppermute | solution.py:21
  68.6 2.7 %collective-permute-start.11 = (bf16[256,1280]{1,0:T(8,128)(2,1)S(1)}, bf16[256,1280]{1,0:T(8,128)(2,1)S(1)}, u32[]{:S(2)}, u32[]{:S(2)}) collective-permute-start(bf16[256,1280]{1,0:T(8,128)(2,1)S(1)} %pad_maximum_fusion.refs_2_.refs_0_), channel_id=1, source_target_pairs={{0,1},{1,0},{2,3},{3,2},{4,5},{5,4},{6,7},{7,6},{8,9},{9,8},{10,11... | collective-permute-start | bytes 1966088 | tf_op jit(solution)/shard_map/ppermute | solution.py:25
  68.8 2.5 %collective-permute-start.12 = (bf16[8,1280]{1,0:T(8,128)(2,1)S(1)}, bf16[8,1280]{1,0:T(8,128)(2,1)S(1)}, u32[]{:S(2)}, u32[]{:S(2)}) collective-permute-start(bf16[8,1280]{1,0:T(8,128)(2,1)S(1)} %pad_maximum_fusion.8.refs_2_), channel_id=1, source_target_pairs={{0,1},{1,0},{2,3},{3,2},{4,5},{5,4},{6,7},{7,6},{8,9},{9,8},{10,11... | collective-permute-start | bytes 61448 | tf_op jit(solution)/shard_map/ppermute | solution.py:25

commit v7 on v6

--- a/solution.py
+++ b/solution.py
@@ -122,7 +122,7 @@
 ):
     members, nodes, width = own.shape
     points = adj.shape[0]
-    tile = 256
+    tile = 512
     odd = (here_index() & 1) == 1
     for member in range(members):
         for part in range(2):
@@ -266,8 +266,8 @@
     grad_pred_t[...] = grad_wide[...].astype(BF16)
     for m in range(members):
         rows = slice(m * points, (m + 1) * points)
-        for column in range(0, width, 256):
-            columns = slice(column, column + 256)
+        for column in range(0, width, 512):
+            columns = slice(column, column + 512)
             grad_hid = dot(grad_pred[rows, :], output_weight[:, columns])
             grad_pre[rows, columns] = (grad_hid * slope[rows, columns].astype(F32)).astype(BF16)
     products(normed_t, grad_pre, slice(0, sent.shape[0]), sent)
@@ -275,16 +275,16 @@
 
 def products(normed_t, grad_pre, rows, target):
     width = grad_pre.shape[1]
-    for column in range(0, width, 256):
-        columns = slice(column, column + 256)
+    for column in range(0, width, 512):
+        columns = slice(column, column + 512)
         target[:, columns] = dot(normed_t[rows, :], grad_pre[:, columns]).astype(target.dtype)
 
 
 def product_kernel(first, normed_t, grad_pre, received, *refs):
     narrow, (sent, kept) = refs[:-2], refs[-2:]
     width, rows = grad_pre.shape[1], sent.shape[0]
-    for column in range(0, width, 256):
-        columns = slice(column, column + 256)
+    for column in range(0, width, 512):
+        columns = slice(column, column + 512)
         value = dot(normed_t[first : first + 2 * rows, :], grad_pre[:, columns])
         value = (value + received[:, columns].astype(F32)).astype(BF16)
         sent[:, columns] = value[:rows]
@@ -320,8 +320,8 @@
     nodes, width = inner.shape
     points = adj_t.shape[1]
     inverse_gain = 1.0 / gain[...]
-    for column in range(0, width, 256):
-        columns = slice(column, column + 256)
+    for column in range(0, width, 512):
+        columns = slice(column, column + 512)
         product[:, columns] = dot(
             grad_pre[member * points : (member + 1) * points, :], hidden_weight[columns, :], ((1,), (1,))
         )

time: 73 us -> 72.5 us (level)
  no operation moved by 1% of the time
where the time goes in v7:
time: 72.5 us; the launch traced here: 72.3 us
  starting transfers between devices  32.3 us (45%)
  Pallas kernels  22.4 us (31%)
  waiting for transfers between devices  14.8 us (20%)
  other arithmetic  1.47 us (2%)
  between operations  1.08 us (1%)
    ppermute x10, starting transfers between devices, swap_bits(): return lax.ppermute(value, ('space', 'member'), pairs)  23.2 us
    ppermute x10, waiting for transfers between devices, swap_bits(): return lax.ppermute(value, ('space', 'member'), pairs)  13.9 us
    ppermute x4, starting transfers between devices, swap_pairs(): return lax.ppermute(value, axis, pairs + [(b, a) for a, b in pairs])  7.81 us
    pallas_call x2, Pallas kernels, backward(): pl.pallas_call(lambda *refs: backward_kernel(member, *refs), out_shape=(j...  6.43 us
    pallas_call x1, Pallas kernels, local(): pl.pallas_call(forward_kernel, out_shape=(pltpu.VMEM((rows, width), BF16)...  4.74 us
    pallas_call x1, Pallas kernels, local(): pl.pallas_call(prepare_kernel, out_shape=(pltpu.VMEM((points, 2 * LANES),...  2.2 us
    pallas_call x1, Pallas kernels, local(): pl.pallas_call(score_kernel, out_shape=(jax.ShapeDtypeStruct((1, 1), F32)...  2.12 us
    pallas_call x1, Pallas kernels, local(): pl.pallas_call(lambda *refs: write_kernel(count, pieces, members, *refs),...  1.95 us
  transfers between devices with their start and end apart: 20, of which 9 were waited for; matrix products, arithmetic and copies ran while one was open for 1% of the time, Pallas kernels for 20%

profile of v7, /device:TPU:0, one launch (start us, length us, event | category | flops | bytes accessed | tf_op | source)
XLA Modules:
  0.0 72.3 jit_solution(11967090281507774287)
XLA Ops:
  0.6 0.9 %broadcast_select_fusion = (bf16[2,16,1024]{2,1,0:T(8,128)(2,1)S(1)}, bf16[2,16,1024]{2,1,0:T(8,128)(2,1)S(1)}) fusion(pred[]{:T(512)S(6)} %eq.3, bf16[2,64,1024]{2,1,0:T(8,128)(2,1)} %own_in.1), kind=kLoop, calls=%fused_computation.14 | loop fusion | flops 65536 | bytes 262145 | tf_op jit(solution)/shard_map/jit(_where)/select_n | solution.py:518
  1.5 3.0 %collective-permute-start = (bf16[2,16,1024]{2,1,0:T(8,128)(2,1)S(1)}, bf16[2,16,1024]{2,1,0:T(8,128)(2,1)S(1)}, u32[]{:S(2)}, u32[]{:S(2)}) collective-permute-start(bf16[2,16,1024]{2,1,0:T(8,128)(2,1)S(1)} %get-tuple-element.106), channel_id=1, source_target_pairs={{0,2},{4,6},{8,10},{12,14},{2,0},{6,4},{10,8},{14,12},{1,3},{5,7},... | collective-permute-start | bytes 196616 | tf_op jit(solution)/shard_map/ppermute | solution.py:21
  4.6 0.7 collective-permute-start.1
  5.2 2.2 %prepare.1 = (bf16[512,256]{1,0:T(8,128)(2,1)S(1)}, bf16[256,512]{1,0:T(8,128)(2,1)S(1)}, f32[100,512]{1,0:T(8,128)S(1)}, bf16[128,1024]{1,0:T(8,128)(2,1)S(1)},...) custom-call(s32[4,512]{1,0:T(4,128)} %bitcast.24, ...), custom_call_target="tpu_custom_call" | custom-call | tf_op jit(solution)/shard_map/prepare/pallas_call | solution.py:520
  7.5 4.7 %forward.1 = (bf16[1024,1024]{1,0:T(8,128)(2,1)S(1)}, bf16[1024,1024]{1,0:T(8,128)(2,1)S(1)}, bf16[1024,1024]{1,0:T(8,128)(2,1)S(1)}, f32[2,100,512]{2,1,0:T(8,128)S(1)}, f32[1024,1]{1,0:T(8,128)S(1)}) custom-call(bf16[512,256]{1,0:T(8,128)(2,1)S(1)} %get-tuple-element.52.adj, bf16[2,16,1024]{2,1,0:T(8,128)(2,1)S(1)} %collective-permute-done.near, ...), custom_call_target="tpu_custom_call" | custom-call | tf_op jit(solution)/shard_map/forward/pallas_call | solution.py:564
  12.3 0.9 %transpose.29 = (bf16[1024,1024]{1,0:T(8,128)(2,1)S(1)}, f32[100,512]{1,0:T(8,128)S(1)}, f32[2,100,512]{2,1,0:T(8,128)S(1)}) custom-call(bf16[1024,1024]{1,0:T(8,128)(2,1)S(1)} %get-tuple-element.57.refs_0_.refs_2_, f32[2,100,512]{2,1,0:T(8,128)S(1)} %get-tuple-element.58.refs_1_.outputs, f32[100,512]{1,0:T(8,128)S(1)} %get-tuple-element.59.refs_2_), custom_call_target="tpu_custom_call" | custom-call | flops 1 | bytes 1 | tf_op jit(solution)/shard_map/transpose/pallas_call | solution.py:584
  13.2 0.9 %collective-permute-done.2.others = f32[2,100,512]{2,1,0:T(8,128)S(1)} collective-permute-done((f32[2,100,512]{2,1,0:T(8,128)S(1)}, f32[2,100,512]{2,1,0:T(8,128)S(1)}, u32[]{:S(2)}, u32[]{:S(2)}) %collective-permute-start.2) | collective-permute-done | bytes 409632 | tf_op jit(solution)/shard_map/ppermute | solution.py:25
  14.0 2.1 %score.1 = (f32[1,1]{1,0:T(1,128)}, bf16[1024,1024]{1,0:T(8,128)(2,1)S(1)}, bf16[128,1024]{1,0:T(8,128)(2,1)S(1)}, bf16[256,1024]{1,0:T(8,128)(2,1)S(1)}) custom-call(f32[2,100,512]{2,1,0:T(8,128)S(1)} %get-tuple-element.58.refs_1_.outputs, f32[2,100,512]{2,1,0:T(8,128)S(1)} %collective-permute-done.2.others, f32[100,512]{1,0:T(8,128)S(1)} %get-tuple-element.61.own_score, ...), custom_call_target="tpu_custom_call" | custom-call | tf_op jit(solution)/shard_map/score/pallas_call | solution.py:597
  16.3 1.4 %sent.1 = (bf16[256,1280]{1,0:T(8,128)(2,1)S(1)}, f32[256,256]{1,0:T(8,128)S(1)}) custom-call(bf16[1024,1024]{1,0:T(8,128)(2,1)S(1)} %get-tuple-element.60.normed_t.refs_0_, bf16[1024,1024]{1,0:T(8,128)(2,1)S(1)} %get-tuple-element.65.refs_1_.refs_0_, bf16[128,1024]{1,0:T(8,128)(2,1)S(1)} %get-tuple-element.66.refs_2_, ...), custom_call_target="tpu_custom_call" | custom-call | flops 1 | bytes 1 | tf_op jit(solution)/shard_map/sent/pallas_call | solution.py:628
  18.1 0.7 product.2
  18.8 4.3 %collective-permute-start.6 = (bf16[128,1024]{1,0:T(8,128)(2,1)S(1)}, bf16[128,1024]{1,0:T(8,128)(2,1)S(1)}, u32[]{:S(2)}, u32[]{:S(2)}) collective-permute-start(bf16[128,1024]{1,0:T(8,128)(2,1)S(1)} %get-tuple-element.70), channel_id=1, source_target_pairs={{0,2},{1,5},{2,0},{3,7},{4,6},{5,1},{6,4},{7,3},{8,10},{9,13},{10,... | collective-permute-start | bytes 786440 | tf_op jit(solution)/shard_map/ppermute | solution.py:34
  23.2 0.7 product.3
  23.9 2.9 %backward.2 = (f32[8,1024]{1,0:T(8,128)S(1)}, f32[64,1024]{1,0:T(8,128)S(1)}, bf16[16,1024]{1,0:T(8,128)(2,1)S(1)}, bf16[16,1024]{1,0:T(8,128)(2,1)S(1)}) custom-call(bf16[1024,1024]{1,0:T(8,128)(2,1)S(1)} %get-tuple-element.65.refs_1_.refs_0_, bf16[1024,1024]{1,0:T(8,128)(2,1)S(1)} %get-tuple-element.55.hidden_weight.refs_1_, ...), custom_call_target="tpu_custom_call" | custom-call | flops 1 | bytes 1 | tf_op jit(solution)/shard_map/backward/pallas_call | solution.py:649
  26.8 0.7 %collective-permute-done.6 = bf16[128,1024]{1,0:T(8,128)(2,1)S(1)} collective-permute-done((bf16[128,1024]{1,0:T(8,128)(2,1)S(1)}, bf16[128,1024]{1,0:T(8,128)(2,1)S(1)}, u32[]{:S(2)}, u32[]{:S(2)}) %collective-permute-start.6) | collective-permute-done | bytes 262176 | tf_op jit(solution)/shard_map/ppermute | solution.py:34
  27.6 3.5 %collective-permute-start.13 = (bf16[64,1024]{1,0:T(8,128)(2,1)S(1)}, bf16[64,1024]{1,0:T(8,128)(2,1)S(1)}, u32[]{:S(2)}, u32[]{:S(2)}) collective-permute-start(bf16[64,1024]{1,0:T(8,128)(2,1)S(1)} %slice.77), channel_id=1, source_target_pairs={{0,4},{1,3},{2,6},{3,1},{4,0},{5,7},{6,2},{7,5},{8,12},{9,11},{10,... | collective-permute-start | bytes 393224 | tf_op jit(solution)/shard_map/ppermute | solution.py:34
  31.7 3.5 %backward.3 = (bf16[8,1280]{1,0:T(8,128)(2,1)S(1)}, f32[64,1024]{1,0:T(8,128)S(1)}, bf16[16,1024]{1,0:T(8,128)(2,1)S(1)}, bf16[16,1024]{1,0:T(8,128)(2,1)S(1)}) custom-call(bf16[1024,1024]{1,0:T(8,128)(2,1)S(1)} %get-tuple-element.65.refs_1_.refs_0_, bf16[1024,1024]{1,0:T(8,128)(2,1)S(1)} %get-tuple-element.55.hidden_weight.refs_1_, ...), custom_call_target="tpu_custom_call" | custom-call | flops 1 | bytes 1 | tf_op jit(solution)/shard_map/backward/pallas_call | solution.py:649
  35.6 3.1 %collective-permute-start.14 = (bf16[64,1024]{1,0:T(8,128)(2,1)S(1)}, bf16[64,1024]{1,0:T(8,128)(2,1)S(1)}, u32[]{:S(2)}, u32[]{:S(2)}) collective-permute-start(bf16[64,1024]{1,0:T(8,128)(2,1)S(1)} %add_convert_fusion.5), channel_id=1, source_target_pairs={{0,8},{1,9},{2,10},{3,11},{4,12},{5,13},{6,14},{7,15},{8,0},{9,1},... | collective-permute-start | bytes 393224 | tf_op jit(solution)/shard_map/ppermute | solution.py:34
  38.9 1.7 %collective-permute-start.7 = (bf16[72,1280]{1,0:T(8,128)(2,1)S(1)}, bf16[72,1280]{1,0:T(8,128)(2,1)S(1)}, u32[]{:S(2)}, u32[]{:S(2)}) collective-permute-start(bf16[72,1280]{1,0:T(8,128)(2,1)S(1)} %pad_maximum_fusion.4), channel_id=1, source_target_pairs={{0,4},{1,3},{2,6},{3,1},{4,0},{5,7},{6,2},{7,5},{8,12},{9,11},{10,... | collective-permute-start | bytes 552968 | tf_op jit(solution)/shard_map/ppermute | solution.py:34
  40.5 2.8 %collective-permute-done.14 = bf16[64,1024]{1,0:T(8,128)(2,1)S(1)} collective-permute-done((bf16[64,1024]{1,0:T(8,128)(2,1)S(1)}, bf16[64,1024]{1,0:T(8,128)(2,1)S(1)}, u32[]{:S(2)}, u32[]{:S(2)}) %collective-permute-start.14) | collective-permute-done | bytes 131104 | tf_op jit(solution)/shard_map/ppermute | solution.py:34
  43.3 0.9 %collective-permute-start.15 = (bf16[64,1024]{1,0:T(8,128)(2,1)S(1)}, bf16[64,1024]{1,0:T(8,128)(2,1)S(1)}, u32[]{:S(2)}, u32[]{:S(2)}) collective-permute-start(bf16[64,1024]{1,0:T(8,128)(2,1)S(1)} %add_convert_fusion.4), channel_id=1, source_target_pairs={{0,4},{1,3},{2,6},{3,1},{4,0},{5,7},{6,2},{7,5},{8,12},{9,11},{10,... | collective-permute-start | bytes 393224 | tf_op jit(solution)/shard_map/ppermute | solution.py:34
  44.6 3.2 %collective-permute-start.8 = (bf16[72,1280]{1,0:T(8,128)(2,1)S(1)}, bf16[72,1280]{1,0:T(8,128)(2,1)S(1)}, u32[]{:S(2)}, u32[]{:S(2)}) collective-permute-start(bf16[72,1280]{1,0:T(8,128)(2,1)S(1)} %pad_maximum_fusion.5), channel_id=1, source_target_pairs={{0,8},{1,9},{2,10},{3,11},{4,12},{5,13},{6,14},{7,15},{8,0},{9,1},... | collective-permute-start | bytes 552968 | tf_op jit(solution)/shard_map/ppermute | solution.py:34
  47.9 0.6 collective-permute-done.15
  48.5 2.7 %collective-permute-start.16 = (bf16[128,1024]{1,0:T(8,128)(2,1)S(1)}, bf16[128,1024]{1,0:T(8,128)(2,1)S(1)}, u32[]{:S(2)}, u32[]{:S(2)}) collective-permute-start(bf16[128,1024]{1,0:T(8,128)(2,1)S(1)} %pad_maximum_fusion.3), channel_id=1, source_target_pairs={{0,2},{1,5},{2,0},{3,7},{4,6},{5,1},{6,4},{7,3},{8,10},{9,13},{10,... | collective-permute-start | bytes 786440 | tf_op jit(solution)/shard_map/ppermute | solution.py:34
  51.2 2.8 %collective-permute-done.8 = bf16[72,1280]{1,0:T(8,128)(2,1)S(1)} collective-permute-done((bf16[72,1280]{1,0:T(8,128)(2,1)S(1)}, bf16[72,1280]{1,0:T(8,128)(2,1)S(1)}, u32[]{:S(2)}, u32[]{:S(2)}) %collective-permute-start.8) | collective-permute-done | bytes 184352 | tf_op jit(solution)/shard_map/ppermute | solution.py:34
  54.0 1.6 %collective-permute-start.9 = (bf16[64,1280]{1,0:T(8,128)(2,1)S(1)}, bf16[64,1280]{1,0:T(8,128)(2,1)S(1)}, u32[]{:S(2)}, u32[]{:S(2)}) collective-permute-start(bf16[64,1280]{1,0:T(8,128)(2,1)S(1)} %add_convert_fusion.2), channel_id=1, source_target_pairs={{0,4},{1,3},{2,6},{3,1},{4,0},{5,7},{6,2},{7,5},{8,12},{9,11},{10,... | collective-permute-start | bytes 491528 | tf_op jit(solution)/shard_map/ppermute | solution.py:34
  55.7 3.7 %collective-permute-done.9 = bf16[64,1280]{1,0:T(8,128)(2,1)S(1)} collective-permute-done((bf16[64,1280]{1,0:T(8,128)(2,1)S(1)}, bf16[64,1280]{1,0:T(8,128)(2,1)S(1)}, u32[]{:S(2)}, u32[]{:S(2)}) %collective-permute-start.9) | collective-permute-done | bytes 163872 | tf_op jit(solution)/shard_map/ppermute | solution.py:34
  59.6 1.6 %collective-permute-start.10 = (bf16[136,1280]{1,0:T(8,128)(2,1)S(1)}, bf16[136,1280]{1,0:T(8,128)(2,1)S(1)}, u32[]{:S(2)}, u32[]{:S(2)}) collective-permute-start(bf16[136,1280]{1,0:T(8,128)(2,1)S(1)} %concatenate.29), channel_id=1, source_target_pairs={{0,2},{1,5},{2,0},{3,7},{4,6},{5,1},{6,4},{7,3},{8,10},{9,13},{10,... | collective-permute-start | bytes 1044488 | tf_op jit(solution)/shard_map/ppermute | solution.py:34
  61.3 0.7 collective-permute-start.19
  62.0 3.5 %collective-permute-start.18 = (bf16[2,16,1024]{2,1,0:T(8,128)(2,1)S(1)}, bf16[2,16,1024]{2,1,0:T(8,128)(2,1)S(1)}, u32[]{:S(2)}, u32[]{:S(2)}) collective-permute-start(bf16[2,16,1024]{2,1,0:T(8,128)(2,1)S(1)} %pad_maximum_fusion.6), channel_id=1, source_target_pairs={{0,2},{4,6},{8,10},{12,14},{2,0},{6,4},{10,8},{14,12},{1,3},{5,7},... | collective-permute-start | bytes 196616 | tf_op jit(solution)/shard_map/ppermute | solution.py:21
  65.5 2.6 %collective-permute-done.10 = bf16[136,1280]{1,0:T(8,128)(2,1)S(1)} collective-permute-done((bf16[136,1280]{1,0:T(8,128)(2,1)S(1)}, bf16[136,1280]{1,0:T(8,128)(2,1)S(1)}, u32[]{:S(2)}, u32[]{:S(2)}) %collective-permute-start.10) | collective-permute-done | bytes 348192 | tf_op jit(solution)/shard_map/ppermute | solution.py:34
  68.9 2.0 %write.1 = (f32[1024,1024]{1,0:T(8,128)}, f32[2,64,1024]{2,1,0:T(8,128)}) custom-call(bf16[256,1024]{1,0:T(8,128)(2,1)S(1)} %pad_maximum_fusion.1.refs_0_, bf16[256,1024]{1,0:T(8,128)(2,1)S(1)} %collective-permute-done.17.refs_1_, bf16[256,1280]{1,0:T(8,128)(2,1)S(1)} %pad_maximum_fusion.refs_2_.refs_0_, f32[64,1024]{1,0:T(8,128)S(1)} %get-tuple-element.79.refs_3_, ...), custom_call_target="tpu_custom_call" | custom-call | flops 1 | bytes 1 | tf_op jit(solution)/shard_map/write/pallas_call | solution.py:694
  70.9 1.3 %last_write.1 = (f32[1024,1024]{1,0:T(8,128)}, f32[100,1024]{1,0:T(8,128)}, f32[1,1024]{1,0:T(1,128)}, f32[1,1]{1,0:T(1,128)}) custom-call(bf16[256,1280]{1,0:T(8,128)(2,1)S(1)} %pad_maximum_fusion.refs_2_.refs_0_, bf16[256,1280]{1,0:T(8,128)(2,1)S(1)} %collective-permute-done.11.refs_1_, ...), custom_call_target="tpu_custom_call", output_to_operand_aliasing={{0}: (4, {})} | custom-call | tf_op jit(solution)/shard_map/last_write/pallas_call | solution.py:709
  (45 shorter events, 3.3 us)
Async XLA Ops:
  1.5 5.9 %collective-permute-start = (bf16[2,16,1024]{2,1,0:T(8,128)(2,1)S(1)}, bf16[2,16,1024]{2,1,0:T(8,128)(2,1)S(1)}, u32[]{:S(2)}, u32[]{:S(2)}) collective-permute-start(bf16[2,16,1024]{2,1,0:T(8,128)(2,1)S(1)} %get-tuple-element.106), channel_id=1, source_target_pairs={{0,2},{4,6},{8,10},{12,14},{2,0},{6,4},{10,8},{14,12},{1,3},{5,7},... | collective-permute-start | bytes 196616 | tf_op jit(solution)/shard_map/ppermute | solution.py:21
  4.6 2.9 %collective-permute-start.1 = (bf16[2,16,1024]{2,1,0:T(8,128)(2,1)S(1)}, bf16[2,16,1024]{2,1,0:T(8,128)(2,1)S(1)}, u32[]{:S(2)}, u32[]{:S(2)}) collective-permute-start(bf16[2,16,1024]{2,1,0:T(8,128)(2,1)S(1)} %get-tuple-element.105), channel_id=1, source_target_pairs={{2,4},{6,8},{10,12},{4,2},{8,6},{12,10},{3,5},{7,9},{11,13},{5,3},... | collective-permute-start | bytes 196616 | tf_op jit(solution)/shard_map/ppermute | solution.py:21
  12.2 1.8 %collective-permute-start.2 = (f32[2,100,512]{2,1,0:T(8,128)S(1)}, f32[2,100,512]{2,1,0:T(8,128)S(1)}, u32[]{:S(2)}, u32[]{:S(2)}) collective-permute-start(f32[2,100,512]{2,1,0:T(8,128)S(1)} %get-tuple-element.58.refs_1_.outputs), channel_id=1, source_target_pairs={{0,1},{1,0},{2,3},{3,2},{4,5},{5,4},{6,7},{7,6},{8,9},{9,8},{10,11... | collective-permute-start | bytes 1228808 | tf_op jit(solution)/shard_map/ppermute | solution.py:25
  16.2 2.0 %collective-permute-start.4 = (bf16[256,1024]{1,0:T(8,128)(2,1)S(1)}, bf16[256,1024]{1,0:T(8,128)(2,1)S(1)}, u32[]{:S(2)}, u32[]{:S(2)}) collective-permute-start(bf16[256,1024]{1,0:T(8,128)(2,1)S(1)} %get-tuple-element.69), channel_id=1, source_target_pairs={{0,1},{1,0},{2,3},{3,2},{4,5},{5,4},{6,7},{7,6},{8,9},{9,8},{10,11... | collective-permute-start | bytes 1572872 | tf_op jit(solution)/shard_map/ppermute | solution.py:25
  17.7 5.5 %collective-permute-start.3 = (bf16[256,1280]{1,0:T(8,128)(2,1)S(1)}, bf16[256,1280]{1,0:T(8,128)(2,1)S(1)}, u32[]{:S(2)}, u32[]{:S(2)}) collective-permute-start(bf16[256,1280]{1,0:T(8,128)(2,1)S(1)} %get-tuple-element.68), channel_id=1, source_target_pairs={{0,1},{1,0},{2,3},{3,2},{4,5},{5,4},{6,7},{7,6},{8,9},{9,8},{10,11... | collective-permute-start | bytes 1966088 | tf_op jit(solution)/shard_map/ppermute | solution.py:25
  18.8 8.7 %collective-permute-start.6 = (bf16[128,1024]{1,0:T(8,128)(2,1)S(1)}, bf16[128,1024]{1,0:T(8,128)(2,1)S(1)}, u32[]{:S(2)}, u32[]{:S(2)}) collective-permute-start(bf16[128,1024]{1,0:T(8,128)(2,1)S(1)} %get-tuple-element.70), channel_id=1, source_target_pairs={{0,2},{1,5},{2,0},{3,7},{4,6},{5,1},{6,4},{7,3},{8,10},{9,13},{10,... | collective-permute-start | bytes 786440 | tf_op jit(solution)/shard_map/ppermute | solution.py:34
  27.6 7.9 %collective-permute-start.13 = (bf16[64,1024]{1,0:T(8,128)(2,1)S(1)}, bf16[64,1024]{1,0:T(8,128)(2,1)S(1)}, u32[]{:S(2)}, u32[]{:S(2)}) collective-permute-start(bf16[64,1024]{1,0:T(8,128)(2,1)S(1)} %slice.77), channel_id=1, source_target_pairs={{0,4},{1,3},{2,6},{3,1},{4,0},{5,7},{6,2},{7,5},{8,12},{9,11},{10,... | collective-permute-start | bytes 393224 | tf_op jit(solution)/shard_map/ppermute | solution.py:34
  31.2 7.5 %collective-permute-start.5 = (bf16[128,1280]{1,0:T(8,128)(2,1)S(1)}, bf16[128,1280]{1,0:T(8,128)(2,1)S(1)}, u32[]{:S(2)}, u32[]{:S(2)}) collective-permute-start(bf16[128,1280]{1,0:T(8,128)(2,1)S(1)} %get-tuple-element.74), channel_id=1, source_target_pairs={{0,2},{1,5},{2,0},{3,7},{4,6},{5,1},{6,4},{7,3},{8,10},{9,13},{10,... | collective-permute-start | bytes 983048 | tf_op jit(solution)/shard_map/ppermute | solution.py:34
  35.6 7.7 %collective-permute-start.14 = (bf16[64,1024]{1,0:T(8,128)(2,1)S(1)}, bf16[64,1024]{1,0:T(8,128)(2,1)S(1)}, u32[]{:S(2)}, u32[]{:S(2)}) collective-permute-start(bf16[64,1024]{1,0:T(8,128)(2,1)S(1)} %add_convert_fusion.5), channel_id=1, source_target_pairs={{0,8},{1,9},{2,10},{3,11},{4,12},{5,13},{6,14},{7,15},{8,0},{9,1},... | collective-permute-start | bytes 393224 | tf_op jit(solution)/shard_map/ppermute | solution.py:34
  38.9 5.7 %collective-permute-start.7 = (bf16[72,1280]{1,0:T(8,128)(2,1)S(1)}, bf16[72,1280]{1,0:T(8,128)(2,1)S(1)}, u32[]{:S(2)}, u32[]{:S(2)}) collective-permute-start(bf16[72,1280]{1,0:T(8,128)(2,1)S(1)} %pad_maximum_fusion.4), channel_id=1, source_target_pairs={{0,4},{1,3},{2,6},{3,1},{4,0},{5,7},{6,2},{7,5},{8,12},{9,11},{10,... | collective-permute-start | bytes 552968 | tf_op jit(solution)/shard_map/ppermute | solution.py:34
  43.3 5.1 %collective-permute-start.15 = (bf16[64,1024]{1,0:T(8,128)(2,1)S(1)}, bf16[64,1024]{1,0:T(8,128)(2,1)S(1)}, u32[]{:S(2)}, u32[]{:S(2)}) collective-permute-start(bf16[64,1024]{1,0:T(8,128)(2,1)S(1)} %add_convert_fusion.4), channel_id=1, source_target_pairs={{0,4},{1,3},{2,6},{3,1},{4,0},{5,7},{6,2},{7,5},{8,12},{9,11},{10,... | collective-permute-start | bytes 393224 | tf_op jit(solution)/shard_map/ppermute | solution.py:34
  44.6 9.3 %collective-permute-start.8 = (bf16[72,1280]{1,0:T(8,128)(2,1)S(1)}, bf16[72,1280]{1,0:T(8,128)(2,1)S(1)}, u32[]{:S(2)}, u32[]{:S(2)}) collective-permute-start(bf16[72,1280]{1,0:T(8,128)(2,1)S(1)} %pad_maximum_fusion.5), channel_id=1, source_target_pairs={{0,8},{1,9},{2,10},{3,11},{4,12},{5,13},{6,14},{7,15},{8,0},{9,1},... | collective-permute-start | bytes 552968 | tf_op jit(solution)/shard_map/ppermute | solution.py:34
  48.5 12.7 %collective-permute-start.16 = (bf16[128,1024]{1,0:T(8,128)(2,1)S(1)}, bf16[128,1024]{1,0:T(8,128)(2,1)S(1)}, u32[]{:S(2)}, u32[]{:S(2)}) collective-permute-start(bf16[128,1024]{1,0:T(8,128)(2,1)S(1)} %pad_maximum_fusion.3), channel_id=1, source_target_pairs={{0,2},{1,5},{2,0},{3,7},{4,6},{5,1},{6,4},{7,3},{8,10},{9,13},{10,... | collective-permute-start | bytes 786440 | tf_op jit(solution)/shard_map/ppermute | solution.py:34
  54.0 5.4 %collective-permute-start.9 = (bf16[64,1280]{1,0:T(8,128)(2,1)S(1)}, bf16[64,1280]{1,0:T(8,128)(2,1)S(1)}, u32[]{:S(2)}, u32[]{:S(2)}) collective-permute-start(bf16[64,1280]{1,0:T(8,128)(2,1)S(1)} %add_convert_fusion.2), channel_id=1, source_target_pairs={{0,4},{1,3},{2,6},{3,1},{4,0},{5,7},{6,2},{7,5},{8,12},{9,11},{10,... | collective-permute-start | bytes 491528 | tf_op jit(solution)/shard_map/ppermute | solution.py:34
  59.6 8.5 %collective-permute-start.10 = (bf16[136,1280]{1,0:T(8,128)(2,1)S(1)}, bf16[136,1280]{1,0:T(8,128)(2,1)S(1)}, u32[]{:S(2)}, u32[]{:S(2)}) collective-permute-start(bf16[136,1280]{1,0:T(8,128)(2,1)S(1)} %concatenate.29), channel_id=1, source_target_pairs={{0,2},{1,5},{2,0},{3,7},{4,6},{5,1},{6,4},{7,3},{8,10},{9,13},{10,... | collective-permute-start | bytes 1044488 | tf_op jit(solution)/shard_map/ppermute | solution.py:34
  61.2 7.6 %collective-permute-start.17 = (bf16[256,1024]{1,0:T(8,128)(2,1)S(1)}, bf16[256,1024]{1,0:T(8,128)(2,1)S(1)}, u32[]{:S(2)}, u32[]{:S(2)}) collective-permute-start(bf16[256,1024]{1,0:T(8,128)(2,1)S(1)} %pad_maximum_fusion.1.refs_0_), channel_id=1, source_target_pairs={{0,1},{1,0},{2,3},{3,2},{4,5},{5,4},{6,7},{7,6},{8,9},{9,8},{10,11... | collective-permute-start | bytes 1572872 | tf_op jit(solution)/shard_map/ppermute | solution.py:25
  61.3 7.5 %collective-permute-start.19 = (bf16[2,16,1024]{2,1,0:T(8,128)(2,1)S(1)}, bf16[2,16,1024]{2,1,0:T(8,128)(2,1)S(1)}, u32[]{:S(2)}, u32[]{:S(2)}) collective-permute-start(bf16[2,16,1024]{2,1,0:T(8,128)(2,1)S(1)} %pad_maximum_fusion.7), channel_id=1, source_target_pairs={{2,4},{6,8},{10,12},{4,2},{8,6},{12,10},{3,5},{7,9},{11,13},{5,3},... | collective-permute-start | bytes 196616 | tf_op jit(solution)/shard_map/ppermute | solution.py:21
  62.0 6.9 %collective-permute-start.18 = (bf16[2,16,1024]{2,1,0:T(8,128)(2,1)S(1)}, bf16[2,16,1024]{2,1,0:T(8,128)(2,1)S(1)}, u32[]{:S(2)}, u32[]{:S(2)}) collective-permute-start(bf16[2,16,1024]{2,1,0:T(8,128)(2,1)S(1)} %pad_maximum_fusion.6), channel_id=1, source_target_pairs={{0,2},{4,6},{8,10},{12,14},{2,0},{6,4},{10,8},{14,12},{1,3},{5,7},... | collective-permute-start | bytes 196616 | tf_op jit(solution)/shard_map/ppermute | solution.py:21
  68.2 2.7 %collective-permute-start.11 = (bf16[256,1280]{1,0:T(8,128)(2,1)S(1)}, bf16[256,1280]{1,0:T(8,128)(2,1)S(1)}, u32[]{:S(2)}, u32[]{:S(2)}) collective-permute-start(bf16[256,1280]{1,0:T(8,128)(2,1)S(1)} %pad_maximum_fusion.refs_2_.refs_0_), channel_id=1, source_target_pairs={{0,1},{1,0},{2,3},{3,2},{4,5},{5,4},{6,7},{7,6},{8,9},{9,8},{10,11... | collective-permute-start | bytes 1966088 | tf_op jit(solution)/shard_map/ppermute | solution.py:25
  68.3 2.5 %collective-permute-start.12 = (bf16[8,1280]{1,0:T(8,128)(2,1)S(1)}, bf16[8,1280]{1,0:T(8,128)(2,1)S(1)}, u32[]{:S(2)}, u32[]{:S(2)}) collective-permute-start(bf16[8,1280]{1,0:T(8,128)(2,1)S(1)} %pad_maximum_fusion.8.refs_2_), channel_id=1, source_target_pairs={{0,1},{1,0},{2,3},{3,2},{4,5},{5,4},{6,7},{7,6},{8,9},{9,8},{10,11... | collective-permute-start | bytes 61448 | tf_op jit(solution)/shard_map/ppermute | solution.py:25

commit v8 on v7

--- a/solution.py
+++ b/solution.py
@@ -122,7 +122,7 @@
 ):
     members, nodes, width = own.shape
     points = adj.shape[0]
-    tile = 512
+    tile = 1024
     odd = (here_index() & 1) == 1
     for member in range(members):
         for part in range(2):

time: 72.5 us -> 72.4 us (level)
  no operation moved by 1% of the time
where the time goes in v8:
time: 72.4 us; the launch traced here: 72.2 us
  starting transfers between devices  32.3 us (45%)
  Pallas kernels  22.3 us (31%)
  waiting for transfers between devices  14.8 us (20%)
  other arithmetic  1.47 us (2%)
  between operations  1.08 us (1%)
    ppermute x10, starting transfers between devices, swap_bits(): return lax.ppermute(value, ('space', 'member'), pairs)  23.2 us
    ppermute x10, waiting for transfers between devices, swap_bits(): return lax.ppermute(value, ('space', 'member'), pairs)  13.9 us
    ppermute x4, starting transfers between devices, swap_pairs(): return lax.ppermute(value, axis, pairs + [(b, a) for a, b in pairs])  7.8 us
    pallas_call x2, Pallas kernels, backward(): pl.pallas_call(lambda *refs: backward_kernel(member, *refs), out_shape=(j...  6.43 us
    pallas_call x1, Pallas kernels, local(): pl.pallas_call(forward_kernel, out_shape=(pltpu.VMEM((rows, width), BF16)...  4.6 us
    pallas_call x1, Pallas kernels, local(): pl.pallas_call(prepare_kernel, out_shape=(pltpu.VMEM((points, 2 * LANES),...  2.2 us
    pallas_call x1, Pallas kernels, local(): pl.pallas_call(score_kernel, out_shape=(jax.ShapeDtypeStruct((1, 1), F32)...  2.12 us
    pallas_call x1, Pallas kernels, local(): pl.pallas_call(lambda *refs: write_kernel(count, pieces, members, *refs),...  1.95 us
  transfers between devices with their start and end apart: 20, of which 9 were waited for; matrix products, arithmetic and copies ran while one was open for 1% of the time, Pallas kernels for 20%

profile of v8, /device:TPU:0, one launch (start us, length us, event | category | flops | bytes accessed | tf_op | source)
XLA Modules:
  0.0 72.2 jit_solution(1018644276380519740)
XLA Ops:
  0.6 0.9 %broadcast_select_fusion = (bf16[2,16,1024]{2,1,0:T(8,128)(2,1)S(1)}, bf16[2,16,1024]{2,1,0:T(8,128)(2,1)S(1)}) fusion(pred[]{:T(512)S(6)} %eq.3, bf16[2,64,1024]{2,1,0:T(8,128)(2,1)} %own_in.1), kind=kLoop, calls=%fused_computation.14 | loop fusion | flops 65536 | bytes 262145 | tf_op jit(solution)/shard_map/jit(_where)/select_n | solution.py:518
  1.5 3.0 %collective-permute-start = (bf16[2,16,1024]{2,1,0:T(8,128)(2,1)S(1)}, bf16[2,16,1024]{2,1,0:T(8,128)(2,1)S(1)}, u32[]{:S(2)}, u32[]{:S(2)}) collective-permute-start(bf16[2,16,1024]{2,1,0:T(8,128)(2,1)S(1)} %get-tuple-element.106), channel_id=1, source_target_pairs={{0,2},{4,6},{8,10},{12,14},{2,0},{6,4},{10,8},{14,12},{1,3},{5,7},... | collective-permute-start | bytes 196616 | tf_op jit(solution)/shard_map/ppermute | solution.py:21
  4.6 0.7 collective-permute-start.1
  5.2 2.2 %prepare.1 = (bf16[512,256]{1,0:T(8,128)(2,1)S(1)}, bf16[256,512]{1,0:T(8,128)(2,1)S(1)}, f32[100,512]{1,0:T(8,128)S(1)}, bf16[128,1024]{1,0:T(8,128)(2,1)S(1)},...) custom-call(s32[4,512]{1,0:T(4,128)} %bitcast.24, ...), custom_call_target="tpu_custom_call" | custom-call | tf_op jit(solution)/shard_map/prepare/pallas_call | solution.py:520
  7.5 4.6 %forward.1 = (bf16[1024,1024]{1,0:T(8,128)(2,1)S(1)}, bf16[1024,1024]{1,0:T(8,128)(2,1)S(1)}, bf16[1024,1024]{1,0:T(8,128)(2,1)S(1)}, f32[2,100,512]{2,1,0:T(8,128)S(1)}, f32[1024,1]{1,0:T(8,128)S(1)}) custom-call(bf16[512,256]{1,0:T(8,128)(2,1)S(1)} %get-tuple-element.52.adj, bf16[2,16,1024]{2,1,0:T(8,128)(2,1)S(1)} %collective-permute-done.near, ...), custom_call_target="tpu_custom_call" | custom-call | tf_op jit(solution)/shard_map/forward/pallas_call | solution.py:564
  12.1 0.9 %transpose.29 = (bf16[1024,1024]{1,0:T(8,128)(2,1)S(1)}, f32[100,512]{1,0:T(8,128)S(1)}, f32[2,100,512]{2,1,0:T(8,128)S(1)}) custom-call(bf16[1024,1024]{1,0:T(8,128)(2,1)S(1)} %get-tuple-element.57.refs_0_.refs_2_, f32[2,100,512]{2,1,0:T(8,128)S(1)} %get-tuple-element.58.refs_1_.outputs, f32[100,512]{1,0:T(8,128)S(1)} %get-tuple-element.59.refs_2_), custom_call_target="tpu_custom_call" | custom-call | flops 1 | bytes 1 | tf_op jit(solution)/shard_map/transpose/pallas_call | solution.py:584
  13.0 0.9 %collective-permute-done.2.others = f32[2,100,512]{2,1,0:T(8,128)S(1)} collective-permute-done((f32[2,100,512]{2,1,0:T(8,128)S(1)}, f32[2,100,512]{2,1,0:T(8,128)S(1)}, u32[]{:S(2)}, u32[]{:S(2)}) %collective-permute-start.2) | collective-permute-done | bytes 409632 | tf_op jit(solution)/shard_map/ppermute | solution.py:25
  13.9 2.1 %score.1 = (f32[1,1]{1,0:T(1,128)}, bf16[1024,1024]{1,0:T(8,128)(2,1)S(1)}, bf16[128,1024]{1,0:T(8,128)(2,1)S(1)}, bf16[256,1024]{1,0:T(8,128)(2,1)S(1)}) custom-call(f32[2,100,512]{2,1,0:T(8,128)S(1)} %get-tuple-element.58.refs_1_.outputs, f32[2,100,512]{2,1,0:T(8,128)S(1)} %collective-permute-done.2.others, f32[100,512]{1,0:T(8,128)S(1)} %get-tuple-element.61.own_score, ...), custom_call_target="tpu_custom_call" | custom-call | tf_op jit(solution)/shard_map/score/pallas_call | solution.py:597
  16.2 1.4 %sent.1 = (bf16[256,1280]{1,0:T(8,128)(2,1)S(1)}, f32[256,256]{1,0:T(8,128)S(1)}) custom-call(bf16[1024,1024]{1,0:T(8,128)(2,1)S(1)} %get-tuple-element.60.normed_t.refs_0_, bf16[1024,1024]{1,0:T(8,128)(2,1)S(1)} %get-tuple-element.65.refs_1_.refs_0_, bf16[128,1024]{1,0:T(8,128)(2,1)S(1)} %get-tuple-element.66.refs_2_, ...), custom_call_target="tpu_custom_call" | custom-call | flops 1 | bytes 1 | tf_op jit(solution)/shard_map/sent/pallas_call | solution.py:628
  18.0 0.7 product.2
  18.7 4.3 %collective-permute-start.6 = (bf16[128,1024]{1,0:T(8,128)(2,1)S(1)}, bf16[128,1024]{1,0:T(8,128)(2,1)S(1)}, u32[]{:S(2)}, u32[]{:S(2)}) collective-permute-start(bf16[128,1024]{1,0:T(8,128)(2,1)S(1)} %get-tuple-element.70), channel_id=1, source_target_pairs={{0,2},{1,5},{2,0},{3,7},{4,6},{5,1},{6,4},{7,3},{8,10},{9,13},{10,... | collective-permute-start | bytes 786440 | tf_op jit(solution)/shard_map/ppermute | solution.py:34
  23.1 0.7 product.3
  23.8 2.9 %backward.2 = (f32[8,1024]{1,0:T(8,128)S(1)}, f32[64,1024]{1,0:T(8,128)S(1)}, bf16[16,1024]{1,0:T(8,128)(2,1)S(1)}, bf16[16,1024]{1,0:T(8,128)(2,1)S(1)}) custom-call(bf16[1024,1024]{1,0:T(8,128)(2,1)S(1)} %get-tuple-element.65.refs_1_.refs_0_, bf16[1024,1024]{1,0:T(8,128)(2,1)S(1)} %get-tuple-element.55.hidden_weight.refs_1_, ...), custom_call_target="tpu_custom_call" | custom-call | flops 1 | bytes 1 | tf_op jit(solution)/shard_map/backward/pallas_call | solution.py:649
  26.7 0.7 %collective-permute-done.6 = bf16[128,1024]{1,0:T(8,128)(2,1)S(1)} collective-permute-done((bf16[128,1024]{1,0:T(8,128)(2,1)S(1)}, bf16[128,1024]{1,0:T(8,128)(2,1)S(1)}, u32[]{:S(2)}, u32[]{:S(2)}) %collective-permute-start.6) | collective-permute-done | bytes 262176 | tf_op jit(solution)/shard_map/ppermute | solution.py:34
  27.5 3.5 %collective-permute-start.13 = (bf16[64,1024]{1,0:T(8,128)(2,1)S(1)}, bf16[64,1024]{1,0:T(8,128)(2,1)S(1)}, u32[]{:S(2)}, u32[]{:S(2)}) collective-permute-start(bf16[64,1024]{1,0:T(8,128)(2,1)S(1)} %slice.77), channel_id=1, source_target_pairs={{0,4},{1,3},{2,6},{3,1},{4,0},{5,7},{6,2},{7,5},{8,12},{9,11},{10,... | collective-permute-start | bytes 393224 | tf_op jit(solution)/shard_map/ppermute | solution.py:34
  31.5 3.5 %backward.3 = (bf16[8,1280]{1,0:T(8,128)(2,1)S(1)}, f32[64,1024]{1,0:T(8,128)S(1)}, bf16[16,1024]{1,0:T(8,128)(2,1)S(1)}, bf16[16,1024]{1,0:T(8,128)(2,1)S(1)}) custom-call(bf16[1024,1024]{1,0:T(8,128)(2,1)S(1)} %get-tuple-element.65.refs_1_.refs_0_, bf16[1024,1024]{1,0:T(8,128)(2,1)S(1)} %get-tuple-element.55.hidden_weight.refs_1_, ...), custom_call_target="tpu_custom_call" | custom-call | flops 1 | bytes 1 | tf_op jit(solution)/shard_map/backward/pallas_call | solution.py:649
  35.4 3.1 %collective-permute-start.14 = (bf16[64,1024]{1,0:T(8,128)(2,1)S(1)}, bf16[64,1024]{1,0:T(8,128)(2,1)S(1)}, u32[]{:S(2)}, u32[]{:S(2)}) collective-permute-start(bf16[64,1024]{1,0:T(8,128)(2,1)S(1)} %add_convert_fusion.5), channel_id=1, source_target_pairs={{0,8},{1,9},{2,10},{3,11},{4,12},{5,13},{6,14},{7,15},{8,0},{9,1},... | collective-permute-start | bytes 393224 | tf_op jit(solution)/shard_map/ppermute | solution.py:34
  38.7 1.7 %collective-permute-start.7 = (bf16[72,1280]{1,0:T(8,128)(2,1)S(1)}, bf16[72,1280]{1,0:T(8,128)(2,1)S(1)}, u32[]{:S(2)}, u32[]{:S(2)}) collective-permute-start(bf16[72,1280]{1,0:T(8,128)(2,1)S(1)} %pad_maximum_fusion.4), channel_id=1, source_target_pairs={{0,4},{1,3},{2,6},{3,1},{4,0},{5,7},{6,2},{7,5},{8,12},{9,11},{10,... | collective-permute-start | bytes 552968 | tf_op jit(solution)/shard_map/ppermute | solution.py:34
  40.4 2.8 %collective-permute-done.14 = bf16[64,1024]{1,0:T(8,128)(2,1)S(1)} collective-permute-done((bf16[64,1024]{1,0:T(8,128)(2,1)S(1)}, bf16[64,1024]{1,0:T(8,128)(2,1)S(1)}, u32[]{:S(2)}, u32[]{:S(2)}) %collective-permute-start.14) | collective-permute-done | bytes 131104 | tf_op jit(solution)/shard_map/ppermute | solution.py:34
  43.2 0.9 %collective-permute-start.15 = (bf16[64,1024]{1,0:T(8,128)(2,1)S(1)}, bf16[64,1024]{1,0:T(8,128)(2,1)S(1)}, u32[]{:S(2)}, u32[]{:S(2)}) collective-permute-start(bf16[64,1024]{1,0:T(8,128)(2,1)S(1)} %add_convert_fusion.4), channel_id=1, source_target_pairs={{0,4},{1,3},{2,6},{3,1},{4,0},{5,7},{6,2},{7,5},{8,12},{9,11},{10,... | collective-permute-start | bytes 393224 | tf_op jit(solution)/shard_map/ppermute | solution.py:34
  44.5 3.2 %collective-permute-start.8 = (bf16[72,1280]{1,0:T(8,128)(2,1)S(1)}, bf16[72,1280]{1,0:T(8,128)(2,1)S(1)}, u32[]{:S(2)}, u32[]{:S(2)}) collective-permute-start(bf16[72,1280]{1,0:T(8,128)(2,1)S(1)} %pad_maximum_fusion.5), channel_id=1, source_target_pairs={{0,8},{1,9},{2,10},{3,11},{4,12},{5,13},{6,14},{7,15},{8,0},{9,1},... | collective-permute-start | bytes 552968 | tf_op jit(solution)/shard_map/ppermute | solution.py:34
  47.7 0.6 collective-permute-done.15
  48.3 2.7 %collective-permute-start.16 = (bf16[128,1024]{1,0:T(8,128)(2,1)S(1)}, bf16[128,1024]{1,0:T(8,128)(2,1)S(1)}, u32[]{:S(2)}, u32[]{:S(2)}) collective-permute-start(bf16[128,1024]{1,0:T(8,128)(2,1)S(1)} %pad_maximum_fusion.3), channel_id=1, source_target_pairs={{0,2},{1,5},{2,0},{3,7},{4,6},{5,1},{6,4},{7,3},{8,10},{9,13},{10,... | collective-permute-start | bytes 786440 | tf_op jit(solution)/shard_map/ppermute | solution.py:34
  51.1 2.8 %collective-permute-done.8 = bf16[72,1280]{1,0:T(8,128)(2,1)S(1)} collective-permute-done((bf16[72,1280]{1,0:T(8,128)(2,1)S(1)}, bf16[72,1280]{1,0:T(8,128)(2,1)S(1)}, u32[]{:S(2)}, u32[]{:S(2)}) %collective-permute-start.8) | collective-permute-done | bytes 184352 | tf_op jit(solution)/shard_map/ppermute | solution.py:34
  53.9 1.6 %collective-permute-start.9 = (bf16[64,1280]{1,0:T(8,128)(2,1)S(1)}, bf16[64,1280]{1,0:T(8,128)(2,1)S(1)}, u32[]{:S(2)}, u32[]{:S(2)}) collective-permute-start(bf16[64,1280]{1,0:T(8,128)(2,1)S(1)} %add_convert_fusion.2), channel_id=1, source_target_pairs={{0,4},{1,3},{2,6},{3,1},{4,0},{5,7},{6,2},{7,5},{8,12},{9,11},{10,... | collective-permute-start | bytes 491528 | tf_op jit(solution)/shard_map/ppermute | solution.py:34
  55.5 3.7 %collective-permute-done.9 = bf16[64,1280]{1,0:T(8,128)(2,1)S(1)} collective-permute-done((bf16[64,1280]{1,0:T(8,128)(2,1)S(1)}, bf16[64,1280]{1,0:T(8,128)(2,1)S(1)}, u32[]{:S(2)}, u32[]{:S(2)}) %collective-permute-start.9) | collective-permute-done | bytes 163872 | tf_op jit(solution)/shard_map/ppermute | solution.py:34
  59.4 1.6 %collective-permute-start.10 = (bf16[136,1280]{1,0:T(8,128)(2,1)S(1)}, bf16[136,1280]{1,0:T(8,128)(2,1)S(1)}, u32[]{:S(2)}, u32[]{:S(2)}) collective-permute-start(bf16[136,1280]{1,0:T(8,128)(2,1)S(1)} %concatenate.29), channel_id=1, source_target_pairs={{0,2},{1,5},{2,0},{3,7},{4,6},{5,1},{6,4},{7,3},{8,10},{9,13},{10,... | collective-permute-start | bytes 1044488 | tf_op jit(solution)/shard_map/ppermute | solution.py:34
  61.2 0.7 collective-permute-start.19
  61.9 3.5 %collective-permute-start.18 = (bf16[2,16,1024]{2,1,0:T(8,128)(2,1)S(1)}, bf16[2,16,1024]{2,1,0:T(8,128)(2,1)S(1)}, u32[]{:S(2)}, u32[]{:S(2)}) collective-permute-start(bf16[2,16,1024]{2,1,0:T(8,128)(2,1)S(1)} %pad_maximum_fusion.6), channel_id=1, source_target_pairs={{0,2},{4,6},{8,10},{12,14},{2,0},{6,4},{10,8},{14,12},{1,3},{5,7},... | collective-permute-start | bytes 196616 | tf_op jit(solution)/shard_map/ppermute | solution.py:21
  65.3 2.6 %collective-permute-done.10 = bf16[136,1280]{1,0:T(8,128)(2,1)S(1)} collective-permute-done((bf16[136,1280]{1,0:T(8,128)(2,1)S(1)}, bf16[136,1280]{1,0:T(8,128)(2,1)S(1)}, u32[]{:S(2)}, u32[]{:S(2)}) %collective-permute-start.10) | collective-permute-done | bytes 348192 | tf_op jit(solution)/shard_map/ppermute | solution.py:34
  68.7 2.0 %write.1 = (f32[1024,1024]{1,0:T(8,128)}, f32[2,64,1024]{2,1,0:T(8,128)}) custom-call(bf16[256,1024]{1,0:T(8,128)(2,1)S(1)} %pad_maximum_fusion.1.refs_0_, bf16[256,1024]{1,0:T(8,128)(2,1)S(1)} %collective-permute-done.17.refs_1_, bf16[256,1280]{1,0:T(8,128)(2,1)S(1)} %pad_maximum_fusion.refs_2_.refs_0_, f32[64,1024]{1,0:T(8,128)S(1)} %get-tuple-element.79.refs_3_, ...), custom_call_target="tpu_custom_call" | custom-call | flops 1 | bytes 1 | tf_op jit(solution)/shard_map/write/pallas_call | solution.py:694
  70.7 1.3 %last_write.1 = (f32[1024,1024]{1,0:T(8,128)}, f32[100,1024]{1,0:T(8,128)}, f32[1,1024]{1,0:T(1,128)}, f32[1,1]{1,0:T(1,128)}) custom-call(bf16[256,1280]{1,0:T(8,128)(2,1)S(1)} %pad_maximum_fusion.refs_2_.refs_0_, bf16[256,1280]{1,0:T(8,128)(2,1)S(1)} %collective-permute-done.11.refs_1_, ...), custom_call_target="tpu_custom_call", output_to_operand_aliasing={{0}: (4, {})} | custom-call | tf_op jit(solution)/shard_map/last_write/pallas_call | solution.py:709
  (45 shorter events, 3.3 us)
Async XLA Ops:
  1.5 5.9 %collective-permute-start = (bf16[2,16,1024]{2,1,0:T(8,128)(2,1)S(1)}, bf16[2,16,1024]{2,1,0:T(8,128)(2,1)S(1)}, u32[]{:S(2)}, u32[]{:S(2)}) collective-permute-start(bf16[2,16,1024]{2,1,0:T(8,128)(2,1)S(1)} %get-tuple-element.106), channel_id=1, source_target_pairs={{0,2},{4,6},{8,10},{12,14},{2,0},{6,4},{10,8},{14,12},{1,3},{5,7},... | collective-permute-start | bytes 196616 | tf_op jit(solution)/shard_map/ppermute | solution.py:21
  4.6 2.9 %collective-permute-start.1 = (bf16[2,16,1024]{2,1,0:T(8,128)(2,1)S(1)}, bf16[2,16,1024]{2,1,0:T(8,128)(2,1)S(1)}, u32[]{:S(2)}, u32[]{:S(2)}) collective-permute-start(bf16[2,16,1024]{2,1,0:T(8,128)(2,1)S(1)} %get-tuple-element.105), channel_id=1, source_target_pairs={{2,4},{6,8},{10,12},{4,2},{8,6},{12,10},{3,5},{7,9},{11,13},{5,3},... | collective-permute-start | bytes 196616 | tf_op jit(solution)/shard_map/ppermute | solution.py:21
  12.1 1.8 %collective-permute-start.2 = (f32[2,100,512]{2,1,0:T(8,128)S(1)}, f32[2,100,512]{2,1,0:T(8,128)S(1)}, u32[]{:S(2)}, u32[]{:S(2)}) collective-permute-start(f32[2,100,512]{2,1,0:T(8,128)S(1)} %get-tuple-element.58.refs_1_.outputs), channel_id=1, source_target_pairs={{0,1},{1,0},{2,3},{3,2},{4,5},{5,4},{6,7},{7,6},{8,9},{9,8},{10,11... | collective-permute-start | bytes 1228808 | tf_op jit(solution)/shard_map/ppermute | solution.py:25
  16.0 2.0 %collective-permute-start.4 = (bf16[256,1024]{1,0:T(8,128)(2,1)S(1)}, bf16[256,1024]{1,0:T(8,128)(2,1)S(1)}, u32[]{:S(2)}, u32[]{:S(2)}) collective-permute-start(bf16[256,1024]{1,0:T(8,128)(2,1)S(1)} %get-tuple-element.69), channel_id=1, source_target_pairs={{0,1},{1,0},{2,3},{3,2},{4,5},{5,4},{6,7},{7,6},{8,9},{9,8},{10,11... | collective-permute-start | bytes 1572872 | tf_op jit(solution)/shard_map/ppermute | solution.py:25
  17.6 5.5 %collective-permute-start.3 = (bf16[256,1280]{1,0:T(8,128)(2,1)S(1)}, bf16[256,1280]{1,0:T(8,128)(2,1)S(1)}, u32[]{:S(2)}, u32[]{:S(2)}) collective-permute-start(bf16[256,1280]{1,0:T(8,128)(2,1)S(1)} %get-tuple-element.68), channel_id=1, source_target_pairs={{0,1},{1,0},{2,3},{3,2},{4,5},{5,4},{6,7},{7,6},{8,9},{9,8},{10,11... | collective-permute-start | bytes 1966088 | tf_op jit(solution)/shard_map/ppermute | solution.py:25
  18.7 8.7 %collective-permute-start.6 = (bf16[128,1024]{1,0:T(8,128)(2,1)S(1)}, bf16[128,1024]{1,0:T(8,128)(2,1)S(1)}, u32[]{:S(2)}, u32[]{:S(2)}) collective-permute-start(bf16[128,1024]{1,0:T(8,128)(2,1)S(1)} %get-tuple-element.70), channel_id=1, source_target_pairs={{0,2},{1,5},{2,0},{3,7},{4,6},{5,1},{6,4},{7,3},{8,10},{9,13},{10,... | collective-permute-start | bytes 786440 | tf_op jit(solution)/shard_map/ppermute | solution.py:34
  27.5 7.9 %collective-permute-start.13 = (bf16[64,1024]{1,0:T(8,128)(2,1)S(1)}, bf16[64,1024]{1,0:T(8,128)(2,1)S(1)}, u32[]{:S(2)}, u32[]{:S(2)}) collective-permute-start(bf16[64,1024]{1,0:T(8,128)(2,1)S(1)} %slice.77), channel_id=1, source_target_pairs={{0,4},{1,3},{2,6},{3,1},{4,0},{5,7},{6,2},{7,5},{8,12},{9,11},{10,... | collective-permute-start | bytes 393224 | tf_op jit(solution)/shard_map/ppermute | solution.py:34
  31.0 7.5 %collective-permute-start.5 = (bf16[128,1280]{1,0:T(8,128)(2,1)S(1)}, bf16[128,1280]{1,0:T(8,128)(2,1)S(1)}, u32[]{:S(2)}, u32[]{:S(2)}) collective-permute-start(bf16[128,1280]{1,0:T(8,128)(2,1)S(1)} %get-tuple-element.74), channel_id=1, source_target_pairs={{0,2},{1,5},{2,0},{3,7},{4,6},{5,1},{6,4},{7,3},{8,10},{9,13},{10,... | collective-permute-start | bytes 983048 | tf_op jit(solution)/shard_map/ppermute | solution.py:34
  35.4 7.7 %collective-permute-start.14 = (bf16[64,1024]{1,0:T(8,128)(2,1)S(1)}, bf16[64,1024]{1,0:T(8,128)(2,1)S(1)}, u32[]{:S(2)}, u32[]{:S(2)}) collective-permute-start(bf16[64,1024]{1,0:T(8,128)(2,1)S(1)} %add_convert_fusion.5), channel_id=1, source_target_pairs={{0,8},{1,9},{2,10},{3,11},{4,12},{5,13},{6,14},{7,15},{8,0},{9,1},... | collective-permute-start | bytes 393224 | tf_op jit(solution)/shard_map/ppermute | solution.py:34
  38.7 5.7 %collective-permute-start.7 = (bf16[72,1280]{1,0:T(8,128)(2,1)S(1)}, bf16[72,1280]{1,0:T(8,128)(2,1)S(1)}, u32[]{:S(2)}, u32[]{:S(2)}) collective-permute-start(bf16[72,1280]{1,0:T(8,128)(2,1)S(1)} %pad_maximum_fusion.4), channel_id=1, source_target_pairs={{0,4},{1,3},{2,6},{3,1},{4,0},{5,7},{6,2},{7,5},{8,12},{9,11},{10,... | collective-permute-start | bytes 552968 | tf_op jit(solution)/shard_map/ppermute | solution.py:34
  43.2 5.1 %collective-permute-start.15 = (bf16[64,1024]{1,0:T(8,128)(2,1)S(1)}, bf16[64,1024]{1,0:T(8,128)(2,1)S(1)}, u32[]{:S(2)}, u32[]{:S(2)}) collective-permute-start(bf16[64,1024]{1,0:T(8,128)(2,1)S(1)} %add_convert_fusion.4), channel_id=1, source_target_pairs={{0,4},{1,3},{2,6},{3,1},{4,0},{5,7},{6,2},{7,5},{8,12},{9,11},{10,... | collective-permute-start | bytes 393224 | tf_op jit(solution)/shard_map/ppermute | solution.py:34
  44.5 9.3 %collective-permute-start.8 = (bf16[72,1280]{1,0:T(8,128)(2,1)S(1)}, bf16[72,1280]{1,0:T(8,128)(2,1)S(1)}, u32[]{:S(2)}, u32[]{:S(2)}) collective-permute-start(bf16[72,1280]{1,0:T(8,128)(2,1)S(1)} %pad_maximum_fusion.5), channel_id=1, source_target_pairs={{0,8},{1,9},{2,10},{3,11},{4,12},{5,13},{6,14},{7,15},{8,0},{9,1},... | collective-permute-start | bytes 552968 | tf_op jit(solution)/shard_map/ppermute | solution.py:34
  48.3 12.7 %collective-permute-start.16 = (bf16[128,1024]{1,0:T(8,128)(2,1)S(1)}, bf16[128,1024]{1,0:T(8,128)(2,1)S(1)}, u32[]{:S(2)}, u32[]{:S(2)}) collective-permute-start(bf16[128,1024]{1,0:T(8,128)(2,1)S(1)} %pad_maximum_fusion.3), channel_id=1, source_target_pairs={{0,2},{1,5},{2,0},{3,7},{4,6},{5,1},{6,4},{7,3},{8,10},{9,13},{10,... | collective-permute-start | bytes 786440 | tf_op jit(solution)/shard_map/ppermute | solution.py:34
  53.9 5.4 %collective-permute-start.9 = (bf16[64,1280]{1,0:T(8,128)(2,1)S(1)}, bf16[64,1280]{1,0:T(8,128)(2,1)S(1)}, u32[]{:S(2)}, u32[]{:S(2)}) collective-permute-start(bf16[64,1280]{1,0:T(8,128)(2,1)S(1)} %add_convert_fusion.2), channel_id=1, source_target_pairs={{0,4},{1,3},{2,6},{3,1},{4,0},{5,7},{6,2},{7,5},{8,12},{9,11},{10,... | collective-permute-start | bytes 491528 | tf_op jit(solution)/shard_map/ppermute | solution.py:34
  59.4 8.5 %collective-permute-start.10 = (bf16[136,1280]{1,0:T(8,128)(2,1)S(1)}, bf16[136,1280]{1,0:T(8,128)(2,1)S(1)}, u32[]{:S(2)}, u32[]{:S(2)}) collective-permute-start(bf16[136,1280]{1,0:T(8,128)(2,1)S(1)} %concatenate.29), channel_id=1, source_target_pairs={{0,2},{1,5},{2,0},{3,7},{4,6},{5,1},{6,4},{7,3},{8,10},{9,13},{10,... | collective-permute-start | bytes 1044488 | tf_op jit(solution)/shard_map/ppermute | solution.py:34
  61.1 7.6 %collective-permute-start.17 = (bf16[256,1024]{1,0:T(8,128)(2,1)S(1)}, bf16[256,1024]{1,0:T(8,128)(2,1)S(1)}, u32[]{:S(2)}, u32[]{:S(2)}) collective-permute-start(bf16[256,1024]{1,0:T(8,128)(2,1)S(1)} %pad_maximum_fusion.1.refs_0_), channel_id=1, source_target_pairs={{0,1},{1,0},{2,3},{3,2},{4,5},{5,4},{6,7},{7,6},{8,9},{9,8},{10,11... | collective-permute-start | bytes 1572872 | tf_op jit(solution)/shard_map/ppermute | solution.py:25
  61.2 7.6 %collective-permute-start.19 = (bf16[2,16,1024]{2,1,0:T(8,128)(2,1)S(1)}, bf16[2,16,1024]{2,1,0:T(8,128)(2,1)S(1)}, u32[]{:S(2)}, u32[]{:S(2)}) collective-permute-start(bf16[2,16,1024]{2,1,0:T(8,128)(2,1)S(1)} %pad_maximum_fusion.7), channel_id=1, source_target_pairs={{2,4},{6,8},{10,12},{4,2},{8,6},{12,10},{3,5},{7,9},{11,13},{5,3},... | collective-permute-start | bytes 196616 | tf_op jit(solution)/shard_map/ppermute | solution.py:21
  61.9 6.9 %collective-permute-start.18 = (bf16[2,16,1024]{2,1,0:T(8,128)(2,1)S(1)}, bf16[2,16,1024]{2,1,0:T(8,128)(2,1)S(1)}, u32[]{:S(2)}, u32[]{:S(2)}) collective-permute-start(bf16[2,16,1024]{2,1,0:T(8,128)(2,1)S(1)} %pad_maximum_fusion.6), channel_id=1, source_target_pairs={{0,2},{4,6},{8,10},{12,14},{2,0},{6,4},{10,8},{14,12},{1,3},{5,7},... | collective-permute-start | bytes 196616 | tf_op jit(solution)/shard_map/ppermute | solution.py:21
  68.0 2.7 %collective-permute-start.11 = (bf16[256,1280]{1,0:T(8,128)(2,1)S(1)}, bf16[256,1280]{1,0:T(8,128)(2,1)S(1)}, u32[]{:S(2)}, u32[]{:S(2)}) collective-permute-start(bf16[256,1280]{1,0:T(8,128)(2,1)S(1)} %pad_maximum_fusion.refs_2_.refs_0_), channel_id=1, source_target_pairs={{0,1},{1,0},{2,3},{3,2},{4,5},{5,4},{6,7},{7,6},{8,9},{9,8},{10,11... | collective-permute-start | bytes 1966088 | tf_op jit(solution)/shard_map/ppermute | solution.py:25
  68.2 2.5 %collective-permute-start.12 = (bf16[8,1280]{1,0:T(8,128)(2,1)S(1)}, bf16[8,1280]{1,0:T(8,128)(2,1)S(1)}, u32[]{:S(2)}, u32[]{:S(2)}) collective-permute-start(bf16[8,1280]{1,0:T(8,128)(2,1)S(1)} %pad_maximum_fusion.8.refs_2_), channel_id=1, source_target_pairs={{0,1},{1,0},{2,3},{3,2},{4,5},{5,4},{6,7},{7,6},{8,9},{9,8},{10,11... | collective-permute-start | bytes 61448 | tf_op jit(solution)/shard_map/ppermute | solution.py:25
